TPU v7x, 32 devices: a whole 2x2x4 slice. The times are simulated.
32 devices in a mesh: seq: 8 (over z, x), fsdp: 4 (over y, core).
Axes of the slice: x: 2, y: 2, z: 4, core: 2. Of those that a mesh axis runs over, the one named last changes fastest.
Arguments:
- tokens: bfloat16 [4, 4096, 1536], P('fsdp', 'seq'), may hold values from -6 to 6
- norm_gain: float32 [1536], replicated, may hold values from 0.25 to 1.75
- w_in: bfloat16 [1536, 6448], P('fsdp'), may hold values from -0.15625 to 0.15625
- conv_weight: float32 [4, 3328], replicated, may hold values from -3 to 3
- conv_bias: float32 [3328], replicated, may hold values from -1.5 to 1.5
- dt_bias: float32 [48], replicated, may hold values from -6 to -2
- a_log: float32 [48], replicated, may hold values from -4 to 1
- skip_gain: float32 [48], replicated, may hold values from 0.5 to 1.5
- out_gain: float32 [3072], replicated, may hold values from 0.25 to 1.75
- w_out: bfloat16 [3072, 1536], P('fsdp'), may hold values from -0.109375 to 0.109375
- cotangent: bfloat16 [4, 4096, 1536], P('fsdp', 'seq'), may hold values from -6 to 6
Outputs:
- block_out: float32 [4, 4096, 1536], P('fsdp', 'seq')
- d_tokens: float32 [4, 4096, 1536], P('fsdp', 'seq')
- d_norm_gain: float32 [1536], replicated
- d_w_in: float32 [1536, 6448], P(('seq', 'fsdp'))
- d_conv_weight: float32 [4, 3328], replicated
- d_conv_bias: float32 [3328], replicated
- d_dt_bias: float32 [48], replicated
- d_a_log: float32 [48], replicated
- d_skip_gain: float32 [48], replicated
- d_out_gain: float32 [3072], replicated
- d_w_out: float32 [3072, 1536], P(('seq', 'fsdp'))
All inputs are finite; a program needn't handle non-finite values.
Results may differ from a plain program's by a relative error of at most 0.0089.
Values may be sent and summed in bfloat16 or wider, within the bound.
No kernel may reach another device: no remote copies, remote signals or barrier semaphores. Data moves between devices by JAX's collectives and lax.ppermute only.
A program may use at most 256 MiB of HBM per device.

v0:
```python
import jax
import jax.numpy as jnp
from jax import lax
from jax.sharding import PartitionSpec as P

HEADS = 48
HEAD_DIM = 64
STATE = 128
KW = 4
SPAN = 256
INNER = 3072


EPSILON = 1e-05
HIGHEST = lax.Precision.HIGHEST
CONTRACT_ROWS = (((0,), (0,)), ((), ()))
CONTRACT_COLS = (((1,), (1,)), ((), ()))


def pre_norm(values, gain_vec):
    inverse = lax.rsqrt(jnp.mean(values * values, axis=-1, keepdims=True) + EPSILON)
    return values * inverse * gain_vec


def gate_norm(mixed_in, gate_in, gain_vec):
    gated = mixed_in * jax.nn.silu(gate_in)
    inverse = lax.rsqrt(jnp.mean(gated * gated, axis=-1, keepdims=True) + EPSILON)
    return gated * inverse * gain_vec


def causal_conv(values, kernel, offset):
    width_k = kernel.shape[0]
    length = values.shape[0]
    padded = jnp.pad(values, ((width_k - 1, 0), (0, 0)))
    result = offset + kernel[0] * padded[0:length]
    for tap_idx in range(1, width_k):
        result = result + kernel[tap_idx] * padded[tap_idx : tap_idx + length]
    return result


def head_mix(
    x_pre, bc_pre, dt_raw, conv_x_w, conv_x_b, conv_bc_w, conv_bc_b, dt_shift, log_rate, skip_vec
):
    length = x_pre.shape[0]
    head_count = dt_raw.shape[1]
    head_width = x_pre.shape[1] // head_count
    x_act = jax.nn.silu(causal_conv(x_pre, conv_x_w, conv_x_b))
    bc_act = jax.nn.silu(causal_conv(bc_pre, conv_bc_w, conv_bc_b))
    state_width = bc_act.shape[1] // 2
    step_len = jax.nn.softplus(dt_raw + dt_shift)
    decay_rate = -jnp.exp(log_rate)
    block_count = length // SPAN
    x_blocks = x_act.reshape(block_count, SPAN, head_count, head_width)
    b_blocks = bc_act[:, :state_width].reshape(block_count, SPAN, state_width)
    c_blocks = bc_act[:, state_width:].reshape(block_count, SPAN, state_width)
    d_blocks = step_len.reshape(block_count, SPAN, head_count)
    lower_mask = (jnp.arange(SPAN)[:, None] >= jnp.arange(SPAN)[None, :])[:, :, None]

    def one_block(carry_state, pieces):
        x_blk, b_blk, c_blk, d_blk = pieces
        cumulative = jnp.cumsum(d_blk * decay_rate, axis=0)
        scores = jnp.dot(c_blk, b_blk.T, precision=HIGHEST)
        differ = cumulative[:, None, :] - cumulative[None, :, :]
        weights = (
            scores[:, :, None] * jnp.exp(jnp.where(lower_mask, differ, -1e30)) * d_blk[None, :, :]
        )
        inside = jnp.einsum("tsh,shp->thp", weights, x_blk, precision=HIGHEST)
        earlier = (
            jnp.einsum("tn,hnp->thp", c_blk, carry_state, precision=HIGHEST)
            * jnp.exp(cumulative)[:, :, None]
        )
        remain = jnp.exp(cumulative[-1:, :] - cumulative) * d_blk
        fresh_part = jnp.einsum("sn,shp->hnp", b_blk, x_blk * remain[:, :, None], precision=HIGHEST)
        new_state = jnp.exp(cumulative[-1])[:, None, None] * carry_state + fresh_part
        return (new_state, inside + earlier)

    start_state = jnp.zeros((head_count, state_width, head_width), x_act.dtype)
    _, outputs = lax.scan(
        jax.checkpoint(one_block), start_state, (x_blocks, b_blocks, c_blocks, d_blocks)
    )
    outputs = outputs.reshape(length, head_count, head_width) + skip_vec[:, None] * x_act.reshape(
        length, head_count, head_width
    )
    return outputs.reshape(length, head_count * head_width)


def on_device(
    tokens,
    norm_gain,
    w_in,
    conv_weight,
    conv_bias,
    dt_bias,
    a_log,
    skip_gain,
    out_gain,
    w_out,
    cotangent,
):
    seq_count = lax.axis_size("seq")
    seq_index = lax.axis_index("seq")
    local_heads = HEADS // seq_count
    local_width = local_heads * HEAD_DIM
    values = tokens[0].astype(jnp.float32)
    normed_f, pre_back = jax.vjp(pre_norm, values, norm_gain)
    normed = normed_f.astype(jnp.bfloat16)
    left_part = normed
    projected = jnp.dot(
        left_part,
        lax.all_gather(w_in, "fsdp", axis=0, tiled=True),
        preferred_element_type=jnp.float32,
    )
    projected = projected.astype(jnp.bfloat16)
    gate_in = projected[:, :INNER]
    x_pre = projected[:, INNER : 2 * INNER]
    bc_pre = projected[:, 2 * INNER : 2 * INNER + 2 * STATE]
    dt_raw = projected[:, 2 * INNER + 2 * STATE :]
    x_heads, dt_heads = (
        lax.all_to_all(x_pre, "seq", split_axis=1, concat_axis=0, tiled=True),
        lax.all_to_all(dt_raw, "seq", split_axis=1, concat_axis=0, tiled=True),
    )
    bc_full = lax.all_gather(bc_pre, "seq", axis=0, tiled=True)
    channel_start = seq_index * local_width
    head_start = seq_index * local_heads
    local_params = (
        lax.dynamic_slice_in_dim(conv_weight[:, :INNER], channel_start, local_width, 1),
        lax.dynamic_slice_in_dim(conv_bias[:INNER], channel_start, local_width, 0),
        conv_weight[:, INNER:],
        conv_bias[INNER:],
        lax.dynamic_slice_in_dim(dt_bias, head_start, local_heads, 0),
        lax.dynamic_slice_in_dim(a_log, head_start, local_heads, 0),
        lax.dynamic_slice_in_dim(skip_gain, head_start, local_heads, 0),
    )
    mixed_out, head_back = jax.vjp(
        head_mix,
        x_heads.astype(jnp.float32),
        bc_full.astype(jnp.float32),
        dt_heads.astype(jnp.float32),
        *local_params
    )
    mixed_tok = lax.all_to_all(
        mixed_out.astype(jnp.bfloat16), "seq", split_axis=0, concat_axis=1, tiled=True
    )
    normed_out_f, norm_back = jax.vjp(
        gate_norm, mixed_tok.astype(jnp.float32), gate_in.astype(jnp.float32), out_gain
    )
    normed_out = normed_out_f.astype(jnp.bfloat16)
    left_part = normed_out
    branch_out = jnp.dot(
        left_part,
        lax.all_gather(w_out, "fsdp", axis=0, tiled=True),
        preferred_element_type=jnp.float32,
    )
    result = values + branch_out
    cotan_rows = cotangent[0]
    left_part = normed_out
    d_w_out = lax.psum_scatter(
        lax.dot_general(left_part, cotan_rows, CONTRACT_ROWS, preferred_element_type=jnp.float32),
        ("seq", "fsdp"),
        scatter_dimension=0,
        tiled=True,
    )
    d_normed_out = lax.dot_general(
        cotan_rows,
        lax.all_gather(w_out, "fsdp", axis=0, tiled=True),
        CONTRACT_COLS,
        preferred_element_type=jnp.float32,
    )
    d_mixed_tok, d_gate, d_gain_out = norm_back(d_normed_out)
    d_heads = lax.all_to_all(
        d_mixed_tok.astype(jnp.bfloat16), "seq", split_axis=1, concat_axis=0, tiled=True
    )
    head_grads = head_back(d_heads.astype(jnp.float32))
    (
        d_x_heads,
        d_bc_full,
        d_dt_heads,
        d_conv_xw,
        d_conv_xb,
        d_conv_bcw,
        d_conv_bcb,
        d_dt_local,
        d_alog_local,
        d_skip_local,
    ) = head_grads
    d_x_tok, d_dt_tok = (
        lax.all_to_all(
            d_x_heads.astype(jnp.bfloat16), "seq", split_axis=0, concat_axis=1, tiled=True
        ),
        lax.all_to_all(
            d_dt_heads.astype(jnp.bfloat16), "seq", split_axis=0, concat_axis=1, tiled=True
        ),
    )
    d_bc_tok = lax.psum_scatter(d_bc_full, "seq", scatter_dimension=0, tiled=True)
    d_projected = jnp.concatenate(
        [d_gate.astype(jnp.bfloat16), d_x_tok, d_bc_tok.astype(jnp.bfloat16), d_dt_tok], axis=1
    )
    left_part = normed
    d_w_in = lax.psum_scatter(
        lax.dot_general(left_part, d_projected, CONTRACT_ROWS, preferred_element_type=jnp.float32),
        ("seq", "fsdp"),
        scatter_dimension=0,
        tiled=True,
    )
    d_normed = lax.dot_general(
        d_projected,
        lax.all_gather(w_in, "fsdp", axis=0, tiled=True),
        CONTRACT_COLS,
        preferred_element_type=jnp.float32,
    )
    d_values, d_gain_in = pre_back(d_normed)
    d_tokens = cotan_rows.astype(jnp.float32) + d_values
    conv_w_grad = jnp.concatenate(
        [
            lax.dynamic_update_slice_in_dim(
                jnp.zeros((KW, INNER), jnp.float32), d_conv_xw, channel_start, 1
            ),
            d_conv_bcw,
        ],
        axis=1,
    )
    conv_b_grad = jnp.concatenate(
        [
            lax.dynamic_update_slice_in_dim(
                jnp.zeros((INNER,), jnp.float32), d_conv_xb, channel_start, 0
            ),
            d_conv_bcb,
        ],
        axis=0,
    )
    dt_grad = lax.dynamic_update_slice_in_dim(
        jnp.zeros((HEADS,), jnp.float32), d_dt_local, head_start, 0
    )
    alog_grad = lax.dynamic_update_slice_in_dim(
        jnp.zeros((HEADS,), jnp.float32), d_alog_local, head_start, 0
    )
    skip_grad = lax.dynamic_update_slice_in_dim(
        jnp.zeros((HEADS,), jnp.float32), d_skip_local, head_start, 0
    )
    reduced = lax.psum(
        (d_gain_in, d_gain_out, conv_w_grad, conv_b_grad, dt_grad, alog_grad, skip_grad),
        ("seq", "fsdp"),
    )
    return (
        result[None],
        d_tokens[None],
        reduced[0],
        d_w_in,
        reduced[2],
        reduced[3],
        reduced[4],
        reduced[5],
        reduced[6],
        reduced[1],
        d_w_out,
    )


def solution(mesh):
    return jax.shard_map(
        on_device,
        mesh=mesh,
        in_specs=(
            P("fsdp", "seq", None),
            P(),
            P("fsdp", None),
            P(),
            P(),
            P(),
            P(),
            P(),
            P(),
            P("fsdp", None),
            P("fsdp", "seq", None),
        ),
        out_specs=(
            P("fsdp", "seq", None),
            P("fsdp", "seq", None),
            P(),
            P(("seq", "fsdp"), None),
            P(),
            P(),
            P(),
            P(),
            P(),
            P(),
            P(("seq", "fsdp"), None),
        ),
        check_vma=False,
    )
```

profile of v0, /device:TPU:0, one launch (start us, length us, event | category | flops | bytes accessed | tf_op | source)
XLA Modules:
  0.0 2404.2 jit_solution(4750977716097558571)
XLA Ops:
  9.5 127.7 %all-gather.4.cloned.1.call-done = bf16[1536,6448]{0,1:T(8,128)(2,1)} async-done(((bf16[384,6448]{0,1:T(8,128)(2,1)}), bf16[1536,6448]{0,1:T(8,128)(2,1)}) %all-gather.4.cloned.1.call-update) | async-done | bytes 19808272 | tf_op jit(solution)/shard_map/all_gather | solution.py:110
  137.2 15.2 convolution_convert_fusion
  183.4 72.2 %all-gather.6.cloned.1.call-done = bf16[4096,256]{0,1:T(8,128)(2,1)} async-done(((bf16[512,256]{0,1:T(8,128)(2,1)}), bf16[4096,256]{0,1:T(8,128)(2,1)}) %all-gather.6.cloned.1.call-update) | async-done | bytes 2097168 | tf_op jit(solution)/shard_map/all_gather | solution.py:122
  303.0 343.7 %while.41 = (s32[]{:T(128)}, f32[6,128,64]{1,2,0:T(8,128)S(1)}, f32[16,256,6,64]{1,0,3,2:T(8,128)}, f32[16,6,128,64]{2,3,1,0:T(8,128)}, f32[16,256,6]{1,2,0:T(8,...) while((s32[]{:T(128)}, f32[6,128,64]{1,2,0:T(8,128)S(1)}, ...), condition=%wide.region_4.5_spmd.clone, body=%wide.region_1.4_spmd.clone.sunk | while | flops 706859520 | bytes 5966715 | solution.py:78
  314.6 9.9 dynamic_update_slice.89
  336.1 9.9 dynamic_update_slice.89
  357.6 9.9 dynamic_update_slice.89
  379.0 9.9 dynamic_update_slice.89
  400.5 9.9 dynamic_update_slice.89
  422.0 9.9 dynamic_update_slice.89
  443.5 9.9 dynamic_update_slice.89
  465.0 9.9 dynamic_update_slice.89
  486.4 9.9 dynamic_update_slice.89
  507.9 9.9 dynamic_update_slice.89
  529.4 9.9 dynamic_update_slice.89
  572.3 9.9 dynamic_update_slice.89
  646.7 11.4 copy.401
  669.9 73.7 %all_to_all.87 = bf16[8,512,384]{2,1,0:T(8,128)(2,1)S(1)} all-to-all(bf16[8,512,384]{2,1,0:T(8,128)(2,1)S(1)} %bitcast.524), channel_id=1, replica_groups=mesh['seq'=8,'fsdp'=4] {'seq'}, dimensions={0} | all-to-all | bytes 6291456 | tf_op jit(solution)/shard_map/all_to_all | solution.py:141
  760.2 12.8 multiply_reduce_fusion.4
  787.3 70.3 %all-to-all-done.3 = bf16[512,8,384]{2,0,1:T(8,128)(2,1)S(1)} async-done(((bf16[512,8,384]{2,0,1:T(8,128)(2,1)}), bf16[512,8,384]{2,0,1:T(8,128)(2,1)S(1)}, u32[]{:S(2)}, u32[]{:S(2)}) %all-to-all-start.3) | async-done | bytes 3145760 | tf_op jit(solution)/shard_map/all_to_all | solution.py:170
  881.6 596.0 %while.42 = (s32[]{:T(128)}, f32[6]{0:T(128)S(1)}, f32[6,128,64]{1,2,0:T(8,128)S(1)}, f32[16,256,6,64]{1,0,3,2:T(8,128)}, f32[16,256,128]{2,1,0:T(8,128)}, /*ind...) while((s32[]{:T(128)}, f32[6]{0:T(128)S(1)}, ...), condition=%wide.region_21.22_spmd.clone, body=%wide.region_7.21_spmd.clone.sunk | while | flops 1669247488 | bytes 15717112 | solution.py:78
  905.3 9.9 dynamic_update_slice.93
  942.6 9.9 dynamic_update_slice.93
  979.8 9.9 dynamic_update_slice.93
  1017.0 9.9 dynamic_update_slice.93
  1054.2 9.9 dynamic_update_slice.93
  1091.4 9.9 dynamic_update_slice.93
  1128.6 9.9 dynamic_update_slice.93
  1165.8 9.9 dynamic_update_slice.93
  1203.1 9.9 dynamic_update_slice.93
  1240.3 9.9 dynamic_update_slice.93
  1277.5 9.9 dynamic_update_slice.93
  1314.8 9.9 dynamic_update_slice.93
  1352.0 9.9 dynamic_update_slice.93
  1389.2 9.9 dynamic_update_slice.93
  1426.5 9.9 dynamic_update_slice.93
  1463.7 9.9 dynamic_update_slice.93
  1486.9 12.2 multiply_reduce_fusion.13
  1513.0 11.4 copy.402
  1531.1 19.1 multiply_reduce_fusion.7
  1566.1 84.4 %all-to-all-done.4 = bf16[8,512,384]{2,1,0:T(8,128)(2,1)} async-done(((bf16[8,512,384]{2,1,0:T(8,128)(2,1)}), bf16[8,512,384]{2,1,0:T(8,128)(2,1)}, u32[]{:S(2)}, u32[]{:S(2)}) %all-to-all-start.4) | async-done | bytes 3145760 | tf_op jit(solution)/shard_map/all_to_all | solution.py:187
  1656.3 20.7 fusion.119
  1677.1 12.5 fusion.124
  1689.7 21.9 fusion.128
  1711.7 11.4 fusion.117
  1725.6 74.1 %all-reduce.25.cloned.1.call-done = (f32[1536]{0:T(1024)}, f32[4,3328]{1,0:T(4,128)}, f32[3328]{0:T(1024)}, f32[48]{0:T(128)}, f32[48]{0:T(128)}, /*index=5*/f32[48]{0:T(128)}, f32[3072]{0:T(1024)}) async-done(((f32[1536]{0:T(1024)}, f32[4,3328]{1,0:T(4,128)}, f32[3328]{0:T(1024)}, f32[48]{0:T(128)}, f32[48]{0:T(128)}, /*index=5*/f32[48]{0:T(128)}, f32[3072]{0:T(1024)}), (f32[1536]{0:T(1024)}, ...) | async-done | bytes 85584 | tf_op jit(solution)/shard_map/psum | solution.py:240
  1799.7 215.8 %reduce-scatter.8.cloned.1.call-done = f32[96,1536]{1,0:T(8,128)} async-done(((f32[3072,1536]{1,0:T(8,128)}), f32[96,1536]{1,0:T(8,128)}) %reduce-scatter.8.cloned.1.call-update) | async-done | bytes 589840 | tf_op jit(solution)/shard_map/reduce_scatter | solution.py:157
  2015.5 372.5 %reduce-scatter.6.cloned.1.call-done = f32[48,6448]{1,0:T(8,128)} async-done(((f32[1536,6448]{1,0:T(8,128)}), f32[48,6448]{1,0:T(8,128)}) %reduce-scatter.6.cloned.1.call-update) | async-done | bytes 1238032 | tf_op jit(solution)/shard_map/reduce_scatter | solution.py:199
  (1298 shorter events, 869.3 us)
Async XLA Ops:
  7.2 130.0 %copy-start.43 = (f32[1536]{0:T(1024)S(1)}, f32[1536]{0:T(1024)}, u32[]{:S(2)}) copy-start(f32[1536]{0:T(1024)} %param.16) | copy-start | bytes 18436
  7.2 130.0 %all-gather.4.cloned.1.call-start = ((), (), s32[]{:S(2)}) async-start(), calls=%async_computation.9 | async-start | bytes 24760320 | tf_op jit(solution)/shard_map/all_gather | solution.py:110
  7.9 247.7 %all-gather.6.cloned.1.call-start = ((), (), s32[]{:S(2)}) async-start(), calls=%async_computation.10 | async-start | bytes 2359296 | tf_op jit(solution)/shard_map/all_gather | solution.py:122
  9.5 142.9 %copy-start.45 = (f32[512]{0:T(512)}, f32[512]{0:T(512)S(1)}, u32[]{:S(2)}) copy-start(f32[512]{0:T(512)S(1)} %fusion.147) | copy-start | bytes 6148
  157.5 13.2 all-to-all-start
  165.8 13.9 copy-start.15
  170.6 101.5 %all-to-all-start.1 = ((bf16[512,8,384]{2,0,1:T(8,128)(2,1)}), bf16[512,8,384]{2,0,1:T(8,128)(2,1)S(1)}, u32[]{:S(2)}, u32[]{:S(2)}) async-start(bf16[512,8,384]{2,0,1:T(8,128)(2,1)} %copy.321), calls=%async_computation.1 | async-start | bytes 6291456 | tf_op jit(solution)/shard_map/all_to_all | solution.py:119
  174.3 585.8 %all-gather.8.cloned.1.call-start = ((), (), s32[]{:S(2)}) async-start(), calls=%async_computation.11 | async-start | bytes 11796480 | tf_op jit(solution)/shard_map/all_gather | solution.py:151
  176.4 488.2 %copy-start.18 = (f32[384]{0:T(512)}, f32[384]{0:T(512)S(1)}, u32[]{:S(2)}) copy-start(f32[384]{0:T(512)S(1)} %mul.775) | copy-start | bytes 4612
  177.8 96.0 %copy-start.20 = (f32[384]{0:T(512)}, f32[384]{0:T(512)S(1)}, u32[]{:S(2)}) copy-start(f32[384]{0:T(512)S(1)} %get-tuple-element.714) | copy-start | bytes 4612
  177.8 96.0 %copy-start.22 = (f32[384]{0:T(512)}, f32[384]{0:T(512)S(1)}, u32[]{:S(2)}) copy-start(f32[384]{0:T(512)S(1)} %get-tuple-element.715) | copy-start | bytes 4612
  177.8 96.0 %copy-start.24 = (f32[384]{0:T(512)}, f32[384]{0:T(512)S(1)}, u32[]{:S(2)}) copy-start(f32[384]{0:T(512)S(1)} %get-tuple-element.716) | copy-start | bytes 4612
  180.9 76.8 %copy-start.35 = (f32[1,256]{1,0:T(1,128)S(1)}, f32[1,256]{1,0:T(1,128)}, u32[]{:S(2)}) copy-start(f32[1,256]{1,0:T(1,128)} %get-tuple-element.811) | copy-start | bytes 3076
  180.9 76.8 %copy-start.37 = (f32[1,256]{1,0:T(1,128)S(1)}, f32[1,256]{1,0:T(1,128)}, u32[]{:S(2)}) copy-start(f32[1,256]{1,0:T(1,128)} %get-tuple-element.812) | copy-start | bytes 3076
  181.0 76.8 %copy-start.39 = (f32[1,256]{1,0:T(1,128)S(1)}, f32[1,256]{1,0:T(1,128)}, u32[]{:S(2)}) copy-start(f32[1,256]{1,0:T(1,128)} %get-tuple-element.813) | copy-start | bytes 3076
  181.0 76.8 %copy-start.41 = (f32[1,256]{1,0:T(1,128)S(1)}, f32[1,256]{1,0:T(1,128)}, u32[]{:S(2)}) copy-start(f32[1,256]{1,0:T(1,128)} %get-tuple-element.814) | copy-start | bytes 3076
  181.0 76.8 %copy-start.50 = (f32[256]{0:T(256)S(1)}, f32[256]{0:T(256)}, u32[]{:S(2)}) copy-start(f32[256]{0:T(256)} %slice.152) | copy-start | bytes 3076
  181.9 81.1 %copy-start.11 = (f32[16,256,6]{1,0,2:T(8,128)}, f32[16,256,6]{1,0,2:T(8,128)S(1)}, u32[]{:S(2)}) copy-start(f32[16,256,6]{1,0,2:T(8,128)S(1)} %reshape.396) | copy-start | bytes 294916
  753.3 19.8 slice-start.4
  760.1 13.0 copy-start.16
  760.1 12.9 slice-start
  760.1 12.9 slice-start.2
  760.1 12.9 slice-start.1
  760.2 12.9 slice-start.3
  760.2 12.9 slice-start.5
  783.4 74.2 %all-to-all-start.3 = ((bf16[512,8,384]{2,0,1:T(8,128)(2,1)}), bf16[512,8,384]{2,0,1:T(8,128)(2,1)S(1)}, u32[]{:S(2)}, u32[]{:S(2)}) async-start(bf16[512,8,384]{2,0,1:T(8,128)(2,1)} %copy.331), calls=%async_computation.3 | async-start | bytes 6291456 | tf_op jit(solution)/shard_map/all_to_all | solution.py:170
  881.6 596.0 %copy-start.48 = (f32[6]{0:T(128)S(1)}, f32[6]{0:T(128)}, u32[]{:S(2)}) copy-start(f32[6]{0:T(128)} %dynamic_slice.93) | copy-start | bytes 76
  1478.5 78.7 %all-to-all-start.5 = ((bf16[8,512,6]{1,2,0:T(8,128)(2,1)}), bf16[8,512,6]{1,2,0:T(8,128)(2,1)S(1)}, u32[]{:S(2)}, u32[]{:S(2)}) async-start(bf16[8,512,6]{1,2,0:T(8,128)(2,1)} %fusion.142), calls=%async_computation.6 | async-start | bytes 131072 | tf_op jit(solution)/shard_map/all_to_all | solution.py:190
  1482.1 173.0 %reduce-scatter.4.cloned.1.call-start = ((), (), s32[]{:S(2)}) async-start(), calls=%async_computation.12 | async-start | bytes 4718592 | tf_op jit(solution)/shard_map/reduce_scatter | solution.py:194
  1486.9 12.2 copy-start.38
  1486.9 12.2 copy-start.40
  1486.9 12.2 copy-start.42
  1531.1 19.2 copy-start.21
  1531.1 19.2 copy-start.23
  1531.1 19.2 copy-start.25
  1531.1 19.2 copy-start.27
  1557.2 93.3 %all-to-all-start.4 = ((bf16[8,512,384]{2,1,0:T(8,128)(2,1)}), bf16[8,512,384]{2,1,0:T(8,128)(2,1)}, u32[]{:S(2)}, u32[]{:S(2)}) async-start(bf16[8,512,384]{2,1,0:T(8,128)(2,1)} %bitcast.522), calls=%async_computation.4 | async-start | bytes 6291456 | tf_op jit(solution)/shard_map/all_to_all | solution.py:187
  1563.3 93.0 %copy-start.7 = (bf16[1,512,1536]{2,1,0:T(8,128)(2,1)S(1)}, bf16[1,512,1536]{2,1,0:T(8,128)(2,1)}, u32[]{:S(2)}) copy-start(bf16[1,512,1536]{2,1,0:T(8,128)(2,1)} %param.15) | copy-start | bytes 4718596
  1563.3 93.0 %copy-start.44 = (f32[1536]{0:T(1024)S(1)}, f32[1536]{0:T(1024)}, u32[]{:S(2)}) copy-start(f32[1536]{0:T(1024)} %param.16) | copy-start | bytes 18436
  1563.3 93.0 %copy-start.46 = (f32[512]{0:T(512)S(1)}, f32[512]{0:T(512)}, u32[]{:S(2)}) copy-start(f32[512]{0:T(512)} %copy-done.45) | copy-start | bytes 6148
  1563.3 236.4 %all-reduce.25.cloned.1.call-start = ((), (), s32[]{:S(2)}) async-start(), calls=%async_computation.15 | async-start | bytes 183296 | tf_op jit(solution)/shard_map/psum | solution.py:240
  1564.2 112.8 %copy-start.52 = (f32[48]{0:T(128)}, f32[48]{0:T(128)S(1)}, u32[]{:S(2)}) copy-start(f32[48]{0:T(128)S(1)} %dynamic_update_slice.67) | copy-start | bytes 580
  1564.6 112.5 %copy-start.53 = (f32[48]{0:T(128)}, f32[48]{0:T(128)S(1)}, u32[]{:S(2)}) copy-start(f32[48]{0:T(128)S(1)} %dynamic_update_slice.69) | copy-start | bytes 580
  1565.4 111.6 %copy-start.51 = (f32[48]{0:T(128)}, f32[48]{0:T(128)S(1)}, u32[]{:S(2)}) copy-start(f32[48]{0:T(128)S(1)} %multiply_dynamic-update-slice_fusion) | copy-start | bytes 580
  1656.3 20.8 copy-start.10
  1656.3 20.8 copy-start.17
  1677.1 338.4 %reduce-scatter.8.cloned.1.call-start = ((), (), s32[]{:S(2)}) async-start(), calls=%async_computation.14 | async-start | bytes 19464192 | tf_op jit(solution)/shard_map/reduce_scatter | solution.py:157
  1689.7 698.4 %reduce-scatter.6.cloned.1.call-start = ((), (), s32[]{:S(2)}) async-start(), calls=%async_computation.13 | async-start | bytes 41361408 | tf_op jit(solution)/shard_map/reduce_scatter | solution.py:199
  (31 other events, 202.4 us)
Sparse Core Ops, SparseCore 0:
  9.6 127.5 all-gather.3
  156.0 99.5 all-gather.5
  257.2 61.1 all-gather.7
  1513.1 131.1 reduce-scatter.3
  1677.2 122.4 all-reduce.24
  1807.7 207.7 reduce-scatter.7
  2023.7 364.3 reduce-scatter.5
where the time goes:
time: 2420 us; the launch traced here: 2400 us
  waiting for transfers between devices  1020 us (42%)
  local copies, waits for them, and re-layouts  577 us (24%)
  matrix products  363 us (15%)
  other arithmetic  325 us (13%)
  blocking collectives  73.7 us (3%)
    reduce_scatter x1, waiting for transfers between devices, on_device(): lax.psum_scatter(lax.dot_general(left_part, d_projected, CONTRACT_ROWS, p...  373 us
    dynamic_update_slice x64, local copies, waits for them, and re-layouts, head_mix(): lax.scan(jax.checkpoint(one_block), start_state, (x_blocks, b_blocks, c_b...  330 us
    reduce_scatter x1, waiting for transfers between devices, on_device(): lax.psum_scatter(lax.dot_general(left_part, cotan_rows, CONTRACT_ROWS, pr...  216 us
    another operation x145, other arithmetic  199 us
    all_gather x1, waiting for transfers between devices, on_device(): lax.all_gather(w_in, 'fsdp', axis=0, tiled=True)  128 us
    dot_general x48, matrix products, one_block(): inside = jnp.einsum('tsh,shp->thp', weights, x_blk, precision=HIGHEST)  109 us
    all_to_all x1, waiting for transfers between devices, on_device(): lax.all_to_all(d_x_heads.astype(jnp.bfloat16), 'seq', split_axis=0, conca...  84.4 us
    psum x1, waiting for transfers between devices, on_device(): lax.psum((d_gain_in, d_gain_out, conv_w_grad, conv_b_grad, dt_grad, alog_...  74.1 us
  transfers between devices with their start and end apart: 12, of which 8 were waited for; matrix products, arithmetic and copies ran while one was open for 24% of the time, Pallas kernels for 0%

commit v1 on v0

v1 whole, which is shorter than its diff:
```python
import functools

import jax
import jax.numpy as jnp
from jax import lax
from jax.experimental import pallas as pl
from jax.experimental.pallas import tpu as pltpu
from jax.sharding import PartitionSpec as P

HEADS = 48
HEAD_DIM = 64
STATE = 128
KW = 4
INNER = 3072
D = 1536
CONV = INNER + 2 * STATE

EPSILON = 1e-05
CHUNK = 128
QUAD = 256
QUADS = INNER // QUAD
HALO = 16
VMEM_LIMIT = 56 * 1024 * 1024
F32 = jnp.float32
BF16 = jnp.bfloat16
HIGHEST = lax.Precision.HIGHEST
NT = (((1,), (1,)), ((), ()))
TN = (((0,), (0,)), ((), ()))


def iota(shape, axis):
    return lax.broadcasted_iota(jnp.int32, shape, axis)


def mm(a, b):
    return jnp.dot(a, b, preferred_element_type=F32)


def mm_nt(a, b):
    return lax.dot_general(a, b, NT, preferred_element_type=F32)


def sigmoid(v):
    return 0.5 * jnp.tanh(0.5 * v) + 0.5


def split3(v):
    high = v.astype(BF16)
    rest = v - high.astype(F32)
    mid = rest.astype(BF16)
    low = (rest - mid.astype(F32)).astype(BF16)
    return high, mid, low


def mm_exact(v, ones):
    high, mid, low = split3(v)
    return mm(high, ones) + mm(mid, ones) + mm(low, ones)


def head_ones():
    return jnp.where((iota((128, INNER), 1) >> 6) == iota((128, INNER), 0), 1.0, 0.0).astype(BF16)


def two_heads(first, second):
    return jnp.where(iota((CHUNK, 128), 1) < HEAD_DIM, first, second)


def spread(cols, start):
    wide = [jnp.broadcast_to(cols[:, start + i : start + i + 1], (CHUNK, 128)) for i in range(4)]
    return wide, jnp.concatenate([two_heads(wide[0], wide[1]), two_heads(wide[2], wide[3])], axis=1)


def columns_of(rows):
    count, length = rows.shape
    return jnp.concatenate([rows, jnp.zeros((128 - count, length), F32)], axis=0).T


def step_kernel(dt_ref, bias_ref, alog_ref, rows_ref, ecd_ref, total_ref):
    length = dt_ref.shape[0]
    raw = dt_ref[...].astype(F32) + bias_ref[...]
    step = jnp.maximum(raw, 0.0) + jnp.log1p(jnp.exp(-jnp.abs(raw)))
    sig = 1.0 / (1.0 + jnp.exp(-raw))
    rate = -jnp.exp(alog_ref[...])
    pace = step * rate
    lower = jnp.where(iota((CHUNK, CHUNK), 0) >= iota((CHUNK, CHUNK), 1), 1.0, 0.0).astype(F32)
    inside, along = [], []
    offset = jnp.zeros((1, 128), F32)
    for start in range(0, length, CHUNK):
        part = jnp.dot(lower, pace[start : start + CHUNK], precision=HIGHEST, preferred_element_type=F32)
        inside.append(part)
        along.append(part + offset)
        offset = offset + part[CHUNK - 1 : CHUNK]
    cum = jnp.concatenate(inside, axis=0)
    along = jnp.concatenate(along, axis=0)
    ecd_ref[...] = jnp.exp(along)
    total_ref[...] = jnp.broadcast_to(jnp.exp(offset), (8, 128))
    left = jnp.exp(offset - along) * step
    for place, array in enumerate((cum, step, left, sig, jnp.broadcast_to(rate, (length, 128)))):
        turned = array.T
        for quad in range(QUADS):
            rows_ref[quad, 8 * place : 8 * place + 4, :] = turned[4 * quad : 4 * quad + 4, :]
            rows_ref[quad, 8 * place + 4 : 8 * place + 8, :] = jnp.zeros((4, length), F32)


def step_call(dt_raw, dt_bias, a_log):
    length = dt_raw.shape[0]
    return pl.pallas_call(
        step_kernel,
        out_shape=(
            jax.ShapeDtypeStruct((QUADS, 40, length), F32),
            jax.ShapeDtypeStruct((length, 128), F32),
            jax.ShapeDtypeStruct((8, 128), F32),
        ),
        compiler_params=pltpu.CompilerParams(vmem_limit_bytes=VMEM_LIMIT),
        name="steps",
    )(dt_raw, dt_bias, a_log)


def conv_kernel(ranks, me_ref, v_ref, cw_ref, cb_ref, rows_ref, total_ref, *rest):
    x_ref, slope_ref, b_ref, c_ref, bt_ref, ct_ref = rest[:6]
    out_refs = rest[6 : 6 + ranks]
    ext, weighted, state = rest[6 + ranks :]
    length = v_ref.shape[0] - HALO
    share = STATE // ranks
    grid = pl.program_id(0)
    ext[...] = v_ref[...].astype(F32)

    def act(start):
        total = cb_ref[...] + cw_ref[0:1, :] * ext[HALO - 3 + start : HALO - 3 + start + CHUNK, :]
        for tap in range(1, KW):
            at = HALO - 3 + tap + start
            total = total + cw_ref[tap : tap + 1, :] * ext[at : at + CHUNK, :]
        sig = sigmoid(total)
        slope_ref[start : start + CHUNK, :] = (sig * (1.0 + total * (1.0 - sig))).astype(BF16)
        return total * sig

    @pl.when(grid == 0)
    def _():
        for start in range(0, length, CHUNK):
            both = act(start)
            b_part, c_part = both[:, :STATE], both[:, STATE:]
            b_ref[start : start + CHUNK, :] = b_part.astype(BF16)
            c_ref[start : start + CHUNK, :] = c_part.astype(BF16)
            bt_ref[:, start : start + CHUNK] = b_part.T.astype(BF16)
            ct_ref[:, start : start + CHUNK] = c_part.T.astype(BF16)
        high, mid, low = split3(total_ref[0:1, :])
        row = iota((share, 128), 0)
        told = jnp.where(row == 0, high.astype(F32), jnp.where(row == 1, mid.astype(F32), jnp.where(row == 2, low.astype(F32), 0.0)))
        for out_ref in out_refs:
            out_ref[:, INNER : INNER + 128] = told.astype(BF16)

    @pl.when(grid > 0)
    def _():
        cols = columns_of(rows_ref[0])
        for start in range(0, length, CHUNK):
            x_part = act(start)
            x_ref[start : start + CHUNK, :] = x_part.astype(BF16)
            _, left = spread(cols[start : start + CHUNK], 16)
            weighted[start : start + CHUNK, :] = (x_part * left).astype(BF16)
        state[...] = mm(bt_ref[...], weighted[...])
        lanes = pl.ds(pl.multiple_of((grid - 1) * QUAD, QUAD), QUAD)
        for step, out_ref in enumerate(out_refs):
            other = me_ref[0] ^ step
            out_ref[:, lanes] = state[pl.ds(pl.multiple_of(other * share, share), share), :].astype(BF16)


def conv_call(ranks, me, v, conv_weight, conv_bias, rows, total):
    length = v.shape[0] - HALO
    share = STATE // ranks
    last = QUADS
    block = lambda g, *_: (0, (g + last) % (last + 1))
    quad = lambda g, *_: (0, jnp.maximum(g - 1, 0))
    whole = lambda g, *_: (0, 0)
    grid_spec = pltpu.PrefetchScalarGridSpec(
        num_scalar_prefetch=1,
        grid=(last + 1,),
        in_specs=[
            pl.BlockSpec((length + HALO, QUAD), block),
            pl.BlockSpec((KW, QUAD), block),
            pl.BlockSpec((1, QUAD), block),
            pl.BlockSpec((1, 40, length), lambda g, *_: (jnp.maximum(g - 1, 0), 0, 0)),
            pl.BlockSpec((8, 128), whole),
        ],
        out_specs=[
            pl.BlockSpec((length, QUAD), quad),
            pl.BlockSpec((length, QUAD), block),
            pl.BlockSpec((length, STATE), whole),
            pl.BlockSpec((length, STATE), whole),
            pl.BlockSpec((STATE, length), whole),
            pl.BlockSpec((STATE, length), whole),
        ]
        + [pl.BlockSpec((share, INNER + 128), whole)] * ranks,
        scratch_shapes=[
            pltpu.VMEM((length + HALO, QUAD), F32),
            pltpu.VMEM((length, QUAD), BF16),
            pltpu.VMEM((STATE, QUAD), F32),
        ],
    )
    return pl.pallas_call(
        functools.partial(conv_kernel, ranks),
        grid_spec=grid_spec,
        out_shape=[
            jax.ShapeDtypeStruct((length, INNER), BF16),
            jax.ShapeDtypeStruct((length, CONV), BF16),
            jax.ShapeDtypeStruct((length, STATE), BF16),
            jax.ShapeDtypeStruct((length, STATE), BF16),
            jax.ShapeDtypeStruct((STATE, length), BF16),
            jax.ShapeDtypeStruct((STATE, length), BF16),
        ]
        + [jax.ShapeDtypeStruct((share, INNER + 128), BF16)] * ranks,
        compiler_params=pltpu.CompilerParams(vmem_limit_bytes=VMEM_LIMIT),
        cost_estimate=pl.CostEstimate(flops=int(4e8), bytes_accessed=int(2e7), transcendentals=0),
        name="conv_states",
    )(me, v, conv_weight, conv_bias, rows, total)


def carry_kernel(ranks, backward, me_ref, *rest):
    share = STATE // ranks
    if backward:
        in_refs, total_ref, out_refs = rest[:ranks], rest[ranks], rest[ranks + 1 : 2 * ranks + 1]
        held, decays = rest[2 * ranks + 1 :], total_ref[...]
        (held,) = held
    else:
        in_refs, out_refs, total_ref = rest[:ranks], rest[ranks : 2 * ranks], rest[2 * ranks]
        (held,) = rest[2 * ranks + 1 :]
    for step, in_ref in enumerate(in_refs):
        other = me_ref[0] ^ step
        held[other] = in_ref[:, :INNER].astype(F32)
        if not backward:
            told = in_ref[:, INNER : INNER + 128].astype(F32)
            total_ref[pl.ds(other, 1), :] = told[0:1] + told[1:2] + told[2:3]
    if not backward:
        decays = total_ref[...]
    wide = mm_exact(decays, head_ones())
    carry = jnp.zeros((share, INNER), F32)
    for place in range(ranks - 1, -1, -1) if backward else range(ranks):
        fresh = held[place]
        held[place] = carry
        carry = wide[place : place + 1] * carry + fresh
    for step, out_ref in enumerate(out_refs):
        out_ref[...] = held[me_ref[0] ^ step].astype(BF16)


def carry_call(ranks, me, parts, totals=None):
    share = STATE // ranks
    backward = totals is not None
    smem = pl.BlockSpec(memory_space=pltpu.SMEM)
    vmem = pl.BlockSpec(memory_space=pltpu.VMEM)
    outs = [jax.ShapeDtypeStruct((share, INNER), BF16)] * ranks
    args = list(parts) + ([totals] if backward else [])
    if not backward:
        outs.append(jax.ShapeDtypeStruct((ranks, 128), F32))
    return pl.pallas_call(
        functools.partial(carry_kernel, ranks, backward),
        in_specs=[smem] + [vmem] * len(args),
        out_specs=[vmem] * len(outs),
        out_shape=outs,
        scratch_shapes=[pltpu.VMEM((ranks, share, INNER), F32)],
        compiler_params=pltpu.CompilerParams(vmem_limit_bytes=VMEM_LIMIT),
        name="carry_back" if backward else "carry",
    )(me, *args)


def inside_kernel(x_ref, b_ref, c_ref, bt_ref, rows_ref, skip_ref, y_ref, scores, state):
    length = x_ref.shape[0]
    grid = pl.program_id(0)

    @pl.when(grid == 0)
    def _():
        for start in range(0, length, CHUNK):
            part = slice(start, start + CHUNK)
            scores[part, :] = mm_nt(c_ref[part, :], b_ref[part, :])

    cols = columns_of(rows_ref[0])
    lower = iota((CHUNK, CHUNK), 0) >= iota((CHUNK, CHUNK), 1)
    first = iota((CHUNK, 128), 1) < HEAD_DIM
    for start in range(0, length, CHUNK):
        part = slice(start, start + CHUNK)
        x_f = x_ref[part, :].astype(F32)
        wide, cum = spread(cols[part], 0)
        _, step = spread(cols[part], 8)
        weights = []
        for head in range(4):
            cum_row = rows_ref[0, head : head + 1, part]
            step_row = rows_ref[0, 8 + head : 9 + head, part]
            fade = jnp.exp(jnp.where(lower, wide[head] - cum_row, -1e30))
            weights.append((scores[part, :] * fade * step_row).astype(BF16))
        pieces = []
        for pair in range(2):
            x_pair = x_f[:, 128 * pair : 128 * pair + 128]
            both = jnp.concatenate([jnp.where(first, x_pair, 0.0), jnp.where(first, 0.0, x_pair)], axis=0)
            pieces.append(mm(jnp.concatenate(weights[2 * pair : 2 * pair + 2], axis=1), both.astype(BF16)))
        y_part = jnp.concatenate(pieces, axis=1) + skip_ref[...] * x_f
        if start > 0:
            y_part = y_part + jnp.exp(cum) * mm(c_ref[part, :], state[...].astype(BF16))
        y_ref[part, :] = y_part
        if start + CHUNK < length:
            end = cum[CHUNK - 1 : CHUNK]
            fresh = mm(bt_ref[:, part], (x_f * (jnp.exp(end - cum) * step)).astype(BF16))
            state[...] = fresh if start == 0 else jnp.exp(end) * state[...] + fresh


def inside_call(x_act, b_act, c_act, b_turned, rows, skip_wide):
    length = x_act.shape[0]
    whole = lambda g: (0, 0)
    quad = lambda g: (0, g)
    return pl.pallas_call(
        inside_kernel,
        grid=(QUADS,),
        in_specs=[
            pl.BlockSpec((length, QUAD), quad),
            pl.BlockSpec((length, STATE), whole),
            pl.BlockSpec((length, STATE), whole),
            pl.BlockSpec((STATE, length), whole),
            pl.BlockSpec((1, 40, length), lambda g: (g, 0, 0)),
            pl.BlockSpec((1, QUAD), quad),
        ],
        out_specs=pl.BlockSpec((length, QUAD), quad),
        out_shape=jax.ShapeDtypeStruct((length, INNER), F32),
        scratch_shapes=[pltpu.VMEM((length, CHUNK), F32), pltpu.VMEM((STATE, QUAD), F32)],
        compiler_params=pltpu.CompilerParams(vmem_limit_bytes=VMEM_LIMIT),
        cost_estimate=pl.CostEstimate(flops=int(8e9), bytes_accessed=int(2e7), transcendentals=0),
        name="ssd_inside",
    )(x_act, b_act, c_act, b_turned, rows, skip_wide)


def gate_kernel(ranks, me_ref, y_ref, gate_ref, dn_ref, c_ref, ct_ref, ecd_ref, gain_ref, *rest):
    in_refs = rest[:ranks]
    normed_ref, dgate_ref, dm_ref, dgain_ref, sin_ref = rest[ranks : ranks + 5]
    out_refs = rest[ranks + 5 : 2 * ranks + 5]
    sin, ones, ecd, gated, silu, slope, back = rest[2 * ranks + 5 :]
    share = STATE // ranks
    grid = pl.program_id(0)

    @pl.when(grid == 0)
    def _():
        for step, in_ref in enumerate(in_refs):
            other = me_ref[0] ^ step
            sin[pl.ds(pl.multiple_of(other * share, share), share), :] = in_ref[...].astype(F32)
        sin_ref[...] = sin[...].astype(BF16)
        ones[...] = head_ones()
        back[...] = jnp.zeros_like(back)
        dgain_ref[...] = jnp.zeros_like(dgain_ref)

    high, mid, _ = split3(ecd_ref[...])
    squares = jnp.zeros((CHUNK, QUAD), F32)
    product = jnp.zeros((CHUNK, QUAD), F32)
    for at in range(0, INNER, QUAD):
        lanes = slice(at, at + QUAD)
        grown = mm(high, ones[:, lanes]) + mm(mid, ones[:, lanes])
        ecd[:, lanes] = grown
        mixed = y_ref[:, lanes] + grown * mm(c_ref[...], sin_ref[:, lanes])
        mixed = mixed.astype(BF16).astype(F32)
        gate = gate_ref[:, lanes].astype(F32)
        sig = sigmoid(gate)
        open_part = gate * sig
        value = mixed * open_part
        silu[:, lanes] = open_part
        slope[:, lanes] = mixed * (sig * (1.0 + gate * (1.0 - sig)))
        gated[:, lanes] = value
        squares = squares + value * value
        product = product + dn_ref[:, lanes] * gain_ref[:, lanes] * value
    inverse = lax.rsqrt(jnp.sum(squares, axis=1, keepdims=True) * (1.0 / INNER) + EPSILON)
    shift = inverse * inverse * inverse * (jnp.sum(product, axis=1, keepdims=True) * (1.0 / INNER))
    inverse = jnp.broadcast_to(inverse, (CHUNK, QUAD))
    shift = jnp.broadcast_to(shift, (CHUNK, QUAD))
    for at in range(0, INNER, QUAD):
        lanes = slice(at, at + QUAD)
        value = gated[:, lanes]
        scaled = value * inverse
        gain = gain_ref[:, lanes]
        dn = dn_ref[:, lanes]
        normed_ref[:, lanes] = (scaled * gain).astype(BF16)
        dgain_ref[:, lanes] += jnp.sum(dn * scaled, axis=0, keepdims=True)
        d_gated = inverse * (dn * gain) - value * shift
        dgate_ref[:, lanes] = (d_gated * slope[:, lanes]).astype(BF16)
        d_mixed = (d_gated * silu[:, lanes]).astype(BF16)
        dm_ref[:, lanes] = d_mixed
        back[:, lanes] += mm(ct_ref[...], (d_mixed.astype(F32) * ecd[:, lanes]).astype(BF16))

    @pl.when(grid == pl.num_programs(0) - 1)
    def _():
        for step, out_ref in enumerate(out_refs):
            other = me_ref[0] ^ step
            out_ref[...] = back[pl.ds(pl.multiple_of(other * share, share), share), :].astype(BF16)


def gate_call(ranks, me, y_inside, gate_in, d_normed, c_act, c_turned, ecd, out_gain, parts):
    length = y_inside.shape[0]
    share = STATE // ranks
    whole = lambda g, *_: (0, 0)
    down = lambda g, *_: (g, 0)
    wide = pl.BlockSpec((CHUNK, INNER), down)
    grid_spec = pltpu.PrefetchScalarGridSpec(
        num_scalar_prefetch=1,
        grid=(length // CHUNK,),
        in_specs=[
            wide,
            wide,
            wide,
            pl.BlockSpec((CHUNK, STATE), down),
            pl.BlockSpec((STATE, CHUNK), lambda g, *_: (0, g)),
            pl.BlockSpec((CHUNK, 128), down),
            pl.BlockSpec((1, INNER), whole),
        ]
        + [pl.BlockSpec((share, INNER), whole)] * ranks,
        out_specs=[wide, wide, wide, pl.BlockSpec((1, INNER), whole), pl.BlockSpec((STATE, INNER), whole)]
        + [pl.BlockSpec((share, INNER), whole)] * ranks,
        scratch_shapes=[
            pltpu.VMEM((STATE, INNER), F32),
            pltpu.VMEM((128, INNER), BF16),
            pltpu.VMEM((CHUNK, INNER), F32),
            pltpu.VMEM((CHUNK, INNER), F32),
            pltpu.VMEM((CHUNK, INNER), F32),
            pltpu.VMEM((CHUNK, INNER), F32),
            pltpu.VMEM((STATE, INNER), F32),
        ],
    )
    rows = jax.ShapeDtypeStruct((length, INNER), BF16)
    return pl.pallas_call(
        functools.partial(gate_kernel, ranks),
        grid_spec=grid_spec,
        out_shape=[rows, rows, rows, jax.ShapeDtypeStruct((1, INNER), F32), jax.ShapeDtypeStruct((STATE, INNER), BF16)]
        + [jax.ShapeDtypeStruct((share, INNER), BF16)] * ranks,
        compiler_params=pltpu.CompilerParams(vmem_limit_bytes=VMEM_LIMIT),
        cost_estimate=pl.CostEstimate(flops=int(2e9), bytes_accessed=int(3e7), transcendentals=0),
        name="gated_norm",
    )(me, y_inside, gate_in, d_normed, c_act, c_turned, ecd, out_gain, *parts)


def back_kernel(ranks, me_ref, x_ref, dm_ref, slope_ref, v_ref, cw_ref, b_ref, c_ref, bt_ref, ct_ref, rows_ref, skip_ref, sin_ref, *rest):
    in_refs = rest[:ranks]
    dv_ref, sums_ref, heads_ref = rest[ranks : ranks + 3]
    scores, d_scores, d_b, d_c, states, back, grads, ext, d_step = rest[ranks + 3 :]
    length = x_ref.shape[0]
    share = STATE // ranks
    chunks = length // CHUNK
    grid = pl.program_id(0)

    @pl.when(grid == 0)
    def _():
        for start in range(0, length, CHUNK):
            part = slice(start, start + CHUNK)
            scores[part, :] = mm_nt(b_ref[part, :], c_ref[part, :])
        d_scores[...] = jnp.zeros_like(d_scores)
        d_b[...] = jnp.zeros_like(d_b)
        d_c[...] = jnp.zeros_like(d_c)
        d_step[...] = jnp.zeros_like(d_step)
        grads[0:HALO, :] = jnp.zeros((HALO, QUAD), F32)
        grads[HALO + length :, :] = jnp.zeros((HALO, QUAD), F32)

    def finish(extra):
        ext[...] = v_ref[...].astype(F32)
        total = [jnp.zeros((1, QUAD), F32)] * (KW + 1)
        for start in range(0, length, CHUNK):
            here = grads[HALO + start : HALO + start + CHUNK, :]
            for tap in range(KW):
                at = HALO - 3 + tap + start
                total[tap] = total[tap] + jnp.sum(here * ext[at : at + CHUNK, :], axis=0, keepdims=True)
            total[KW] = total[KW] + jnp.sum(here, axis=0, keepdims=True)
        for at, row in enumerate(total + [extra]):
            sums_ref[at : at + 1, :] = row
        sums_ref[KW + 2 : 8, :] = jnp.zeros((8 - KW - 2, QUAD), F32)
        for start in [0] + list(range(HALO, HALO + length, CHUNK)):
            count = HALO if start == 0 else CHUNK
            value = cw_ref[KW - 1 : KW, :] * grads[start : start + count, :]
            for tap in range(KW - 1):
                at = start + KW - 1 - tap
                value = value + cw_ref[tap : tap + 1, :] * grads[at : at + count, :]
            dv_ref[start : start + count, :] = value.astype(BF16)

    @pl.when(grid < QUADS)
    def _():
        cols = columns_of(rows_ref[0])
        upper = iota((CHUNK, CHUNK), 0) <= iota((CHUNK, CHUNK), 1)
        first = iota((CHUNK, 128), 1) < HEAD_DIM
        lane = iota((CHUNK, 128), 1)
        line = iota((8, 128), 0)
        head_of = iota((QUAD, 128), 0) >> 6
        ones_v = jnp.where(iota((QUAD, 128), 1) == head_of + 8, 1.0, 0.0).astype(BF16)
        ones_u = jnp.where(iota((QUAD, 128), 1) == head_of + 16, 1.0, 0.0).astype(BF16)
        square = (CHUNK, CHUNK)
        later = jnp.where(iota(square, 0) >= iota(square, 1), 1.0, 0.0).astype(BF16)
        before = jnp.where(iota(square, 0) < iota(square, 1), 1.0, 0.0).astype(BF16)
        skip = skip_ref[...]
        for step, in_ref in enumerate(in_refs):
            other = me_ref[0] ^ step
            back[pl.ds(pl.multiple_of(other * share, share), share), :] = in_ref[...].astype(F32)
        state = sin_ref[...].astype(F32)
        for chunk in range(chunks):
            part = slice(chunk * CHUNK, chunk * CHUNK + CHUNK)
            states[chunk] = state
            if chunk + 1 < chunks:
                _, cum = spread(cols[part], 0)
                _, step = spread(cols[part], 8)
                end = cum[CHUNK - 1 : CHUNK]
                fed = (x_ref[part, :].astype(F32) * (jnp.exp(end - cum) * step)).astype(BF16)
                state = jnp.exp(end) * state + mm(bt_ref[:, part], fed)
        skip_sum = jnp.zeros((1, QUAD), F32)
        bias_sum = jnp.zeros((8, 1), F32)
        rate_sum = jnp.zeros((8, 1), F32)
        for chunk in range(chunks - 1, -1, -1):
            part = slice(chunk * CHUNK, chunk * CHUNK + CHUNK)
            x_f = x_ref[part, :].astype(F32)
            dm = dm_ref[part, :]
            dm_f = dm.astype(F32)
            cum_wide, cum = spread(cols[part], 0)
            step_wide, step = spread(cols[part], 8)
            end = cum[CHUNK - 1 : CHUNK]
            after = back[...]
            after_low = after.astype(BF16)
            state = states[chunk]
            left = jnp.exp(end - cum)
            grown = dm_f * jnp.exp(cum)
            grown_low = grown.astype(BF16)
            faded = x_f * left
            from_after = mm(b_ref[part, :], after_low)
            from_state = mm(c_ref[part, :], state.astype(BF16))
            d_b[part, :] += mm_nt((faded * step).astype(BF16), after_low)
            d_c[part, :] += mm_nt(grown_low, state.astype(BF16))
            marks = mm((grown * from_state).astype(BF16), ones_v) + mm((faded * from_after).astype(BF16), ones_u)
            pair_sum = jnp.zeros((8, CHUNK), F32)
            crossing = jnp.zeros((8, 1), F32)
            cross = jnp.sum(state * after, axis=0, keepdims=True) * jnp.exp(end)
            pieces = []
            for pair in range(2):
                x_pair = x_f[:, 128 * pair : 128 * pair + 128]
                dm_pair = dm_f[:, 128 * pair : 128 * pair + 128]
                x_both = jnp.concatenate([jnp.where(first, x_pair, 0.0), jnp.where(first, 0.0, x_pair)], axis=0)
                dm_both = jnp.concatenate([jnp.where(first, dm_pair, 0.0), jnp.where(first, 0.0, dm_pair)], axis=0)
                d_weights = mm_nt(x_both.astype(BF16), dm[:, 128 * pair : 128 * pair + 128])
                kept = []
                for half in range(2):
                    head = 2 * pair + half
                    cum_row = rows_ref[0, head : head + 1, part]
                    fade = jnp.exp(jnp.where(upper, cum_row - cum_wide[head], -1e30))
                    faded_grad = d_weights[half * CHUNK : half * CHUNK + CHUNK] * fade
                    d_scores[part, :] += faded_grad * step_wide[head]
                    joint = faded_grad * scores[part, :]
                    marks = marks + jnp.where(lane == head, jnp.sum(joint, axis=1, keepdims=True), 0.0)
                    row = jnp.sum(joint * step_wide[head], axis=0, keepdims=True)
                    pair_sum = pair_sum + jnp.where(line == head, row, 0.0)
                    kept.append((scores[part, :] * fade).astype(BF16))
                    low, high = 64 * head, 64 * head + 64
                    here = (iota((1, QUAD), 1) >= low) & (iota((1, QUAD), 1) < high)
                    amount = jnp.sum(jnp.where(here, cross, 0.0), axis=1, keepdims=True)
                    crossing = crossing + jnp.where(iota((8, 1), 0) == head, amount, 0.0)
                pieces.append(mm(jnp.concatenate(kept, axis=1), dm_both.astype(BF16)))
            direct = jnp.concatenate(pieces, axis=1) + left * from_after
            d_x = step * direct + skip * dm_f
            grads[HALO + chunk * CHUNK : HALO + chunk * CHUNK + CHUNK, :] = d_x * slope_ref[part, :].astype(F32)
            skip_sum = skip_sum + jnp.sum(x_f * dm_f, axis=0, keepdims=True)
            back[...] = jnp.exp(end) * after + mm(ct_ref[:, part], grown_low)
            marks = marks.T
            within, carried, outward = marks[0:8], marks[8:16], marks[16:24]
            step_rows = rows_ref[0, 8:16, part]
            change = pair_sum - step_rows * within + carried
            decay = mm_exact(change, later) + mm_exact(step_rows * outward, before) + crossing
            d_raw = (within + outward + rows_ref[0, 32:40, part] * decay) * rows_ref[0, 24:32, part]
            d_step[pl.ds(pl.multiple_of(grid * 8, 8), 8), part] = d_raw
            bias_sum = bias_sum + jnp.sum(d_raw, axis=1, keepdims=True)
            rate_sum = rate_sum + jnp.sum(step_rows * decay, axis=1, keepdims=True)
        heads_ref[0, 0:8, :] = jnp.broadcast_to(bias_sum, (8, 128))
        heads_ref[0, 8:16, :] = jnp.broadcast_to(rate_sum, (8, 128))
        finish(skip_sum)

    @pl.when(grid == QUADS)
    def _():
        for start in range(0, length, CHUNK):
            part = slice(start, start + CHUNK)
            low = d_scores[part, :].astype(BF16)
            into_b = d_b[part, :] + mm(low, c_ref[part, :])
            into_c = d_c[part, :] + mm(d_scores[part, :].T.astype(BF16), b_ref[part, :])
            both = jnp.concatenate([into_b, into_c], axis=1)
            grads[HALO + start : HALO + start + CHUNK, :] = both * slope_ref[part, :].astype(F32)
        finish(jnp.zeros((1, QUAD), F32))

    @pl.when(grid == QUADS + 1)
    def _():
        row, column = iota((128, QUAD), 0), iota((128, QUAD), 1)
        pick = (column < HEADS) & (row == 8 * (column >> 2) + (column & 3))
        turned = d_step[...].T.astype(BF16)
        dv_ref[0:HALO, :] = jnp.zeros((HALO, QUAD), BF16)
        dv_ref[HALO:, :] = mm(turned, jnp.where(pick, 1.0, 0.0).astype(BF16)).astype(BF16)


def back_call(ranks, me, x_act, d_mixed, slope, v, conv_weight, b_act, c_act, b_turned, c_turned, rows, skip_wide, s_in, parts):
    length = x_act.shape[0]
    share = STATE // ranks
    whole = lambda g, *_: (0, 0)
    quad = lambda g, *_: (0, jnp.minimum(g, QUADS - 1))
    block = lambda g, *_: (0, jnp.minimum(g, QUADS))
    lead = lambda g, *_: (jnp.minimum(g, QUADS - 1), 0, 0)
    grid_spec = pltpu.PrefetchScalarGridSpec(
        num_scalar_prefetch=1,
        grid=(QUADS + 2,),
        in_specs=[
            pl.BlockSpec((length, QUAD), quad),
            pl.BlockSpec((length, QUAD), quad),
            pl.BlockSpec((length, QUAD), block),
            pl.BlockSpec((length + HALO, QUAD), block),
            pl.BlockSpec((KW, QUAD), block),
            pl.BlockSpec((length, STATE), whole),
            pl.BlockSpec((length, STATE), whole),
            pl.BlockSpec((STATE, length), whole),
            pl.BlockSpec((STATE, length), whole),
            pl.BlockSpec((1, 40, length), lead),
            pl.BlockSpec((1, QUAD), quad),
            pl.BlockSpec((STATE, QUAD), quad),
        ]
        + [pl.BlockSpec((share, QUAD), quad)] * ranks,
        out_specs=[
            pl.BlockSpec((length + HALO, QUAD), lambda g, *_: (0, g)),
            pl.BlockSpec((8, QUAD), block),
            pl.BlockSpec((1, 16, 128), lead),
        ],
        scratch_shapes=[
            pltpu.VMEM((length, CHUNK), F32),
            pltpu.VMEM((length, CHUNK), F32),
            pltpu.VMEM((length, STATE), F32),
            pltpu.VMEM((length, STATE), F32),
            pltpu.VMEM((length // CHUNK, STATE, QUAD), F32),
            pltpu.VMEM((STATE, QUAD), F32),
            pltpu.VMEM((length + 2 * HALO, QUAD), F32),
            pltpu.VMEM((length + HALO, QUAD), F32),
            pltpu.VMEM((128, length), F32),
        ],
    )
    return pl.pallas_call(
        functools.partial(back_kernel, ranks),
        grid_spec=grid_spec,
        out_shape=[
            jax.ShapeDtypeStruct((length + HALO, CONV + QUAD), BF16),
            jax.ShapeDtypeStruct((8, CONV), F32),
            jax.ShapeDtypeStruct((QUADS, 16, 128), F32),
        ],
        compiler_params=pltpu.CompilerParams(vmem_limit_bytes=VMEM_LIMIT),
        cost_estimate=pl.CostEstimate(flops=int(2e10), bytes_accessed=int(4e7), transcendentals=0),
        name="ssd_back",
    )(me, x_act, d_mixed, slope, v, conv_weight, b_act, c_act, b_turned, c_turned, rows, skip_wide, s_in, *parts)


def on_device(
    ranks,
    shards,
    tokens,
    norm_gain,
    w_in,
    conv_weight,
    conv_bias,
    dt_bias,
    a_log,
    skip_gain,
    out_gain,
    w_out,
    cotangent,
):
    both = ("seq", "fsdp")
    rank = lax.axis_index("seq")
    shard = lax.axis_index("fsdp")
    me = rank.astype(jnp.int32).reshape(1)

    def move(value, target):
        pairs = []
        for s in range(ranks):
            for f in range(shards):
                goal = target(s, f)
                if goal is not None:
                    pairs.append((s * shards + f, goal[0] * shards + goal[1]))
        return lax.ppermute(value, both, pairs)

    def gather(value):
        got = [value]
        for step in range(2, shards, 2):
            got.append(move(value, lambda s, f: (s, f ^ step)))
        pieces = []
        for piece in got:
            pieces += [piece, move(piece, lambda s, f: (s, f ^ 1))]
        return pieces

    def exchange(parts):
        return [part if step == 0 else move(part, lambda s, f: (s ^ step, f)) for step, part in enumerate(parts)]

    def total(value):
        step = 1
        while step < shards:
            value = value + move(value, lambda s, f: (s, f ^ step))
            step *= 2
        step = 1
        while step < ranks:
            value = value + move(value, lambda s, f: (s ^ step, f))
            step *= 2
        return value

    def ordered(pieces):
        stack = jnp.stack(pieces)
        return stack[jnp.arange(shards) ^ shard].reshape((-1,) + pieces[0].shape[1:])

    halo = move(tokens[0, -HALO:], lambda s, f: (s + 1, f) if s + 1 < ranks else None)
    values = tokens[0].astype(F32)
    longer = jnp.concatenate([halo, tokens[0]], axis=0).astype(F32)
    inverse = lax.rsqrt(jnp.mean(longer * longer, axis=-1, keepdims=True) + EPSILON)
    normed_long = (longer * inverse * norm_gain).astype(BF16)
    inverse = inverse[HALO:]
    normed = normed_long[HALO:]

    w_v = ordered(gather(w_in[:, INNER:]))
    w_g = ordered(gather(w_in[:, :INNER]))
    w_o = ordered(gather(w_out))

    projected = mm(normed_long, w_v).astype(BF16)
    dt_raw = jnp.pad(projected[HALO:, CONV:], ((0, 0), (0, 128 - HEADS)))
    lanes = lambda vec: jnp.pad(vec, (0, 128 - HEADS)).reshape(1, 128)
    rows, ecd, decay_all = step_call(dt_raw, lanes(dt_bias), lanes(a_log))
    v = projected[:, :CONV]
    made = conv_call(ranks, me, v, conv_weight, conv_bias.reshape(1, CONV), rows, decay_all)
    x_act, slope, b_act, c_act, b_turned, c_turned = made[:6]
    carried = carry_call(ranks, me, exchange(made[6:]))
    parts, totals = exchange(carried[:ranks]), carried[ranks]
    skip_wide = jnp.repeat(skip_gain, HEAD_DIM).reshape(1, INNER)
    y_inside = inside_call(x_act, b_act, c_act, b_turned, rows, skip_wide)
    gate_in = mm(normed, w_g).astype(BF16)
    cotan = cotangent[0]
    d_normed_out = mm_nt(cotan, w_o)
    made = gate_call(ranks, me, y_inside, gate_in, d_normed_out, c_act, c_turned, ecd, out_gain.reshape(1, INNER), parts)
    normed_out, d_gate, d_mixed, d_gain_out, s_in = made[:5]
    parts = exchange(carry_call(ranks, me, exchange(made[5:]), totals))
    block_out = values + mm(normed_out, w_o)

    def scattered(left, right):
        partial = lax.dot_general(left, right, TN, preferred_element_type=F32).astype(BF16)
        return lax.psum_scatter(partial, both, scatter_dimension=0, tiled=True).astype(F32)

    d_w_out = scattered(normed_out, cotan)
    d_w_gate = scattered(normed, d_gate)
    d_v_long, sums, heads = back_call(
        ranks, me, x_act, d_mixed, slope, v, conv_weight, b_act, c_act, b_turned, c_turned, rows, skip_wide, s_in, parts
    )
    d_w_rest = scattered(normed_long, d_v_long[:, : CONV + HEADS])
    d_w_in = jnp.concatenate([d_w_gate, d_w_rest], axis=1)

    spill = move(d_v_long[:HALO], lambda s, f: (s - 1, f) if s > 0 else None)
    ends = (d_v_long[-HALO:].astype(F32) + spill.astype(F32)).astype(BF16)
    d_v = lax.dynamic_update_slice(d_v_long, ends, (d_v_long.shape[0] - HALO, 0))[HALO:, : CONV + HEADS]
    d_normed = mm_nt(d_gate, w_g) + mm_nt(d_v, w_v)
    d_norm_gain = jnp.sum(d_normed * values * inverse, axis=0)
    scaled = d_normed * norm_gain
    shift = inverse * inverse * inverse * jnp.mean(scaled * values, axis=-1, keepdims=True)
    d_tokens = cotan.astype(F32) + inverse * scaled - values * shift

    d_skip = sums[KW + 1, :INNER].reshape(HEADS, HEAD_DIM).sum(axis=1)
    pieces = [
        d_norm_gain,
        sums[:KW].reshape(-1),
        sums[KW],
        heads[:, 0:4, 0].reshape(-1),
        heads[:, 8:12, 0].reshape(-1) * -jnp.exp(a_log),
        d_skip,
        d_gain_out.reshape(-1),
    ]
    flat = jnp.concatenate(pieces)
    width = flat.shape[0]
    flat = total(jnp.pad(flat, (0, -width % 1024)).reshape(-1, 128)).reshape(-1)
    small, at = [], 0
    for piece in pieces:
        small.append(flat[at : at + piece.shape[0]])
        at += piece.shape[0]
    d_norm_gain, d_conv_weight, d_conv_bias, d_dt_bias, d_a_log, d_skip, d_gain_out = small
    return (
        block_out[None],
        d_tokens[None],
        d_norm_gain,
        d_w_in,
        d_conv_weight.reshape(KW, CONV),
        d_conv_bias,
        d_dt_bias,
        d_a_log,
        d_skip,
        d_gain_out,
        d_w_out,
    )


def solution(mesh):
    split = P("fsdp", "seq", None)
    rows = P("fsdp", None)
    last = P(("seq", "fsdp"), None)
    return jax.shard_map(
        functools.partial(on_device, mesh.shape["seq"], mesh.shape["fsdp"]),
        mesh=mesh,
        in_specs=(split, P(), rows, P(), P(), P(), P(), P(), P(), rows, split),
        out_specs=(split, split, P(), last, P(), P(), P(), P(), P(), P(), last),
        check_vma=False,
    )
```

time: 2420 us -> 842 us (0.35)
  waiting for transfers between devices: 1020 us -> 406 us
  local copies, waits for them, and re-layouts: 577 us -> 82.5 us
  matrix products: 363 us -> 90.2 us
  other arithmetic: 325 us -> 58.3 us
  Pallas kernels: 0 us -> 110 us
  blocking collectives: 73.7 us -> 0 us
  starting transfers between devices: 23.3 us -> 76.3 us
    reduce_scatter x3, waiting for transfers between devices: 588 us -> 235 us  [scattered(): lax.psum_scatter(partial, both, scatter_dimension=0, tiled=True).astype(F32)]
    dynamic_update_slice x67 -> x0, local copies, waits for them, and re-layouts: 330 us -> none  [the longest x64 330 us: head_mix(): lax.scan(jax.checkpoint(one_block), start_state, (x_blocks, b_blocks, c_b...]
    dot_general x198 -> x9, matrix products: 333 us -> 90.2 us  [the longest x3 32.4 us: scattered(): lax.dot_general(left, right, TN, preferred_element_type=F32).astype(BF16)]
    all_gather x3 -> x0, waiting for transfers between devices: 200 us -> none  [the longest x1 128 us: on_device(): lax.all_gather(w_in, 'fsdp', axis=0, tiled=True)]
    another operation x161 -> x3, other arithmetic: 199 us -> 20 us  [ordered(): stack = jnp.stack(pieces)]
    ppermute x0 -> x44, waiting for transfers between devices: none -> 171 us  [move(): return lax.ppermute(value, both, pairs)]
    all_to_all x5 -> x0, waiting for transfers between devices: 160 us -> none  [the longest x1 84.4 us: on_device(): lax.all_to_all(d_x_heads.astype(jnp.bfloat16), 'seq', split_axis=0, conca...]
    pallas_call x0 -> x7, Pallas kernels: none -> 110 us  [the longest x1 53 us: back_call(): pl.pallas_call(functools.partial(back_kernel, ranks), grid_spec=grid_spec...]
  transfers between devices with their start and end apart: 12 -> 47, of which waited for: 8 -> 15; matrix products, arithmetic and copies ran while one was open for 24% -> 18% of each run, Pallas kernels for 0% -> 8%
where the time goes in v1:
time: 842 us; the launch traced here: 838 us
  waiting for transfers between devices  406 us (48%)
  Pallas kernels  110 us (13%)
  matrix products  90.2 us (11%)
  local copies, waits for them, and re-layouts  82.5 us (10%)
  starting transfers between devices  76.3 us (9%)
  other arithmetic  58.3 us (7%)
  between operations  14.7 us (2%)
    reduce_scatter x3, waiting for transfers between devices, scattered(): lax.psum_scatter(partial, both, scatter_dimension=0, tiled=True).astype(F32)  235 us
    ppermute x44, waiting for transfers between devices, move(): return lax.ppermute(value, both, pairs)  171 us
    ppermute x44, starting transfers between devices, move(): return lax.ppermute(value, both, pairs)  76.1 us
    pallas_call x1, Pallas kernels, back_call(): pl.pallas_call(functools.partial(back_kernel, ranks), grid_spec=grid_spec...  53 us
    gather x9, local copies, waits for them, and re-layouts, ordered(): stack[jnp.arange(shards) ^ shard].reshape((-1,) + pieces[0].shape[1:])  48.7 us
    dot_general x3, matrix products, scattered(): lax.dot_general(left, right, TN, preferred_element_type=F32).astype(BF16)  32.4 us
    dot_general x3, matrix products, mm(): return jnp.dot(a, b, preferred_element_type=F32)  31.4 us
    dot_general x3, matrix products, mm_nt(): return lax.dot_general(a, b, NT, preferred_element_type=F32)  26.5 us
  transfers between devices with their start and end apart: 47, of which 15 were waited for; matrix products, arithmetic and copies ran while one was open for 18% of the time, Pallas kernels for 8%

profile of v1, /device:TPU:0, one launch (start us, length us, event | category | flops | bytes accessed | tf_op | source)
XLA Modules:
  0.0 837.7 jit_solution(16179489367074756241)
XLA Ops:
  7.2 3.0 collective-permute-start.8
  14.5 4.5 slice_bitcast_fusion.3
  19.5 43.2 %collective-permute-done.8 = bf16[768,1536]{1,0:T(8,128)(2,1)} collective-permute-done((bf16[768,1536]{1,0:T(8,128)(2,1)}, bf16[768,1536]{1,0:T(8,128)(2,1)}, u32[]{:S(2)}, u32[]{:S(2)}) %collective-permute-start.8) | collective-permute-done | bytes 2359328 | tf_op jit(solution)/shard_map/ppermute | solution.py:670
  62.7 3.9 collective-permute-start
  69.2 44.0 %collective-permute-done.5 = bf16[384,3072]{1,0:T(8,128)(2,1)} collective-permute-done((bf16[384,3072]{1,0:T(8,128)(2,1)}, bf16[384,3072]{1,0:T(8,128)(2,1)}, u32[]{:S(2)}, u32[]{:S(2)}) %collective-permute-start.5) | collective-permute-done | bytes 2359328 | tf_op jit(solution)/shard_map/ppermute | solution.py:670
  115.4 52.6 %collective-permute-done.2 = bf16[384,3376]{0,1:T(8,128)(2,1)} collective-permute-done((bf16[384,3376]{0,1:T(8,128)(2,1)}, bf16[384,3376]{0,1:T(8,128)(2,1)}, u32[]{:S(2)}, u32[]{:S(2)}) %collective-permute-start.2) | collective-permute-done | bytes 2592800 | tf_op jit(solution)/shard_map/ppermute | solution.py:670
  168.0 4.9 pad_maximum_fusion.4
  172.8 4.2 fusion.20
  177.0 5.4 gather_fusion.4
  182.4 5.4 gather_fusion.5
  187.8 4.7 pad_maximum_fusion.5
  192.5 10.0 %pad_maximum_fusion.2 = bf16[4,384,3072]{2,1,0:T(8,128)(2,1)} fusion(bf16[1,384,3072]{2,1,0:T(8,128)(2,1)} %bitcast.14, bf16[1,384,3072]{2,1,0:T(8,128)(2,1)} %bitcast.13, bf16[1,384,3072]{2,1,0:T(8,128)(2,1)} %bitcast.12, bf16[1,384,3072]{2,1,0:T(8,128)(2,1)S(1)} %bitcast.74), kind=kLoop, calls=%fused_computation.11 | loop fusion | flops 14155776 | bytes 18874368 | tf_op jit(solution)/shard_map/stack | solution.py:696
  202.5 7.0 convolution_bitcast_fusion.dn_ref
  209.5 5.0 pad_maximum_fusion.6
  214.5 5.2 pad_maximum_fusion
  219.7 2.9 mini-gather-slice.6
  222.6 6.3 gather_fusion
  229.0 5.9 gather_fusion.1
  234.8 9.2 %pad_maximum_fusion.1 = bf16[4,384,3376]{1,2,0:T(8,128)(2,1)} fusion(bf16[4,384,1584]{1,2,0:T(8,128)(2,1)} %gather_fusion.1, bf16[4,384,1792]{1,2,0:T(8,128)(2,1)} %gather_fusion), kind=kLoop, calls=%fused_computation.10 | loop fusion | flops 20742144 | bytes 20742144
  244.1 13.9 %copy.25 = bf16[4,384,3376]{2,1,0:T(8,128)(2,1)} copy(bf16[4,384,3376]{1,2,0:T(8,128)(2,1)} %pad_maximum_fusion.1) | data formatting | bytes 20742144
  258.0 10.2 %convolution_convert_fusion.3 = bf16[528,3376]{1,0:T(8,128)(2,1)S(1)} fusion(bf16[528,1536]{1,0:T(8,128)(2,1)S(1)} %copy-done.6, bf16[1536,3376]{1,0:T(8,128)(2,1)} %bitcast.72), kind=kOutput, calls=%fused_computation.15 | convolution fusion | flops 5477708800 | bytes 15558144 | tf_op jit(solution)/shard_map/dot_general | solution.py:36
  273.5 17.9 %conv_states.1 = (bf16[512,3072]{1,0:T(8,128)(2,1)}, bf16[512,3328]{1,0:T(8,128)(2,1)}, bf16[512,128]{1,0:T(8,128)(2,1)}, bf16[512,128]{1,0:T(8,128)(2,1)}, bf16...) custom-call(s32[1]{0:T(128)} %bitcast.1.me_ref, ...), custom_call_target="tpu_custom_call" | custom-call | flops 400000000 | bytes 20000000 | tf_op jit(solution)/shard_map/conv_states/pallas_call | solution.py:199
  294.7 7.9 fusion.21
  302.7 5.3 gather_fusion.2
  308.0 5.3 gather_fusion.3
  313.5 2.8 collective-permute-start.13
  317.6 3.6 collective-permute-start.15
  321.3 9.1 %pad_maximum_fusion.3 = bf16[4,384,3072]{2,1,0:T(8,128)(2,1)} fusion(bf16[4,384,1536]{2,1,0:T(8,128)(2,1)} %gather_fusion.3, bf16[4,384,1536]{2,1,0:T(8,128)(2,1)} %gather_fusion.2), kind=kLoop, calls=%fused_computation.12 | loop fusion | flops 18874368 | bytes 18874368
  336.2 4.2 collective-permute-start.18
  340.5 10.1 %convolution_convert_fusion.4.gate_ref = bf16[512,3072]{1,0:T(8,128)(2,1)} fusion(bf16[1536,3072]{1,0:T(8,128)(2,1)} %bitcast.77, bf16[528,1536]{1,0:T(8,128)(2,1)S(1)} %copy-done.6), kind=kOutput, calls=%fused_computation.22 | convolution fusion | flops 4833411072 | bytes 14155776 | tf_op jit(solution)/shard_map/dot_general | solution.py:36
  351.3 3.8 collective-permute-start.20
  360.0 15.5 %ssd_inside.1.y_ref = f32[512,3072]{1,0:T(8,128)} custom-call(bf16[512,3072]{1,0:T(8,128)(2,1)} %get-tuple-element.63.x_ref, bf16[512,128]{1,0:T(8,128)(2,1)} %get-tuple-element.64.b_ref, bf16[512,128]{1,0:T(8,128)(2,1)} %get-tuple-element.65.c_ref, bf16[128,512]{1,0:T(8,128)(2,1)} %get-tuple-element.66.bt_ref, f32[12,40,512]{2,1,0:T(8,128)} %get-tuple-element.61.rows_ref, ...), custom_call_target="tpu_custom_call" | custom-call | flops 8000000000 | bytes 20000000 | tf_op jit(solution)/shard_map/ssd_inside/pallas_call | solution.py:307
  376.3 15.8 %gated_norm.1 = (bf16[512,3072]{1,0:T(8,128)(2,1)}, bf16[512,3072]{1,0:T(8,128)(2,1)}, bf16[512,3072]{1,0:T(8,128)(2,1)}, f32[1,3072]{1,0:T(1,128)}, bf16[128,30...) custom-call(s32[1]{0:T(128)} %bitcast.1.me_ref, ...), custom_call_target="tpu_custom_call" | custom-call | flops 2000000000 | bytes 30000000 | tf_op jit(solution)/shard_map/gated_norm/pallas_call | solution.py:420
  392.2 10.0 %convolution_convert_fusion.1 = bf16[3072,1536]{1,0:T(8,128)(2,1)} fusion(bf16[512,3072]{1,0:T(8,128)(2,1)} %get-tuple-element.85, bf16[1,512,1536]{2,1,0:T(8,128)(2,1)S(1)} %copy-done.7), kind=kOutput, calls=%fused_computation.7 | convolution fusion | flops 4836556800 | bytes 14155776 | tf_op jit(solution)/shard_map/dot_general | solution.py:731
  402.2 9.4 %convolution_convert_fusion.2 = bf16[1536,3072]{1,0:T(8,128)(2,1)} fusion(bf16[512,3072]{1,0:T(8,128)(2,1)} %get-tuple-element.86, bf16[528,1536]{1,0:T(8,128)(2,1)S(1)} %copy-done.6), kind=kOutput, calls=%fused_computation.8 | convolution fusion | flops 4836556800 | bytes 14155776 | tf_op jit(solution)/shard_map/dot_general | solution.py:731
  412.3 2.9 collective-permute-start.26
  423.0 6.1 collective-permute-done.27.rest_4_
  446.9 5.7 collective-permute-done.34.rest_4_
  456.0 53.0 %ssd_back.1 = (bf16[528,3584]{1,0:T(8,128)(2,1)}, f32[8,3328]{1,0:T(8,128)}, f32[12,16,128]{2,1,0:T(8,128)}) custom-call(s32[1]{0:T(128)} %bitcast.1.me_ref, bf16[512,3072]{1,0:T(8,128)(2,1)} %get-tuple-element.63.x_ref, bf16[512,3072]{1,0:T(8,128)(2,1)} %get-tuple-element.87.dm_ref, bf16[512,3328]{1,0:T(8,128)(2,1)} %get-tuple-element.88.slope_ref, ...), custom_call_target="tpu_custom_call" | custom-call | flops 20000000000 | bytes 40000000 | tf_op jit(solution)/shard_map/ssd_back/pallas_call | solution.py:629
  508.9 13.0 %convolution_convert_fusion = bf16[1536,3376]{1,0:T(8,128)(2,1)} fusion(bf16[528,1536]{1,0:T(8,128)(2,1)S(1)} %copy-done.6, bf16[528,3584]{1,0:T(8,128)(2,1)} %get-tuple-element.107), kind=kOutput, calls=%fused_computation.6 | convolution fusion | flops 5481111552 | bytes 15642624 | tf_op jit(solution)/shard_map/dot_general | solution.py:731
  525.6 5.8 collective-permute-done.38
  533.0 10.1 %fusion.1 = f32[512,1536]{1,0:T(8,128)S(1)} fusion(bf16[1536,3376]{1,0:T(8,128)(2,1)} %bitcast.73, bf16[528,3584]{1,0:T(8,128)(2,1)} %fusion.16), kind=kOutput, calls=%fused_computation.26 | convolution fusion | flops 5309988864 | bytes 17301504 | tf_op jit(solution)/shard_map/dot_general | solution.py:40
  543.2 9.4 %fusion.11 = (f32[1536]{0:T(1024)S(1)}, f32[512]{0:T(512)S(1)}, f32[512,1536]{1,0:T(8,128)}) fusion(f32[512]{0:T(512)S(1)} %slice.85, bf16[1,512,1536]{2,1,0:T(8,128)(2,1)S(1)} %copy-done.2, f32[1536]{0:T(1024)S(1)} %copy-done.31, f32[512,1536]{1,0:T(8,128)S(1)} %fusion.1, bf16[512,3072]{1,0:T(8,128)(2,1)S(1)} %copy-done.41, bf16[1536,3072]{1,0:T(8,128)(2,1)} %bitcast.78), kind=kOutput, calls=%fused_computation.37 | convolution fusion | flops 4838127616 | bytes 20463616 | tf_op jit(solution)/shard_map/dot_general | solution.py:40
  555.6 11.0 %fusion.6 = f32[1,512,1536]{2,1,0:T(8,128)} fusion(bf16[512,3072]{1,0:T(8,128)(2,1)} %get-tuple-element.85, bf16[3072,1536]{1,0:T(8,128)(2,1)} %bitcast.76, bf16[1,512,1536]{2,1,0:T(8,128)(2,1)S(1)} %copy-done.2), kind=kOutput, calls=%fused_computation.32 | convolution fusion | flops 4833411072 | bytes 17301504 | tf_op jit(solution)/shard_map/dot_general | solution.py:36
  566.6 8.5 %collective-permute-start.41 = (f32[168,128]{1,0:T(8,128)S(1)}, f32[168,128]{1,0:T(8,128)S(1)}, u32[]{:S(2)}, u32[]{:S(2)}) collective-permute-start(f32[168,128]{1,0:T(8,128)S(1)} %fusion.35), channel_id=1, source_target_pairs={{0,4},{1,5},{2,6},{3,7},{4,0},{5,1},{6,2},{7,3},{8,12},{9,13},{10,... | collective-permute-start | bytes 258056 | tf_op jit(solution)/shard_map/ppermute | solution.py:670
  582.9 3.3 collective-permute-start.43
  593.7 88.0 %reduce-scatter.4.cloned.1.call-done = bf16[48,3072]{1,0:T(8,128)(2,1)} async-done(((bf16[1536,3072]{1,0:T(8,128)(2,1)}), bf16[48,3072]{1,0:T(8,128)(2,1)}) %reduce-scatter.4.cloned.1.call-update) | async-done | bytes 294928 | tf_op jit(solution)/shard_map/reduce_scatter | solution.py:732
  681.8 147.0 %reduce-scatter.6.cloned.1.call-done = bf16[48,3376]{1,0:T(8,128)(2,1)} async-done(((bf16[1536,3376]{1,0:T(8,128)(2,1)}), bf16[48,3376]{1,0:T(8,128)(2,1)}) %reduce-scatter.6.cloned.1.call-update) | async-done | bytes 324112 | tf_op jit(solution)/shard_map/reduce_scatter | solution.py:732
  (246 shorter events, 87.0 us)
Async XLA Ops:
  7.2 584.7 %reduce-scatter.8.cloned.1.call-start = ((), (), s32[]{:S(2)}) async-start(), calls=%async_computation.5 | async-start | bytes 9732096 | tf_op jit(solution)/shard_map/reduce_scatter | solution.py:732
  7.2 55.4 %collective-permute-start.8 = (bf16[768,1536]{1,0:T(8,128)(2,1)}, bf16[768,1536]{1,0:T(8,128)(2,1)}, u32[]{:S(2)}, u32[]{:S(2)}) collective-permute-start(bf16[768,1536]{1,0:T(8,128)(2,1)} %param.20), channel_id=1, source_target_pairs={{0,2},{1,3},{2,0},{3,1},{4,6},{5,7},{6,4},{7,5},{8,10},{9,11},{10,... | collective-permute-start | bytes 7077896 | tf_op jit(solution)/shard_map/ppermute | solution.py:670
  12.9 100.4 %copy-start.30 = (f32[1536]{0:T(1024)S(1)}, f32[1536]{0:T(1024)}, u32[]{:S(2)}) copy-start(f32[1536]{0:T(1024)} %param.12) | copy-start | bytes 18436
  12.9 100.3 %collective-permute-start.5 = (bf16[384,3072]{1,0:T(8,128)(2,1)}, bf16[384,3072]{1,0:T(8,128)(2,1)}, u32[]{:S(2)}, u32[]{:S(2)}) collective-permute-start(bf16[384,3072]{1,0:T(8,128)(2,1)} %copy.29), channel_id=1, source_target_pairs={{0,2},{1,3},{2,0},{3,1},{4,6},{5,7},{6,4},{7,5},{8,10},{9,11},{10,... | collective-permute-start | bytes 7077896 | tf_op jit(solution)/shard_map/ppermute | solution.py:670
  19.0 148.9 %collective-permute-start.2 = (bf16[384,3376]{0,1:T(8,128)(2,1)}, bf16[384,3376]{0,1:T(8,128)(2,1)}, u32[]{:S(2)}, u32[]{:S(2)}) collective-permute-start(bf16[384,3376]{0,1:T(8,128)(2,1)} %get-tuple-element.120), channel_id=1, source_target_pairs={{0,2},{1,3},{2,0},{3,1},{4,6},{5,7},{6,4},{7,5},{8,10},{9,11},{10,... | collective-permute-start | bytes 7778312 | tf_op jit(solution)/shard_map/ppermute | solution.py:670
  19.5 95.4 %collective-permute-start.7 = (bf16[768,1536]{1,0:T(8,128)(2,1)}, bf16[768,1536]{1,0:T(8,128)(2,1)}, u32[]{:S(2)}, u32[]{:S(2)}) collective-permute-start(bf16[768,1536]{1,0:T(8,128)(2,1)} %param.20), channel_id=1, source_target_pairs={{0,1},{1,0},{2,3},{3,2},{4,5},{5,4},{6,7},{7,6},{8,9},{9,8},{10,11... | collective-permute-start | bytes 7077896 | tf_op jit(solution)/shard_map/ppermute | solution.py:670
  62.7 105.3 %collective-permute-start.9 = (bf16[768,1536]{1,0:T(8,128)(2,1)}, bf16[768,1536]{1,0:T(8,128)(2,1)}, u32[]{:S(2)}, u32[]{:S(2)}) collective-permute-start(bf16[768,1536]{1,0:T(8,128)(2,1)} %collective-permute-done.8), channel_id=1, source_target_pairs={{0,1},{1,0},{2,3},{3,2},{4,5},{5,4},{6,7},{7,6},{8,9},{9,8},{10,11... | collective-permute-start | bytes 7077896 | tf_op jit(solution)/shard_map/ppermute | solution.py:670
  62.7 5.9 collective-permute-start
  68.6 123.9 %collective-permute-start.4 = (bf16[384,3072]{1,0:T(8,128)(2,1)}, bf16[384,3072]{1,0:T(8,128)(2,1)}, u32[]{:S(2)}, u32[]{:S(2)}) collective-permute-start(bf16[384,3072]{1,0:T(8,128)(2,1)} %copy.29), channel_id=1, source_target_pairs={{0,1},{1,0},{2,3},{3,2},{4,5},{5,4},{6,7},{7,6},{8,9},{9,8},{10,11... | collective-permute-start | bytes 7077896 | tf_op jit(solution)/shard_map/ppermute | solution.py:670
  113.2 79.3 %collective-permute-start.6 = (bf16[384,3072]{1,0:T(8,128)(2,1)}, bf16[384,3072]{1,0:T(8,128)(2,1)}, u32[]{:S(2)}, u32[]{:S(2)}) collective-permute-start(bf16[384,3072]{1,0:T(8,128)(2,1)} %collective-permute-done.5), channel_id=1, source_target_pairs={{0,1},{1,0},{2,3},{3,2},{4,5},{5,4},{6,7},{7,6},{8,9},{9,8},{10,11... | collective-permute-start | bytes 7077896 | tf_op jit(solution)/shard_map/ppermute | solution.py:670
  114.8 94.6 %collective-permute-start.1 = (bf16[384,3376]{0,1:T(8,128)(2,1)}, bf16[384,3376]{0,1:T(8,128)(2,1)}, u32[]{:S(2)}, u32[]{:S(2)}) collective-permute-start(bf16[384,3376]{0,1:T(8,128)(2,1)} %get-tuple-element.120), channel_id=1, source_target_pairs={{0,1},{1,0},{2,3},{3,2},{4,5},{5,4},{6,7},{7,6},{8,9},{9,8},{10,11... | collective-permute-start | bytes 7778312 | tf_op jit(solution)/shard_map/ppermute | solution.py:670
  168.0 41.5 %collective-permute-start.3 = (bf16[384,3376]{0,1:T(8,128)(2,1)}, bf16[384,3376]{0,1:T(8,128)(2,1)}, u32[]{:S(2)}, u32[]{:S(2)}) collective-permute-start(bf16[384,3376]{0,1:T(8,128)(2,1)} %collective-permute-done.2), channel_id=1, source_target_pairs={{0,1},{1,0},{2,3},{3,2},{4,5},{5,4},{6,7},{7,6},{8,9},{9,8},{10,11... | collective-permute-start | bytes 7778312 | tf_op jit(solution)/shard_map/ppermute | solution.py:670
  291.4 26.2 %collective-permute-start.10 = (bf16[16,3200]{1,0:T(8,128)(2,1)}, bf16[16,3200]{1,0:T(8,128)(2,1)S(1)}, u32[]{:S(2)}, u32[]{:S(2)}) collective-permute-start(bf16[16,3200]{1,0:T(8,128)(2,1)} %get-tuple-element.70), channel_id=1, source_target_pairs={{0,4},{1,5},{2,6},{3,7},{4,0},{5,1},{6,2},{7,3},{8,12},{9,13},{10,... | collective-permute-start | bytes 307208 | tf_op jit(solution)/shard_map/ppermute | solution.py:670
  293.2 28.0 %collective-permute-start.11 = (bf16[16,3200]{1,0:T(8,128)(2,1)}, bf16[16,3200]{1,0:T(8,128)(2,1)S(1)}, u32[]{:S(2)}, u32[]{:S(2)}) collective-permute-start(bf16[16,3200]{1,0:T(8,128)(2,1)} %get-tuple-element.71), channel_id=1, source_target_pairs={{0,8},{1,9},{2,10},{3,11},{4,12},{5,13},{6,14},{7,15},{8,0},{9,1},... | collective-permute-start | bytes 307208 | tf_op jit(solution)/shard_map/ppermute | solution.py:670
  313.3 17.1 %collective-permute-start.12 = (bf16[16,3200]{1,0:T(8,128)(2,1)}, bf16[16,3200]{1,0:T(8,128)(2,1)S(1)}, u32[]{:S(2)}, u32[]{:S(2)}) collective-permute-start(bf16[16,3200]{1,0:T(8,128)(2,1)} %get-tuple-element.72), channel_id=1, source_target_pairs={{0,12},{1,13},{2,14},{3,15},{4,8},{5,9},{6,10},{7,11},{8,4},{9,5},... | collective-permute-start | bytes 307208 | tf_op jit(solution)/shard_map/ppermute | solution.py:670
  313.5 16.9 %collective-permute-start.13 = (bf16[16,3200]{1,0:T(8,128)(2,1)}, bf16[16,3200]{1,0:T(8,128)(2,1)S(1)}, u32[]{:S(2)}, u32[]{:S(2)}) collective-permute-start(bf16[16,3200]{1,0:T(8,128)(2,1)} %get-tuple-element.73), channel_id=1, source_target_pairs={{0,16},{1,17},{2,18},{3,19},{4,20},{5,21},{6,22},{7,23},{8,24},{9,... | collective-permute-start | bytes 307208 | tf_op jit(solution)/shard_map/ppermute | solution.py:670
  316.3 15.7 %collective-permute-start.14 = (bf16[16,3200]{1,0:T(8,128)(2,1)}, bf16[16,3200]{1,0:T(8,128)(2,1)S(1)}, u32[]{:S(2)}, u32[]{:S(2)}) collective-permute-start(bf16[16,3200]{1,0:T(8,128)(2,1)} %get-tuple-element.74), channel_id=1, source_target_pairs={{0,20},{1,21},{2,22},{3,23},{4,16},{5,17},{6,18},{7,19},{8,28},{9,... | collective-permute-start | bytes 307208 | tf_op jit(solution)/shard_map/ppermute | solution.py:670
  317.6 14.5 %collective-permute-start.15 = (bf16[16,3200]{1,0:T(8,128)(2,1)}, bf16[16,3200]{1,0:T(8,128)(2,1)S(1)}, u32[]{:S(2)}, u32[]{:S(2)}) collective-permute-start(bf16[16,3200]{1,0:T(8,128)(2,1)} %get-tuple-element.75), channel_id=1, source_target_pairs={{0,24},{1,25},{2,26},{3,27},{4,28},{5,29},{6,30},{7,31},{8,16},{9,... | collective-permute-start | bytes 307208 | tf_op jit(solution)/shard_map/ppermute | solution.py:670
  321.2 10.9 %collective-permute-start.16 = (bf16[16,3200]{1,0:T(8,128)(2,1)S(1)}, bf16[16,3200]{1,0:T(8,128)(2,1)S(1)}, u32[]{:S(2)}, u32[]{:S(2)}) collective-permute-start(bf16[16,3200]{1,0:T(8,128)(2,1)S(1)} %copy-done.42), channel_id=1, source_target_pairs={{0,28},{1,29},{2,30},{3,31},{4,24},{5,25},{6,26},{7,27},{8,20},{9,... | collective-permute-start | bytes 307208 | tf_op jit(solution)/shard_map/ppermute | solution.py:670
  335.4 19.7 %collective-permute-start.17 = (bf16[16,3072]{1,0:T(8,128)(2,1)}, bf16[16,3072]{1,0:T(8,128)(2,1)S(1)}, u32[]{:S(2)}, u32[]{:S(2)}) collective-permute-start(bf16[16,3072]{1,0:T(8,128)(2,1)} %get-tuple-element.78), channel_id=1, source_target_pairs={{0,4},{1,5},{2,6},{3,7},{4,0},{5,1},{6,2},{7,3},{8,12},{9,13},{10,... | collective-permute-start | bytes 294920 | tf_op jit(solution)/shard_map/ppermute | solution.py:670
  336.2 21.4 %collective-permute-start.18 = (bf16[16,3072]{1,0:T(8,128)(2,1)}, bf16[16,3072]{1,0:T(8,128)(2,1)S(1)}, u32[]{:S(2)}, u32[]{:S(2)}) collective-permute-start(bf16[16,3072]{1,0:T(8,128)(2,1)} %get-tuple-element.79), channel_id=1, source_target_pairs={{0,8},{1,9},{2,10},{3,11},{4,12},{5,13},{6,14},{7,15},{8,0},{9,1},... | collective-permute-start | bytes 294920 | tf_op jit(solution)/shard_map/ppermute | solution.py:670
  350.6 24.9 %collective-permute-start.19 = (bf16[16,3072]{1,0:T(8,128)(2,1)S(1)}, bf16[16,3072]{1,0:T(8,128)(2,1)S(1)}, u32[]{:S(2)}, u32[]{:S(2)}) collective-permute-start(bf16[16,3072]{1,0:T(8,128)(2,1)S(1)} %copy-done.55), channel_id=1, source_target_pairs={{0,12},{1,13},{2,14},{3,15},{4,8},{5,9},{6,10},{7,11},{8,4},{9,5},... | collective-permute-start | bytes 294920 | tf_op jit(solution)/shard_map/ppermute | solution.py:670
  351.3 24.2 %collective-permute-start.20 = (bf16[16,3072]{1,0:T(8,128)(2,1)S(1)}, bf16[16,3072]{1,0:T(8,128)(2,1)S(1)}, u32[]{:S(2)}, u32[]{:S(2)}) collective-permute-start(bf16[16,3072]{1,0:T(8,128)(2,1)S(1)} %copy-done.54), channel_id=1, source_target_pairs={{0,16},{1,17},{2,18},{3,19},{4,20},{5,21},{6,22},{7,23},{8,24},{9,... | collective-permute-start | bytes 294920 | tf_op jit(solution)/shard_map/ppermute | solution.py:670
  355.1 20.5 %collective-permute-start.21 = (bf16[16,3072]{1,0:T(8,128)(2,1)S(1)}, bf16[16,3072]{1,0:T(8,128)(2,1)S(1)}, u32[]{:S(2)}, u32[]{:S(2)}) collective-permute-start(bf16[16,3072]{1,0:T(8,128)(2,1)S(1)} %copy-done.52), channel_id=1, source_target_pairs={{0,20},{1,21},{2,22},{3,23},{4,16},{5,17},{6,18},{7,19},{8,28},{9,... | collective-permute-start | bytes 294920 | tf_op jit(solution)/shard_map/ppermute | solution.py:670
  355.1 20.4 %collective-permute-start.22 = (bf16[16,3072]{1,0:T(8,128)(2,1)S(1)}, bf16[16,3072]{1,0:T(8,128)(2,1)S(1)}, u32[]{:S(2)}, u32[]{:S(2)}) collective-permute-start(bf16[16,3072]{1,0:T(8,128)(2,1)S(1)} %copy-done.50), channel_id=1, source_target_pairs={{0,24},{1,25},{2,26},{3,27},{4,28},{5,29},{6,30},{7,31},{8,16},{9,... | collective-permute-start | bytes 294920 | tf_op jit(solution)/shard_map/ppermute | solution.py:670
  357.6 18.0 %collective-permute-start.23 = (bf16[16,3072]{1,0:T(8,128)(2,1)S(1)}, bf16[16,3072]{1,0:T(8,128)(2,1)S(1)}, u32[]{:S(2)}, u32[]{:S(2)}) collective-permute-start(bf16[16,3072]{1,0:T(8,128)(2,1)S(1)} %copy-done.48), channel_id=1, source_target_pairs={{0,28},{1,29},{2,30},{3,31},{4,24},{5,25},{6,26},{7,27},{8,20},{9,... | collective-permute-start | bytes 294920 | tf_op jit(solution)/shard_map/ppermute | solution.py:670
  402.2 279.6 %reduce-scatter.4.cloned.1.call-start = ((), (), s32[]{:S(2)}) async-start(), calls=%async_computation.3 | async-start | bytes 9732096 | tf_op jit(solution)/shard_map/reduce_scatter | solution.py:732
  411.6 417.1 %reduce-scatter.6.cloned.1.call-start = ((), (), s32[]{:S(2)}) async-start(), calls=%async_computation.4 | async-start | bytes 10948608 | tf_op jit(solution)/shard_map/reduce_scatter | solution.py:732
  411.7 6.5 collective-permute-start.24
  412.3 8.3 collective-permute-start.25
  412.3 10.7 %collective-permute-start.26 = (bf16[16,3072]{1,0:T(8,128)(2,1)}, bf16[16,3072]{1,0:T(8,128)(2,1)S(1)}, u32[]{:S(2)}, u32[]{:S(2)}) collective-permute-start(bf16[16,3072]{1,0:T(8,128)(2,1)} %get-tuple-element.93), channel_id=1, source_target_pairs={{0,12},{1,13},{2,14},{3,15},{4,8},{5,9},{6,10},{7,11},{8,4},{9,5},... | collective-permute-start | bytes 294920 | tf_op jit(solution)/shard_map/ppermute | solution.py:670
  415.2 13.9 %collective-permute-start.27 = (bf16[16,3072]{1,0:T(8,128)(2,1)}, bf16[16,3072]{1,0:T(8,128)(2,1)S(1)}, u32[]{:S(2)}, u32[]{:S(2)}) collective-permute-start(bf16[16,3072]{1,0:T(8,128)(2,1)} %get-tuple-element.94), channel_id=1, source_target_pairs={{0,16},{1,17},{2,18},{3,19},{4,20},{5,21},{6,22},{7,23},{8,24},{9,... | collective-permute-start | bytes 294920 | tf_op jit(solution)/shard_map/ppermute | solution.py:670
  416.3 14.9 %collective-permute-start.28 = (bf16[16,3072]{1,0:T(8,128)(2,1)S(1)}, bf16[16,3072]{1,0:T(8,128)(2,1)S(1)}, u32[]{:S(2)}, u32[]{:S(2)}) collective-permute-start(bf16[16,3072]{1,0:T(8,128)(2,1)S(1)} %copy-done.45), channel_id=1, source_target_pairs={{0,20},{1,21},{2,22},{3,23},{4,16},{5,17},{6,18},{7,19},{8,28},{9,... | collective-permute-start | bytes 294920 | tf_op jit(solution)/shard_map/ppermute | solution.py:670
  418.2 13.0 %collective-permute-start.29 = (bf16[16,3072]{1,0:T(8,128)(2,1)S(1)}, bf16[16,3072]{1,0:T(8,128)(2,1)S(1)}, u32[]{:S(2)}, u32[]{:S(2)}) collective-permute-start(bf16[16,3072]{1,0:T(8,128)(2,1)S(1)} %copy-done.44), channel_id=1, source_target_pairs={{0,24},{1,25},{2,26},{3,27},{4,28},{5,29},{6,30},{7,31},{8,16},{9,... | collective-permute-start | bytes 294920 | tf_op jit(solution)/shard_map/ppermute | solution.py:670
  420.6 10.6 %collective-permute-start.30 = (bf16[16,3072]{1,0:T(8,128)(2,1)S(1)}, bf16[16,3072]{1,0:T(8,128)(2,1)S(1)}, u32[]{:S(2)}, u32[]{:S(2)}) collective-permute-start(bf16[16,3072]{1,0:T(8,128)(2,1)S(1)} %copy-done.43), channel_id=1, source_target_pairs={{0,28},{1,29},{2,30},{3,31},{4,24},{5,25},{6,26},{7,27},{8,20},{9,... | collective-permute-start | bytes 294920 | tf_op jit(solution)/shard_map/ppermute | solution.py:670
  434.7 7.9 collective-permute-start.31
  436.1 8.8 %collective-permute-start.32 = (bf16[16,3072]{1,0:T(8,128)(2,1)}, bf16[16,3072]{1,0:T(8,128)(2,1)S(1)}, u32[]{:S(2)}, u32[]{:S(2)}) collective-permute-start(bf16[16,3072]{1,0:T(8,128)(2,1)} %get-tuple-element.101), channel_id=1, source_target_pairs={{0,8},{1,9},{2,10},{3,11},{4,12},{5,13},{6,14},{7,15},{8,0},{9,1},... | collective-permute-start | bytes 294920 | tf_op jit(solution)/shard_map/ppermute | solution.py:670
  438.8 8.2 collective-permute-start.33
  438.8 13.9 %collective-permute-start.34 = (bf16[16,3072]{1,0:T(8,128)(2,1)}, bf16[16,3072]{1,0:T(8,128)(2,1)S(1)}, u32[]{:S(2)}, u32[]{:S(2)}) collective-permute-start(bf16[16,3072]{1,0:T(8,128)(2,1)} %get-tuple-element.103), channel_id=1, source_target_pairs={{0,16},{1,17},{2,18},{3,19},{4,20},{5,21},{6,22},{7,23},{8,24},{9,... | collective-permute-start | bytes 294920 | tf_op jit(solution)/shard_map/ppermute | solution.py:670
  441.6 13.7 %collective-permute-start.35 = (bf16[16,3072]{1,0:T(8,128)(2,1)}, bf16[16,3072]{1,0:T(8,128)(2,1)S(1)}, u32[]{:S(2)}, u32[]{:S(2)}) collective-permute-start(bf16[16,3072]{1,0:T(8,128)(2,1)} %get-tuple-element.104), channel_id=1, source_target_pairs={{0,20},{1,21},{2,22},{3,23},{4,16},{5,17},{6,18},{7,19},{8,28},{9,... | collective-permute-start | bytes 294920 | tf_op jit(solution)/shard_map/ppermute | solution.py:670
  442.6 12.7 %collective-permute-start.36 = (bf16[16,3072]{1,0:T(8,128)(2,1)}, bf16[16,3072]{1,0:T(8,128)(2,1)S(1)}, u32[]{:S(2)}, u32[]{:S(2)}) collective-permute-start(bf16[16,3072]{1,0:T(8,128)(2,1)} %get-tuple-element.105), channel_id=1, source_target_pairs={{0,24},{1,25},{2,26},{3,27},{4,28},{5,29},{6,30},{7,31},{8,16},{9,... | collective-permute-start | bytes 294920 | tf_op jit(solution)/shard_map/ppermute | solution.py:670
  444.9 10.4 %collective-permute-start.37 = (bf16[16,3072]{1,0:T(8,128)(2,1)}, bf16[16,3072]{1,0:T(8,128)(2,1)S(1)}, u32[]{:S(2)}, u32[]{:S(2)}) collective-permute-start(bf16[16,3072]{1,0:T(8,128)(2,1)} %get-tuple-element.106), channel_id=1, source_target_pairs={{0,28},{1,29},{2,30},{3,31},{4,24},{5,25},{6,26},{7,27},{8,20},{9,... | collective-permute-start | bytes 294920 | tf_op jit(solution)/shard_map/ppermute | solution.py:670
  524.1 7.3 collective-permute-start.38
  552.6 1.3 collective-permute-start.39
  554.0 12.6 %collective-permute-start.40 = (f32[168,128]{1,0:T(8,128)S(1)}, f32[168,128]{1,0:T(8,128)S(1)}, u32[]{:S(2)}, u32[]{:S(2)}) collective-permute-start(f32[168,128]{1,0:T(8,128)S(1)} %fusion.19), channel_id=1, source_target_pairs={{0,2},{1,3},{2,0},{3,1},{4,6},{5,7},{6,4},{7,5},{8,10},{9,11},{10,... | collective-permute-start | bytes 258056 | tf_op jit(solution)/shard_map/ppermute | solution.py:670
  566.6 11.1 %collective-permute-start.41 = (f32[168,128]{1,0:T(8,128)S(1)}, f32[168,128]{1,0:T(8,128)S(1)}, u32[]{:S(2)}, u32[]{:S(2)}) collective-permute-start(f32[168,128]{1,0:T(8,128)S(1)} %fusion.35), channel_id=1, source_target_pairs={{0,4},{1,5},{2,6},{3,7},{4,0},{5,1},{6,2},{7,3},{8,12},{9,13},{10,... | collective-permute-start | bytes 258056 | tf_op jit(solution)/shard_map/ppermute | solution.py:670
  577.7 5.2 collective-permute-start.42
  582.9 5.8 collective-permute-start.43
  (58 other events, 736.4 us)
Sparse Core Ops, SparseCore 0:
  402.3 138.2 reduce-scatter.7
  547.5 134.2 reduce-scatter.3
  687.8 140.8 reduce-scatter.5

commit v2 on v1

v2 whole, which is shorter than its diff:
```python
import functools

import jax
import jax.numpy as jnp
from jax import lax
from jax.experimental import pallas as pl
from jax.experimental.pallas import tpu as pltpu
from jax.sharding import PartitionSpec as P

HEADS = 48
HEAD_DIM = 64
STATE = 128
KW = 4
INNER = 3072
D = 1536
CONV = INNER + 2 * STATE

EPSILON = 1e-05
CHUNK = 128
QUAD = 256
QUADS = INNER // QUAD
HALO = 16
VMEM_LIMIT = 56 * 1024 * 1024
COST = pl.CostEstimate(flops=1000000, bytes_accessed=1000000, transcendentals=0)
F32 = jnp.float32
BF16 = jnp.bfloat16
HIGHEST = lax.Precision.HIGHEST
NT = (((1,), (1,)), ((), ()))
TN = (((0,), (0,)), ((), ()))


def iota(shape, axis):
    return lax.broadcasted_iota(jnp.int32, shape, axis)


def mm(a, b):
    return jnp.dot(a, b, preferred_element_type=F32)


def mm_nt(a, b):
    return lax.dot_general(a, b, NT, preferred_element_type=F32)


def sigmoid(v):
    return 0.5 * jnp.tanh(0.5 * v) + 0.5


def split3(v):
    high = v.astype(BF16)
    rest = v - high.astype(F32)
    mid = rest.astype(BF16)
    low = (rest - mid.astype(F32)).astype(BF16)
    return high, mid, low


def mm_exact(v, ones):
    high, mid, low = split3(v)
    return mm(high, ones) + mm(mid, ones) + mm(low, ones)


def head_ones():
    return jnp.where((iota((128, INNER), 1) >> 6) == iota((128, INNER), 0), 1.0, 0.0).astype(BF16)


def two_heads(first, second):
    return jnp.where(iota((CHUNK, 128), 1) < HEAD_DIM, first, second)


def spread(cols, start):
    wide = [jnp.broadcast_to(cols[:, start + i : start + i + 1], (CHUNK, 128)) for i in range(4)]
    return wide, jnp.concatenate([two_heads(wide[0], wide[1]), two_heads(wide[2], wide[3])], axis=1)


def fold_rows(value):
    return jnp.sum(value.reshape(-1, 8, value.shape[1]), axis=0)


def columns_of(rows):
    count, length = rows.shape
    return jnp.concatenate([rows, jnp.zeros((128 - count, length), F32)], axis=0).T


def step_kernel(dt_ref, bias_ref, alog_ref, rows_ref, ecd_ref, total_ref):
    length = dt_ref.shape[0] - HALO
    raw = dt_ref[HALO:, :].astype(F32) + bias_ref[...]
    step = jnp.maximum(raw, 0.0) + jnp.log1p(jnp.exp(-jnp.abs(raw)))
    sig = 1.0 / (1.0 + jnp.exp(-raw))
    rate = -jnp.exp(alog_ref[...])
    pace = step * rate
    lower = jnp.where(iota((CHUNK, CHUNK), 0) >= iota((CHUNK, CHUNK), 1), 1.0, 0.0).astype(F32)
    inside, along = [], []
    offset = jnp.zeros((1, 128), F32)
    for start in range(0, length, CHUNK):
        part = jnp.dot(lower, pace[start : start + CHUNK], precision=HIGHEST, preferred_element_type=F32)
        inside.append(part)
        along.append(part + offset)
        offset = offset + part[CHUNK - 1 : CHUNK]
    cum = jnp.concatenate(inside, axis=0)
    along = jnp.concatenate(along, axis=0)
    ecd_ref[...] = jnp.exp(along)
    total_ref[...] = jnp.broadcast_to(jnp.exp(offset), (8, 128))
    left = jnp.exp(offset - along) * step
    for place, array in enumerate((cum, step, left, sig, jnp.broadcast_to(rate, (length, 128)))):
        turned = array.T
        for quad in range(QUADS):
            rows_ref[quad, 8 * place : 8 * place + 4, :] = turned[4 * quad : 4 * quad + 4, :]
            rows_ref[quad, 8 * place + 4 : 8 * place + 8, :] = jnp.zeros((4, length), F32)


def step_call(projected, dt_bias, a_log):
    length = projected.shape[0] - HALO
    line = pl.BlockSpec((1, 128), lambda g: (0, 0))
    return pl.pallas_call(
        step_kernel,
        grid=(1,),
        in_specs=[pl.BlockSpec((length + HALO, 128), lambda g: (0, CONV // 128)), line, line],
        out_specs=(
            pl.BlockSpec((QUADS, 40, length), lambda g: (0, 0, 0)),
            pl.BlockSpec((length, 128), lambda g: (0, 0)),
            pl.BlockSpec((8, 128), lambda g: (0, 0)),
        ),
        out_shape=(
            jax.ShapeDtypeStruct((QUADS, 40, length), F32),
            jax.ShapeDtypeStruct((length, 128), F32),
            jax.ShapeDtypeStruct((8, 128), F32),
        ),
        compiler_params=pltpu.CompilerParams(vmem_limit_bytes=VMEM_LIMIT),
        cost_estimate=COST,
        name="steps",
    )(projected, dt_bias, a_log)


def conv_kernel(
    share, v_ref, cw_ref, cb_ref, rows_ref, total_ref, *rest
):
    x_ref, slope_ref, b_ref, c_ref, bt_ref, ct_ref, state_ref, ext, weighted = rest[-9:]
    length = v_ref.shape[0] - HALO
    grid = pl.program_id(0)
    for plane in range(2):
        ext[plane] = v_ref[:, 128 * plane : 128 * plane + 128].astype(F32)

    def act(start):
        made = []
        for plane in range(2):
            lanes = slice(128 * plane, 128 * plane + 128)
            total = cb_ref[:, lanes] + cw_ref[0:1, lanes] * ext[plane, HALO - 3 + start : HALO - 3 + start + CHUNK, :]
            for tap in range(1, KW):
                at = HALO - 3 + tap + start
                total = total + cw_ref[tap : tap + 1, lanes] * ext[plane, at : at + CHUNK, :]
            sig = sigmoid(total)
            slope_ref[start : start + CHUNK, lanes] = (sig * (1.0 + total * (1.0 - sig))).astype(BF16)
            made.append(total * sig)
        return jnp.concatenate(made, axis=1)

    @pl.when(grid == 0)
    def _():
        for start in range(0, length, CHUNK):
            both = act(start)
            b_part, c_part = both[:, :STATE], both[:, STATE:]
            b_ref[start : start + CHUNK, :] = b_part.astype(BF16)
            c_ref[start : start + CHUNK, :] = c_part.astype(BF16)
            bt_ref[:, start : start + CHUNK] = b_part.T.astype(BF16)
            ct_ref[:, start : start + CHUNK] = c_part.T.astype(BF16)
        high, mid, low = split3(total_ref[0:1, :])
        row = iota((STATE, 128), 0) % share
        told = jnp.where(row == 0, high.astype(F32), jnp.where(row == 1, mid.astype(F32), jnp.where(row == 2, low.astype(F32), 0.0)))
        state_ref[:, :128] = told.astype(BF16)
        state_ref[:, 128:] = jnp.zeros((STATE, QUAD - 128), BF16)

    @pl.when(grid > 0)
    def _():
        cols = columns_of(rows_ref[0])
        for start in range(0, length, CHUNK):
            x_part = act(start)
            x_ref[start : start + CHUNK, :] = x_part.astype(BF16)
            _, left = spread(cols[start : start + CHUNK], 16)
            weighted[start : start + CHUNK, :] = (x_part * left).astype(BF16)
        state_ref[...] = mm(bt_ref[...], weighted[...]).astype(BF16)


def conv_call(ranks, v, conv_weight, conv_bias, rows, total, after):
    length = v.shape[0] - HALO
    last = QUADS
    block = lambda g: (0, (g + last) % (last + 1))
    quad = lambda g: (0, jnp.maximum(g - 1, 0))
    whole = lambda g: (0, 0)
    return pl.pallas_call(
        functools.partial(conv_kernel, STATE // ranks),
        grid=(last + 1,),
        in_specs=[
            pl.BlockSpec((length + HALO, QUAD), block),
            pl.BlockSpec((KW, QUAD), block),
            pl.BlockSpec((1, QUAD), block),
            pl.BlockSpec((1, 40, length), lambda g: (jnp.maximum(g - 1, 0), 0, 0)),
            pl.BlockSpec((8, 128), whole),
        ]
        + [pl.BlockSpec(memory_space=pl.ANY)] * len(after),
        out_specs=[
            pl.BlockSpec((length, QUAD), quad),
            pl.BlockSpec((length, QUAD), block),
            pl.BlockSpec((length, STATE), whole),
            pl.BlockSpec((length, STATE), whole),
            pl.BlockSpec((STATE, length), whole),
            pl.BlockSpec((STATE, length), whole),
            pl.BlockSpec((STATE, QUAD), block),
        ],
        scratch_shapes=[pltpu.VMEM((2, length + HALO, 128), F32), pltpu.VMEM((length, QUAD), BF16)],
        out_shape=[
            jax.ShapeDtypeStruct((length, INNER), BF16),
            jax.ShapeDtypeStruct((length, CONV), BF16),
            jax.ShapeDtypeStruct((length, STATE), BF16),
            jax.ShapeDtypeStruct((length, STATE), BF16),
            jax.ShapeDtypeStruct((STATE, length), BF16),
            jax.ShapeDtypeStruct((STATE, length), BF16),
            jax.ShapeDtypeStruct((STATE, CONV), BF16),
        ],
        compiler_params=pltpu.CompilerParams(vmem_limit_bytes=VMEM_LIMIT),
        cost_estimate=COST,
        name="conv_states",
    )(v, conv_weight, conv_bias, rows, total, *after)


def carry_kernel(ranks, backward, in_ref, *rest):
    share = STATE // ranks
    if backward:
        total_ref, out_ref = rest[0], rest[-1]
        decays = total_ref[...]
    else:
        out_ref, total_ref = rest[-2:]
        for place in range(ranks):
            told = in_ref[place * share : (place + 1) * share, INNER : INNER + 128].astype(F32)
            total_ref[place : place + 1, :] = told[0:1] + told[1:2] + told[2:3]
        decays = total_ref[...]
    wide = mm_exact(decays, head_ones())
    carry = jnp.zeros((share, INNER), F32)
    for place in range(ranks - 1, -1, -1) if backward else range(ranks):
        part = slice(place * share, (place + 1) * share)
        out_ref[part, :] = carry.astype(BF16)
        carry = wide[place : place + 1] * carry + in_ref[part, :INNER].astype(F32)


def carry_call(ranks, states, totals=None, after=()):
    backward = totals is not None
    vmem = pl.BlockSpec(memory_space=pltpu.VMEM)
    outs = [jax.ShapeDtypeStruct((STATE, INNER), BF16)]
    args = [states] + ([totals] if backward else [])
    if not backward:
        outs.append(jax.ShapeDtypeStruct((ranks, 128), F32))
    return pl.pallas_call(
        functools.partial(carry_kernel, ranks, backward),
        in_specs=[vmem] * len(args) + [pl.BlockSpec(memory_space=pl.ANY)] * len(after),
        out_specs=[vmem] * len(outs),
        out_shape=outs,
        compiler_params=pltpu.CompilerParams(vmem_limit_bytes=VMEM_LIMIT),
        cost_estimate=COST,
        name="carry_back" if backward else "carry",
    )(*args, *after)


def inside_kernel(x_ref, b_ref, c_ref, bt_ref, rows_ref, skip_ref, y_ref, scores, state):
    length = x_ref.shape[0]
    grid = pl.program_id(0)

    @pl.when(grid == 0)
    def _():
        for start in range(0, length, CHUNK):
            part = slice(start, start + CHUNK)
            scores[part, :] = mm_nt(c_ref[part, :], b_ref[part, :])

    cols = columns_of(rows_ref[0])
    lower = iota((CHUNK, CHUNK), 0) >= iota((CHUNK, CHUNK), 1)
    first = iota((CHUNK, 128), 1) < HEAD_DIM
    for start in range(0, length, CHUNK):
        part = slice(start, start + CHUNK)
        x_f = x_ref[part, :].astype(F32)
        wide, cum = spread(cols[part], 0)
        _, step = spread(cols[part], 8)
        weights = []
        for head in range(4):
            cum_row = rows_ref[0, head : head + 1, part]
            step_row = rows_ref[0, 8 + head : 9 + head, part]
            fade = jnp.exp(jnp.where(lower, wide[head] - cum_row, -1e30))
            weights.append((scores[part, :] * fade * step_row).astype(BF16))
        pieces = []
        for pair in range(2):
            x_pair = x_f[:, 128 * pair : 128 * pair + 128]
            both = jnp.concatenate([jnp.where(first, x_pair, 0.0), jnp.where(first, 0.0, x_pair)], axis=0)
            pieces.append(mm(jnp.concatenate(weights[2 * pair : 2 * pair + 2], axis=1), both.astype(BF16)))
        y_part = jnp.concatenate(pieces, axis=1) + skip_ref[...] * x_f
        if start > 0:
            y_part = y_part + jnp.exp(cum) * mm(c_ref[part, :], state[...].astype(BF16))
        y_ref[part, :] = y_part
        if start + CHUNK < length:
            end = cum[CHUNK - 1 : CHUNK]
            fresh = mm(bt_ref[:, part], (x_f * (jnp.exp(end - cum) * step)).astype(BF16))
            state[...] = fresh if start == 0 else jnp.exp(end) * state[...] + fresh


def inside_call(x_act, b_act, c_act, b_turned, rows, skip_wide):
    length = x_act.shape[0]
    whole = lambda g: (0, 0)
    quad = lambda g: (0, g)
    return pl.pallas_call(
        inside_kernel,
        grid=(QUADS,),
        in_specs=[
            pl.BlockSpec((length, QUAD), quad),
            pl.BlockSpec((length, STATE), whole),
            pl.BlockSpec((length, STATE), whole),
            pl.BlockSpec((STATE, length), whole),
            pl.BlockSpec((1, 40, length), lambda g: (g, 0, 0)),
            pl.BlockSpec((1, QUAD), quad),
        ],
        out_specs=pl.BlockSpec((length, QUAD), quad),
        out_shape=jax.ShapeDtypeStruct((length, INNER), F32),
        scratch_shapes=[pltpu.VMEM((length, CHUNK), F32), pltpu.VMEM((STATE, QUAD), F32)],
        compiler_params=pltpu.CompilerParams(vmem_limit_bytes=VMEM_LIMIT),
        cost_estimate=COST,
        name="ssd_inside",
    )(x_act, b_act, c_act, b_turned, rows, skip_wide)


def gate_kernel(
    y_ref, gate_ref, dn_ref, c_ref, ct_ref, ecd_ref, gain_ref, sin_ref,
    normed_ref, dgate_ref, dm_ref, dgain_ref, out_ref, ones, ecd, gated, silu, slope, back,
):
    grid = pl.program_id(0)

    @pl.when(grid == 0)
    def _():
        ones[...] = head_ones()
        back[...] = jnp.zeros_like(back)
        dgain_ref[...] = jnp.zeros_like(dgain_ref)

    high, mid, _ = split3(ecd_ref[...])
    squares = jnp.zeros((CHUNK, QUAD), F32)
    product = jnp.zeros((CHUNK, QUAD), F32)
    for at in range(0, INNER, QUAD):
        lanes = slice(at, at + QUAD)
        grown = mm(high, ones[:, lanes]) + mm(mid, ones[:, lanes])
        ecd[:, lanes] = grown
        mixed = y_ref[:, lanes] + grown * mm(c_ref[...], sin_ref[:, lanes])
        mixed = mixed.astype(BF16).astype(F32)
        gate = gate_ref[:, lanes].astype(F32)
        sig = sigmoid(gate)
        open_part = gate * sig
        value = mixed * open_part
        silu[:, lanes] = open_part
        slope[:, lanes] = mixed * (sig * (1.0 + gate * (1.0 - sig)))
        gated[:, lanes] = value
        squares = squares + value * value
        product = product + dn_ref[:, lanes] * gain_ref[:, lanes] * value
    inverse = lax.rsqrt(jnp.sum(squares, axis=1, keepdims=True) * (1.0 / INNER) + EPSILON)
    shift = inverse * inverse * inverse * (jnp.sum(product, axis=1, keepdims=True) * (1.0 / INNER))
    inverse = jnp.broadcast_to(inverse, (CHUNK, QUAD))
    shift = jnp.broadcast_to(shift, (CHUNK, QUAD))
    for at in range(0, INNER, QUAD):
        lanes = slice(at, at + QUAD)
        value = gated[:, lanes]
        scaled = value * inverse
        gain = gain_ref[:, lanes]
        dn = dn_ref[:, lanes]
        normed_ref[:, lanes] = (scaled * gain).astype(BF16)
        dgain_ref[:, lanes] += jnp.sum(dn * scaled, axis=0, keepdims=True)
        d_gated = inverse * (dn * gain) - value * shift
        dgate_ref[:, lanes] = (d_gated * slope[:, lanes]).astype(BF16)
        d_mixed = (d_gated * silu[:, lanes]).astype(BF16)
        dm_ref[:, lanes] = d_mixed
        back[:, lanes] += mm(ct_ref[...], (d_mixed.astype(F32) * ecd[:, lanes]).astype(BF16))

    @pl.when(grid == pl.num_programs(0) - 1)
    def _():
        out_ref[...] = back[...].astype(BF16)


def gate_call(y_inside, gate_in, d_normed, c_act, c_turned, ecd, out_gain, s_in):
    length = y_inside.shape[0]
    whole = lambda g: (0, 0)
    down = lambda g: (g, 0)
    wide = pl.BlockSpec((CHUNK, INNER), down)
    rows = jax.ShapeDtypeStruct((length, INNER), BF16)
    state = pl.BlockSpec((STATE, INNER), whole)
    line = pl.BlockSpec((1, INNER), whole)
    return pl.pallas_call(
        gate_kernel,
        grid=(length // CHUNK,),
        in_specs=[
            wide,
            wide,
            wide,
            pl.BlockSpec((CHUNK, STATE), down),
            pl.BlockSpec((STATE, CHUNK), lambda g: (0, g)),
            pl.BlockSpec((CHUNK, 128), down),
            line,
            state,
        ],
        out_specs=[wide, wide, wide, line, state],
        out_shape=[rows, rows, rows, jax.ShapeDtypeStruct((1, INNER), F32), jax.ShapeDtypeStruct((STATE, INNER), BF16)],
        scratch_shapes=[pltpu.VMEM((128, INNER), BF16)]
        + [pltpu.VMEM((CHUNK, INNER), F32)] * 4
        + [pltpu.VMEM((STATE, INNER), F32)],
        compiler_params=pltpu.CompilerParams(vmem_limit_bytes=VMEM_LIMIT),
        cost_estimate=COST,
        name="gated_norm",
    )(y_inside, gate_in, d_normed, c_act, c_turned, ecd, out_gain, s_in)


def back_kernel(x_ref, dm_ref, slope_ref, v_ref, cw_ref, b_ref, c_ref, bt_ref, ct_ref, rows_ref, skip_ref, sin_ref, rin_ref, *rest):
    dv_ref, sums_ref, heads_ref, scores, d_scores, d_b, d_c, states, back, grads, ext, d_step = rest[-12:]
    length = x_ref.shape[0]
    chunks = length // CHUNK
    grid = pl.program_id(0)

    @pl.when(grid == 0)
    def _():
        for start in range(0, length, CHUNK):
            part = slice(start, start + CHUNK)
            scores[part, :] = mm_nt(b_ref[part, :], c_ref[part, :])
        d_scores[...] = jnp.zeros_like(d_scores)
        d_b[...] = jnp.zeros_like(d_b)
        d_c[...] = jnp.zeros_like(d_c)
        d_step[...] = jnp.zeros_like(d_step)
        grads[:, 0:HALO, :] = jnp.zeros((2, HALO, 128), F32)
        grads[:, HALO + length :, :] = jnp.zeros((2, HALO, 128), F32)

    def finish(extra):
        for plane in range(2):
            lanes = slice(128 * plane, 128 * plane + 128)
            ext[plane] = v_ref[:, lanes].astype(F32)
            total = [jnp.zeros((8, 128), F32)] * (KW + 1)
            for start in range(0, length, CHUNK):
                here = grads[plane, HALO + start : HALO + start + CHUNK, :]
                for tap in range(KW):
                    at = HALO - 3 + tap + start
                    total[tap] = total[tap] + fold_rows(here * ext[plane, at : at + CHUNK, :])
                total[KW] = total[KW] + fold_rows(here)
            for at, rows in enumerate(total):
                sums_ref[at : at + 1, lanes] = jnp.sum(rows, axis=0, keepdims=True)
            for start in [0] + list(range(HALO, HALO + length, CHUNK)):
                count = HALO if start == 0 else CHUNK
                value = cw_ref[KW - 1 : KW, lanes] * grads[plane, start : start + count, :]
                for tap in range(KW - 1):
                    at = start + KW - 1 - tap
                    value = value + cw_ref[tap : tap + 1, lanes] * grads[plane, at : at + count, :]
                place = length if start == 0 else start - HALO
                dv_ref[place : place + count, lanes] = value.astype(BF16)
        sums_ref[KW + 1 : KW + 2, :] = extra
        sums_ref[KW + 2 : 8, :] = jnp.zeros((8 - KW - 2, QUAD), F32)

    def keep(start, value):
        for plane in range(2):
            grads[plane, HALO + start : HALO + start + CHUNK, :] = value[:, 128 * plane : 128 * plane + 128]

    @pl.when(grid < QUADS)
    def _():
        cols = columns_of(rows_ref[0])
        upper = iota((CHUNK, CHUNK), 0) <= iota((CHUNK, CHUNK), 1)
        first = iota((CHUNK, 128), 1) < HEAD_DIM
        lane = iota((CHUNK, 128), 1)
        line = iota((8, 128), 0)
        head_of = iota((QUAD, 128), 0) >> 6
        ones_v = jnp.where(iota((QUAD, 128), 1) == head_of + 8, 1.0, 0.0).astype(BF16)
        ones_u = jnp.where(iota((QUAD, 128), 1) == head_of + 16, 1.0, 0.0).astype(BF16)
        square = (CHUNK, CHUNK)
        later = jnp.where(iota(square, 0) >= iota(square, 1), 1.0, 0.0).astype(BF16)
        before = jnp.where(iota(square, 0) < iota(square, 1), 1.0, 0.0).astype(BF16)
        skip = skip_ref[...]
        back[...] = rin_ref[...].astype(F32)
        state = sin_ref[...].astype(F32)
        for chunk in range(chunks):
            part = slice(chunk * CHUNK, chunk * CHUNK + CHUNK)
            states[chunk] = state
            if chunk + 1 < chunks:
                _, cum = spread(cols[part], 0)
                _, step = spread(cols[part], 8)
                end = cum[CHUNK - 1 : CHUNK]
                fed = (x_ref[part, :].astype(F32) * (jnp.exp(end - cum) * step)).astype(BF16)
                state = jnp.exp(end) * state + mm(bt_ref[:, part], fed)
        skip_sum = jnp.zeros((1, QUAD), F32)
        bias_sum = jnp.zeros((8, 1), F32)
        rate_sum = jnp.zeros((8, 1), F32)
        for chunk in range(chunks - 1, -1, -1):
            part = slice(chunk * CHUNK, chunk * CHUNK + CHUNK)
            x_f = x_ref[part, :].astype(F32)
            dm = dm_ref[part, :]
            dm_f = dm.astype(F32)
            cum_wide, cum = spread(cols[part], 0)
            step_wide, step = spread(cols[part], 8)
            end = cum[CHUNK - 1 : CHUNK]
            after = back[...]
            after_low = after.astype(BF16)
            state = states[chunk]
            left = jnp.exp(end - cum)
            grown = dm_f * jnp.exp(cum)
            grown_low = grown.astype(BF16)
            faded = x_f * left
            from_after = mm(b_ref[part, :], after_low)
            from_state = mm(c_ref[part, :], state.astype(BF16))
            d_b[part, :] += mm_nt((faded * step).astype(BF16), after_low)
            d_c[part, :] += mm_nt(grown_low, state.astype(BF16))
            marks = mm((grown * from_state).astype(BF16), ones_v) + mm((faded * from_after).astype(BF16), ones_u)
            pair_sum = jnp.zeros((8, CHUNK), F32)
            crossing = jnp.zeros((8, 1), F32)
            cross = jnp.sum(state * after, axis=0, keepdims=True) * jnp.exp(end)
            pieces = []
            for pair in range(2):
                x_pair = x_f[:, 128 * pair : 128 * pair + 128]
                dm_pair = dm_f[:, 128 * pair : 128 * pair + 128]
                x_both = jnp.concatenate([jnp.where(first, x_pair, 0.0), jnp.where(first, 0.0, x_pair)], axis=0)
                dm_both = jnp.concatenate([jnp.where(first, dm_pair, 0.0), jnp.where(first, 0.0, dm_pair)], axis=0)
                d_weights = mm_nt(x_both.astype(BF16), dm[:, 128 * pair : 128 * pair + 128])
                kept = []
                for half in range(2):
                    head = 2 * pair + half
                    cum_row = rows_ref[0, head : head + 1, part]
                    fade = jnp.exp(jnp.where(upper, cum_row - cum_wide[head], -1e30))
                    faded_grad = d_weights[half * CHUNK : half * CHUNK + CHUNK] * fade
                    d_scores[part, :] += faded_grad * step_wide[head]
                    joint = faded_grad * scores[part, :]
                    marks = marks + jnp.where(lane == head, jnp.sum(joint, axis=1, keepdims=True), 0.0)
                    row = jnp.sum(joint * step_wide[head], axis=0, keepdims=True)
                    pair_sum = pair_sum + jnp.where(line == head, row, 0.0)
                    kept.append((scores[part, :] * fade).astype(BF16))
                    low, high = 64 * head, 64 * head + 64
                    here = (iota((1, QUAD), 1) >= low) & (iota((1, QUAD), 1) < high)
                    amount = jnp.sum(jnp.where(here, cross, 0.0), axis=1, keepdims=True)
                    crossing = crossing + jnp.where(iota((8, 1), 0) == head, amount, 0.0)
                pieces.append(mm(jnp.concatenate(kept, axis=1), dm_both.astype(BF16)))
            direct = jnp.concatenate(pieces, axis=1) + left * from_after
            d_x = step * direct + skip * dm_f
            keep(chunk * CHUNK, d_x * slope_ref[part, :].astype(F32))
            skip_sum = skip_sum + jnp.sum(x_f * dm_f, axis=0, keepdims=True)
            back[...] = jnp.exp(end) * after + mm(ct_ref[:, part], grown_low)
            marks = marks.T
            within, carried, outward = marks[0:8], marks[8:16], marks[16:24]
            step_rows = rows_ref[0, 8:16, part]
            change = pair_sum - step_rows * within + carried
            decay = mm_exact(change, later) + mm_exact(step_rows * outward, before) + crossing
            d_raw = (within + outward + rows_ref[0, 32:40, part] * decay) * rows_ref[0, 24:32, part]
            d_step[pl.ds(pl.multiple_of(grid * 8, 8), 8), part] = d_raw
            bias_sum = bias_sum + jnp.sum(d_raw, axis=1, keepdims=True)
            rate_sum = rate_sum + jnp.sum(step_rows * decay, axis=1, keepdims=True)
        heads_ref[0, 0:8, :] = jnp.broadcast_to(bias_sum, (8, 128))
        heads_ref[0, 8:16, :] = jnp.broadcast_to(rate_sum, (8, 128))
        finish(skip_sum)

    @pl.when(grid == QUADS)
    def _():
        for start in range(0, length, CHUNK):
            part = slice(start, start + CHUNK)
            low = d_scores[part, :].astype(BF16)
            into_b = d_b[part, :] + mm(low, c_ref[part, :])
            into_c = d_c[part, :] + mm(d_scores[part, :].T.astype(BF16), b_ref[part, :])
            both = jnp.concatenate([into_b, into_c], axis=1)
            keep(start, both * slope_ref[part, :].astype(F32))
        finish(jnp.zeros((1, QUAD), F32))

    @pl.when(grid == QUADS + 1)
    def _():
        row, column = iota((128, QUAD), 0), iota((128, QUAD), 1)
        pick = (column < HEADS) & (row == 8 * (column >> 2) + (column & 3))
        turned = d_step[...].T.astype(BF16)
        dv_ref[length:, :] = jnp.zeros((HALO, QUAD), BF16)
        dv_ref[0:length, :] = mm(turned, jnp.where(pick, 1.0, 0.0).astype(BF16)).astype(BF16)


def back_call(x_act, d_mixed, slope, v, conv_weight, b_act, c_act, b_turned, c_turned, rows, skip_wide, s_in, r_in, after):
    length = x_act.shape[0]
    whole = lambda g: (0, 0)
    quad = lambda g: (0, jnp.minimum(g, QUADS - 1))
    block = lambda g: (0, jnp.minimum(g, QUADS))
    lead = lambda g: (jnp.minimum(g, QUADS - 1), 0, 0)
    return pl.pallas_call(
        back_kernel,
        grid=(QUADS + 2,),
        in_specs=[
            pl.BlockSpec((length, QUAD), quad),
            pl.BlockSpec((length, QUAD), quad),
            pl.BlockSpec((length, QUAD), block),
            pl.BlockSpec((length + HALO, QUAD), block),
            pl.BlockSpec((KW, QUAD), block),
            pl.BlockSpec((length, STATE), whole),
            pl.BlockSpec((length, STATE), whole),
            pl.BlockSpec((STATE, length), whole),
            pl.BlockSpec((STATE, length), whole),
            pl.BlockSpec((1, 40, length), lead),
            pl.BlockSpec((1, QUAD), quad),
            pl.BlockSpec((STATE, QUAD), quad),
            pl.BlockSpec((STATE, QUAD), quad),
        ]
        + [pl.BlockSpec(memory_space=pl.ANY)] * len(after),
        out_specs=[
            pl.BlockSpec((length + HALO, QUAD), lambda g: (0, g)),
            pl.BlockSpec((8, QUAD), block),
            pl.BlockSpec((1, 16, 128), lead),
        ],
        scratch_shapes=[
            pltpu.VMEM((length, CHUNK), F32),
            pltpu.VMEM((length, CHUNK), F32),
            pltpu.VMEM((length, STATE), F32),
            pltpu.VMEM((length, STATE), F32),
            pltpu.VMEM((length // CHUNK, STATE, QUAD), F32),
            pltpu.VMEM((STATE, QUAD), F32),
            pltpu.VMEM((2, length + 2 * HALO, 128), F32),
            pltpu.VMEM((2, length + HALO, 128), F32),
            pltpu.VMEM((128, length), F32),
        ],
        out_shape=[
            jax.ShapeDtypeStruct((length + HALO, CONV + QUAD), BF16),
            jax.ShapeDtypeStruct((8, CONV), F32),
            jax.ShapeDtypeStruct((QUADS, 16, 128), F32),
        ],
        compiler_params=pltpu.CompilerParams(vmem_limit_bytes=VMEM_LIMIT),
        cost_estimate=COST,
        name="ssd_back",
    )(x_act, d_mixed, slope, v, conv_weight, b_act, c_act, b_turned, c_turned, rows, skip_wide, s_in, r_in, *after)


def weight_kernel(height, halves, place_ref, x_ref, *rest):
    piece_refs, (out_ref, w_ref) = rest[:-2], rest[-2:]
    block = w_ref.shape[0]
    if halves:
        grid = pl.program_id(0)
        lower = grid < pl.num_programs(0) // 2

        @pl.when(lower == (place_ref[len(piece_refs)] == 0))
        def _():
            for at, piece_ref in enumerate(piece_refs):
                if at < 2 or at % 2 == 0:
                    w_ref[:, pl.ds(pl.multiple_of(place_ref[at] * height, 128), height)] = piece_ref[...]

        @pl.when(lower != (place_ref[len(piece_refs)] == 0))
        def _():
            for at, piece_ref in enumerate(piece_refs):
                if at < 2 or at % 2 == 1:
                    w_ref[:, pl.ds(pl.multiple_of(place_ref[at] * height, 128), height)] = piece_ref[...]
    else:
        for at, piece_ref in enumerate(piece_refs):
            w_ref[:, pl.ds(pl.multiple_of(place_ref[at] * height, 128), height)] = piece_ref[...]
    out_ref[...] = mm_nt(x_ref[...], w_ref[...]).astype(BF16)


def weight_call(x, pieces, places, width, block, halves, name):
    rows, depth = x.shape
    height = pieces[0].shape[1]
    steps = width // block
    half = steps // 2

    def spec(at):
        if not halves or at < 2:
            return pl.BlockSpec((block, height), lambda g, place: (g, 0))
        return pl.BlockSpec((block, height), lambda g, place: (g % half, 0))

    grid_spec = pltpu.PrefetchScalarGridSpec(
        num_scalar_prefetch=1,
        grid=(steps,),
        in_specs=[pl.BlockSpec((rows, depth), lambda g, place: (0, 0))] + [spec(at) for at in range(len(pieces))],
        out_specs=[
            pl.BlockSpec((rows, block), lambda g, place: (0, g)),
            pl.BlockSpec((block, depth), lambda g, place: (g, 0)),
        ],
    )
    return pl.pallas_call(
        functools.partial(weight_kernel, height, halves),
        grid_spec=grid_spec,
        out_shape=[jax.ShapeDtypeStruct((rows, width), BF16), jax.ShapeDtypeStruct((width, depth), BF16)],
        compiler_params=pltpu.CompilerParams(vmem_limit_bytes=VMEM_LIMIT),
        cost_estimate=COST,
        name=name,
    )(places, x, *pieces)


def weight_back_kernel(per, place_ref, g_ref, *rest):
    piece_refs, (out_ref, w_ref) = rest[:-2], rest[-2:]
    for at, piece_ref in enumerate(piece_refs):

        @pl.when(pl.program_id(0) // per == at)
        def _():
            w_ref[...] = piece_ref[...]
            out_ref[...] = mm_nt(g_ref[...], piece_ref[...])


def weight_back_call(g, pieces, places):
    rows, width = g.shape
    block = 384
    per = pieces[0].shape[0] // block
    steps = per * len(pieces)
    total = steps * block
    step_of = lambda at: lambda k, place: (jnp.clip(k - at * per, 0, per - 1), 0)
    target = lambda k, place: place[k // per] * per + k % per
    grid_spec = pltpu.PrefetchScalarGridSpec(
        num_scalar_prefetch=1,
        grid=(steps,),
        in_specs=[pl.BlockSpec((rows, width), lambda k, place: (0, 0))]
        + [pl.BlockSpec((block, width), step_of(at)) for at in range(len(pieces))],
        out_specs=[
            pl.BlockSpec((rows, block), lambda k, place: (0, target(k, place))),
            pl.BlockSpec((block, width), lambda k, place: (target(k, place), 0)),
        ],
    )
    return pl.pallas_call(
        functools.partial(weight_back_kernel, per),
        grid_spec=grid_spec,
        out_shape=[jax.ShapeDtypeStruct((rows, total), F32), jax.ShapeDtypeStruct((total, width), BF16)],
        compiler_params=pltpu.CompilerParams(vmem_limit_bytes=VMEM_LIMIT),
        cost_estimate=COST,
        name="d_normed_out",
    )(places, g, *pieces)


def pick_kernel(parts, table_ref, *rest):
    ins, outs = rest[: 4 * parts], rest[-3 * parts :]
    for part in range(parts):
        own, other, own_halo, other_halo = ins[4 * part : 4 * part + 4]
        own_out, other_out, halo_out = outs[3 * part : 3 * part + 3]
        own_out[...] = own[...]
        other_out[...] = other[...]
        halo_out[:, :, :HALO] = own_halo[...]
        halo_out[:, :, HALO:] = other_halo[...]


def pick_call(table, own, other, own_halo, other_halo, after):
    parts, blocks = table.shape
    _, height, length = own.shape
    in_specs, out_specs, shapes = [], [], []
    for part in range(parts):
        pick = functools.partial(lambda part, g, table_ref: (table_ref[part, g], 0, 0), part)
        here = lambda g, *_: (g, 0, 0)
        in_specs += [pl.BlockSpec((1, height, length), pick)] * 2 + [pl.BlockSpec((1, height, HALO), pick)] * 2
        out_specs += [pl.BlockSpec((1, height, length), here)] * 2 + [pl.BlockSpec((1, height, 2 * HALO), here)]
        shapes += [jax.ShapeDtypeStruct((blocks, height, length), BF16)] * 2
        shapes += [jax.ShapeDtypeStruct((blocks, height, 2 * HALO), BF16)]
    in_specs += [pl.BlockSpec(memory_space=pl.ANY)] * len(after)
    made = pl.pallas_call(
        functools.partial(pick_kernel, parts),
        grid_spec=pltpu.PrefetchScalarGridSpec(num_scalar_prefetch=1, grid=(blocks,), in_specs=in_specs, out_specs=out_specs),
        out_shape=shapes,
        compiler_params=pltpu.CompilerParams(vmem_limit_bytes=VMEM_LIMIT),
        cost_estimate=COST,
        name="pick_rows",
    )(table, *([own, other, own_halo, other_halo] * parts), *after)
    return [[array.reshape(blocks * height, -1) for array in made[3 * part : 3 * part + 3]] for part in range(parts)]


def grad_kernel(halo, *refs):
    kept_ref, sent_ref = refs[-2:]
    if halo:
        own, other, edge, right, right_other, edge_right, edge_other = refs[:7]
    else:
        own, other, right, right_other = refs[:4]
    total = mm(own[...], right[...]) + mm(other[...], right_other[...])
    if halo:
        total = total + mm(edge[...], jnp.concatenate([edge_right[...], edge_other[...]], axis=0))
    half = total.shape[0] // 2
    kept_ref[...] = total[:half].astype(BF16)
    sent_ref[...] = total[half:].astype(BF16)


def grad_call(left, right, right_other, first, width, block, halo, name, after):
    own, other, edge = left
    rows, length = own.shape
    whole = lambda g: (0, 0)
    column = lambda g: (0, first // block + g)
    below = lambda g: (length // HALO, first // block + g)
    specs = [pl.BlockSpec((rows, length), whole)] * 2
    args = [own, other]
    if halo:
        specs.append(pl.BlockSpec((rows, 2 * HALO), whole))
        args.append(edge)
    specs += [pl.BlockSpec((length, block), column)] * 2
    args += [right, right_other]
    if halo:
        specs += [pl.BlockSpec((HALO, block), below)] * 2
        args += [right, right_other]
    specs += [pl.BlockSpec(memory_space=pl.ANY)] * len(after)
    args += list(after)
    return pl.pallas_call(
        functools.partial(grad_kernel, halo),
        grid=(width // block,),
        in_specs=specs,
        out_specs=[pl.BlockSpec((rows // 2, block), lambda g: (0, g))] * 2,
        out_shape=[jax.ShapeDtypeStruct((rows // 2, width), BF16)] * 2,
        compiler_params=pltpu.CompilerParams(vmem_limit_bytes=VMEM_LIMIT),
        cost_estimate=COST,
        name=name,
    )(*args)


def fold_kernel(parts, groups, last, *refs):
    ins, outs = refs[: 2 * parts * groups], refs[-(1 if last else 2 * parts) :]
    for part in range(parts):
        at = 0
        for group in range(groups):
            kept, got = ins[2 * (part * groups + group)], ins[2 * (part * groups + group) + 1]
            width = kept.shape[1]
            total = kept[...].astype(F32) + got[...].astype(F32)
            if last:
                gate = INNER // parts
                other = width - gate
                outs[0][:, part * gate : (part + 1) * gate] = total[:, :gate]
                begin = INNER + part * other
                end = min(begin + other, outs[0].shape[1])
                outs[0][:, begin:end] = total[:, gate : gate + end - begin]
            else:
                half = total.shape[0] // 2
                outs[2 * part][:, at : at + width] = total[:half].astype(BF16)
                outs[2 * part + 1][:, at : at + width] = total[half:].astype(BF16)
            at += width


def fold_call(pairs, width, after=()):
    parts, groups = len(pairs), len(pairs[0])
    arrays = [array for part in pairs for pair in part for array in pair]
    vmem = pl.BlockSpec(memory_space=pltpu.VMEM)
    rows = arrays[0].shape[0]
    if width:
        shapes = [jax.ShapeDtypeStruct((rows, width), F32)]
    else:
        shapes = []
        for part in pairs:
            total = sum(kept.shape[1] for kept, _ in part)
            shapes += [jax.ShapeDtypeStruct((rows // 2, total), BF16)] * 2
    made = pl.pallas_call(
        functools.partial(fold_kernel, parts, groups, bool(width)),
        in_specs=[vmem] * len(arrays) + [pl.BlockSpec(memory_space=pl.ANY)] * len(after),
        out_specs=[vmem] * len(shapes),
        out_shape=shapes,
        compiler_params=pltpu.CompilerParams(vmem_limit_bytes=VMEM_LIMIT),
        cost_estimate=COST,
        name="fold",
    )(*arrays, *after)
    return made[0] if width else [(made[2 * part], made[2 * part + 1]) for part in range(parts)]


def residual_kernel(x_ref, w_ref, tokens_ref, *rest):
    out_ref = rest[-1]
    out_ref[0] = tokens_ref[0].astype(F32) + mm(x_ref[...], w_ref[...])


def residual_call(x, w, tokens, after=()):
    rows, depth = x.shape
    width = w.shape[1]
    block = 256
    whole = pl.BlockSpec((1, rows, block), lambda g: (0, 0, g))
    return pl.pallas_call(
        residual_kernel,
        grid=(width // block,),
        in_specs=[pl.BlockSpec((rows, depth), lambda g: (0, 0)), pl.BlockSpec((depth, block), lambda g: (0, g)), whole]
        + [pl.BlockSpec(memory_space=pl.ANY)] * len(after),
        out_specs=whole,
        out_shape=jax.ShapeDtypeStruct((1, rows, width), F32),
        compiler_params=pltpu.CompilerParams(vmem_limit_bytes=VMEM_LIMIT),
        cost_estimate=COST,
        name="block_out",
    )(x, w, tokens, *after)


def tokens_kernel(dg_ref, dv_ref, spill_ref, wg_ref, wv_ref, tokens_ref, cotan_ref, gain_ref, *rest):
    out_ref, dgain_ref, fixed, d_normed, inverse = rest[-5:]
    length = dg_ref.shape[0]
    block = wg_ref.shape[1]
    grid = pl.program_id(0)

    @pl.when(grid == 0)
    def _():
        fixed[...] = dv_ref[...]
        ends = dv_ref[length - HALO :, :].astype(F32) + spill_ref[...].astype(F32)
        fixed[length - HALO :, :] = ends.astype(BF16)
        for start in range(0, length, CHUNK):
            part = slice(start, start + CHUNK)
            values = tokens_ref[0, part, :].astype(F32)
            mean = jnp.sum(values * values, axis=1, keepdims=True) * (1.0 / D)
            inverse[part, :] = jnp.broadcast_to(lax.rsqrt(mean + EPSILON), (CHUNK, 128))

    lanes = pl.ds(pl.multiple_of(grid * block, block), block)
    total = mm(dg_ref[...], wg_ref[...]) + mm(fixed[...], wv_ref[...])
    d_normed[:, lanes] = total
    scaled = jnp.concatenate([inverse[...]] * (block // 128), axis=1) * tokens_ref[0, :, lanes].astype(F32)
    dgain_ref[...] = jnp.sum(total * scaled, axis=0, keepdims=True)

    @pl.when(grid == pl.num_programs(0) - 1)
    def _():
        for start in range(0, length, CHUNK):
            part = slice(start, start + CHUNK)
            values = tokens_ref[0, part, :].astype(F32)
            a = d_normed[part, :] * gain_ref[...]
            inv = inverse[part, 0:1]
            shift = inv * inv * inv * (jnp.sum(a * values, axis=1, keepdims=True) * (1.0 / D))
            out_ref[0, part, :] = cotan_ref[0, part, :].astype(F32) + inv * a - values * shift


def tokens_call(d_gate, d_v, spill, w_g, w_v, tokens, cotangent, gain, after):
    length = d_gate.shape[0]
    block = 256
    wide = w_v.shape[0]
    whole = lambda g: (0, 0)
    all_rows = pl.BlockSpec((1, length, D), lambda g: (0, 0, 0))
    return pl.pallas_call(
        tokens_kernel,
        grid=(D // block,),
        in_specs=[
            pl.BlockSpec((length, INNER), whole),
            pl.BlockSpec((length, wide), whole),
            pl.BlockSpec((HALO, wide), whole),
            pl.BlockSpec((INNER, block), lambda g: (0, g)),
            pl.BlockSpec((wide, block), lambda g: (0, g)),
            all_rows,
            all_rows,
            pl.BlockSpec((1, D), whole),
        ]
        + [pl.BlockSpec(memory_space=pl.ANY)] * len(after),
        out_specs=[all_rows, pl.BlockSpec((1, block), lambda g: (0, g))],
        out_shape=[jax.ShapeDtypeStruct((1, length, D), F32), jax.ShapeDtypeStruct((1, D), F32)],
        scratch_shapes=[pltpu.VMEM((length, wide), BF16), pltpu.VMEM((length, D), F32), pltpu.VMEM((length, 128), F32)],
        compiler_params=pltpu.CompilerParams(vmem_limit_bytes=VMEM_LIMIT),
        cost_estimate=COST,
        name="d_tokens",
    )(d_gate, d_v, spill, w_g, w_v, tokens, cotangent, gain, *after)


def on_device(
    ranks,
    shards,
    tokens,
    norm_gain,
    w_in,
    conv_weight,
    conv_bias,
    dt_bias,
    a_log,
    skip_gain,
    out_gain,
    w_out,
    cotangent,
):
    both = ("seq", "fsdp")
    rank = lax.axis_index("seq")
    shard = lax.axis_index("fsdp")

    def move(value, target):
        pairs = []
        for s in range(ranks):
            for f in range(shards):
                goal = target(s, f)
                if goal is not None:
                    pairs.append((s * shards + f, goal[0] * shards + goal[1]))
        return lax.ppermute(value, both, pairs)

    def across(value):
        return move(value, lambda s, f: (s, f ^ 1))

    def tie(value, *others):
        if others:
            value = lax.optimization_barrier((value,) + others)[0]
        return value

    def gather(value, crossed, middle, near):
        pieces = [(value, 0), (crossed, 1)] + near
        pieces += [(across(tie(piece, middle)), step ^ 1) for piece, step in near]
        return [piece for piece, _ in pieces], jnp.stack([shard ^ step for _, step in pieces]).astype(jnp.int32)

    def send_near(value):
        return [(move(value, lambda s, f: (s, f ^ step)), step) for step in range(2, shards, 2)]

    def gather_halves(value, crossed, middle):
        height = value.shape[0]
        side = rank & 1
        half = lax.dynamic_slice_in_dim(value, side * (height // 2), height // 2, 0)
        pairs = []
        for step in range(2, shards, 2):
            near = move(half, lambda s, f: (s, f ^ step))
            far = move(tie(near, *middle), lambda s, f: (s ^ 1, f))
            pairs += [(near, step), (far, step)]
        pieces = [(value, 0), (crossed, 1)] + pairs + [(across(piece), step ^ 1) for piece, step in pairs]
        places = [shard ^ step for _, step in pieces] + [side]
        return [piece for piece, _ in pieces], jnp.stack(places).astype(jnp.int32)

    def in_order(pieces, places, halves):
        height = pieces[0].shape[1]
        whole = jnp.zeros((pieces[0].shape[0], height * shards), pieces[0].dtype)
        for at, piece in enumerate(pieces):
            first = 0
            if halves and at >= 2:
                first = (places[-1] if at % 2 == 0 else 1 - places[-1]) * piece.shape[0]
            whole = lax.dynamic_update_slice(whole, piece, (first, places[at] * height))
        return [whole], jnp.zeros((1,), jnp.int32)

    def exchange(states):
        return lax.all_to_all(states, "seq", split_axis=0, concat_axis=0, tiled=True)

    halo = move(tokens[0, -HALO:], lambda s, f: (s + 1, f) if s + 1 < ranks else None)
    longer = jnp.concatenate([halo, tokens[0]], axis=0).astype(F32)
    inverse = lax.rsqrt(jnp.mean(longer * longer, axis=-1, keepdims=True) + EPSILON)
    normed_long = (longer * inverse * norm_gain).astype(BF16)
    normed = normed_long[HALO:]

    cotan = cotangent[0]
    turned = w_in.T
    width_v = CONV + QUAD
    own_v = jnp.pad(turned[INNER:], ((0, width_v - (turned.shape[0] - INNER)), (0, 0)))
    chip_bits = [("fsdp", bit) for bit in (2, 4, 8) if bit < shards]
    seq_bits = [("seq", bit) for bit in (1, 2, 4, 8) if bit < ranks]
    first_bits = [seq_bits[0], chip_bits[0], seq_bits[1]] if chip_bits else [seq_bits[0], seq_bits[1], seq_bits[0]]
    orders = []
    for part in range(3):
        lead = list(dict.fromkeys(first_bits[part:] + first_bits[:part]))
        orders.append(lead + [bit for bit in chip_bits + seq_bits if bit not in lead])
    chips = ranks * (shards // 2)
    table = []
    for order in orders:
        line = []
        for place in range(chips):
            s, f = rank, shard
            for at, (axis, bit) in enumerate(order):
                if place >> (len(order) - 1 - at) & 1:
                    s, f = (s ^ bit, f) if axis == "seq" else (s, f ^ bit)
            line.append(s * (shards // 2) + (f >> 1))
        table.append(jnp.stack(line))
    table = jnp.stack(table).astype(jnp.int32)

    def halves(turned):
        blocks = turned.reshape(chips, 2, -1, turned.shape[1])
        core = shard & 1
        return lax.dynamic_index_in_dim(blocks, core, 1, False), lax.dynamic_index_in_dim(blocks, 1 - core, 1, False)

    own, other = halves(normed.T)
    own_halo, other_halo = halves(normed_long[:HALO].T)
    lefts = pick_call(table, own, across(other), own_halo, across(other_halo), [])
    own_g = turned[:INNER]
    crossed_v, crossed_g, crossed_o = across(own_v), across(own_g), across(w_out)
    pieces_v, places_v = gather_halves(own_v, crossed_v, (lefts[0][0], crossed_v, crossed_g, crossed_o))

    def flip(axis, bit):
        return lambda s, f: (s ^ bit, f) if axis == "seq" else (s, f ^ bit)

    def first_terms(right, width, block, halo, name, *ahead):
        right_other = tie(across(right), *ahead)
        return [grad_call(lefts[part], right, right_other, part * width, width, block, halo, name, ()) for part in range(3)]

    def first_step(terms, *ahead):
        return [(kept, move(tie(sent, *ahead), flip(*orders[part][0]))) for part, (kept, sent) in enumerate(terms)]

    lanes_whole = w_in.shape[0] % 128 == 0
    if lanes_whole:
        projected, w_v = weight_call(normed_long, pieces_v, places_v, width_v, width_v // 4, True, "project_v")
    else:
        projected, w_v = weight_call(normed_long, *in_order(pieces_v, places_v, True), width_v, width_v // 4, False, "project_v")
    near_g = send_near(tie(own_g, pieces_v[2]))
    pieces_g, places = gather(own_g, crossed_g, projected, near_g)
    near_o = send_near(tie(w_out, near_g[0][0], projected))
    lanes = lambda vec: jnp.pad(vec, (0, 128 - HEADS)).reshape(1, 128)
    rows, ecd, decay_all = step_call(projected, lanes(dt_bias), lanes(a_log))
    v = projected
    made = conv_call(ranks, v, conv_weight, conv_bias.reshape(1, CONV), rows, decay_all, ())
    x_act, slope, b_act, c_act, b_turned, c_turned, states = made
    skip_wide = jnp.repeat(skip_gain, HEAD_DIM).reshape(1, INNER)
    y_inside = inside_call(x_act, b_act, c_act, b_turned, rows, skip_wide)
    carried, totals = carry_call(ranks, exchange(states), None, [y_inside])
    s_in = exchange(carried)
    pieces_o, _ = gather(w_out, crossed_o, carried, near_o)
    gate_pieces = (pieces_g, places) if lanes_whole else in_order(pieces_g, places, False)
    gate_in, w_g = weight_call(normed, *gate_pieces, INNER, 768, False, "project_gate")
    d_normed_out, w_o = weight_back_call(cotan, pieces_o, places)
    made = gate_call(y_inside, gate_in, d_normed_out, c_act, c_turned, ecd, out_gain.reshape(1, INNER), s_in)
    normed_out, d_gate, d_mixed, d_gain_out, states = made
    d_w_out = lax.dot_general(normed_out, cotan, TN, preferred_element_type=F32).astype(BF16)
    d_w_out_sum = lax.psum_scatter(d_w_out, both, scatter_dimension=0, tiled=True).astype(F32)
    block_out = residual_call(normed_out, w_o, tokens, [states])
    gate_terms = first_terms(d_gate, INNER // 3, 512, False, "d_w_gate")
    (carried,) = carry_call(ranks, exchange(states), totals, [d_w_out, block_out])
    r_in = exchange(carried)
    gate_parts = first_step(gate_terms, r_in)
    d_v_long, sums, heads = back_call(
        x_act, d_mixed, slope, v, conv_weight, b_act, c_act, b_turned, c_turned, rows, skip_wide, s_in, r_in, ()
    )
    d_v_long = tie(d_v_long, *[got for _, got in gate_parts])
    spill = move(d_v_long[tokens.shape[1] :], lambda s, f: (s - 1, f) if s > 0 else None)
    rest_parts = first_step(first_terms(d_v_long, (CONV + 128) // 3, 384, True, "d_w_rest", spill))
    d_tokens, d_norm_gain = tokens_call(
        d_gate, d_v_long, spill, w_g, w_v, tokens, cotangent, norm_gain.reshape(1, D), [kept for kept, _ in rest_parts]
    )

    d_skip = sums[KW + 1, :INNER].reshape(HEADS, HEAD_DIM).sum(axis=1)
    pieces = [
        d_norm_gain.reshape(-1),
        sums[:KW].reshape(-1),
        sums[KW],
        heads[:, 0:4, 0].reshape(-1),
        heads[:, 8:12, 0].reshape(-1) * -jnp.exp(a_log),
        d_skip,
        d_gain_out.reshape(-1),
    ]
    flat = jnp.concatenate(pieces)
    width = flat.shape[0]
    flat = jnp.pad(flat, (0, -width % 1024)).reshape(-1, 128)
    flat = flat + across(flat)
    small_bits = seq_bits[:1] + chip_bits + seq_bits[1:]
    flat = flat + move(flat, flip(*small_bits[0]))

    pairs = [[gate_parts[part], rest_parts[part]] for part in range(3)]
    for at in range(1, len(orders[0])):
        halves_now = fold_call(pairs, 0, [flat])
        pairs = [[(kept, move(sent, flip(*orders[part][at])))] for part, (kept, sent) in enumerate(halves_now)]
        flat = flat + move(tie(flat, halves_now[0][0]), flip(*small_bits[at]))
    d_w_in = fold_call(pairs, w_in.shape[1], [flat])
    flat = flat.reshape(-1)
    small, at = [], 0
    for piece in pieces:
        small.append(flat[at : at + piece.shape[0]])
        at += piece.shape[0]
    d_norm_gain, d_conv_weight, d_conv_bias, d_dt_bias, d_a_log, d_skip, d_gain_out = small
    return (
        block_out,
        d_tokens,
        d_norm_gain,
        d_w_in,
        d_conv_weight.reshape(KW, CONV),
        d_conv_bias,
        d_dt_bias,
        d_a_log,
        d_skip,
        d_gain_out,
        d_w_out_sum,
    )


def solution(mesh):
    split = P("fsdp", "seq", None)
    rows = P("fsdp", None)
    last = P(("seq", "fsdp"), None)
    return jax.shard_map(
        functools.partial(on_device, mesh.shape["seq"], mesh.shape["fsdp"]),
        mesh=mesh,
        in_specs=(split, P(), rows, P(), P(), P(), P(), P(), P(), rows, split),
        out_specs=(split, split, P(), last, P(), P(), P(), P(), P(), P(), last),
        check_vma=False,
    )
```

time: 842 us -> 520 us (0.62)
  waiting for transfers between devices: 406 us -> 149 us
  Pallas kernels: 110 us -> 240 us
  matrix products: 90.2 us -> 9.49 us
  other arithmetic: 58.3 us -> 7.55 us
  local copies, waits for them, and re-layouts: 82.5 us -> 33.4 us
  starting transfers between devices: 76.3 us -> 65.3 us
    reduce_scatter x3 -> x1, waiting for transfers between devices: 235 us -> 0.01 us  [on_device(): lax.psum_scatter(d_w_out, both, scatter_dimension=0, tiled=True).astype(F32)]
    pallas_call x4 -> x20, Pallas kernels: 89.2 us -> 219 us  [the longest x1 52.5 us: back_call(): pl.pallas_call(back_kernel, grid=(QUADS + 2,), in_specs=[pl.BlockSpec((le...]
    dot_general x9 -> x1, matrix products: 90.2 us -> 9.49 us  [on_device(): lax.dot_general(normed_out, cotan, TN, preferred_element_type=F32)]
    ppermute x44 -> x37, waiting for transfers between devices: 171 us -> 107 us  [move(): return lax.ppermute(value, both, pairs)]
    gather x9 -> x0, local copies, waits for them, and re-layouts: 48.7 us -> none  [ordered(): stack[jnp.arange(shards) ^ shard].reshape((-1,) + pieces[0].shape[1:])]
    all_to_all x0 -> x4, waiting for transfers between devices: none -> 42.6 us  [exchange(): lax.all_to_all(states, 'seq', split_axis=0, concat_axis=0, tiled=True)]
    ppermute x44 -> x37, starting transfers between devices: 76.1 us -> 34.2 us  [move(): return lax.ppermute(value, both, pairs)]
    all_to_all x0 -> x4, starting transfers between devices: none -> 30.7 us  [exchange(): lax.all_to_all(states, 'seq', split_axis=0, concat_axis=0, tiled=True)]
  transfers between devices with their start and end apart: 47 -> 42, of which waited for: 15 -> 19; matrix products, arithmetic and copies ran while one was open for 18% -> 6% of each run, Pallas kernels for 8% -> 43%
where the time goes in v2:
time: 520 us
  Pallas kernels  240 us (46%)
  waiting for transfers between devices  149 us (29%)
  starting transfers between devices  65.3 us (13%)
  local copies, waits for them, and re-layouts  33.4 us (6%)
  between operations  14.7 us (3%)
  matrix products  9.49 us (2%)
  other arithmetic  7.55 us (1%)
    ppermute x37, waiting for transfers between devices, move(): return lax.ppermute(value, both, pairs)  107 us
    pallas_call x1, Pallas kernels, back_call(): pl.pallas_call(back_kernel, grid=(QUADS + 2,), in_specs=[pl.BlockSpec((le...  52.5 us
    all_to_all x4, waiting for transfers between devices, exchange(): lax.all_to_all(states, 'seq', split_axis=0, concat_axis=0, tiled=True)  42.6 us
    ppermute x37, starting transfers between devices, move(): return lax.ppermute(value, both, pairs)  34.2 us
    pallas_call x6, Pallas kernels, grad_call(): pl.pallas_call(functools.partial(grad_kernel, halo), grid=(width // block...  32 us
    all_to_all x4, starting transfers between devices, exchange(): lax.all_to_all(states, 'seq', split_axis=0, concat_axis=0, tiled=True)  30.7 us
    pallas_call x2, Pallas kernels, weight_call(): pl.pallas_call(functools.partial(weight_kernel, height, halves), grid_spe...  27.2 us
    pallas_call x1, Pallas kernels, tokens_call(): pl.pallas_call(tokens_kernel, grid=(D // block,), in_specs=[pl.BlockSpec(...  20.2 us
  transfers between devices with their start and end apart: 42, of which 19 were waited for; matrix products, arithmetic and copies ran while one was open for 6% of the time, Pallas kernels for 43%

profile of v2, /device:TPU:0, one launch (start us, length us, event | category | flops | bytes accessed | tf_op | source)
XLA Modules:
  0.0 519.5 jit_solution(967595164625040980)
XLA Ops:
  8.0 4.8 collective-permute-start
  19.4 3.3 slice.84.rest_0_
  34.1 11.9 %pick_rows.1 = (bf16[16,48,512]{2,1,0:T(8,128)(2,1)}, bf16[16,48,512]{2,1,0:T(8,128)(2,1)}, bf16[16,48,32]{2,1,0:T(8,128)(2,1)}, bf16[16,48,512]{2,1,0:T(8,128)(...) custom-call(s32[3,16]{1,0:T(4,128)} %pad_add_fusion.table_ref, ...), custom_call_target="tpu_custom_call" | custom-call | flops 1000000 | bytes 1000000 | tf_op jit(solution)/shard_map/pick_rows/pallas_call | solution.py:734
  46.1 4.8 collective-permute-done.2.rest_2_
  54.0 29.1 %collective-permute-done.7.rest_3_ = bf16[1792,384]{1,0:T(8,128)(2,1)} collective-permute-done((bf16[1792,384]{1,0:T(8,128)(2,1)}, bf16[1792,384]{1,0:T(8,128)(2,1)}, u32[]{:S(2)}, u32[]{:S(2)}) %collective-permute-start.7) | collective-permute-done | bytes 1376288 | tf_op jit(solution)/shard_map/ppermute | solution.py:947
  83.6 2.9 collective-permute-done.9.rest_5_
  86.5 15.3 %project_v.1 = (bf16[528,3584]{1,0:T(8,128)(2,1)}, bf16[3584,1536]{1,0:T(8,128)(2,1)}) custom-call(s32[7]{0:T(128)} %stack.141.place_ref, bf16[528,1536]{1,0:T(8,128)(2,1)} %copy-done.2, bf16[3584,384]{1,0:T(8,128)(2,1)} %pad.15.rest_0_, bf16[3584,384]{1,0:T(8,128)(2,1)} %collective-permute-done.1.rest_1_, bf16[1792,384]{1,0:T(8,128)(2,1)} %collective-permute-done.2.rest_2_, ...), custom_call_target="tpu_custom_call" | custom-call | flops 1000000 | bytes 1000000 | tf_op jit(solution)/shard_map/project_v/pallas_call | solution.py:663
  101.8 3.5 collective-permute-done.10.rest_2_
  107.9 2.6 steps.1
  110.5 14.2 %conv_states.1 = (bf16[512,3072]{1,0:T(8,128)(2,1)}, bf16[512,3328]{1,0:T(8,128)(2,1)}, bf16[512,128]{1,0:T(8,128)(2,1)}, bf16[512,128]{1,0:T(8,128)(2,1)}, bf16...) custom-call(bf16[528,3584]{1,0:T(8,128)(2,1)} %get-tuple-element.93.dt_ref.v_ref, ...), custom_call_target="tpu_custom_call" | custom-call | flops 1000000 | bytes 1000000 | tf_op jit(solution)/shard_map/conv_states/pallas_call | solution.py:187
  124.7 4.8 all-to-all-start
  130.3 15.5 %ssd_inside.1.rest_0_.y_ref = f32[512,3072]{1,0:T(8,128)} custom-call(bf16[512,3072]{1,0:T(8,128)(2,1)} %get-tuple-element.96.x_ref, bf16[512,128]{1,0:T(8,128)(2,1)} %get-tuple-element.97.b_ref, bf16[512,128]{1,0:T(8,128)(2,1)} %get-tuple-element.98.c_ref, bf16[128,512]{1,0:T(8,128)(2,1)} %get-tuple-element.99.bt_ref, ...), custom_call_target="tpu_custom_call" | custom-call | flops 1000000 | bytes 1000000 | tf_op jit(solution)/shard_map/ssd_inside/pallas_call | solution.py:303
  145.7 3.9 all-to-all-done
  150.5 2.6 carry.1
  153.2 4.1 collective-permute-done.12.rest_2_
  157.3 4.8 all-to-all-start.1
  162.9 12.0 %project_gate.1 = (bf16[512,3072]{1,0:T(8,128)(2,1)}, bf16[3072,1536]{1,0:T(8,128)(2,1)}) custom-call(s32[4]{0:T(128)} %pad_add_fusion.1.place_ref, bf16[512,1536]{1,0:T(8,128)(2,1)} %get-tuple-element.173.x_ref, bf16[3072,384]{1,0:T(8,128)(2,1)} %slice.84.rest_0_, bf16[3072,384]{1,0:T(8,128)(2,1)} %collective-permute-done.5.rest_1_, ...), custom_call_target="tpu_custom_call" | custom-call | flops 1000000 | bytes 1000000 | tf_op jit(solution)/shard_map/project_gate/pallas_call | solution.py:663
  174.9 16.4 %d_normed_out.1 = (f32[512,3072]{1,0:T(8,128)}, bf16[3072,1536]{1,0:T(8,128)(2,1)}) custom-call(s32[4]{0:T(128)} %pad_add_fusion.1.place_ref, bf16[512,1536]{1,0:T(8,128)(2,1)} %bitcast.87, bf16[768,1536]{1,0:T(8,128)(2,1)} %rest_0_.1, bf16[768,1536]{1,0:T(8,128)(2,1)} %collective-permute-done.6.rest_1_, bf16[768,1536]{1,0:T(8,128)(2,1)} %collective-permute-done.12.rest_2_, ...), custom_call_target="tpu_custom_call" | custom-call | flops 1000000 | bytes 1000000 | tf_op jit(solution)/shard_map/d_normed_out/pallas_call | solution.py:701
  192.2 15.3 %gated_norm.1 = (bf16[512,3072]{1,0:T(8,128)(2,1)}, bf16[512,3072]{1,0:T(8,128)(2,1)}, bf16[512,3072]{1,0:T(8,128)(2,1)}, f32[1,3072]{1,0:T(1,128)}, bf16[128,3072]{1,0:T(8,128)(2,1)}) custom-call(f32[512,3072]{1,0:T(8,128)} %ssd_inside.1.rest_0_.y_ref, bf16[512,3072]{1,0:T(8,128)(2,1)} %get-tuple-element.102.gate_ref, ...), custom_call_target="tpu_custom_call" | custom-call | flops 1000000 | bytes 1000000 | tf_op jit(solution)/shard_map/gated_norm/pallas_call | solution.py:384
  207.6 9.5 %convolution_convert_fusion.rest_1_ = bf16[3072,1536]{1,0:T(8,128)(2,1)} fusion(bf16[512,3072]{1,0:T(8,128)(2,1)} %get-tuple-element.110.x_ref, bf16[1,512,1536]{2,1,0:T(8,128)(2,1)S(1)} %copy-done.5), kind=kOutput, calls=%fused_computation | convolution fusion | flops 4836556800 | bytes 14155776 | tf_op jit(solution)/shard_map/dot_general | solution.py:1066
  219.2 5.7 %all-to-all-start.2 = ((bf16[8,16,3072]{2,1,0:T(8,128)(2,1)}), bf16[8,16,3072]{2,1,0:T(8,128)(2,1)}, u32[]{:S(2)}, u32[]{:S(2)}) async-start(bf16[8,16,3072]{2,1,0:T(8,128)(2,1)} %bitcast.95), calls=%async_computation.2 | async-start | bytes 1572864 | tf_op jit(solution)/shard_map/all_to_all | solution.py:989
  224.9 11.2 %block_out.1.rest_2_ = f32[1,512,1536]{2,1,0:T(8,128)} custom-call(bf16[512,3072]{1,0:T(8,128)(2,1)} %get-tuple-element.110.x_ref, bf16[3072,1536]{1,0:T(8,128)(2,1)} %get-tuple-element.111.w_ref, bf16[1,512,1536]{2,1,0:T(8,128)(2,1)} %tokens_ref.3, bf16[128,3072]{1,0:T(8,128)(2,1)} %get-tuple-element.112.rest_0_), custom_call_target="tpu_custom_call" | custom-call | flops 1000000 | bytes 1000000 | tf_op jit(solution)/shard_map/block_out/pallas_call | solution.py:845
  236.1 9.7 %all-to-all-done.2 = bf16[8,16,3072]{2,1,0:T(8,128)(2,1)} async-done(((bf16[8,16,3072]{2,1,0:T(8,128)(2,1)}), bf16[8,16,3072]{2,1,0:T(8,128)(2,1)}, u32[]{:S(2)}, u32[]{:S(2)}) %all-to-all-start.2) | async-done | bytes 786464 | tf_op jit(solution)/shard_map/all_to_all | solution.py:989
  245.8 2.7 carry_back.1
  248.5 15.4 %all-to-all-start.3 = ((bf16[8,16,3072]{2,1,0:T(8,128)(2,1)}), bf16[8,16,3072]{2,1,0:T(8,128)(2,1)}, u32[]{:S(2)}, u32[]{:S(2)}) async-start(bf16[8,16,3072]{2,1,0:T(8,128)(2,1)} %bitcast.108), calls=%async_computation.3 | async-start | bytes 1572864 | tf_op jit(solution)/shard_map/all_to_all | solution.py:989
  263.9 4.5 d_w_gate.3
  268.4 28.9 %all-to-all-done.3 = bf16[8,16,3072]{2,1,0:T(8,128)(2,1)} async-done(((bf16[8,16,3072]{2,1,0:T(8,128)(2,1)}), bf16[8,16,3072]{2,1,0:T(8,128)(2,1)}, u32[]{:S(2)}, u32[]{:S(2)}) %all-to-all-start.3) | async-done | bytes 786464 | tf_op jit(solution)/shard_map/all_to_all | solution.py:989
  298.7 4.6 d_w_gate.4
  304.7 4.5 d_w_gate.5
  309.3 52.5 %ssd_back.1 = (bf16[528,3584]{1,0:T(8,128)(2,1)}, f32[8,3328]{1,0:T(8,128)}, f32[12,16,128]{2,1,0:T(8,128)}) custom-call(bf16[512,3072]{1,0:T(8,128)(2,1)} %get-tuple-element.96.x_ref, bf16[512,3072]{1,0:T(8,128)(2,1)} %get-tuple-element.114.dm_ref, bf16[512,3328]{1,0:T(8,128)(2,1)} %get-tuple-element.115.slope_ref, ...), custom_call_target="tpu_custom_call" | custom-call | flops 1000000 | bytes 1000000 | tf_op jit(solution)/shard_map/ssd_back/pallas_call | solution.py:573
  365.9 6.1 %collective-permute-done.18.spill_ref = bf16[16,3584]{1,0:T(8,128)(2,1)} collective-permute-done((bf16[16,3584]{1,0:T(8,128)(2,1)S(1)}, bf16[16,3584]{1,0:T(8,128)(2,1)}, u32[]{:S(2)}, u32[]{:S(2)}) %collective-permute-start.18) | collective-permute-done | bytes 114720 | tf_op jit(solution)/shard_map/ppermute | solution.py:947
  372.0 6.1 %d_w_rest.3 = (bf16[384,1152]{1,0:T(8,128)(2,1)}, bf16[384,1152]{1,0:T(8,128)(2,1)}) custom-call(bf16[768,512]{1,0:T(8,128)(2,1)} %bitcast.105, bf16[768,512]{1,0:T(8,128)(2,1)} %bitcast.107, bf16[768,32]{1,0:T(8,128)(2,1)} %bitcast.115, bf16[528,3584]{1,0:T(8,128)(2,1)} %get-tuple-element.129.refs_3_.refs_5_.dv_ref, ...), custom_call_target="tpu_custom_call" | custom-call | flops 1000000 | bytes 1000000 | tf_op jit(solution)/shard_map/d_w_rest/pallas_call | solution.py:777
  378.1 2.5 collective-permute-start.22
  380.7 6.1 %d_w_rest.4 = (bf16[384,1152]{1,0:T(8,128)(2,1)}, bf16[384,1152]{1,0:T(8,128)(2,1)}) custom-call(bf16[768,512]{1,0:T(8,128)(2,1)} %bitcast.101, bf16[768,512]{1,0:T(8,128)(2,1)} %bitcast.103, bf16[768,32]{1,0:T(8,128)(2,1)} %bitcast.114, bf16[528,3584]{1,0:T(8,128)(2,1)} %get-tuple-element.129.refs_3_.refs_5_.dv_ref, ...), custom_call_target="tpu_custom_call" | custom-call | flops 1000000 | bytes 1000000 | tf_op jit(solution)/shard_map/d_w_rest/pallas_call | solution.py:777
  388.0 6.1 %d_w_rest.5 = (bf16[384,1152]{1,0:T(8,128)(2,1)}, bf16[384,1152]{1,0:T(8,128)(2,1)}) custom-call(bf16[768,512]{1,0:T(8,128)(2,1)} %bitcast.97, bf16[768,512]{1,0:T(8,128)(2,1)} %bitcast.99, bf16[768,32]{1,0:T(8,128)(2,1)} %bitcast.113, bf16[528,3584]{1,0:T(8,128)(2,1)} %get-tuple-element.129.refs_3_.refs_5_.dv_ref, ...), custom_call_target="tpu_custom_call" | custom-call | flops 1000000 | bytes 1000000 | tf_op jit(solution)/shard_map/d_w_rest/pallas_call | solution.py:777
  395.9 20.2 %d_tokens.1 = (f32[1,512,1536]{2,1,0:T(8,128)}, f32[1,1536]{1,0:T(1,128)}) custom-call(bf16[512,3072]{1,0:T(8,128)(2,1)} %get-tuple-element.113.refs_2_.dg_ref, bf16[528,3584]{1,0:T(8,128)(2,1)} %get-tuple-element.129.refs_3_.refs_5_.dv_ref, bf16[16,3584]{1,0:T(8,128)(2,1)} %collective-permute-done.18.spill_ref, ...), custom_call_target="tpu_custom_call" | custom-call | flops 1000000 | bytes 1000000 | tf_op jit(solution)/shard_map/d_tokens/pallas_call | solution.py:898
  418.3 4.5 collective-permute-done.21
  425.0 6.4 %fold.4 = (bf16[192,2176]{1,0:T(8,128)(2,1)}, bf16[192,2176]{1,0:T(8,128)(2,1)}, bf16[192,2176]{1,0:T(8,128)(2,1)}, bf16[192,2176]{1,0:T(8,128)(2,1)}, bf16[192,...) custom-call(bf16[384,1024]{1,0:T(8,128)(2,1)} %get-tuple-element.144.refs_0_, bf16[384,1024]{1,0:T(8,128)(2,1)} %copy-done.16, ...), custom_call_target="tpu_custom_call" | custom-call | flops 1000000 | bytes 1000000 | tf_op jit(solution)/shard_map/fold/pallas_call | solution.py:823
  434.4 18.8 %collective-permute-done.25 = f32[168,128]{1,0:T(8,128)S(1)} collective-permute-done((f32[168,128]{1,0:T(8,128)S(1)}, f32[168,128]{1,0:T(8,128)S(1)}, u32[]{:S(2)}, u32[]{:S(2)}) %collective-permute-start.25) | collective-permute-done | bytes 86048 | tf_op jit(solution)/shard_map/ppermute | solution.py:947
  455.3 4.0 fold.5
  463.0 8.3 %collective-permute-done.29 = f32[168,128]{1,0:T(8,128)S(1)} collective-permute-done((f32[168,128]{1,0:T(8,128)S(1)}, f32[168,128]{1,0:T(8,128)S(1)}, u32[]{:S(2)}, u32[]{:S(2)}) %collective-permute-start.29) | collective-permute-done | bytes 86048 | tf_op jit(solution)/shard_map/ppermute | solution.py:947
  473.0 2.7 fold.6
  475.7 2.9 collective-permute-start.34
  478.7 2.9 collective-permute-start.36
  481.6 12.7 %collective-permute-done.33 = f32[168,128]{1,0:T(8,128)S(1)} collective-permute-done((f32[168,128]{1,0:T(8,128)}, f32[168,128]{1,0:T(8,128)S(1)}, u32[]{:S(2)}, u32[]{:S(2)}) %collective-permute-start.33) | collective-permute-done | bytes 86048 | tf_op jit(solution)/shard_map/ppermute | solution.py:947
  498.8 4.5 collective-permute-done.35.refs_3_
  503.2 4.2 collective-permute-done.36.refs_5_
  508.1 2.5 fold.7
  (178 shorter events, 62.2 us)
Async XLA Ops:
  8.0 15.3 %collective-permute-start = (bf16[16,1536]{1,0:T(8,128)(2,1)S(1)}, bf16[16,1536]{1,0:T(8,128)(2,1)S(1)}, u32[]{:S(2)}, u32[]{:S(2)}) collective-permute-start(bf16[16,1536]{1,0:T(8,128)(2,1)S(1)} %slice_bitcast_fusion.1), channel_id=1, source_target_pairs={{0,4},{1,5},{2,6},{3,7},{4,8},{5,9},{6,10},{7,11},{8,12},{9,13},{1... | collective-permute-start | bytes 147464 | tf_op jit(solution)/shard_map/ppermute | solution.py:947
  16.6 34.2 %collective-permute-start.1 = (bf16[3584,384]{1,0:T(8,128)(2,1)}, bf16[3584,384]{1,0:T(8,128)(2,1)}, u32[]{:S(2)}, u32[]{:S(2)}) collective-permute-start(bf16[3584,384]{1,0:T(8,128)(2,1)} %pad.15.rest_0_), channel_id=1, source_target_pairs={{0,1},{1,0},{2,3},{3,2},{4,5},{5,4},{6,7},{7,6},{8,9},{9,8},{10,11... | collective-permute-start | bytes 8257544 | tf_op jit(solution)/shard_map/ppermute | solution.py:947
  17.9 32.9 %collective-permute-start.2 = (bf16[1792,384]{1,0:T(8,128)(2,1)}, bf16[1792,384]{1,0:T(8,128)(2,1)}, u32[]{:S(2)}, u32[]{:S(2)}) collective-permute-start(bf16[1792,384]{1,0:T(8,128)(2,1)} %constant_dynamic-slice_fusion.2), channel_id=1, source_target_pairs={{0,2},{1,3},{2,0},{3,1},{4,6},{5,7},{6,4},{7,5},{8,10},{9,11},{10,... | collective-permute-start | bytes 4128776 | tf_op jit(solution)/shard_map/ppermute | solution.py:947
  22.7 28.1 %collective-permute-start.5 = (bf16[3072,384]{1,0:T(8,128)(2,1)}, bf16[3072,384]{1,0:T(8,128)(2,1)}, u32[]{:S(2)}, u32[]{:S(2)}) collective-permute-start(bf16[3072,384]{1,0:T(8,128)(2,1)} %slice.84.rest_0_), channel_id=1, source_target_pairs={{0,1},{1,0},{2,3},{3,2},{4,5},{5,4},{6,7},{7,6},{8,9},{9,8},{10,11... | collective-permute-start | bytes 7077896 | tf_op jit(solution)/shard_map/ppermute | solution.py:947
  23.0 27.9 %collective-permute-start.6 = (bf16[768,1536]{1,0:T(8,128)(2,1)}, bf16[768,1536]{1,0:T(8,128)(2,1)}, u32[]{:S(2)}, u32[]{:S(2)}) collective-permute-start(bf16[768,1536]{1,0:T(8,128)(2,1)} %rest_0_.1), channel_id=1, source_target_pairs={{0,1},{1,0},{2,3},{3,2},{4,5},{5,4},{6,7},{7,6},{8,9},{9,8},{10,11... | collective-permute-start | bytes 7077896 | tf_op jit(solution)/shard_map/ppermute | solution.py:947
  28.6 2.4 collective-permute-start.4
  30.9 2.3 collective-permute-start.3
  50.8 32.2 %collective-permute-start.7 = (bf16[1792,384]{1,0:T(8,128)(2,1)}, bf16[1792,384]{1,0:T(8,128)(2,1)}, u32[]{:S(2)}, u32[]{:S(2)}) collective-permute-start(bf16[1792,384]{1,0:T(8,128)(2,1)} %collective-permute-done.2.rest_2_), channel_id=1, source_target_pairs={{0,4},{1,5},{2,6},{3,7},{4,0},{5,1},{6,2},{7,3},{8,12},{9,13},{10,... | collective-permute-start | bytes 4128776 | tf_op jit(solution)/shard_map/ppermute | solution.py:947
  52.4 52.8 %collective-permute-start.10 = (bf16[3072,384]{1,0:T(8,128)(2,1)}, bf16[3072,384]{1,0:T(8,128)(2,1)S(1)}, u32[]{:S(2)}, u32[]{:S(2)}) collective-permute-start(bf16[3072,384]{1,0:T(8,128)(2,1)} %slice.84.rest_0_), channel_id=1, source_target_pairs={{0,2},{1,3},{2,0},{3,1},{4,6},{5,7},{6,4},{7,5},{8,10},{9,11},{10,... | collective-permute-start | bytes 7077896 | tf_op jit(solution)/shard_map/ppermute | solution.py:947
  54.0 29.7 %collective-permute-start.8 = (bf16[1792,384]{1,0:T(8,128)(2,1)}, bf16[1792,384]{1,0:T(8,128)(2,1)}, u32[]{:S(2)}, u32[]{:S(2)}) collective-permute-start(bf16[1792,384]{1,0:T(8,128)(2,1)} %collective-permute-done.2.rest_2_), channel_id=1, source_target_pairs={{0,1},{1,0},{2,3},{3,2},{4,5},{5,4},{6,7},{7,6},{8,9},{9,8},{10,11... | collective-permute-start | bytes 4128776 | tf_op jit(solution)/shard_map/ppermute | solution.py:947
  83.0 3.5 collective-permute-start.9
  83.6 23.2 %copy-start.27 = (f32[3328]{0:T(1024)S(1)}, f32[3328]{0:T(1024)}, u32[]{:S(2)}) copy-start(f32[3328]{0:T(1024)} %param.15) | copy-start | bytes 39940
  83.6 23.8 %copy-start.30 = (f32[48]{0:T(128)S(1)}, f32[48]{0:T(128)}, u32[]{:S(2)}) copy-start(f32[48]{0:T(128)} %param.16) | copy-start | bytes 580
  83.6 23.8 %copy-start.31 = (f32[48]{0:T(128)S(1)}, f32[48]{0:T(128)}, u32[]{:S(2)}) copy-start(f32[48]{0:T(128)} %param.17) | copy-start | bytes 580
  105.3 25.0 %copy-start.7 = (bf16[3072,384]{1,0:T(8,128)(2,1)}, bf16[3072,384]{1,0:T(8,128)(2,1)S(1)}, u32[]{:S(2)}) copy-start(bf16[3072,384]{1,0:T(8,128)(2,1)S(1)} %collective-permute-done.10.rest_2_) | copy-start | bytes 7077892
  105.3 52.0 %collective-permute-start.12 = (bf16[768,1536]{1,0:T(8,128)(2,1)}, bf16[768,1536]{1,0:T(8,128)(2,1)}, u32[]{:S(2)}, u32[]{:S(2)}) collective-permute-start(bf16[768,1536]{1,0:T(8,128)(2,1)} %rest_0_.1), channel_id=1, source_target_pairs={{0,2},{1,3},{2,0},{3,1},{4,6},{5,7},{6,4},{7,5},{8,10},{9,11},{10,... | collective-permute-start | bytes 7077896 | tf_op jit(solution)/shard_map/ppermute | solution.py:947
  110.5 19.0 %copy-start.29 = (f32[48]{0:T(128)S(1)}, f32[48]{0:T(128)}, u32[]{:S(2)}) copy-start(f32[48]{0:T(128)} %param.18) | copy-start | bytes 580
  124.7 24.9 %all-to-all-start = ((bf16[8,16,3328]{2,1,0:T(8,128)(2,1)}), bf16[8,16,3328]{2,1,0:T(8,128)(2,1)S(1)}, u32[]{:S(2)}, u32[]{:S(2)}) async-start(bf16[8,16,3328]{2,1,0:T(8,128)(2,1)} %bitcast.109), calls=%async_computation | async-start | bytes 1703936 | tf_op jit(solution)/shard_map/all_to_all | solution.py:989
  130.3 32.7 %collective-permute-start.11 = (bf16[3072,384]{1,0:T(8,128)(2,1)S(1)}, bf16[3072,384]{1,0:T(8,128)(2,1)}, u32[]{:S(2)}, u32[]{:S(2)}) collective-permute-start(bf16[3072,384]{1,0:T(8,128)(2,1)S(1)} %collective-permute-done.10.rest_2_), channel_id=1, source_target_pairs={{0,1},{1,0},{2,3},{3,2},{4,5},{5,4},{6,7},{7,6},{8,9},{9,8},{10,11... | collective-permute-start | bytes 7077896 | tf_op jit(solution)/shard_map/ppermute | solution.py:947
  157.3 17.7 %collective-permute-start.13 = (bf16[768,1536]{1,0:T(8,128)(2,1)}, bf16[768,1536]{1,0:T(8,128)(2,1)}, u32[]{:S(2)}, u32[]{:S(2)}) collective-permute-start(bf16[768,1536]{1,0:T(8,128)(2,1)} %collective-permute-done.12.rest_2_), channel_id=1, source_target_pairs={{0,1},{1,0},{2,3},{3,2},{4,5},{5,4},{6,7},{7,6},{8,9},{9,8},{10,11... | collective-permute-start | bytes 7077896 | tf_op jit(solution)/shard_map/ppermute | solution.py:947
  157.3 34.1 %all-to-all-start.1 = ((bf16[8,16,3072]{2,1,0:T(8,128)(2,1)}), bf16[8,16,3072]{2,1,0:T(8,128)(2,1)S(1)}, u32[]{:S(2)}, u32[]{:S(2)}) async-start(bf16[8,16,3072]{2,1,0:T(8,128)(2,1)} %bitcast.112), calls=%async_computation.1 | async-start | bytes 1572864 | tf_op jit(solution)/shard_map/all_to_all | solution.py:989
  162.1 348.6 %reduce-scatter.2.cloned.1.call-start = ((), (), s32[]{:S(2)}) async-start(), calls=%async_computation.5 | async-start | bytes 9732096 | tf_op jit(solution)/shard_map/reduce_scatter | solution.py:1067
  218.9 45.0 %collective-permute-start.14 = (bf16[512,3072]{1,0:T(8,128)(2,1)S(1)}, bf16[512,3072]{1,0:T(8,128)(2,1)}, u32[]{:S(2)}, u32[]{:S(2)}) collective-permute-start(bf16[512,3072]{1,0:T(8,128)(2,1)S(1)} %copy-done), channel_id=1, source_target_pairs={{0,1},{1,0},{2,3},{3,2},{4,5},{5,4},{6,7},{7,6},{8,9},{9,8},{10,11... | collective-permute-start | bytes 9437192 | tf_op jit(solution)/shard_map/ppermute | solution.py:947
  219.2 26.7 %all-to-all-start.2 = ((bf16[8,16,3072]{2,1,0:T(8,128)(2,1)}), bf16[8,16,3072]{2,1,0:T(8,128)(2,1)}, u32[]{:S(2)}, u32[]{:S(2)}) async-start(bf16[8,16,3072]{2,1,0:T(8,128)(2,1)} %bitcast.95), calls=%async_computation.2 | async-start | bytes 1572864 | tf_op jit(solution)/shard_map/all_to_all | solution.py:989
  248.5 48.9 %all-to-all-start.3 = ((bf16[8,16,3072]{2,1,0:T(8,128)(2,1)}), bf16[8,16,3072]{2,1,0:T(8,128)(2,1)}, u32[]{:S(2)}, u32[]{:S(2)}) async-start(bf16[8,16,3072]{2,1,0:T(8,128)(2,1)} %bitcast.108), calls=%async_computation.3 | async-start | bytes 1572864 | tf_op jit(solution)/shard_map/all_to_all | solution.py:989
  297.3 64.5 %collective-permute-start.15 = (bf16[384,1024]{1,0:T(8,128)(2,1)}, bf16[384,1024]{1,0:T(8,128)(2,1)S(1)}, u32[]{:S(2)}, u32[]{:S(2)}) collective-permute-start(bf16[384,1024]{1,0:T(8,128)(2,1)} %get-tuple-element.120), channel_id=1, source_target_pairs={{0,4},{1,5},{2,6},{3,7},{4,0},{5,1},{6,2},{7,3},{8,12},{9,13},{10,... | collective-permute-start | bytes 2359304 | tf_op jit(solution)/shard_map/ppermute | solution.py:947
  303.3 58.6 %collective-permute-start.16 = (bf16[384,1024]{1,0:T(8,128)(2,1)}, bf16[384,1024]{1,0:T(8,128)(2,1)}, u32[]{:S(2)}, u32[]{:S(2)}) collective-permute-start(bf16[384,1024]{1,0:T(8,128)(2,1)} %get-tuple-element.124), channel_id=1, source_target_pairs={{0,2},{1,3},{2,0},{3,1},{4,6},{5,7},{6,4},{7,5},{8,10},{9,11},{10,... | collective-permute-start | bytes 2359304 | tf_op jit(solution)/shard_map/ppermute | solution.py:947
  309.3 52.6 %collective-permute-start.17 = (bf16[384,1024]{1,0:T(8,128)(2,1)}, bf16[384,1024]{1,0:T(8,128)(2,1)}, u32[]{:S(2)}, u32[]{:S(2)}) collective-permute-start(bf16[384,1024]{1,0:T(8,128)(2,1)} %get-tuple-element.128), channel_id=1, source_target_pairs={{0,8},{1,9},{2,10},{3,11},{4,12},{5,13},{6,14},{7,15},{8,0},{9,1},... | collective-permute-start | bytes 2359304 | tf_op jit(solution)/shard_map/ppermute | solution.py:947
  361.9 10.1 %collective-permute-start.19 = (bf16[528,3584]{1,0:T(8,128)(2,1)}, bf16[528,3584]{1,0:T(8,128)(2,1)}, u32[]{:S(2)}, u32[]{:S(2)}) collective-permute-start(bf16[528,3584]{1,0:T(8,128)(2,1)} %get-tuple-element.129.refs_3_.refs_5_.dv_ref), channel_id=1, source_target_pairs={{0,1},{1,0},{2,3},{3,2},{4,5},{5,4},{6,7},{7,6},{8,9},{9,8},{10,11... | collective-permute-start | bytes 11354120 | tf_op jit(solution)/shard_map/ppermute | solution.py:947
  364.6 7.4 %collective-permute-start.18 = (bf16[16,3584]{1,0:T(8,128)(2,1)S(1)}, bf16[16,3584]{1,0:T(8,128)(2,1)}, u32[]{:S(2)}, u32[]{:S(2)}) collective-permute-start(bf16[16,3584]{1,0:T(8,128)(2,1)S(1)} %slice.66), channel_id=1, source_target_pairs={{4,0},{5,1},{6,2},{7,3},{8,4},{9,5},{10,6},{11,7},{12,8},{13,9},{1... | collective-permute-start | bytes 344072 | tf_op jit(solution)/shard_map/ppermute | solution.py:947
  378.1 45.4 %collective-permute-start.22 = (bf16[384,1152]{1,0:T(8,128)(2,1)}, bf16[384,1152]{1,0:T(8,128)(2,1)S(1)}, u32[]{:S(2)}, u32[]{:S(2)}) collective-permute-start(bf16[384,1152]{1,0:T(8,128)(2,1)} %get-tuple-element.145), channel_id=1, source_target_pairs={{0,4},{1,5},{2,6},{3,7},{4,0},{5,1},{6,2},{7,3},{8,12},{9,13},{10,... | collective-permute-start | bytes 2654216 | tf_op jit(solution)/shard_map/ppermute | solution.py:947
  386.8 36.8 %collective-permute-start.23 = (bf16[384,1152]{1,0:T(8,128)(2,1)}, bf16[384,1152]{1,0:T(8,128)(2,1)S(1)}, u32[]{:S(2)}, u32[]{:S(2)}) collective-permute-start(bf16[384,1152]{1,0:T(8,128)(2,1)} %get-tuple-element.147), channel_id=1, source_target_pairs={{0,2},{1,3},{2,0},{3,1},{4,6},{5,7},{6,4},{7,5},{8,10},{9,11},{10,... | collective-permute-start | bytes 2654216 | tf_op jit(solution)/shard_map/ppermute | solution.py:947
  394.1 29.4 %collective-permute-start.24 = (bf16[384,1152]{1,0:T(8,128)(2,1)}, bf16[384,1152]{1,0:T(8,128)(2,1)S(1)}, u32[]{:S(2)}, u32[]{:S(2)}) collective-permute-start(bf16[384,1152]{1,0:T(8,128)(2,1)} %get-tuple-element.149), channel_id=1, source_target_pairs={{0,8},{1,9},{2,10},{3,11},{4,12},{5,13},{6,14},{7,15},{8,0},{9,1},... | collective-permute-start | bytes 2654216 | tf_op jit(solution)/shard_map/ppermute | solution.py:947
  395.8 20.9 %copy-start.28 = (f32[1,3072]{1,0:T(1,128)S(1)}, f32[1,3072]{1,0:T(1,128)}, u32[]{:S(2)}) copy-start(f32[1,3072]{1,0:T(1,128)} %get-tuple-element.143) | copy-start | bytes 36868
  416.8 1.3 collective-permute-start.20
  418.2 4.7 collective-permute-start.21
  431.4 22.5 %collective-permute-start.26 = (bf16[192,2176]{1,0:T(8,128)(2,1)}, bf16[192,2176]{1,0:T(8,128)(2,1)S(1)}, u32[]{:S(2)}, u32[]{:S(2)}) collective-permute-start(bf16[192,2176]{1,0:T(8,128)(2,1)} %get-tuple-element.152), channel_id=1, source_target_pairs={{0,2},{1,3},{2,0},{3,1},{4,6},{5,7},{6,4},{7,5},{8,10},{9,11},{10,... | collective-permute-start | bytes 2506760 | tf_op jit(solution)/shard_map/ppermute | solution.py:947
  432.5 21.4 %collective-permute-start.27 = (bf16[192,2176]{1,0:T(8,128)(2,1)}, bf16[192,2176]{1,0:T(8,128)(2,1)S(1)}, u32[]{:S(2)}, u32[]{:S(2)}) collective-permute-start(bf16[192,2176]{1,0:T(8,128)(2,1)} %get-tuple-element.154), channel_id=1, source_target_pairs={{0,8},{1,9},{2,10},{3,11},{4,12},{5,13},{6,14},{7,15},{8,0},{9,1},... | collective-permute-start | bytes 2506760 | tf_op jit(solution)/shard_map/ppermute | solution.py:947
  432.9 21.0 %collective-permute-start.28 = (bf16[192,2176]{1,0:T(8,128)(2,1)}, bf16[192,2176]{1,0:T(8,128)(2,1)S(1)}, u32[]{:S(2)}, u32[]{:S(2)}) collective-permute-start(bf16[192,2176]{1,0:T(8,128)(2,1)} %get-tuple-element.156), channel_id=1, source_target_pairs={{0,4},{1,5},{2,6},{3,7},{4,0},{5,1},{6,2},{7,3},{8,12},{9,13},{10,... | collective-permute-start | bytes 2506760 | tf_op jit(solution)/shard_map/ppermute | solution.py:947
  433.2 20.0 %collective-permute-start.25 = (f32[168,128]{1,0:T(8,128)S(1)}, f32[168,128]{1,0:T(8,128)S(1)}, u32[]{:S(2)}, u32[]{:S(2)}) collective-permute-start(f32[168,128]{1,0:T(8,128)S(1)} %copy-done.18), channel_id=1, source_target_pairs={{0,2},{1,3},{2,0},{3,1},{4,6},{5,7},{6,4},{7,5},{8,10},{9,11},{10,... | collective-permute-start | bytes 258056 | tf_op jit(solution)/shard_map/ppermute | solution.py:947
  459.3 12.7 %collective-permute-start.30 = (bf16[96,2176]{1,0:T(8,128)(2,1)}, bf16[96,2176]{1,0:T(8,128)(2,1)S(1)}, u32[]{:S(2)}, u32[]{:S(2)}) collective-permute-start(bf16[96,2176]{1,0:T(8,128)(2,1)} %get-tuple-element.159), channel_id=1, source_target_pairs={{0,8},{1,9},{2,10},{3,11},{4,12},{5,13},{6,14},{7,15},{8,0},{9,1},... | collective-permute-start | bytes 1253384 | tf_op jit(solution)/shard_map/ppermute | solution.py:947
  460.0 11.9 %collective-permute-start.31 = (bf16[96,2176]{1,0:T(8,128)(2,1)}, bf16[96,2176]{1,0:T(8,128)(2,1)S(1)}, u32[]{:S(2)}, u32[]{:S(2)}) collective-permute-start(bf16[96,2176]{1,0:T(8,128)(2,1)} %get-tuple-element.161), channel_id=1, source_target_pairs={{0,4},{1,5},{2,6},{3,7},{4,0},{5,1},{6,2},{7,3},{8,12},{9,13},{10,... | collective-permute-start | bytes 1253384 | tf_op jit(solution)/shard_map/ppermute | solution.py:947
  460.6 11.4 %collective-permute-start.32 = (bf16[96,2176]{1,0:T(8,128)(2,1)}, bf16[96,2176]{1,0:T(8,128)(2,1)S(1)}, u32[]{:S(2)}, u32[]{:S(2)}) collective-permute-start(bf16[96,2176]{1,0:T(8,128)(2,1)} %get-tuple-element.163), channel_id=1, source_target_pairs={{0,2},{1,3},{2,0},{3,1},{4,6},{5,7},{6,4},{7,5},{8,10},{9,11},{10,... | collective-permute-start | bytes 1253384 | tf_op jit(solution)/shard_map/ppermute | solution.py:947
  461.4 9.9 %collective-permute-start.29 = (f32[168,128]{1,0:T(8,128)S(1)}, f32[168,128]{1,0:T(8,128)S(1)}, u32[]{:S(2)}, u32[]{:S(2)}) collective-permute-start(f32[168,128]{1,0:T(8,128)S(1)} %copy-done.17), channel_id=1, source_target_pairs={{0,8},{1,9},{2,10},{3,11},{4,12},{5,13},{6,14},{7,15},{8,0},{9,1},... | collective-permute-start | bytes 258056 | tf_op jit(solution)/shard_map/ppermute | solution.py:947
  475.7 18.6 %collective-permute-start.33 = (f32[168,128]{1,0:T(8,128)}, f32[168,128]{1,0:T(8,128)S(1)}, u32[]{:S(2)}, u32[]{:S(2)}) collective-permute-start(f32[168,128]{1,0:T(8,128)} %add.166.refs_6_), channel_id=1, source_target_pairs={{0,16},{1,17},{2,18},{3,19},{4,20},{5,21},{6,22},{7,23},{8,24},{9,... | collective-permute-start | bytes 258056 | tf_op jit(solution)/shard_map/ppermute | solution.py:947
  475.7 23.0 %collective-permute-start.34 = (bf16[48,2176]{1,0:T(8,128)(2,1)}, bf16[48,2176]{1,0:T(8,128)(2,1)S(1)}, u32[]{:S(2)}, u32[]{:S(2)}) collective-permute-start(bf16[48,2176]{1,0:T(8,128)(2,1)} %get-tuple-element.166), channel_id=1, source_target_pairs={{0,16},{1,17},{2,18},{3,19},{4,20},{5,21},{6,22},{7,23},{8,24},{9,... | collective-permute-start | bytes 626696 | tf_op jit(solution)/shard_map/ppermute | solution.py:947
  478.7 24.6 %collective-permute-start.35 = (bf16[48,2176]{1,0:T(8,128)(2,1)}, bf16[48,2176]{1,0:T(8,128)(2,1)S(1)}, u32[]{:S(2)}, u32[]{:S(2)}) collective-permute-start(bf16[48,2176]{1,0:T(8,128)(2,1)} %get-tuple-element.168), channel_id=1, source_target_pairs={{0,16},{1,17},{2,18},{3,19},{4,20},{5,21},{6,22},{7,23},{8,24},{9,... | collective-permute-start | bytes 626696 | tf_op jit(solution)/shard_map/ppermute | solution.py:947
  478.7 28.8 %collective-permute-start.36 = (bf16[48,2176]{1,0:T(8,128)(2,1)}, bf16[48,2176]{1,0:T(8,128)(2,1)S(1)}, u32[]{:S(2)}, u32[]{:S(2)}) collective-permute-start(bf16[48,2176]{1,0:T(8,128)(2,1)} %get-tuple-element.170), channel_id=1, source_target_pairs={{0,16},{1,17},{2,18},{3,19},{4,20},{5,21},{6,22},{7,23},{8,24},{9,... | collective-permute-start | bytes 626696 | tf_op jit(solution)/shard_map/ppermute | solution.py:947
  (26 other events, 112.3 us)
Sparse Core Ops, SparseCore 0:
  217.2 155.3 reduce-scatter.1

commit v3 on v2

--- a/solution.py
+++ b/solution.py
@@ -21,6 +21,7 @@
 QUADS = INNER // QUAD
 HALO = 16
 VMEM_LIMIT = 56 * 1024 * 1024
+LONG = pl.CostEstimate(flops=200000000000, bytes_accessed=1000000, transcendentals=0)
 COST = pl.CostEstimate(flops=1000000, bytes_accessed=1000000, transcendentals=0)
 F32 = jnp.float32
 BF16 = jnp.bfloat16
@@ -31,6 +32,10 @@
 
 def iota(shape, axis):
     return lax.broadcasted_iota(jnp.int32, shape, axis)
+
+
+def tie(value, *others):
+    return lax.optimization_barrier((value,) + others)[0] if others else value
 
 
 def mm(a, b):
@@ -611,190 +616,179 @@
             jax.ShapeDtypeStruct((QUADS, 16, 128), F32),
         ],
         compiler_params=pltpu.CompilerParams(vmem_limit_bytes=VMEM_LIMIT),
-        cost_estimate=COST,
+        cost_estimate=LONG,
         name="ssd_back",
     )(x_act, d_mixed, slope, v, conv_weight, b_act, c_act, b_turned, c_turned, rows, skip_wide, s_in, r_in, *after)
 
 
-def weight_kernel(height, halves, place_ref, x_ref, *rest):
+def put_quarters(place_ref, count, step, refs, put):
+    near = (step // 2) == place_ref[count]
+    for at in range(2, count):
+        for index in range(4):
+            wanted = near if index < 2 else jnp.logical_not(near)
+
+            @pl.when(wanted & (step % 2 == index % 2))
+            def _():
+                put(at, refs[2 + 4 * (at - 2) + index])
+
+
+def weight_kernel(height, quarters, count, place_ref, x_ref, *rest):
     piece_refs, (out_ref, w_ref) = rest[:-2], rest[-2:]
-    block = w_ref.shape[0]
-    if halves:
-        grid = pl.program_id(0)
-        lower = grid < pl.num_programs(0) // 2
-
-        @pl.when(lower == (place_ref[len(piece_refs)] == 0))
-        def _():
-            for at, piece_ref in enumerate(piece_refs):
-                if at < 2 or at % 2 == 0:
-                    w_ref[:, pl.ds(pl.multiple_of(place_ref[at] * height, 128), height)] = piece_ref[...]
-
-        @pl.when(lower != (place_ref[len(piece_refs)] == 0))
-        def _():
-            for at, piece_ref in enumerate(piece_refs):
-                if at < 2 or at % 2 == 1:
-                    w_ref[:, pl.ds(pl.multiple_of(place_ref[at] * height, 128), height)] = piece_ref[...]
-    else:
-        for at, piece_ref in enumerate(piece_refs):
-            w_ref[:, pl.ds(pl.multiple_of(place_ref[at] * height, 128), height)] = piece_ref[...]
+
+    def put(at, ref):
+        w_ref[:, pl.ds(pl.multiple_of(place_ref[at] * height, 128), height)] = ref[...]
+
+    for at in range(2 if quarters else count):
+        put(at, piece_refs[at])
+    if quarters:
+        put_quarters(place_ref, count, pl.program_id(0), piece_refs, put)
     out_ref[...] = mm_nt(x_ref[...], w_ref[...]).astype(BF16)
 
 
-def weight_call(x, pieces, places, width, block, halves, name):
+def weight_call(x, pieces, places, count, width, block, quarters, name):
     rows, depth = x.shape
     height = pieces[0].shape[1]
-    steps = width // block
-    half = steps // 2
 
     def spec(at):
-        if not halves or at < 2:
+        if not quarters or at < 2:
             return pl.BlockSpec((block, height), lambda g, place: (g, 0))
-        return pl.BlockSpec((block, height), lambda g, place: (g % half, 0))
+        return pl.BlockSpec((block, height), lambda g, place: (0, 0))
 
     grid_spec = pltpu.PrefetchScalarGridSpec(
         num_scalar_prefetch=1,
-        grid=(steps,),
+        grid=(width // block,),
         in_specs=[pl.BlockSpec((rows, depth), lambda g, place: (0, 0))] + [spec(at) for at in range(len(pieces))],
-        out_specs=[
-            pl.BlockSpec((rows, block), lambda g, place: (0, g)),
-            pl.BlockSpec((block, depth), lambda g, place: (g, 0)),
-        ],
+        out_specs=pl.BlockSpec((rows, block), lambda g, place: (0, g)),
+        scratch_shapes=[pltpu.VMEM((block, depth), BF16)],
     )
     return pl.pallas_call(
-        functools.partial(weight_kernel, height, halves),
+        functools.partial(weight_kernel, height, quarters, count),
         grid_spec=grid_spec,
-        out_shape=[jax.ShapeDtypeStruct((rows, width), BF16), jax.ShapeDtypeStruct((width, depth), BF16)],
+        out_shape=jax.ShapeDtypeStruct((rows, width), BF16),
         compiler_params=pltpu.CompilerParams(vmem_limit_bytes=VMEM_LIMIT),
         cost_estimate=COST,
         name=name,
     )(places, x, *pieces)
 
 
-def weight_back_kernel(per, place_ref, g_ref, *rest):
-    piece_refs, (out_ref, w_ref) = rest[:-2], rest[-2:]
+def weight_back_kernel(place_ref, g_ref, *rest):
+    piece_refs, out_ref = rest[:-1], rest[-1]
     for at, piece_ref in enumerate(piece_refs):
 
-        @pl.when(pl.program_id(0) // per == at)
+        @pl.when(pl.program_id(0) == at)
         def _():
-            w_ref[...] = piece_ref[...]
             out_ref[...] = mm_nt(g_ref[...], piece_ref[...])
 
 
 def weight_back_call(g, pieces, places):
     rows, width = g.shape
-    block = 384
-    per = pieces[0].shape[0] // block
-    steps = per * len(pieces)
-    total = steps * block
-    step_of = lambda at: lambda k, place: (jnp.clip(k - at * per, 0, per - 1), 0)
-    target = lambda k, place: place[k // per] * per + k % per
+    block = pieces[0].shape[0]
     grid_spec = pltpu.PrefetchScalarGridSpec(
         num_scalar_prefetch=1,
-        grid=(steps,),
+        grid=(len(pieces),),
         in_specs=[pl.BlockSpec((rows, width), lambda k, place: (0, 0))]
-        + [pl.BlockSpec((block, width), step_of(at)) for at in range(len(pieces))],
-        out_specs=[
-            pl.BlockSpec((rows, block), lambda k, place: (0, target(k, place))),
-            pl.BlockSpec((block, width), lambda k, place: (target(k, place), 0)),
-        ],
+        + [pl.BlockSpec((block, width), lambda k, place: (0, 0))] * len(pieces),
+        out_specs=pl.BlockSpec((rows, block), lambda k, place: (0, place[k])),
     )
     return pl.pallas_call(
-        functools.partial(weight_back_kernel, per),
+        weight_back_kernel,
         grid_spec=grid_spec,
-        out_shape=[jax.ShapeDtypeStruct((rows, total), F32), jax.ShapeDtypeStruct((total, width), BF16)],
+        out_shape=jax.ShapeDtypeStruct((rows, block * len(pieces)), F32),
         compiler_params=pltpu.CompilerParams(vmem_limit_bytes=VMEM_LIMIT),
         cost_estimate=COST,
         name="d_normed_out",
     )(places, g, *pieces)
 
 
-def pick_kernel(parts, table_ref, *rest):
-    ins, outs = rest[: 4 * parts], rest[-3 * parts :]
+def pick_kernel(table_ref, own, other, own_halo, other_halo, own_out, other_out, halo_out):
+    parts, blocks = own_out.shape[:2]
     for part in range(parts):
-        own, other, own_halo, other_halo = ins[4 * part : 4 * part + 4]
-        own_out, other_out, halo_out = outs[3 * part : 3 * part + 3]
-        own_out[...] = own[...]
-        other_out[...] = other[...]
-        halo_out[:, :, :HALO] = own_halo[...]
-        halo_out[:, :, HALO:] = other_halo[...]
-
-
-def pick_call(table, own, other, own_halo, other_halo, after):
+
+        @pl.loop(0, blocks)
+        def _(at):
+            block = table_ref[part, at]
+            own_out[part, at] = own[block]
+            other_out[part, at] = other[block]
+            halo_out[part, at, :, :HALO] = own_halo[block]
+            halo_out[part, at, :, HALO:] = other_halo[block]
+
+
+def pick_call(table, own, other, own_halo, other_halo):
     parts, blocks = table.shape
     _, height, length = own.shape
-    in_specs, out_specs, shapes = [], [], []
-    for part in range(parts):
-        pick = functools.partial(lambda part, g, table_ref: (table_ref[part, g], 0, 0), part)
-        here = lambda g, *_: (g, 0, 0)
-        in_specs += [pl.BlockSpec((1, height, length), pick)] * 2 + [pl.BlockSpec((1, height, HALO), pick)] * 2
-        out_specs += [pl.BlockSpec((1, height, length), here)] * 2 + [pl.BlockSpec((1, height, 2 * HALO), here)]
-        shapes += [jax.ShapeDtypeStruct((blocks, height, length), BF16)] * 2
-        shapes += [jax.ShapeDtypeStruct((blocks, height, 2 * HALO), BF16)]
-    in_specs += [pl.BlockSpec(memory_space=pl.ANY)] * len(after)
+    vmem = pl.BlockSpec(memory_space=pltpu.VMEM)
     made = pl.pallas_call(
-        functools.partial(pick_kernel, parts),
-        grid_spec=pltpu.PrefetchScalarGridSpec(num_scalar_prefetch=1, grid=(blocks,), in_specs=in_specs, out_specs=out_specs),
-        out_shape=shapes,
+        pick_kernel,
+        in_specs=[pl.BlockSpec(memory_space=pltpu.SMEM)] + [vmem] * 4,
+        out_specs=[vmem] * 3,
+        out_shape=[jax.ShapeDtypeStruct((parts, blocks, height, length), BF16)] * 2
+        + [jax.ShapeDtypeStruct((parts, blocks, height, 2 * HALO), BF16)],
         compiler_params=pltpu.CompilerParams(vmem_limit_bytes=VMEM_LIMIT),
         cost_estimate=COST,
         name="pick_rows",
-    )(table, *([own, other, own_halo, other_halo] * parts), *after)
-    return [[array.reshape(blocks * height, -1) for array in made[3 * part : 3 * part + 3]] for part in range(parts)]
+    )(table, own, other, own_halo, other_halo)
+    return [array.reshape(parts, blocks * height, -1) for array in made]
 
 
 def grad_kernel(halo, *refs):
-    kept_ref, sent_ref = refs[-2:]
+    outs = refs[-6:]
+    own, other = refs[0][0], refs[1][0]
     if halo:
-        own, other, edge, right, right_other, edge_right, edge_other = refs[:7]
+        edge, right, right_other, edge_right, edge_other = refs[2][0], refs[3], refs[4], refs[5], refs[6]
     else:
-        own, other, right, right_other = refs[:4]
-    total = mm(own[...], right[...]) + mm(other[...], right_other[...])
+        right, right_other = refs[2], refs[3]
+    total = mm(own, right[...]) + mm(other, right_other[...])
     if halo:
-        total = total + mm(edge[...], jnp.concatenate([edge_right[...], edge_other[...]], axis=0))
+        total = total + mm(edge, jnp.concatenate([edge_right[...], edge_other[...]], axis=0))
     half = total.shape[0] // 2
-    kept_ref[...] = total[:half].astype(BF16)
-    sent_ref[...] = total[half:].astype(BF16)
-
-
-def grad_call(left, right, right_other, first, width, block, halo, name, after):
-    own, other, edge = left
-    rows, length = own.shape
-    whole = lambda g: (0, 0)
-    column = lambda g: (0, first // block + g)
-    below = lambda g: (length // HALO, first // block + g)
-    specs = [pl.BlockSpec((rows, length), whole)] * 2
+    for part in range(3):
+
+        @pl.when(pl.program_id(0) == part)
+        def _():
+            outs[2 * part][...] = total[:half].astype(BF16)
+            outs[2 * part + 1][...] = total[half:].astype(BF16)
+
+
+def grad_call(lefts, right, right_other, width, halo, name):
+    own, other, edge = lefts
+    _, rows, length = own.shape
+    lead = lambda g: (g, 0, 0)
+    column = lambda g: (0, g)
+    below = lambda g: (length // HALO, g)
+    specs = [pl.BlockSpec((1, rows, length), lead)] * 2
     args = [own, other]
     if halo:
-        specs.append(pl.BlockSpec((rows, 2 * HALO), whole))
+        specs.append(pl.BlockSpec((1, rows, 2 * HALO), lead))
         args.append(edge)
-    specs += [pl.BlockSpec((length, block), column)] * 2
+    specs += [pl.BlockSpec((length, width), column)] * 2
     args += [right, right_other]
     if halo:
-        specs += [pl.BlockSpec((HALO, block), below)] * 2
+        specs += [pl.BlockSpec((HALO, width), below)] * 2
         args += [right, right_other]
-    specs += [pl.BlockSpec(memory_space=pl.ANY)] * len(after)
-    args += list(after)
-    return pl.pallas_call(
+    made = pl.pallas_call(
         functools.partial(grad_kernel, halo),
-        grid=(width // block,),
+        grid=(3,),
         in_specs=specs,
-        out_specs=[pl.BlockSpec((rows // 2, block), lambda g: (0, g))] * 2,
-        out_shape=[jax.ShapeDtypeStruct((rows // 2, width), BF16)] * 2,
+        out_specs=[pl.BlockSpec((rows // 2, width), lambda g: (0, 0))] * 6,
+        out_shape=[jax.ShapeDtypeStruct((rows // 2, width), BF16)] * 6,
         compiler_params=pltpu.CompilerParams(vmem_limit_bytes=VMEM_LIMIT),
         cost_estimate=COST,
         name=name,
     )(*args)
-
-
-def fold_kernel(parts, groups, last, *refs):
-    ins, outs = refs[: 2 * parts * groups], refs[-(1 if last else 2 * parts) :]
+    return [(made[2 * part], made[2 * part + 1]) for part in range(3)]
+
+
+def fold_kernel(parts, groups, which, *refs):
+    ins, outs = refs[: 2 * parts * groups], refs[2 * parts * groups :]
     for part in range(parts):
         at = 0
         for group in range(groups):
             kept, got = ins[2 * (part * groups + group)], ins[2 * (part * groups + group) + 1]
-            width = kept.shape[1]
-            total = kept[...].astype(F32) + got[...].astype(F32)
-            if last:
+            rows, width = kept.shape
+            half = rows // 2
+            lines = slice(0, rows) if which == "last" else slice(0, half) if which == "kept" else slice(half, rows)
+            total = kept[lines, :].astype(F32) + got[lines, :].astype(F32)
+            if which == "last":
                 gate = INNER // parts
                 other = width - gate
                 outs[0][:, part * gate : (part + 1) * gate] = total[:, :gate]
@@ -802,120 +796,193 @@
                 end = min(begin + other, outs[0].shape[1])
                 outs[0][:, begin:end] = total[:, gate : gate + end - begin]
             else:
-                half = total.shape[0] // 2
-                outs[2 * part][:, at : at + width] = total[:half].astype(BF16)
-                outs[2 * part + 1][:, at : at + width] = total[half:].astype(BF16)
+                outs[part][:, at : at + width] = total.astype(BF16)
             at += width
 
 
-def fold_call(pairs, width, after=()):
+def fold_call(pairs, which, width=0):
     parts, groups = len(pairs), len(pairs[0])
     arrays = [array for part in pairs for pair in part for array in pair]
-    vmem = pl.BlockSpec(memory_space=pltpu.VMEM)
     rows = arrays[0].shape[0]
-    if width:
+    half = rows // 2
+    if which == "last":
         shapes = [jax.ShapeDtypeStruct((rows, width), F32)]
     else:
-        shapes = []
-        for part in pairs:
-            total = sum(kept.shape[1] for kept, _ in part)
-            shapes += [jax.ShapeDtypeStruct((rows // 2, total), BF16)] * 2
-    made = pl.pallas_call(
-        functools.partial(fold_kernel, parts, groups, bool(width)),
-        in_specs=[vmem] * len(arrays) + [pl.BlockSpec(memory_space=pl.ANY)] * len(after),
+        shapes = [jax.ShapeDtypeStruct((half, sum(kept.shape[1] for kept, _ in part)), BF16) for part in pairs]
+    vmem = pl.BlockSpec(memory_space=pltpu.VMEM)
+    return pl.pallas_call(
+        functools.partial(fold_kernel, parts, groups, which),
+        in_specs=[vmem] * len(arrays),
         out_specs=[vmem] * len(shapes),
         out_shape=shapes,
         compiler_params=pltpu.CompilerParams(vmem_limit_bytes=VMEM_LIMIT),
         cost_estimate=COST,
-        name="fold",
-    )(*arrays, *after)
-    return made[0] if width else [(made[2 * part], made[2 * part + 1]) for part in range(parts)]
-
-
-def residual_kernel(x_ref, w_ref, tokens_ref, *rest):
-    out_ref = rest[-1]
-    out_ref[0] = tokens_ref[0].astype(F32) + mm(x_ref[...], w_ref[...])
-
-
-def residual_call(x, w, tokens, after=()):
-    rows, depth = x.shape
-    width = w.shape[1]
-    block = 256
-    whole = pl.BlockSpec((1, rows, block), lambda g: (0, 0, g))
+        name="fold_" + which,
+    )(*arrays)
+
+
+def residual_kernel(place_ref, *refs):
+    count = len(refs) // 2 - 1
+    total = refs[2 * count][0].astype(F32)
+    for at in range(count):
+        total = total + mm(refs[at][...], refs[count + at][...])
+    refs[-1][0] = total
+
+
+def residual_call(x, pieces, places, tokens, after):
+    rows = x.shape[0]
+    height, width = pieces[0].shape
+    block = 768
+    part = lambda at: pl.BlockSpec((rows, height), lambda g, place: (0, place[at]))
+    whole = pl.BlockSpec((1, rows, block), lambda g, place: (0, 0, g))
+    grid_spec = pltpu.PrefetchScalarGridSpec(
+        num_scalar_prefetch=1,
+        grid=(width // block,),
+        in_specs=[part(at) for at in range(len(pieces))]
+        + [pl.BlockSpec((height, block), lambda g, place: (0, g))] * len(pieces)
+        + [whole],
+        out_specs=whole,
+    )
     return pl.pallas_call(
         residual_kernel,
-        grid=(width // block,),
-        in_specs=[pl.BlockSpec((rows, depth), lambda g: (0, 0)), pl.BlockSpec((depth, block), lambda g: (0, g)), whole]
-        + [pl.BlockSpec(memory_space=pl.ANY)] * len(after),
-        out_specs=whole,
+        grid_spec=grid_spec,
         out_shape=jax.ShapeDtypeStruct((1, rows, width), F32),
         compiler_params=pltpu.CompilerParams(vmem_limit_bytes=VMEM_LIMIT),
+        cost_estimate=LONG,
+        name="block_out",
+    )(tie(places, after), *([x] * len(pieces)), *pieces, tokens)
+
+
+def columns_kernel(count, place_ref, g_ref, *refs):
+    w_refs, (out_ref, w) = refs[:count], refs[-2:]
+    height = D // count
+    for at in range(count):
+        w[:, pl.ds(pl.multiple_of(place_ref[at] * height, 128), height)] = w_refs[at][...]
+    product = mm(g_ref[...], w[...])
+
+    @pl.when(pl.program_id(0) == 0)
+    def _():
+        out_ref[...] = product
+
+    @pl.when(pl.program_id(0) > 0)
+    def _():
+        out_ref[...] += product
+
+
+def columns_call(g, pieces, places):
+    length, depth = g.shape
+    height = pieces[0].shape[1]
+    count = len(pieces)
+    block = depth // 2
+    down = lambda k, place: (k, 0)
+    grid_spec = pltpu.PrefetchScalarGridSpec(
+        num_scalar_prefetch=1,
+        grid=(depth // block,),
+        in_specs=[pl.BlockSpec((length, block), lambda k, place: (0, k))] + [pl.BlockSpec((block, height), down)] * count,
+        out_specs=pl.BlockSpec((length, D), lambda k, place: (0, 0)),
+        scratch_shapes=[pltpu.VMEM((block, D), BF16)],
+    )
+    return pl.pallas_call(
+        functools.partial(columns_kernel, count),
+        grid_spec=grid_spec,
+        out_shape=jax.ShapeDtypeStruct((length, D), F32),
+        compiler_params=pltpu.CompilerParams(vmem_limit_bytes=VMEM_LIMIT),
         cost_estimate=COST,
-        name="block_out",
-    )(x, w, tokens, *after)
-
-
-def tokens_kernel(dg_ref, dv_ref, spill_ref, wg_ref, wv_ref, tokens_ref, cotan_ref, gain_ref, *rest):
-    out_ref, dgain_ref, fixed, d_normed, inverse = rest[-5:]
-    length = dg_ref.shape[0]
-    block = wg_ref.shape[1]
-    grid = pl.program_id(0)
-
-    @pl.when(grid == 0)
-    def _():
-        fixed[...] = dv_ref[...]
-        ends = dv_ref[length - HALO :, :].astype(F32) + spill_ref[...].astype(F32)
-        fixed[length - HALO :, :] = ends.astype(BF16)
+        name="d_normed_gate",
+    )(places, g, *pieces)
+
+
+def tokens_kernel(count, quarters, place_ref, *refs):
+    part_ref, dv_ref, spill_ref, tokens_ref, cotan_ref, gain_ref = refs[:6]
+    wv_refs = refs[6:-6]
+    out_ref, dgain_ref, fixed, wv, total, inverse = refs[-6:]
+    length = dv_ref.shape[0]
+    height = D // count
+    step, steps = pl.program_id(0), pl.num_programs(0)
+
+    @pl.when(step == 0)
+    def _():
         for start in range(0, length, CHUNK):
             part = slice(start, start + CHUNK)
             values = tokens_ref[0, part, :].astype(F32)
             mean = jnp.sum(values * values, axis=1, keepdims=True) * (1.0 / D)
             inverse[part, :] = jnp.broadcast_to(lax.rsqrt(mean + EPSILON), (CHUNK, 128))
 
-    lanes = pl.ds(pl.multiple_of(grid * block, block), block)
-    total = mm(dg_ref[...], wg_ref[...]) + mm(fixed[...], wv_ref[...])
-    d_normed[:, lanes] = total
-    scaled = jnp.concatenate([inverse[...]] * (block // 128), axis=1) * tokens_ref[0, :, lanes].astype(F32)
-    dgain_ref[...] = jnp.sum(total * scaled, axis=0, keepdims=True)
-
-    @pl.when(grid == pl.num_programs(0) - 1)
-    def _():
+    fixed[...] = dv_ref[...]
+    ends = dv_ref[length - HALO :, :].astype(F32) + spill_ref[...].astype(F32)
+    fixed[length - HALO :, :] = ends.astype(BF16)
+
+    def put(at, ref):
+        wv[:, pl.ds(pl.multiple_of(place_ref[at] * height, 128), height)] = ref[...]
+
+    for at in range(2 if quarters else count):
+        put(at, wv_refs[at])
+    if quarters:
+        put_quarters(place_ref, count, step, wv_refs, put)
+    product = mm(fixed[...], wv[...])
+
+    @pl.when(step == 0)
+    def _():
+        total[...] = part_ref[...] + product
+
+    @pl.when(step > 0)
+    def _():
+        total[...] += product
+
+    @pl.when(step == steps - 1)
+    def _():
+        sums = jnp.zeros((8, D), F32)
         for start in range(0, length, CHUNK):
             part = slice(start, start + CHUNK)
             values = tokens_ref[0, part, :].astype(F32)
-            a = d_normed[part, :] * gain_ref[...]
+            grad = total[part, :]
+            a = grad * gain_ref[...]
             inv = inverse[part, 0:1]
+            sums = sums + fold_rows(grad * values * inv)
             shift = inv * inv * inv * (jnp.sum(a * values, axis=1, keepdims=True) * (1.0 / D))
             out_ref[0, part, :] = cotan_ref[0, part, :].astype(F32) + inv * a - values * shift
-
-
-def tokens_call(d_gate, d_v, spill, w_g, w_v, tokens, cotangent, gain, after):
-    length = d_gate.shape[0]
-    block = 256
-    wide = w_v.shape[0]
-    whole = lambda g: (0, 0)
-    all_rows = pl.BlockSpec((1, length, D), lambda g: (0, 0, 0))
-    return pl.pallas_call(
-        tokens_kernel,
-        grid=(D // block,),
+        dgain_ref[...] = jnp.sum(sums, axis=0, keepdims=True)
+
+
+def tokens_call(part, d_v, spill, pieces, places, quarters, tokens, cotangent, gain):
+    length = part.shape[0]
+    height = pieces[0].shape[1]
+    wide = d_v.shape[1]
+    steps = 4
+    block = wide // steps
+    count = D // height
+    whole = lambda k, place: (0, 0)
+    column = lambda k, place: (0, k)
+    down = lambda k, place: (k, 0)
+    all_rows = pl.BlockSpec((1, length, D), lambda k, place: (0, 0, 0))
+    grid_spec = pltpu.PrefetchScalarGridSpec(
+        num_scalar_prefetch=1,
+        grid=(steps,),
         in_specs=[
-            pl.BlockSpec((length, INNER), whole),
-            pl.BlockSpec((length, wide), whole),
-            pl.BlockSpec((HALO, wide), whole),
-            pl.BlockSpec((INNER, block), lambda g: (0, g)),
-            pl.BlockSpec((wide, block), lambda g: (0, g)),
+            pl.BlockSpec((length, D), whole),
+            pl.BlockSpec((length, block), column),
+            pl.BlockSpec((HALO, block), column),
             all_rows,
             all_rows,
             pl.BlockSpec((1, D), whole),
         ]
-        + [pl.BlockSpec(memory_space=pl.ANY)] * len(after),
-        out_specs=[all_rows, pl.BlockSpec((1, block), lambda g: (0, g))],
+        + [pl.BlockSpec((block, height), whole if quarters and at >= 2 else down) for at in range(len(pieces))],
+        out_specs=[all_rows, pl.BlockSpec((1, D), whole)],
+        scratch_shapes=[
+            pltpu.VMEM((length, block), BF16),
+            pltpu.VMEM((block, D), BF16),
+            pltpu.VMEM((length, D), F32),
+            pltpu.VMEM((length, 128), F32),
+        ],
+    )
+    return pl.pallas_call(
+        functools.partial(tokens_kernel, count, quarters),
+        grid_spec=grid_spec,
         out_shape=[jax.ShapeDtypeStruct((1, length, D), F32), jax.ShapeDtypeStruct((1, D), F32)],
-        scratch_shapes=[pltpu.VMEM((length, wide), BF16), pltpu.VMEM((length, D), F32), pltpu.VMEM((length, 128), F32)],
         compiler_params=pltpu.CompilerParams(vmem_limit_bytes=VMEM_LIMIT),
         cost_estimate=COST,
         name="d_tokens",
-    )(d_gate, d_v, spill, w_g, w_v, tokens, cotangent, gain, *after)
+    )(places, part, d_v, spill, tokens, cotangent, gain, *pieces)
 
 
 def on_device(
@@ -949,11 +1016,6 @@
     def across(value):
         return move(value, lambda s, f: (s, f ^ 1))
 
-    def tie(value, *others):
-        if others:
-            value = lax.optimization_barrier((value,) + others)[0]
-        return value
-
     def gather(value, crossed, middle, near):
         pieces = [(value, 0), (crossed, 1)] + near
         pieces += [(across(tie(piece, middle)), step ^ 1) for piece, step in near]
@@ -962,27 +1024,31 @@
     def send_near(value):
         return [(move(value, lambda s, f: (s, f ^ step)), step) for step in range(2, shards, 2)]
 
-    def gather_halves(value, crossed, middle):
-        height = value.shape[0]
+    def gather_quarters(value, crossed, middle):
+        quarter = value.shape[0] // 4
         side = rank & 1
-        half = lax.dynamic_slice_in_dim(value, side * (height // 2), height // 2, 0)
-        pairs = []
+        remote = []
         for step in range(2, shards, 2):
-            near = move(half, lambda s, f: (s, f ^ step))
-            far = move(tie(near, *middle), lambda s, f: (s ^ 1, f))
-            pairs += [(near, step), (far, step)]
-        pieces = [(value, 0), (crossed, 1)] + pairs + [(across(piece), step ^ 1) for piece, step in pairs]
-        places = [shard ^ step for _, step in pieces] + [side]
-        return [piece for piece, _ in pieces], jnp.stack(places).astype(jnp.int32)
-
-    def in_order(pieces, places, halves):
+            near, far = [], []
+            for part in range(2):
+                sent = lax.dynamic_slice_in_dim(value, (2 * side + part) * quarter, quarter, 0)
+                near.append(move(tie(sent, *near), lambda s, f: (s, f ^ step)))
+                far.append(move(near[part], lambda s, f: (s ^ 1, f)))
+            remote.append((near + far, step))
+        remote += [([across(piece) for piece in pieces[:-1]] + [across(tie(pieces[-1], *middle))], step ^ 1) for pieces, step in remote]
+        places = [shard, shard ^ 1] + [shard ^ step for _, step in remote] + [side]
+        return [value, crossed] + sum([pieces for pieces, _ in remote], []), jnp.stack(places).astype(jnp.int32)
+
+    def in_order(pieces, places, quarters):
         height = pieces[0].shape[1]
         whole = jnp.zeros((pieces[0].shape[0], height * shards), pieces[0].dtype)
         for at, piece in enumerate(pieces):
-            first = 0
-            if halves and at >= 2:
-                first = (places[-1] if at % 2 == 0 else 1 - places[-1]) * piece.shape[0]
-            whole = lax.dynamic_update_slice(whole, piece, (first, places[at] * height))
+            first, place = 0, at
+            if quarters and at >= 2:
+                place, index = 2 + (at - 2) // 4, (at - 2) % 4
+                side = places[shards] if index < 2 else 1 - places[shards]
+                first = (2 * side + index % 2) * piece.shape[0]
+            whole = lax.dynamic_update_slice(whole, piece, (first, places[place] * height))
         return [whole], jnp.zeros((1,), jnp.int32)
 
     def exchange(states):
@@ -1025,27 +1091,24 @@
 
     own, other = halves(normed.T)
     own_halo, other_halo = halves(normed_long[:HALO].T)
-    lefts = pick_call(table, own, across(other), own_halo, across(other_halo), [])
+    lefts = pick_call(table, own, across(other), own_halo, across(other_halo))
     own_g = turned[:INNER]
     crossed_v, crossed_g, crossed_o = across(own_v), across(own_g), across(w_out)
-    pieces_v, places_v = gather_halves(own_v, crossed_v, (lefts[0][0], crossed_v, crossed_g, crossed_o))
+    pieces_v, places_v = gather_quarters(own_v, crossed_v, (lefts[0], crossed_v, crossed_g, crossed_o))
 
     def flip(axis, bit):
         return lambda s, f: (s ^ bit, f) if axis == "seq" else (s, f ^ bit)
 
-    def first_terms(right, width, block, halo, name, *ahead):
-        right_other = tie(across(right), *ahead)
-        return [grad_call(lefts[part], right, right_other, part * width, width, block, halo, name, ()) for part in range(3)]
-
     def first_step(terms, *ahead):
         return [(kept, move(tie(sent, *ahead), flip(*orders[part][0]))) for part, (kept, sent) in enumerate(terms)]
 
     lanes_whole = w_in.shape[0] % 128 == 0
-    if lanes_whole:
-        projected, w_v = weight_call(normed_long, pieces_v, places_v, width_v, width_v // 4, True, "project_v")
-    else:
-        projected, w_v = weight_call(normed_long, *in_order(pieces_v, places_v, True), width_v, width_v // 4, False, "project_v")
-    near_g = send_near(tie(own_g, pieces_v[2]))
+    last_near, first_far, count = pieces_v[3], pieces_v[4], shards
+    if not lanes_whole:
+        pieces_v, places_v = in_order(pieces_v, places_v, True)
+        count = 1
+    projected = weight_call(normed_long, pieces_v, places_v, count, width_v, width_v // 4, lanes_whole, "project_v")
+    near_g = send_near(tie(own_g, last_near, first_far))
     pieces_g, places = gather(own_g, crossed_g, projected, near_g)
     near_o = send_near(tie(w_out, near_g[0][0], projected))
     lanes = lambda vec: jnp.pad(vec, (0, 128 - HEADS)).reshape(1, 128)
@@ -1058,31 +1121,37 @@
     carried, totals = carry_call(ranks, exchange(states), None, [y_inside])
     s_in = exchange(carried)
     pieces_o, _ = gather(w_out, crossed_o, carried, near_o)
-    gate_pieces = (pieces_g, places) if lanes_whole else in_order(pieces_g, places, False)
-    gate_in, w_g = weight_call(normed, *gate_pieces, INNER, 768, False, "project_gate")
-    d_normed_out, w_o = weight_back_call(cotan, pieces_o, places)
+    places_o = places
+    if not lanes_whole:
+        pieces_g, places = in_order(pieces_g, places, False)
+    gate_in = weight_call(normed, pieces_g, places, count, INNER, INNER // 3, False, "project_gate")
+    d_normed_out = weight_back_call(cotan, pieces_o, places_o)
     made = gate_call(y_inside, gate_in, d_normed_out, c_act, c_turned, ecd, out_gain.reshape(1, INNER), s_in)
     normed_out, d_gate, d_mixed, d_gain_out, states = made
     d_w_out = lax.dot_general(normed_out, cotan, TN, preferred_element_type=F32).astype(BF16)
     d_w_out_sum = lax.psum_scatter(d_w_out, both, scatter_dimension=0, tiled=True).astype(F32)
-    block_out = residual_call(normed_out, w_o, tokens, [states])
-    gate_terms = first_terms(d_gate, INNER // 3, 512, False, "d_w_gate")
-    (carried,) = carry_call(ranks, exchange(states), totals, [d_w_out, block_out])
+    gate_terms = grad_call(lefts, d_gate, across(d_gate), INNER // 3, False, "d_w_gate")
+    (carried,) = carry_call(ranks, exchange(states), totals, [d_w_out] + [kept for kept, _ in gate_terms])
+    block_out = residual_call(normed_out, pieces_o, places_o, tokens, carried)
     r_in = exchange(carried)
     gate_parts = first_step(gate_terms, r_in)
     d_v_long, sums, heads = back_call(
-        x_act, d_mixed, slope, v, conv_weight, b_act, c_act, b_turned, c_turned, rows, skip_wide, s_in, r_in, ()
+        x_act, d_mixed, slope, v, conv_weight, b_act, c_act, b_turned, c_turned, rows, skip_wide, s_in, r_in, [block_out]
     )
     d_v_long = tie(d_v_long, *[got for _, got in gate_parts])
     spill = move(d_v_long[tokens.shape[1] :], lambda s, f: (s - 1, f) if s > 0 else None)
-    rest_parts = first_step(first_terms(d_v_long, (CONV + 128) // 3, 384, True, "d_w_rest", spill))
+    part = columns_call(tie(d_gate, d_v_long), pieces_g, places)
+    d_v_other = tie(across(d_v_long), spill, part)
+    rest_terms = grad_call(lefts, d_v_long, d_v_other, (CONV + 128) // 3, True, "d_w_rest")
+    rest_parts = first_step(rest_terms)
     d_tokens, d_norm_gain = tokens_call(
-        d_gate, d_v_long, spill, w_g, w_v, tokens, cotangent, norm_gain.reshape(1, D), [kept for kept, _ in rest_parts]
+        part, tie(d_v_long, rest_terms[0][0]), spill, pieces_v, places_v, lanes_whole,
+        tokens, cotangent, norm_gain.reshape(1, D),
     )
+    rest_parts = [(kept, tie(got, d_tokens)) for kept, got in rest_parts]
 
     d_skip = sums[KW + 1, :INNER].reshape(HEADS, HEAD_DIM).sum(axis=1)
     pieces = [
-        d_norm_gain.reshape(-1),
         sums[:KW].reshape(-1),
         sums[KW],
         heads[:, 0:4, 0].reshape(-1),
@@ -1097,18 +1166,31 @@
     small_bits = seq_bits[:1] + chip_bits + seq_bits[1:]
     flat = flat + move(flat, flip(*small_bits[0]))
 
+    def four(value, first, second):
+        parts = [move(value, flip(*first)), move(value, flip(*second))]
+        corner = lambda s, f: flip(*first)(*flip(*second)(s, f))
+        return (value + parts[0]) + (parts[1] + move(value, corner))
+
+    all_bits = [("fsdp", 1)] + small_bits
     pairs = [[gate_parts[part], rest_parts[part]] for part in range(3)]
     for at in range(1, len(orders[0])):
-        halves_now = fold_call(pairs, 0, [flat])
-        pairs = [[(kept, move(sent, flip(*orders[part][at])))] for part, (kept, sent) in enumerate(halves_now)]
-        flat = flat + move(tie(flat, halves_now[0][0]), flip(*small_bits[at]))
-    d_w_in = fold_call(pairs, w_in.shape[1], [flat])
+        sent = fold_call(pairs, "sent")
+        kept = fold_call(pairs, "kept")
+        pairs = [[(kept[part], move(sent[part], flip(*orders[part][at])))] for part in range(3)]
+        flat = flat + move(tie(flat, kept[0]), flip(*small_bits[at]))
+        use = all_bits[2 * at - 2 : 2 * at]
+        if len(use) == 2:
+            d_norm_gain = four(tie(d_norm_gain, kept[0]), *use)
+        elif use:
+            d_norm_gain = d_norm_gain + move(tie(d_norm_gain, kept[0]), flip(*use[0]))
+    (d_w_in,) = fold_call(pairs, "last", w_in.shape[1])
     flat = flat.reshape(-1)
     small, at = [], 0
     for piece in pieces:
         small.append(flat[at : at + piece.shape[0]])
         at += piece.shape[0]
-    d_norm_gain, d_conv_weight, d_conv_bias, d_dt_bias, d_a_log, d_skip, d_gain_out = small
+    d_norm_gain = d_norm_gain.reshape(-1)
+    d_conv_weight, d_conv_bias, d_dt_bias, d_a_log, d_skip, d_gain_out = small
     return (
         block_out,
         d_tokens,

time: 520 us -> 490 us (0.942); the launches traced: 520 us -> 480 us
  waiting for transfers between devices: 149 us -> 95.3 us
  local copies, waits for them, and re-layouts: 33.4 us -> 43.2 us
    all_to_all x4, waiting for transfers between devices: 42.6 us -> 13.4 us  [exchange(): lax.all_to_all(states, 'seq', split_axis=0, concat_axis=0, tiled=True)]
    ppermute x37 -> x48, waiting for transfers between devices: 107 us -> 81.9 us  [move(): return lax.ppermute(value, both, pairs)]
    ppermute x37 -> x48, starting transfers between devices: 34.2 us -> 46.2 us  [move(): return lax.ppermute(value, both, pairs)]
    all_to_all x4, starting transfers between devices: 30.7 us -> 21.4 us  [exchange(): lax.all_to_all(states, 'seq', split_axis=0, concat_axis=0, tiled=True)]
    unnamed x64 -> x74, local copies, waits for them, and re-layouts: 9.13 us -> 11.7 us
  transfers between devices with their start and end apart: 42 -> 53, of which waited for: 19 -> 23; matrix products, arithmetic and copies ran while one was open for 6% -> 10% of each run, Pallas kernels for 43% -> 47%
where the time goes in v3:
time: 490 us; the launch traced here: 480 us
  Pallas kernels  241 us (49%)
  waiting for transfers between devices  95.3 us (19%)
  starting transfers between devices  68.1 us (14%)
  local copies, waits for them, and re-layouts  43.2 us (9%)
  between operations  14.8 us (3%)
  matrix products  9.69 us (2%)
  other arithmetic  7.56 us (2%)
    ppermute x48, waiting for transfers between devices, move(): return lax.ppermute(value, both, pairs)  81.9 us
    pallas_call x1, Pallas kernels, back_call(): pl.pallas_call(back_kernel, grid=(QUADS + 2,), in_specs=[pl.BlockSpec((le...  52.4 us
    ppermute x48, starting transfers between devices, move(): return lax.ppermute(value, both, pairs)  46.2 us
    pallas_call x7, Pallas kernels, fold_call(): pl.pallas_call(functools.partial(fold_kernel, parts, groups, which), in_s...  25.7 us
    pallas_call x2, Pallas kernels, weight_call(): pl.pallas_call(functools.partial(weight_kernel, height, quarters, count),...  24.7 us
    pallas_call x2, Pallas kernels, grad_call(): pl.pallas_call(functools.partial(grad_kernel, halo), grid=(3,), in_specs=...  23.5 us
    all_to_all x4, starting transfers between devices, exchange(): lax.all_to_all(states, 'seq', split_axis=0, concat_axis=0, tiled=True)  21.4 us
    pallas_call x1, Pallas kernels, tokens_call(): pl.pallas_call(functools.partial(tokens_kernel, count, quarters), grid_sp...  19.5 us
  transfers between devices with their start and end apart: 53, of which 23 were waited for; matrix products, arithmetic and copies ran while one was open for 10% of the time, Pallas kernels for 47%

profile of v3, /device:TPU:0, one launch (start us, length us, event | category | flops | bytes accessed | tf_op | source)
XLA Modules:
  0.0 480.1 jit_solution(39121842431429317)
XLA Ops:
  8.0 4.8 %collective-permute-start = (bf16[16,1536]{1,0:T(8,128)(2,1)S(1)}, bf16[16,1536]{1,0:T(8,128)(2,1)S(1)}, u32[]{:S(2)}, u32[]{:S(2)}) collective-permute-start(bf16[16,1536]{1,0:T(8,128)(2,1)S(1)} %slice_bitcast_fusion.1), channel_id=1, source_target_pairs={{0,4},{1,5},{2,6},{3,7},{4,8},{5,9},{6,10},{7,11},{8,12},{9,13},{1... | collective-permute-start | bytes 147464 | tf_op jit(solution)/shard_map/ppermute | solution.py:1014
  20.4 4.2 slice.76.rest_0_.refs_0_
  28.8 5.0 %collective-permute-done.2.rest_2_.refs_8_ = bf16[896,384]{1,0:T(8,128)(2,1)S(1)} collective-permute-done((bf16[896,384]{1,0:T(8,128)(2,1)}, bf16[896,384]{1,0:T(8,128)(2,1)S(1)}, u32[]{:S(2)}, u32[]{:S(2)}) %collective-permute-start.2) | collective-permute-done | bytes 688160 | tf_op jit(solution)/shard_map/ppermute | solution.py:1014
  37.8 3.3 fusion.5
  41.1 9.1 %collective-permute-done.3.rest_3_.refs_9_ = bf16[896,384]{1,0:T(8,128)(2,1)} collective-permute-done((bf16[896,384]{1,0:T(8,128)(2,1)}, bf16[896,384]{1,0:T(8,128)(2,1)}, u32[]{:S(2)}, u32[]{:S(2)}) %collective-permute-start.3) | collective-permute-done | bytes 688160 | tf_op jit(solution)/shard_map/ppermute | solution.py:1014
  52.7 2.6 copy.26
  57.0 2.4 dynamic-slice_bitcast_fusion
  66.1 7.5 %pick_rows.1 = (bf16[3,16,48,512]{3,2,1,0:T(8,128)(2,1)}, bf16[3,16,48,512]{3,2,1,0:T(8,128)(2,1)}, bf16[3,16,48,32]{3,2,1,0:T(8,128)(2,1)}) custom-call(s32[3,16]{1,0:T(4,128)} %pad_add_fusion.table_ref, bf16[16,48,512]{2,1,0:T(8,128)(2,1)} %get-tuple-element.174.own, bf16[16,48,512]{2,1,0:T(8,128)(2,1)} %collective-permute-done.9.other, ...), custom_call_target="tpu_custom_call" | custom-call | flops 1000000 | bytes 1000000 | tf_op jit(solution)/shard_map/pick_rows/pallas_call | solution.py:720
  73.6 6.3 %collective-permute-done.5.rest_5_.refs_11_ = bf16[896,384]{1,0:T(8,128)(2,1)} collective-permute-done((bf16[896,384]{1,0:T(8,128)(2,1)}, bf16[896,384]{1,0:T(8,128)(2,1)}, u32[]{:S(2)}, u32[]{:S(2)}) %collective-permute-start.5) | collective-permute-done | bytes 688160 | tf_op jit(solution)/shard_map/ppermute | solution.py:1014
  86.2 13.8 %project_v.1.dt_ref.v_ref = bf16[528,3584]{1,0:T(8,128)(2,1)} custom-call(s32[5]{0:T(128)} %stack.140.place_ref, bf16[528,1536]{1,0:T(8,128)(2,1)} %copy-done.3, bf16[3584,384]{1,0:T(8,128)(2,1)} %copy-done, bf16[3584,384]{1,0:T(8,128)(2,1)} %collective-permute-done.1.rest_1_.refs_7_, bf16[896,384]{1,0:T(8,128)(2,1)} %copy-done.15, ...), custom_call_target="tpu_custom_call" | custom-call | flops 1000000 | bytes 1000000 | tf_op jit(solution)/shard_map/project_v/pallas_call | solution.py:664
  104.0 2.6 steps.1
  106.6 14.2 %conv_states.1 = (bf16[512,3072]{1,0:T(8,128)(2,1)}, bf16[512,3328]{1,0:T(8,128)(2,1)}, bf16[512,128]{1,0:T(8,128)(2,1)}, bf16[512,128]{1,0:T(8,128)(2,1)}, bf16...) custom-call(bf16[528,3584]{1,0:T(8,128)(2,1)} %project_v.1.dt_ref.v_ref, ...), custom_call_target="tpu_custom_call" | custom-call | flops 1000000 | bytes 1000000 | tf_op jit(solution)/shard_map/conv_states/pallas_call | solution.py:192
  120.8 4.9 %all-to-all-start = ((bf16[8,16,3328]{2,1,0:T(8,128)(2,1)}), bf16[8,16,3328]{2,1,0:T(8,128)(2,1)S(1)}, u32[]{:S(2)}, u32[]{:S(2)}) async-start(bf16[8,16,3328]{2,1,0:T(8,128)(2,1)} %bitcast.90), calls=%async_computation | async-start | bytes 1703936 | tf_op jit(solution)/shard_map/all_to_all | solution.py:1055
  126.4 15.4 %ssd_inside.1.rest_0_.y_ref = f32[512,3072]{1,0:T(8,128)} custom-call(bf16[512,3072]{1,0:T(8,128)(2,1)} %get-tuple-element.94.x_ref, bf16[512,128]{1,0:T(8,128)(2,1)} %get-tuple-element.95.b_ref, bf16[512,128]{1,0:T(8,128)(2,1)} %get-tuple-element.96.c_ref, bf16[128,512]{1,0:T(8,128)(2,1)} %get-tuple-element.97.bt_ref, ...), custom_call_target="tpu_custom_call" | custom-call | flops 1000000 | bytes 1000000 | tf_op jit(solution)/shard_map/ssd_inside/pallas_call | solution.py:308
  141.9 4.3 all-to-all-done
  147.1 2.6 carry.1
  149.7 4.0 collective-permute-done.16.rest_2_.refs_6_
  153.7 5.1 %all-to-all-start.1 = ((bf16[8,16,3072]{2,1,0:T(8,128)(2,1)}), bf16[8,16,3072]{2,1,0:T(8,128)(2,1)S(1)}, u32[]{:S(2)}, u32[]{:S(2)}) async-start(bf16[8,16,3072]{2,1,0:T(8,128)(2,1)} %bitcast.93), calls=%async_computation.1 | async-start | bytes 1572864 | tf_op jit(solution)/shard_map/all_to_all | solution.py:1055
  160.9 11.0 %project_gate.1.gate_ref = bf16[512,3072]{1,0:T(8,128)(2,1)} custom-call(s32[4]{0:T(128)} %pad_add_fusion.1.place_ref, bf16[512,1536]{1,0:T(8,128)(2,1)} %get-tuple-element.171.x_ref, bf16[3072,384]{1,0:T(8,128)(2,1)} %slice.76.rest_0_.refs_0_, bf16[3072,384]{1,0:T(8,128)(2,1)} %collective-permute-done.11.rest_1_.refs_1_, ...), custom_call_target="tpu_custom_call" | custom-call | flops 1000000 | bytes 1000000 | tf_op jit(solution)/shard_map/project_gate/pallas_call | solution.py:664
  171.9 11.9 %d_normed_out.1.dn_ref = f32[512,3072]{1,0:T(8,128)} custom-call(s32[4]{0:T(128)} %pad_add_fusion.1.place_ref, bf16[512,1536]{1,0:T(8,128)(2,1)} %bitcast.82, bf16[768,1536]{1,0:T(8,128)(2,1)} %refs_4_.2, bf16[768,1536]{1,0:T(8,128)(2,1)} %collective-permute-done.12.rest_1_.refs_5_, bf16[768,1536]{1,0:T(8,128)(2,1)} %collective-permute-done.16.rest_2_.refs_6_, ...), custom_call_target="tpu_custom_call" | custom-call | flops 1000000 | bytes 1000000 | tf_op jit(solution)/shard_map/d_normed_out/pallas_call | solution.py:693
  184.7 15.3 %gated_norm.1 = (bf16[512,3072]{1,0:T(8,128)(2,1)}, bf16[512,3072]{1,0:T(8,128)(2,1)}, bf16[512,3072]{1,0:T(8,128)(2,1)}, f32[1,3072]{1,0:T(1,128)}, bf16[128,3072]{1,0:T(8,128)(2,1)}) custom-call(f32[512,3072]{1,0:T(8,128)} %ssd_inside.1.rest_0_.y_ref, bf16[512,3072]{1,0:T(8,128)(2,1)} %project_gate.1.gate_ref, f32[512,3072]{1,0:T(8,128)} %d_normed_out.1.dn_ref, ...), custom_call_target="tpu_custom_call" | custom-call | flops 1000000 | bytes 1000000 | tf_op jit(solution)/shard_map/gated_norm/pallas_call | solution.py:389
  200.2 5.9 %all-to-all-start.2 = ((bf16[8,16,3072]{2,1,0:T(8,128)(2,1)}), bf16[8,16,3072]{2,1,0:T(8,128)(2,1)S(1)}, u32[]{:S(2)}, u32[]{:S(2)}) async-start(bf16[8,16,3072]{2,1,0:T(8,128)(2,1)} %bitcast.92), calls=%async_computation.2 | async-start | bytes 1572864 | tf_op jit(solution)/shard_map/all_to_all | solution.py:1055
  206.6 9.7 %convolution_convert_fusion.rest_1_ = bf16[3072,1536]{1,0:T(8,128)(2,1)} fusion(bf16[512,3072]{1,0:T(8,128)(2,1)} %get-tuple-element.108.refs_0_.refs_1_.refs_2_.refs_3_, bf16[1,512,1536]{2,1,0:T(8,128)(2,1)S(1)} %copy-done.5), kind=kOutput, calls=%fused_computation | convolution fusion | flops 4836556800 | bytes 14155776 | tf_op jit(solution)/shard_map/dot_general | solution.py:1131
  216.3 10.2 %d_w_gate.1 = (bf16[384,1024]{1,0:T(8,128)(2,1)}, bf16[384,1024]{1,0:T(8,128)(2,1)}, bf16[384,1024]{1,0:T(8,128)(2,1)}, bf16[384,1024]{1,0:T(8,128)(2,1)}, bf16[...) custom-call(bf16[3,768,512]{2,1,0:T(8,128)(2,1)} %bitcast.77, bf16[3,768,512]{2,1,0:T(8,128)(2,1)} %bitcast.79, ...), custom_call_target="tpu_custom_call" | custom-call | flops 1000000 | bytes 1000000 | tf_op jit(solution)/shard_map/d_w_gate/pallas_call | solution.py:768
  227.8 2.6 carry_back.1
  230.4 5.5 %all-to-all-start.3 = ((bf16[8,16,3072]{2,1,0:T(8,128)(2,1)}), bf16[8,16,3072]{2,1,0:T(8,128)(2,1)}, u32[]{:S(2)}, u32[]{:S(2)}) async-start(bf16[8,16,3072]{2,1,0:T(8,128)(2,1)} %bitcast.89), calls=%async_computation.3 | async-start | bytes 1572864 | tf_op jit(solution)/shard_map/all_to_all | solution.py:1055
  236.0 11.8 %block_out.1.rest_0_ = f32[1,512,1536]{2,1,0:T(8,128)} custom-call(s32[4]{0:T(128)} %pad_add_fusion.1.place_ref, bf16[512,3072]{1,0:T(8,128)(2,1)} %get-tuple-element.108.refs_0_.refs_1_.refs_2_.refs_3_, bf16[512,3072]{1,0:T(8,128)(2,1)} %get-tuple-element.108.refs_0_.refs_1_.refs_2_.refs_3_, ...), custom_call_target="tpu_custom_call" | custom-call | flops 199999995904 | bytes 1000000 | tf_op jit(solution)/shard_map/block_out/pallas_call | solution.py:846
  247.7 8.6 %all-to-all-done.3 = bf16[8,16,3072]{2,1,0:T(8,128)(2,1)} async-done(((bf16[8,16,3072]{2,1,0:T(8,128)(2,1)}), bf16[8,16,3072]{2,1,0:T(8,128)(2,1)}, u32[]{:S(2)}, u32[]{:S(2)}) %all-to-all-start.3) | async-done | bytes 786464 | tf_op jit(solution)/shard_map/all_to_all | solution.py:1055
  259.2 52.4 %ssd_back.1 = (bf16[528,3584]{1,0:T(8,128)(2,1)}, f32[8,3328]{1,0:T(8,128)}, f32[12,16,128]{2,1,0:T(8,128)}) custom-call(bf16[512,3072]{1,0:T(8,128)(2,1)} %get-tuple-element.94.x_ref, bf16[512,3072]{1,0:T(8,128)(2,1)} %get-tuple-element.115.dm_ref, bf16[512,3328]{1,0:T(8,128)(2,1)} %get-tuple-element.116.slope_ref, ...), custom_call_target="tpu_custom_call" | custom-call | flops 199999995904 | bytes 1000000 | tf_op jit(solution)/shard_map/ssd_back/pallas_call | solution.py:578
  314.1 11.6 %d_normed_gate.1.refs_0_ = f32[512,1536]{1,0:T(8,128)} custom-call(s32[4]{0:T(128)} %pad_add_fusion.1.place_ref, bf16[512,3072]{1,0:T(8,128)(2,1)} %get-tuple-element.125.refs_2_.g_ref, bf16[3072,384]{1,0:T(8,128)(2,1)} %slice.76.rest_0_.refs_0_, bf16[3072,384]{1,0:T(8,128)(2,1)} %collective-permute-done.11.rest_1_.refs_1_, ...), custom_call_target="tpu_custom_call" | custom-call | flops 1000000 | bytes 1000000 | tf_op jit(solution)/shard_map/d_normed_gate/pallas_call | solution.py:885
  327.7 13.4 %d_w_rest.1 = (bf16[384,1152]{1,0:T(8,128)(2,1)}, bf16[384,1152]{1,0:T(8,128)(2,1)}, bf16[384,1152]{1,0:T(8,128)(2,1)}, bf16[384,1152]{1,0:T(8,128)(2,1)}, bf16[...) custom-call(bf16[3,768,512]{2,1,0:T(8,128)(2,1)} %bitcast.78, bf16[3,768,512]{2,1,0:T(8,128)(2,1)} %bitcast.80, ...), custom_call_target="tpu_custom_call" | custom-call | flops 1000000 | bytes 1000000 | tf_op jit(solution)/shard_map/d_w_rest/pallas_call | solution.py:768
  341.1 3.2 collective-permute-start.26
  347.8 19.5 %d_tokens.1 = (f32[1,512,1536]{2,1,0:T(8,128)}, f32[1,1536]{1,0:T(1,128)}) custom-call(s32[5]{0:T(128)} %stack.140.place_ref, f32[512,1536]{1,0:T(8,128)} %d_normed_gate.1.refs_0_, bf16[528,3584]{1,0:T(8,128)(2,1)} %get-tuple-element.129.refs_3_.refs_5_.refs_1_, bf16[16,3584]{1,0:T(8,128)(2,1)} %copy-done.25, bf16[1,512,1536]{2,1,0:T(8,128)(2,1)} %refs_3_.1, ...), custom_call_target="tpu_custom_call" | custom-call | flops 1000000 | bytes 1000000 | tf_op jit(solution)/shard_map/d_tokens/pallas_call | solution.py:978
  367.3 3.5 collective-permute-done.26.refs_11_
  372.4 5.5 %fold_sent.3 = (bf16[192,2176]{1,0:T(8,128)(2,1)}, bf16[192,2176]{1,0:T(8,128)(2,1)}, bf16[192,2176]{1,0:T(8,128)(2,1)}) custom-call(bf16[384,1024]{1,0:T(8,128)(2,1)} %get-tuple-element.111.rest_2_.refs_0_, bf16[384,1024]{1,0:T(8,128)(2,1)} %collective-permute-done.19.refs_1_, bf16[384,1152]{1,0:T(8,128)(2,1)} %get-tuple-element.128.refs_2_, ...), custom_call_target="tpu_custom_call" | custom-call | flops 1000000 | bytes 1000000 | tf_op jit(solution)/shard_map/fold_sent/pallas_call | solution.py:813
  382.4 5.5 %fold_kept.3 = (bf16[192,2176]{1,0:T(8,128)(2,1)}, bf16[192,2176]{1,0:T(8,128)(2,1)}, bf16[192,2176]{1,0:T(8,128)(2,1)}) custom-call(bf16[384,1024]{1,0:T(8,128)(2,1)} %get-tuple-element.111.rest_2_.refs_0_, bf16[384,1024]{1,0:T(8,128)(2,1)} %collective-permute-done.19.refs_1_, bf16[384,1152]{1,0:T(8,128)(2,1)} %get-tuple-element.128.refs_2_, ...), custom_call_target="tpu_custom_call" | custom-call | flops 1000000 | bytes 1000000 | tf_op jit(solution)/shard_map/fold_kept/pallas_call | solution.py:813
  387.9 13.6 %collective-permute-done.44 = f32[160,128]{1,0:T(8,128)S(1)} collective-permute-done((f32[160,128]{1,0:T(8,128)S(1)}, f32[160,128]{1,0:T(8,128)S(1)}, u32[]{:S(2)}, u32[]{:S(2)}) %collective-permute-start.44) | collective-permute-done | bytes 81952 | tf_op jit(solution)/shard_map/ppermute | solution.py:1014
  408.3 3.6 fold_kept.4
  415.9 3.5 fold_sent.4
  423.1 5.7 %collective-permute-done.36.refs_1_ = bf16[96,2176]{1,0:T(8,128)(2,1)S(1)} collective-permute-done((bf16[96,2176]{1,0:T(8,128)(2,1)}, bf16[96,2176]{1,0:T(8,128)(2,1)S(1)}, u32[]{:S(2)}, u32[]{:S(2)}) %collective-permute-start.36) | collective-permute-done | bytes 417824 | tf_op jit(solution)/shard_map/ppermute | solution.py:1014
  432.0 2.5 fold_kept.5
  435.2 2.4 collective-permute-start.47
  437.6 2.5 fold_sent.5
  440.7 2.3 collective-permute-start.41
  444.3 11.1 %collective-permute-done.47 = f32[160,128]{1,0:T(8,128)S(1)} collective-permute-done((f32[160,128]{1,0:T(8,128)S(1)}, f32[160,128]{1,0:T(8,128)S(1)}, u32[]{:S(2)}, u32[]{:S(2)}) %collective-permute-start.47) | collective-permute-done | bytes 81952 | tf_op jit(solution)/shard_map/ppermute | solution.py:1014
  459.9 4.5 collective-permute-done.41.refs_3_
  464.4 3.6 collective-permute-done.42.refs_5_
  468.6 2.5 fold_last.1
  (211 shorter events, 88.0 us)
Async XLA Ops:
  8.0 17.1 %collective-permute-start = (bf16[16,1536]{1,0:T(8,128)(2,1)S(1)}, bf16[16,1536]{1,0:T(8,128)(2,1)S(1)}, u32[]{:S(2)}, u32[]{:S(2)}) collective-permute-start(bf16[16,1536]{1,0:T(8,128)(2,1)S(1)} %slice_bitcast_fusion.1), channel_id=1, source_target_pairs={{0,4},{1,5},{2,6},{3,7},{4,8},{5,9},{6,10},{7,11},{8,12},{9,13},{1... | collective-permute-start | bytes 147464 | tf_op jit(solution)/shard_map/ppermute | solution.py:1014
  16.8 17.1 %collective-permute-start.2 = (bf16[896,384]{1,0:T(8,128)(2,1)}, bf16[896,384]{1,0:T(8,128)(2,1)S(1)}, u32[]{:S(2)}, u32[]{:S(2)}) collective-permute-start(bf16[896,384]{1,0:T(8,128)(2,1)} %get-tuple-element.170), channel_id=1, source_target_pairs={{0,2},{1,3},{2,0},{3,1},{4,6},{5,7},{6,4},{7,5},{8,10},{9,11},{10,... | collective-permute-start | bytes 2064392 | tf_op jit(solution)/shard_map/ppermute | solution.py:1014
  20.3 60.2 %collective-permute-start.1 = (bf16[3584,384]{1,0:T(8,128)(2,1)S(1)}, bf16[3584,384]{1,0:T(8,128)(2,1)}, u32[]{:S(2)}, u32[]{:S(2)}) collective-permute-start(bf16[3584,384]{1,0:T(8,128)(2,1)S(1)} %pad.15.rest_0_.refs_6_), channel_id=1, source_target_pairs={{0,1},{1,0},{2,3},{3,2},{4,5},{5,4},{6,7},{7,6},{8,9},{9,8},{10,11... | collective-permute-start | bytes 8257544 | tf_op jit(solution)/shard_map/ppermute | solution.py:1014
  24.6 55.3 %collective-permute-start.11 = (bf16[3072,384]{1,0:T(8,128)(2,1)}, bf16[3072,384]{1,0:T(8,128)(2,1)}, u32[]{:S(2)}, u32[]{:S(2)}) collective-permute-start(bf16[3072,384]{1,0:T(8,128)(2,1)} %slice.76.rest_0_.refs_0_), channel_id=1, source_target_pairs={{0,1},{1,0},{2,3},{3,2},{4,5},{5,4},{6,7},{7,6},{8,9},{9,8},{10,11... | collective-permute-start | bytes 7077896 | tf_op jit(solution)/shard_map/ppermute | solution.py:1014
  24.6 55.8 %collective-permute-start.12 = (bf16[768,1536]{1,0:T(8,128)(2,1)}, bf16[768,1536]{1,0:T(8,128)(2,1)}, u32[]{:S(2)}, u32[]{:S(2)}) collective-permute-start(bf16[768,1536]{1,0:T(8,128)(2,1)} %refs_4_.2), channel_id=1, source_target_pairs={{0,1},{1,0},{2,3},{3,2},{4,5},{5,4},{6,7},{7,6},{8,9},{9,8},{10,11... | collective-permute-start | bytes 7077896 | tf_op jit(solution)/shard_map/ppermute | solution.py:1014
  33.9 16.3 %collective-permute-start.3 = (bf16[896,384]{1,0:T(8,128)(2,1)}, bf16[896,384]{1,0:T(8,128)(2,1)}, u32[]{:S(2)}, u32[]{:S(2)}) collective-permute-start(bf16[896,384]{1,0:T(8,128)(2,1)} %get-tuple-element.89), channel_id=1, source_target_pairs={{0,2},{1,3},{2,0},{3,1},{4,6},{5,7},{6,4},{7,5},{8,10},{9,11},{10,... | collective-permute-start | bytes 2064392 | tf_op jit(solution)/shard_map/ppermute | solution.py:1014
  35.4 15.8 %collective-permute-start.4 = (bf16[896,384]{1,0:T(8,128)(2,1)S(1)}, bf16[896,384]{1,0:T(8,128)(2,1)}, u32[]{:S(2)}, u32[]{:S(2)}) collective-permute-start(bf16[896,384]{1,0:T(8,128)(2,1)S(1)} %collective-permute-done.2.rest_2_.refs_8_), channel_id=1, source_target_pairs={{0,4},{1,5},{2,6},{3,7},{4,0},{5,1},{6,2},{7,3},{8,12},{9,13},{10,... | collective-permute-start | bytes 2064392 | tf_op jit(solution)/shard_map/ppermute | solution.py:1014
  51.2 50.9 %collective-permute-start.14 = (bf16[3072,384]{1,0:T(8,128)(2,1)}, bf16[3072,384]{1,0:T(8,128)(2,1)}, u32[]{:S(2)}, u32[]{:S(2)}) collective-permute-start(bf16[3072,384]{1,0:T(8,128)(2,1)} %slice.76.rest_0_.refs_0_), channel_id=1, source_target_pairs={{0,2},{1,3},{2,0},{3,1},{4,6},{5,7},{6,4},{7,5},{8,10},{9,11},{10,... | collective-permute-start | bytes 7077896 | tf_op jit(solution)/shard_map/ppermute | solution.py:1014
  61.9 18.0 %collective-permute-start.5 = (bf16[896,384]{1,0:T(8,128)(2,1)}, bf16[896,384]{1,0:T(8,128)(2,1)}, u32[]{:S(2)}, u32[]{:S(2)}) collective-permute-start(bf16[896,384]{1,0:T(8,128)(2,1)} %collective-permute-done.3.rest_3_.refs_9_), channel_id=1, source_target_pairs={{0,4},{1,5},{2,6},{3,7},{4,0},{5,1},{6,2},{7,3},{8,12},{9,13},{10,... | collective-permute-start | bytes 2064392 | tf_op jit(solution)/shard_map/ppermute | solution.py:1014
  80.0 4.2 collective-permute-start.7
  80.5 4.9 %collective-permute-start.8 = (bf16[896,384]{1,0:T(8,128)(2,1)}, bf16[896,384]{1,0:T(8,128)(2,1)}, u32[]{:S(2)}, u32[]{:S(2)}) collective-permute-start(bf16[896,384]{1,0:T(8,128)(2,1)} %collective-permute-done.4.rest_4_.refs_10_), channel_id=1, source_target_pairs={{0,1},{1,0},{2,3},{3,2},{4,5},{5,4},{6,7},{7,6},{8,9},{9,8},{10,11... | collective-permute-start | bytes 2064392 | tf_op jit(solution)/shard_map/ppermute | solution.py:1014
  80.5 4.9 %collective-permute-start.13 = (bf16[896,384]{1,0:T(8,128)(2,1)}, bf16[896,384]{1,0:T(8,128)(2,1)S(1)}, u32[]{:S(2)}, u32[]{:S(2)}) collective-permute-start(bf16[896,384]{1,0:T(8,128)(2,1)} %collective-permute-done.5.rest_5_.refs_11_), channel_id=1, source_target_pairs={{0,1},{1,0},{2,3},{3,2},{4,5},{5,4},{6,7},{7,6},{8,9},{9,8},{10,11... | collective-permute-start | bytes 2064392 | tf_op jit(solution)/shard_map/ppermute | solution.py:1014
  102.1 51.6 %collective-permute-start.16 = (bf16[768,1536]{1,0:T(8,128)(2,1)}, bf16[768,1536]{1,0:T(8,128)(2,1)}, u32[]{:S(2)}, u32[]{:S(2)}) collective-permute-start(bf16[768,1536]{1,0:T(8,128)(2,1)} %refs_4_.2), channel_id=1, source_target_pairs={{0,2},{1,3},{2,0},{3,1},{4,6},{5,7},{6,4},{7,5},{8,10},{9,11},{10,... | collective-permute-start | bytes 7077896 | tf_op jit(solution)/shard_map/ppermute | solution.py:1014
  120.8 25.4 %all-to-all-start = ((bf16[8,16,3328]{2,1,0:T(8,128)(2,1)}), bf16[8,16,3328]{2,1,0:T(8,128)(2,1)S(1)}, u32[]{:S(2)}, u32[]{:S(2)}) async-start(bf16[8,16,3328]{2,1,0:T(8,128)(2,1)} %bitcast.90), calls=%async_computation | async-start | bytes 1703936 | tf_op jit(solution)/shard_map/all_to_all | solution.py:1055
  141.9 17.6 %collective-permute-start.15 = (bf16[3072,384]{1,0:T(8,128)(2,1)}, bf16[3072,384]{1,0:T(8,128)(2,1)S(1)}, u32[]{:S(2)}, u32[]{:S(2)}) collective-permute-start(bf16[3072,384]{1,0:T(8,128)(2,1)} %collective-permute-done.14.rest_2_.refs_2_), channel_id=1, source_target_pairs={{0,1},{1,0},{2,3},{3,2},{4,5},{5,4},{6,7},{7,6},{8,9},{9,8},{10,11... | collective-permute-start | bytes 7077896 | tf_op jit(solution)/shard_map/ppermute | solution.py:1014
  153.7 18.2 %collective-permute-start.17 = (bf16[768,1536]{1,0:T(8,128)(2,1)}, bf16[768,1536]{1,0:T(8,128)(2,1)}, u32[]{:S(2)}, u32[]{:S(2)}) collective-permute-start(bf16[768,1536]{1,0:T(8,128)(2,1)} %collective-permute-done.16.rest_2_.refs_6_), channel_id=1, source_target_pairs={{0,1},{1,0},{2,3},{3,2},{4,5},{5,4},{6,7},{7,6},{8,9},{9,8},{10,11... | collective-permute-start | bytes 7077896 | tf_op jit(solution)/shard_map/ppermute | solution.py:1014
  153.7 30.1 %all-to-all-start.1 = ((bf16[8,16,3072]{2,1,0:T(8,128)(2,1)}), bf16[8,16,3072]{2,1,0:T(8,128)(2,1)S(1)}, u32[]{:S(2)}, u32[]{:S(2)}) async-start(bf16[8,16,3072]{2,1,0:T(8,128)(2,1)} %bitcast.93), calls=%async_computation.1 | async-start | bytes 1572864 | tf_op jit(solution)/shard_map/all_to_all | solution.py:1055
  200.0 16.3 %collective-permute-start.18 = (bf16[512,3072]{1,0:T(8,128)(2,1)}, bf16[512,3072]{1,0:T(8,128)(2,1)}, u32[]{:S(2)}, u32[]{:S(2)}) collective-permute-start(bf16[512,3072]{1,0:T(8,128)(2,1)} %get-tuple-element.125.refs_2_.g_ref), channel_id=1, source_target_pairs={{0,1},{1,0},{2,3},{3,2},{4,5},{5,4},{6,7},{7,6},{8,9},{9,8},{10,11... | collective-permute-start | bytes 9437192 | tf_op jit(solution)/shard_map/ppermute | solution.py:1014
  200.2 26.7 %all-to-all-start.2 = ((bf16[8,16,3072]{2,1,0:T(8,128)(2,1)}), bf16[8,16,3072]{2,1,0:T(8,128)(2,1)S(1)}, u32[]{:S(2)}, u32[]{:S(2)}) async-start(bf16[8,16,3072]{2,1,0:T(8,128)(2,1)} %bitcast.92), calls=%async_computation.2 | async-start | bytes 1572864 | tf_op jit(solution)/shard_map/all_to_all | solution.py:1055
  206.1 265.0 %reduce-scatter.2.cloned.1.call-start = ((), (), s32[]{:S(2)}) async-start(), calls=%async_computation.5 | async-start | bytes 9732096 | tf_op jit(solution)/shard_map/reduce_scatter | solution.py:1132
  230.4 25.9 %all-to-all-start.3 = ((bf16[8,16,3072]{2,1,0:T(8,128)(2,1)}), bf16[8,16,3072]{2,1,0:T(8,128)(2,1)}, u32[]{:S(2)}, u32[]{:S(2)}) async-start(bf16[8,16,3072]{2,1,0:T(8,128)(2,1)} %bitcast.89), calls=%async_computation.3 | async-start | bytes 1572864 | tf_op jit(solution)/shard_map/all_to_all | solution.py:1055
  256.4 55.3 %collective-permute-start.21 = (bf16[384,1024]{1,0:T(8,128)(2,1)}, bf16[384,1024]{1,0:T(8,128)(2,1)}, u32[]{:S(2)}, u32[]{:S(2)}) collective-permute-start(bf16[384,1024]{1,0:T(8,128)(2,1)} %get-tuple-element.123), channel_id=1, source_target_pairs={{0,8},{1,9},{2,10},{3,11},{4,12},{5,13},{6,14},{7,15},{8,0},{9,1},... | collective-permute-start | bytes 2359304 | tf_op jit(solution)/shard_map/ppermute | solution.py:1014
  256.7 55.0 %collective-permute-start.20 = (bf16[384,1024]{1,0:T(8,128)(2,1)}, bf16[384,1024]{1,0:T(8,128)(2,1)}, u32[]{:S(2)}, u32[]{:S(2)}) collective-permute-start(bf16[384,1024]{1,0:T(8,128)(2,1)} %get-tuple-element.121), channel_id=1, source_target_pairs={{0,2},{1,3},{2,0},{3,1},{4,6},{5,7},{6,4},{7,5},{8,10},{9,11},{10,... | collective-permute-start | bytes 2359304 | tf_op jit(solution)/shard_map/ppermute | solution.py:1014
  258.1 53.5 %collective-permute-start.19 = (bf16[384,1024]{1,0:T(8,128)(2,1)}, bf16[384,1024]{1,0:T(8,128)(2,1)}, u32[]{:S(2)}, u32[]{:S(2)}) collective-permute-start(bf16[384,1024]{1,0:T(8,128)(2,1)} %get-tuple-element.119), channel_id=1, source_target_pairs={{0,4},{1,5},{2,6},{3,7},{4,0},{5,1},{6,2},{7,3},{8,12},{9,13},{10,... | collective-permute-start | bytes 2359304 | tf_op jit(solution)/shard_map/ppermute | solution.py:1014
  311.7 14.1 %collective-permute-start.22 = (bf16[528,3584]{1,0:T(8,128)(2,1)}, bf16[528,3584]{1,0:T(8,128)(2,1)S(1)}, u32[]{:S(2)}, u32[]{:S(2)}) collective-permute-start(bf16[528,3584]{1,0:T(8,128)(2,1)} %get-tuple-element.129.refs_3_.refs_5_.refs_1_), channel_id=1, source_target_pairs={{0,1},{1,0},{2,3},{3,2},{4,5},{5,4},{6,7},{7,6},{8,9},{9,8},{10,11... | collective-permute-start | bytes 11354120 | tf_op jit(solution)/shard_map/ppermute | solution.py:1014
  312.6 13.1 %collective-permute-start.23 = (bf16[16,3584]{1,0:T(8,128)(2,1)S(1)}, bf16[16,3584]{1,0:T(8,128)(2,1)S(1)}, u32[]{:S(2)}, u32[]{:S(2)}) collective-permute-start(bf16[16,3584]{1,0:T(8,128)(2,1)S(1)} %slice.60), channel_id=1, source_target_pairs={{4,0},{5,1},{6,2},{7,3},{8,4},{9,5},{10,6},{11,7},{12,8},{13,9},{1... | collective-permute-start | bytes 344072 | tf_op jit(solution)/shard_map/ppermute | solution.py:1014
  341.1 29.7 %collective-permute-start.26 = (bf16[384,1152]{1,0:T(8,128)(2,1)}, bf16[384,1152]{1,0:T(8,128)(2,1)S(1)}, u32[]{:S(2)}, u32[]{:S(2)}) collective-permute-start(bf16[384,1152]{1,0:T(8,128)(2,1)} %get-tuple-element.138), channel_id=1, source_target_pairs={{0,8},{1,9},{2,10},{3,11},{4,12},{5,13},{6,14},{7,15},{8,0},{9,1},... | collective-permute-start | bytes 2654216 | tf_op jit(solution)/shard_map/ppermute | solution.py:1014
  344.3 26.5 %collective-permute-start.25 = (bf16[384,1152]{1,0:T(8,128)(2,1)}, bf16[384,1152]{1,0:T(8,128)(2,1)S(1)}, u32[]{:S(2)}, u32[]{:S(2)}) collective-permute-start(bf16[384,1152]{1,0:T(8,128)(2,1)} %get-tuple-element.135), channel_id=1, source_target_pairs={{0,2},{1,3},{2,0},{3,1},{4,6},{5,7},{6,4},{7,5},{8,10},{9,11},{10,... | collective-permute-start | bytes 2654216 | tf_op jit(solution)/shard_map/ppermute | solution.py:1014
  344.8 26.0 %collective-permute-start.24 = (bf16[384,1152]{1,0:T(8,128)(2,1)}, bf16[384,1152]{1,0:T(8,128)(2,1)S(1)}, u32[]{:S(2)}, u32[]{:S(2)}) collective-permute-start(bf16[384,1152]{1,0:T(8,128)(2,1)} %get-tuple-element.132), channel_id=1, source_target_pairs={{0,4},{1,5},{2,6},{3,7},{4,0},{5,1},{6,2},{7,3},{8,12},{9,13},{10,... | collective-permute-start | bytes 2654216 | tf_op jit(solution)/shard_map/ppermute | solution.py:1014
  347.2 34.7 %collective-permute-start.43 = (f32[160,128]{1,0:T(8,128)S(1)}, f32[160,128]{1,0:T(8,128)S(1)}, u32[]{:S(2)}, u32[]{:S(2)}) collective-permute-start(f32[160,128]{1,0:T(8,128)S(1)} %pad_bitcast_fusion), channel_id=1, source_target_pairs={{0,1},{1,0},{2,3},{3,2},{4,5},{5,4},{6,7},{7,6},{8,9},{9,8},{10,11... | collective-permute-start | bytes 245768 | tf_op jit(solution)/shard_map/ppermute | solution.py:1014
  378.0 28.8 %collective-permute-start.30 = (bf16[192,2176]{1,0:T(8,128)(2,1)}, bf16[192,2176]{1,0:T(8,128)(2,1)S(1)}, u32[]{:S(2)}, u32[]{:S(2)}) collective-permute-start(bf16[192,2176]{1,0:T(8,128)(2,1)} %get-tuple-element.142), channel_id=1, source_target_pairs={{0,2},{1,3},{2,0},{3,1},{4,6},{5,7},{6,4},{7,5},{8,10},{9,11},{10,... | collective-permute-start | bytes 2506760 | tf_op jit(solution)/shard_map/ppermute | solution.py:1014
  378.5 28.3 %collective-permute-start.31 = (bf16[192,2176]{1,0:T(8,128)(2,1)}, bf16[192,2176]{1,0:T(8,128)(2,1)S(1)}, u32[]{:S(2)}, u32[]{:S(2)}) collective-permute-start(bf16[192,2176]{1,0:T(8,128)(2,1)} %get-tuple-element.144), channel_id=1, source_target_pairs={{0,8},{1,9},{2,10},{3,11},{4,12},{5,13},{6,14},{7,15},{8,0},{9,1},... | collective-permute-start | bytes 2506760 | tf_op jit(solution)/shard_map/ppermute | solution.py:1014
  380.3 26.6 %collective-permute-start.32 = (bf16[192,2176]{1,0:T(8,128)(2,1)}, bf16[192,2176]{1,0:T(8,128)(2,1)S(1)}, u32[]{:S(2)}, u32[]{:S(2)}) collective-permute-start(bf16[192,2176]{1,0:T(8,128)(2,1)} %get-tuple-element.146), channel_id=1, source_target_pairs={{0,4},{1,5},{2,6},{3,7},{4,0},{5,1},{6,2},{7,3},{8,12},{9,13},{10,... | collective-permute-start | bytes 2506760 | tf_op jit(solution)/shard_map/ppermute | solution.py:1014
  381.9 19.7 %collective-permute-start.44 = (f32[160,128]{1,0:T(8,128)S(1)}, f32[160,128]{1,0:T(8,128)S(1)}, u32[]{:S(2)}, u32[]{:S(2)}) collective-permute-start(f32[160,128]{1,0:T(8,128)S(1)} %fusion.4), channel_id=1, source_target_pairs={{0,4},{1,5},{2,6},{3,7},{4,0},{5,1},{6,2},{7,3},{8,12},{9,13},{10,... | collective-permute-start | bytes 245768 | tf_op jit(solution)/shard_map/ppermute | solution.py:1014
  387.9 15.3 %collective-permute-start.27 = (f32[1,1536]{1,0:T(1,128)S(1)}, f32[1,1536]{1,0:T(1,128)S(1)}, u32[]{:S(2)}, u32[]{:S(2)}) collective-permute-start(f32[1,1536]{1,0:T(1,128)S(1)} %copy-done.32), channel_id=1, source_target_pairs={{0,1},{1,0},{2,3},{3,2},{4,5},{5,4},{6,7},{7,6},{8,9},{9,8},{10,11... | collective-permute-start | bytes 18440 | tf_op jit(solution)/shard_map/ppermute | solution.py:1014
  405.2 10.2 %collective-permute-start.45 = (f32[160,128]{1,0:T(8,128)S(1)}, f32[160,128]{1,0:T(8,128)S(1)}, u32[]{:S(2)}, u32[]{:S(2)}) collective-permute-start(f32[160,128]{1,0:T(8,128)S(1)} %fusion.8), channel_id=1, source_target_pairs={{0,2},{1,3},{2,0},{3,1},{4,6},{5,7},{6,4},{7,5},{8,10},{9,11},{10,... | collective-permute-start | bytes 245768 | tf_op jit(solution)/shard_map/ppermute | solution.py:1014
  411.9 9.1 %collective-permute-start.33 = (f32[1,1536]{1,0:T(1,128)S(1)}, f32[1,1536]{1,0:T(1,128)S(1)}, u32[]{:S(2)}, u32[]{:S(2)}) collective-permute-start(f32[1,1536]{1,0:T(1,128)S(1)} %add_add_fusion.1), channel_id=1, source_target_pairs={{0,2},{1,3},{2,0},{3,1},{4,6},{5,7},{6,4},{7,5},{8,10},{9,11},{10,... | collective-permute-start | bytes 18440 | tf_op jit(solution)/shard_map/ppermute | solution.py:1014
  413.0 9.7 %collective-permute-start.34 = (f32[1,1536]{1,0:T(1,128)S(1)}, f32[1,1536]{1,0:T(1,128)S(1)}, u32[]{:S(2)}, u32[]{:S(2)}) collective-permute-start(f32[1,1536]{1,0:T(1,128)S(1)} %add_add_fusion.1), channel_id=1, source_target_pairs={{0,8},{1,9},{2,10},{3,11},{4,12},{5,13},{6,14},{7,15},{8,0},{9,1},... | collective-permute-start | bytes 18440 | tf_op jit(solution)/shard_map/ppermute | solution.py:1014
  413.4 9.8 %collective-permute-start.35 = (f32[1,1536]{1,0:T(1,128)S(1)}, f32[1,1536]{1,0:T(1,128)S(1)}, u32[]{:S(2)}, u32[]{:S(2)}) collective-permute-start(f32[1,1536]{1,0:T(1,128)S(1)} %add_add_fusion.1), channel_id=1, source_target_pairs={{0,10},{1,11},{2,8},{3,9},{4,14},{5,15},{6,12},{7,13},{8,2},{9,3},... | collective-permute-start | bytes 18440 | tf_op jit(solution)/shard_map/ppermute | solution.py:1014
  415.4 19.8 %collective-permute-start.46 = (f32[160,128]{1,0:T(8,128)S(1)}, f32[160,128]{1,0:T(8,128)S(1)}, u32[]{:S(2)}, u32[]{:S(2)}) collective-permute-start(f32[160,128]{1,0:T(8,128)S(1)} %add.201), channel_id=1, source_target_pairs={{0,8},{1,9},{2,10},{3,11},{4,12},{5,13},{6,14},{7,15},{8,0},{9,1},... | collective-permute-start | bytes 245768 | tf_op jit(solution)/shard_map/ppermute | solution.py:1014
  419.5 9.4 %collective-permute-start.36 = (bf16[96,2176]{1,0:T(8,128)(2,1)}, bf16[96,2176]{1,0:T(8,128)(2,1)S(1)}, u32[]{:S(2)}, u32[]{:S(2)}) collective-permute-start(bf16[96,2176]{1,0:T(8,128)(2,1)} %get-tuple-element.149), channel_id=1, source_target_pairs={{0,8},{1,9},{2,10},{3,11},{4,12},{5,13},{6,14},{7,15},{8,0},{9,1},... | collective-permute-start | bytes 1253384 | tf_op jit(solution)/shard_map/ppermute | solution.py:1014
  421.0 8.9 %collective-permute-start.37 = (bf16[96,2176]{1,0:T(8,128)(2,1)}, bf16[96,2176]{1,0:T(8,128)(2,1)S(1)}, u32[]{:S(2)}, u32[]{:S(2)}) collective-permute-start(bf16[96,2176]{1,0:T(8,128)(2,1)} %get-tuple-element.151), channel_id=1, source_target_pairs={{0,4},{1,5},{2,6},{3,7},{4,0},{5,1},{6,2},{7,3},{8,12},{9,13},{10,... | collective-permute-start | bytes 1253384 | tf_op jit(solution)/shard_map/ppermute | solution.py:1014
  422.7 8.5 %collective-permute-start.38 = (bf16[96,2176]{1,0:T(8,128)(2,1)}, bf16[96,2176]{1,0:T(8,128)(2,1)S(1)}, u32[]{:S(2)}, u32[]{:S(2)}) collective-permute-start(bf16[96,2176]{1,0:T(8,128)(2,1)} %get-tuple-element.153), channel_id=1, source_target_pairs={{0,2},{1,3},{2,0},{3,1},{4,6},{5,7},{6,4},{7,5},{8,10},{9,11},{10,... | collective-permute-start | bytes 1253384 | tf_op jit(solution)/shard_map/ppermute | solution.py:1014
  434.6 9.1 %collective-permute-start.39 = (f32[1,1536]{1,0:T(1,128)S(1)}, f32[1,1536]{1,0:T(1,128)S(1)}, u32[]{:S(2)}, u32[]{:S(2)}) collective-permute-start(f32[1,1536]{1,0:T(1,128)S(1)} %add_add_fusion), channel_id=1, source_target_pairs={{0,16},{1,17},{2,18},{3,19},{4,20},{5,21},{6,22},{7,23},{8,24},{9,... | collective-permute-start | bytes 18440 | tf_op jit(solution)/shard_map/ppermute | solution.py:1014
  435.2 20.2 %collective-permute-start.47 = (f32[160,128]{1,0:T(8,128)S(1)}, f32[160,128]{1,0:T(8,128)S(1)}, u32[]{:S(2)}, u32[]{:S(2)}) collective-permute-start(f32[160,128]{1,0:T(8,128)S(1)} %add.202), channel_id=1, source_target_pairs={{0,16},{1,17},{2,18},{3,19},{4,20},{5,21},{6,22},{7,23},{8,24},{9,... | collective-permute-start | bytes 245768 | tf_op jit(solution)/shard_map/ppermute | solution.py:1014
  440.1 19.8 %collective-permute-start.40 = (bf16[48,2176]{1,0:T(8,128)(2,1)}, bf16[48,2176]{1,0:T(8,128)(2,1)S(1)}, u32[]{:S(2)}, u32[]{:S(2)}) collective-permute-start(bf16[48,2176]{1,0:T(8,128)(2,1)} %get-tuple-element.156), channel_id=1, source_target_pairs={{0,16},{1,17},{2,18},{3,19},{4,20},{5,21},{6,22},{7,23},{8,24},{9,... | collective-permute-start | bytes 626696 | tf_op jit(solution)/shard_map/ppermute | solution.py:1014
  440.7 23.6 %collective-permute-start.41 = (bf16[48,2176]{1,0:T(8,128)(2,1)}, bf16[48,2176]{1,0:T(8,128)(2,1)S(1)}, u32[]{:S(2)}, u32[]{:S(2)}) collective-permute-start(bf16[48,2176]{1,0:T(8,128)(2,1)} %get-tuple-element.158), channel_id=1, source_target_pairs={{0,16},{1,17},{2,18},{3,19},{4,20},{5,21},{6,22},{7,23},{8,24},{9,... | collective-permute-start | bytes 626696 | tf_op jit(solution)/shard_map/ppermute | solution.py:1014
  443.0 24.9 %collective-permute-start.42 = (bf16[48,2176]{1,0:T(8,128)(2,1)}, bf16[48,2176]{1,0:T(8,128)(2,1)S(1)}, u32[]{:S(2)}, u32[]{:S(2)}) collective-permute-start(bf16[48,2176]{1,0:T(8,128)(2,1)} %get-tuple-element.160), channel_id=1, source_target_pairs={{0,16},{1,17},{2,18},{3,19},{4,20},{5,21},{6,22},{7,23},{8,24},{9,... | collective-permute-start | bytes 626696 | tf_op jit(solution)/shard_map/ppermute | solution.py:1014
  (42 other events, 354.9 us)
Sparse Core Ops, SparseCore 0:
  216.4 144.4 reduce-scatter.1

commit v4 on v3

--- a/solution.py
+++ b/solution.py
@@ -21,7 +21,7 @@
 QUADS = INNER // QUAD
 HALO = 16
 VMEM_LIMIT = 56 * 1024 * 1024
-LONG = pl.CostEstimate(flops=200000000000, bytes_accessed=1000000, transcendentals=0)
+LONG = pl.CostEstimate(flops=40000000000, bytes_accessed=1000000, transcendentals=0)
 COST = pl.CostEstimate(flops=1000000, bytes_accessed=1000000, transcendentals=0)
 F32 = jnp.float32
 BF16 = jnp.bfloat16
@@ -85,7 +85,7 @@
     return jnp.concatenate([rows, jnp.zeros((128 - count, length), F32)], axis=0).T
 
 
-def step_kernel(dt_ref, bias_ref, alog_ref, rows_ref, ecd_ref, total_ref):
+def step_kernel(dt_ref, bias_ref, alog_ref, rows_ref, heads_ref, ecd_ref, total_ref):
     length = dt_ref.shape[0] - HALO
     raw = dt_ref[HALO:, :].astype(F32) + bias_ref[...]
     step = jnp.maximum(raw, 0.0) + jnp.log1p(jnp.exp(-jnp.abs(raw)))
@@ -105,11 +105,16 @@
     ecd_ref[...] = jnp.exp(along)
     total_ref[...] = jnp.broadcast_to(jnp.exp(offset), (8, 128))
     left = jnp.exp(offset - along) * step
-    for place, array in enumerate((cum, step, left, sig, jnp.broadcast_to(rate, (length, 128)))):
+    heads_ref[...] = jnp.zeros_like(heads_ref)
+    rows_ref[...] = jnp.zeros_like(rows_ref)
+    for place, array in enumerate((cum, step, left)):
         turned = array.T
         for quad in range(QUADS):
             rows_ref[quad, 8 * place : 8 * place + 4, :] = turned[4 * quad : 4 * quad + 4, :]
-            rows_ref[quad, 8 * place + 4 : 8 * place + 8, :] = jnp.zeros((4, length), F32)
+    for place, array in enumerate((step, sig, jnp.broadcast_to(rate, (length, 128)))):
+        turned = array.T
+        for quad in range(QUADS):
+            heads_ref[place, 8 * quad : 8 * quad + 4, :] = turned[4 * quad : 4 * quad + 4, :]
 
 
 def step_call(projected, dt_bias, a_log):
@@ -120,12 +125,14 @@
         grid=(1,),
         in_specs=[pl.BlockSpec((length + HALO, 128), lambda g: (0, CONV // 128)), line, line],
         out_specs=(
-            pl.BlockSpec((QUADS, 40, length), lambda g: (0, 0, 0)),
+            pl.BlockSpec((QUADS, 24, length), lambda g: (0, 0, 0)),
+            pl.BlockSpec((3, 8 * QUADS, length), lambda g: (0, 0, 0)),
             pl.BlockSpec((length, 128), lambda g: (0, 0)),
             pl.BlockSpec((8, 128), lambda g: (0, 0)),
         ),
         out_shape=(
-            jax.ShapeDtypeStruct((QUADS, 40, length), F32),
+            jax.ShapeDtypeStruct((QUADS, 24, length), F32),
+            jax.ShapeDtypeStruct((3, 8 * QUADS, length), F32),
             jax.ShapeDtypeStruct((length, 128), F32),
             jax.ShapeDtypeStruct((8, 128), F32),
         ),
@@ -196,7 +203,7 @@
             pl.BlockSpec((length + HALO, QUAD), block),
             pl.BlockSpec((KW, QUAD), block),
             pl.BlockSpec((1, QUAD), block),
-            pl.BlockSpec((1, 40, length), lambda g: (jnp.maximum(g - 1, 0), 0, 0)),
+            pl.BlockSpec((1, 24, length), lambda g: (jnp.maximum(g - 1, 0), 0, 0)),
             pl.BlockSpec((8, 128), whole),
         ]
         + [pl.BlockSpec(memory_space=pl.ANY)] * len(after),
@@ -262,7 +269,7 @@
     )(*args, *after)
 
 
-def inside_kernel(x_ref, b_ref, c_ref, bt_ref, rows_ref, skip_ref, y_ref, scores, state):
+def inside_kernel(x_ref, b_ref, c_ref, bt_ref, rows_ref, skip_ref, y_ref, scores):
     length = x_ref.shape[0]
     grid = pl.program_id(0)
 
@@ -293,12 +300,12 @@
             pieces.append(mm(jnp.concatenate(weights[2 * pair : 2 * pair + 2], axis=1), both.astype(BF16)))
         y_part = jnp.concatenate(pieces, axis=1) + skip_ref[...] * x_f
         if start > 0:
-            y_part = y_part + jnp.exp(cum) * mm(c_ref[part, :], state[...].astype(BF16))
+            y_part = y_part + jnp.exp(cum) * mm(c_ref[part, :], state.astype(BF16))
         y_ref[part, :] = y_part
         if start + CHUNK < length:
             end = cum[CHUNK - 1 : CHUNK]
             fresh = mm(bt_ref[:, part], (x_f * (jnp.exp(end - cum) * step)).astype(BF16))
-            state[...] = fresh if start == 0 else jnp.exp(end) * state[...] + fresh
+            state = fresh if start == 0 else jnp.exp(end) * state + fresh
 
 
 def inside_call(x_act, b_act, c_act, b_turned, rows, skip_wide):
@@ -313,12 +320,12 @@
             pl.BlockSpec((length, STATE), whole),
             pl.BlockSpec((length, STATE), whole),
             pl.BlockSpec((STATE, length), whole),
-            pl.BlockSpec((1, 40, length), lambda g: (g, 0, 0)),
+            pl.BlockSpec((1, 24, length), lambda g: (g, 0, 0)),
             pl.BlockSpec((1, QUAD), quad),
         ],
         out_specs=pl.BlockSpec((length, QUAD), quad),
         out_shape=jax.ShapeDtypeStruct((length, INNER), F32),
-        scratch_shapes=[pltpu.VMEM((length, CHUNK), F32), pltpu.VMEM((STATE, QUAD), F32)],
+        scratch_shapes=[pltpu.VMEM((length, CHUNK), F32)],
         compiler_params=pltpu.CompilerParams(vmem_limit_bytes=VMEM_LIMIT),
         cost_estimate=COST,
         name="ssd_inside",
@@ -410,8 +417,11 @@
     )(y_inside, gate_in, d_normed, c_act, c_turned, ecd, out_gain, s_in)
 
 
-def back_kernel(x_ref, dm_ref, slope_ref, v_ref, cw_ref, b_ref, c_ref, bt_ref, ct_ref, rows_ref, skip_ref, sin_ref, rin_ref, *rest):
-    dv_ref, sums_ref, heads_ref, scores, d_scores, d_b, d_c, states, back, grads, ext, d_step = rest[-12:]
+def back_kernel(
+    x_ref, dm_ref, slope_ref, v_ref, cw_ref, b_ref, c_ref, bt_ref, ct_ref, rows_ref, table_ref, skip_ref, sin_ref, rin_ref, *rest
+):
+    dv_ref, sums_ref, heads_ref = rest[-14:-11]
+    scores, d_scores, d_b, d_c, states, products, grads, ext, marks, across, crossing = rest[-11:]
     length = x_ref.shape[0]
     chunks = length // CHUNK
     grid = pl.program_id(0)
@@ -424,7 +434,7 @@
         d_scores[...] = jnp.zeros_like(d_scores)
         d_b[...] = jnp.zeros_like(d_b)
         d_c[...] = jnp.zeros_like(d_c)
-        d_step[...] = jnp.zeros_like(d_step)
+        marks[...] = jnp.zeros_like(marks)
         grads[:, 0:HALO, :] = jnp.zeros((2, HALO, 128), F32)
         grads[:, HALO + length :, :] = jnp.zeros((2, HALO, 128), F32)
 
@@ -461,93 +471,84 @@
         cols = columns_of(rows_ref[0])
         upper = iota((CHUNK, CHUNK), 0) <= iota((CHUNK, CHUNK), 1)
         first = iota((CHUNK, 128), 1) < HEAD_DIM
-        lane = iota((CHUNK, 128), 1)
+        lane = iota((CHUNK, 128), 1) - 8 * grid
         line = iota((8, 128), 0)
-        head_of = iota((QUAD, 128), 0) >> 6
-        ones_v = jnp.where(iota((QUAD, 128), 1) == head_of + 8, 1.0, 0.0).astype(BF16)
-        ones_u = jnp.where(iota((QUAD, 128), 1) == head_of + 16, 1.0, 0.0).astype(BF16)
-        square = (CHUNK, CHUNK)
-        later = jnp.where(iota(square, 0) >= iota(square, 1), 1.0, 0.0).astype(BF16)
-        before = jnp.where(iota(square, 0) < iota(square, 1), 1.0, 0.0).astype(BF16)
+        ones = jnp.where(iota((QUAD, 128), 1) - 8 * grid == iota((QUAD, 128), 0) >> 6, 1.0, 0.0).astype(BF16)
+        mine = pl.ds(pl.multiple_of(grid * 8, 8), 8)
         skip = skip_ref[...]
-        back[...] = rin_ref[...].astype(F32)
+        after = rin_ref[...].astype(F32)
         state = sin_ref[...].astype(F32)
+        spreads = []
         for chunk in range(chunks):
             part = slice(chunk * CHUNK, chunk * CHUNK + CHUNK)
             states[chunk] = state
+            spreads.append(spread(cols[part], 0) + spread(cols[part], 8))
+            _, cum, _, step = spreads[chunk]
             if chunk + 1 < chunks:
-                _, cum = spread(cols[part], 0)
-                _, step = spread(cols[part], 8)
                 end = cum[CHUNK - 1 : CHUNK]
                 fed = (x_ref[part, :].astype(F32) * (jnp.exp(end - cum) * step)).astype(BF16)
                 state = jnp.exp(end) * state + mm(bt_ref[:, part], fed)
-        skip_sum = jnp.zeros((1, QUAD), F32)
-        bias_sum = jnp.zeros((8, 1), F32)
-        rate_sum = jnp.zeros((8, 1), F32)
+        skip_sum = jnp.zeros((8, QUAD), F32)
         for chunk in range(chunks - 1, -1, -1):
             part = slice(chunk * CHUNK, chunk * CHUNK + CHUNK)
             x_f = x_ref[part, :].astype(F32)
             dm = dm_ref[part, :]
             dm_f = dm.astype(F32)
-            cum_wide, cum = spread(cols[part], 0)
-            step_wide, step = spread(cols[part], 8)
+            cum_wide, cum, _, step = spreads[chunk]
             end = cum[CHUNK - 1 : CHUNK]
-            after = back[...]
             after_low = after.astype(BF16)
             state = states[chunk]
             left = jnp.exp(end - cum)
             grown = dm_f * jnp.exp(cum)
             grown_low = grown.astype(BF16)
             faded = x_f * left
+            fed = x_f * step
             from_after = mm(b_ref[part, :], after_low)
             from_state = mm(c_ref[part, :], state.astype(BF16))
             d_b[part, :] += mm_nt((faded * step).astype(BF16), after_low)
             d_c[part, :] += mm_nt(grown_low, state.astype(BF16))
-            marks = mm((grown * from_state).astype(BF16), ones_v) + mm((faded * from_after).astype(BF16), ones_u)
+            products[0, part, :] = (grown * from_state).astype(BF16)
+            products[1, part, :] = (faded * from_after).astype(BF16)
+            within = jnp.zeros((CHUNK, 128), F32)
             pair_sum = jnp.zeros((8, CHUNK), F32)
-            crossing = jnp.zeros((8, 1), F32)
+            cross_sum = jnp.zeros((8, 128), F32)
             cross = jnp.sum(state * after, axis=0, keepdims=True) * jnp.exp(end)
+            summed = None
             pieces = []
             for pair in range(2):
-                x_pair = x_f[:, 128 * pair : 128 * pair + 128]
-                dm_pair = dm_f[:, 128 * pair : 128 * pair + 128]
+                lanes = slice(128 * pair, 128 * pair + 128)
+                x_pair, dm_pair = fed[:, lanes], dm_f[:, lanes]
                 x_both = jnp.concatenate([jnp.where(first, x_pair, 0.0), jnp.where(first, 0.0, x_pair)], axis=0)
                 dm_both = jnp.concatenate([jnp.where(first, dm_pair, 0.0), jnp.where(first, 0.0, dm_pair)], axis=0)
-                d_weights = mm_nt(x_both.astype(BF16), dm[:, 128 * pair : 128 * pair + 128])
+                d_weights = mm_nt(x_both.astype(BF16), dm[:, lanes])
                 kept = []
                 for half in range(2):
                     head = 2 * pair + half
                     cum_row = rows_ref[0, head : head + 1, part]
                     fade = jnp.exp(jnp.where(upper, cum_row - cum_wide[head], -1e30))
                     faded_grad = d_weights[half * CHUNK : half * CHUNK + CHUNK] * fade
-                    d_scores[part, :] += faded_grad * step_wide[head]
+                    summed = faded_grad if summed is None else summed + faded_grad
                     joint = faded_grad * scores[part, :]
-                    marks = marks + jnp.where(lane == head, jnp.sum(joint, axis=1, keepdims=True), 0.0)
-                    row = jnp.sum(joint * step_wide[head], axis=0, keepdims=True)
-                    pair_sum = pair_sum + jnp.where(line == head, row, 0.0)
+                    within = jnp.where(lane == head, jnp.sum(joint, axis=1, keepdims=True), within)
+                    pair_sum = jnp.where(line == head, jnp.sum(joint, axis=0, keepdims=True), pair_sum)
                     kept.append((scores[part, :] * fade).astype(BF16))
-                    low, high = 64 * head, 64 * head + 64
-                    here = (iota((1, QUAD), 1) >= low) & (iota((1, QUAD), 1) < high)
+                    here = (iota((1, QUAD), 1) >> 6) == head
                     amount = jnp.sum(jnp.where(here, cross, 0.0), axis=1, keepdims=True)
-                    crossing = crossing + jnp.where(iota((8, 1), 0) == head, amount, 0.0)
+                    cross_sum = jnp.where(line == head, amount, cross_sum)
                 pieces.append(mm(jnp.concatenate(kept, axis=1), dm_both.astype(BF16)))
+            d_scores[part, :] += summed
+            marks[0, part, :] += within
+            across[mine, part] = pair_sum
+            crossing[chunk, mine, :] = cross_sum
             direct = jnp.concatenate(pieces, axis=1) + left * from_after
+            products[2, part, :] = (x_f * direct).astype(BF16)
             d_x = step * direct + skip * dm_f
             keep(chunk * CHUNK, d_x * slope_ref[part, :].astype(F32))
-            skip_sum = skip_sum + jnp.sum(x_f * dm_f, axis=0, keepdims=True)
-            back[...] = jnp.exp(end) * after + mm(ct_ref[:, part], grown_low)
-            marks = marks.T
-            within, carried, outward = marks[0:8], marks[8:16], marks[16:24]
-            step_rows = rows_ref[0, 8:16, part]
-            change = pair_sum - step_rows * within + carried
-            decay = mm_exact(change, later) + mm_exact(step_rows * outward, before) + crossing
-            d_raw = (within + outward + rows_ref[0, 32:40, part] * decay) * rows_ref[0, 24:32, part]
-            d_step[pl.ds(pl.multiple_of(grid * 8, 8), 8), part] = d_raw
-            bias_sum = bias_sum + jnp.sum(d_raw, axis=1, keepdims=True)
-            rate_sum = rate_sum + jnp.sum(step_rows * decay, axis=1, keepdims=True)
-        heads_ref[0, 0:8, :] = jnp.broadcast_to(bias_sum, (8, 128))
-        heads_ref[0, 8:16, :] = jnp.broadcast_to(rate_sum, (8, 128))
-        finish(skip_sum)
+            skip_sum = skip_sum + fold_rows(x_f * dm_f)
+            after = jnp.exp(end) * after + mm(ct_ref[:, part], grown_low)
+        for at in range(3):
+            marks[1 + at] += mm(products[at], ones)
+        finish(jnp.sum(skip_sum, axis=0, keepdims=True))
 
     @pl.when(grid == QUADS)
     def _():
@@ -562,14 +563,32 @@
 
     @pl.when(grid == QUADS + 1)
     def _():
+        square = (CHUNK, CHUNK)
+        later = jnp.where(iota(square, 0) >= iota(square, 1), 1.0, 0.0).astype(BF16)
+        before = jnp.where(iota(square, 0) < iota(square, 1), 1.0, 0.0).astype(BF16)
         row, column = iota((128, QUAD), 0), iota((128, QUAD), 1)
         pick = (column < HEADS) & (row == 8 * (column >> 2) + (column & 3))
-        turned = d_step[...].T.astype(BF16)
+        pick = jnp.where(pick, 1.0, 0.0).astype(BF16)
+        used = 8 * QUADS
+        bias_sum = jnp.zeros((used, 1), F32)
+        rate_sum = jnp.zeros((used, 1), F32)
         dv_ref[length:, :] = jnp.zeros((HALO, QUAD), BF16)
-        dv_ref[0:length, :] = mm(turned, jnp.where(pick, 1.0, 0.0).astype(BF16)).astype(BF16)
-
-
-def back_call(x_act, d_mixed, slope, v, conv_weight, b_act, c_act, b_turned, c_turned, rows, skip_wide, s_in, r_in, after):
+        for chunk in range(chunks):
+            part = slice(chunk * CHUNK, chunk * CHUNK + CHUNK)
+            within, carried, outward, direct = [marks[at, part, :].T[:used] for at in range(4)]
+            step, sig, rate = [table_ref[at, :, part] for at in range(3)]
+            change = across[0:used, part] - within + carried
+            decay = mm_exact(change, later) + mm_exact(step * outward, before) + crossing[chunk]
+            d_raw = (direct + rate * decay) * sig
+            bias_sum = bias_sum + jnp.sum(d_raw, axis=1, keepdims=True)
+            rate_sum = rate_sum + jnp.sum(step * decay, axis=1, keepdims=True)
+            turned = jnp.concatenate([d_raw, jnp.zeros((128 - used, CHUNK), F32)], axis=0).T.astype(BF16)
+            dv_ref[part, :] = mm(turned, pick).astype(BF16)
+        heads_ref[0] = jnp.broadcast_to(bias_sum, (used, 128))
+        heads_ref[1] = jnp.broadcast_to(rate_sum, (used, 128))
+
+
+def back_call(x_act, d_mixed, slope, v, conv_weight, b_act, c_act, b_turned, c_turned, rows, table, skip_wide, s_in, r_in, after):
     length = x_act.shape[0]
     whole = lambda g: (0, 0)
     quad = lambda g: (0, jnp.minimum(g, QUADS - 1))
@@ -588,7 +607,8 @@
             pl.BlockSpec((length, STATE), whole),
             pl.BlockSpec((STATE, length), whole),
             pl.BlockSpec((STATE, length), whole),
-            pl.BlockSpec((1, 40, length), lead),
+            pl.BlockSpec((1, 24, length), lead),
+            pl.BlockSpec((3, 8 * QUADS, length), lambda g: (0, 0, 0)),
             pl.BlockSpec((1, QUAD), quad),
             pl.BlockSpec((STATE, QUAD), quad),
             pl.BlockSpec((STATE, QUAD), quad),
@@ -597,7 +617,7 @@
         out_specs=[
             pl.BlockSpec((length + HALO, QUAD), lambda g: (0, g)),
             pl.BlockSpec((8, QUAD), block),
-            pl.BlockSpec((1, 16, 128), lead),
+            pl.BlockSpec((2, 8 * QUADS, 128), lambda g: (0, 0, 0)),
         ],
         scratch_shapes=[
             pltpu.VMEM((length, CHUNK), F32),
@@ -605,20 +625,22 @@
             pltpu.VMEM((length, STATE), F32),
             pltpu.VMEM((length, STATE), F32),
             pltpu.VMEM((length // CHUNK, STATE, QUAD), F32),
-            pltpu.VMEM((STATE, QUAD), F32),
+            pltpu.VMEM((3, length, QUAD), BF16),
             pltpu.VMEM((2, length + 2 * HALO, 128), F32),
             pltpu.VMEM((2, length + HALO, 128), F32),
+            pltpu.VMEM((4, length, 128), F32),
             pltpu.VMEM((128, length), F32),
+            pltpu.VMEM((length // CHUNK, 8 * QUADS, 128), F32),
         ],
         out_shape=[
             jax.ShapeDtypeStruct((length + HALO, CONV + QUAD), BF16),
             jax.ShapeDtypeStruct((8, CONV), F32),
-            jax.ShapeDtypeStruct((QUADS, 16, 128), F32),
+            jax.ShapeDtypeStruct((2, 8 * QUADS, 128), F32),
         ],
         compiler_params=pltpu.CompilerParams(vmem_limit_bytes=VMEM_LIMIT),
         cost_estimate=LONG,
         name="ssd_back",
-    )(x_act, d_mixed, slope, v, conv_weight, b_act, c_act, b_turned, c_turned, rows, skip_wide, s_in, r_in, *after)
+    )(x_act, d_mixed, slope, v, conv_weight, b_act, c_act, b_turned, c_turned, rows, table, skip_wide, s_in, r_in, *after)
 
 
 def put_quarters(place_ref, count, step, refs, put):
@@ -632,72 +654,103 @@
                 put(at, refs[2 + 4 * (at - 2) + index])
 
 
-def weight_kernel(height, quarters, count, place_ref, x_ref, *rest):
+def put_quarters(place_ref, count, step, refs, put):
+    near = (step // 2) == place_ref[count]
+    for at in range(2, count):
+        for index in range(4):
+            wanted = near if index < 2 else jnp.logical_not(near)
+
+            @pl.when(wanted & (step % 2 == index % 2))
+            def _():
+                put(at, refs[2 + 4 * (at - 2) + index])
+
+
+def weight_kernel(height, split, count, place_ref, x_ref, *rest):
     piece_refs, (out_ref, w_ref) = rest[:-2], rest[-2:]
 
     def put(at, ref):
         w_ref[:, pl.ds(pl.multiple_of(place_ref[at] * height, 128), height)] = ref[...]
 
-    for at in range(2 if quarters else count):
+    for at in range(2 if split else count):
         put(at, piece_refs[at])
-    if quarters:
-        put_quarters(place_ref, count, pl.program_id(0), piece_refs, put)
+    for at in range(2, count if split else 2):
+        for index in range(2):
+
+            @pl.when(pl.program_id(0) == index)
+            def _():
+                put(at, piece_refs[2 + 2 * (at - 2) + index])
+
     out_ref[...] = mm_nt(x_ref[...], w_ref[...]).astype(BF16)
 
 
-def weight_call(x, pieces, places, count, width, block, quarters, name):
+def weight_call(x, pieces, places, count, width, block, name, split="", into=None):
     rows, depth = x.shape
     height = pieces[0].shape[1]
 
+    def block_of(g, place):
+        if not split:
+            return g
+        side = place[count]
+        if split == "halves":
+            return jnp.where(g == 0, side, 1 - side)
+        return 2 * (1 - side if split == "far" else side) + g
+
     def spec(at):
-        if not quarters or at < 2:
-            return pl.BlockSpec((block, height), lambda g, place: (g, 0))
-        return pl.BlockSpec((block, height), lambda g, place: (0, 0))
-
+        if split and at >= 2:
+            return pl.BlockSpec((block, height), lambda g, place: (0, 0))
+        return pl.BlockSpec((block, height), lambda g, place: (block_of(g, place), 0))
+
+    extra = [] if into is None else [into]
     grid_spec = pltpu.PrefetchScalarGridSpec(
         num_scalar_prefetch=1,
-        grid=(width // block,),
-        in_specs=[pl.BlockSpec((rows, depth), lambda g, place: (0, 0))] + [spec(at) for at in range(len(pieces))],
-        out_specs=pl.BlockSpec((rows, block), lambda g, place: (0, g)),
+        grid=(2 if split else width // block,),
+        in_specs=[pl.BlockSpec((rows, depth), lambda g, place: (0, 0))]
+        + [spec(at) for at in range(len(pieces))]
+        + [pl.BlockSpec(memory_space=pl.ANY)] * len(extra),
+        out_specs=pl.BlockSpec((rows, block), lambda g, place: (0, block_of(g, place))),
         scratch_shapes=[pltpu.VMEM((block, depth), BF16)],
     )
     return pl.pallas_call(
-        functools.partial(weight_kernel, height, quarters, count),
+        functools.partial(weight_kernel, height, split, count),
         grid_spec=grid_spec,
         out_shape=jax.ShapeDtypeStruct((rows, width), BF16),
+        input_output_aliases={2 + len(pieces): 0} if extra else {},
         compiler_params=pltpu.CompilerParams(vmem_limit_bytes=VMEM_LIMIT),
         cost_estimate=COST,
         name=name,
-    )(places, x, *pieces)
+    )(places, x, *pieces, *extra)
 
 
 def weight_back_kernel(place_ref, g_ref, *rest):
-    piece_refs, out_ref = rest[:-1], rest[-1]
-    for at, piece_ref in enumerate(piece_refs):
+    out_ref = rest[-1]
+    for at, piece_ref in enumerate(rest[: place_ref.shape[0]]):
 
         @pl.when(pl.program_id(0) == at)
         def _():
             out_ref[...] = mm_nt(g_ref[...], piece_ref[...])
 
 
-def weight_back_call(g, pieces, places):
-    rows, width = g.shape
+def weight_back_call(g, pieces, places, width, into=None):
+    rows, depth = g.shape
     block = pieces[0].shape[0]
+    extra = [] if into is None else [into]
     grid_spec = pltpu.PrefetchScalarGridSpec(
         num_scalar_prefetch=1,
         grid=(len(pieces),),
-        in_specs=[pl.BlockSpec((rows, width), lambda k, place: (0, 0))]
-        + [pl.BlockSpec((block, width), lambda k, place: (0, 0))] * len(pieces),
+        in_specs=[pl.BlockSpec((rows, depth), lambda k, place: (0, 0))]
+        + [pl.BlockSpec((block, depth), lambda k, place: (0, 0))] * len(pieces)
+        + [pl.BlockSpec(memory_space=pl.ANY)] * len(extra),
         out_specs=pl.BlockSpec((rows, block), lambda k, place: (0, place[k])),
     )
     return pl.pallas_call(
         weight_back_kernel,
         grid_spec=grid_spec,
-        out_shape=jax.ShapeDtypeStruct((rows, block * len(pieces)), F32),
+        out_shape=jax.ShapeDtypeStruct((rows, width), F32),
+        input_output_aliases={2 + len(pieces): 0} if extra else {},
         compiler_params=pltpu.CompilerParams(vmem_limit_bytes=VMEM_LIMIT),
         cost_estimate=COST,
         name="d_normed_out",
-    )(places, g, *pieces)
+    )(places, g, *pieces, *extra)
 
 
 def pick_kernel(table_ref, own, other, own_halo, other_halo, own_out, other_out, halo_out):
@@ -749,12 +802,12 @@
             outs[2 * part + 1][...] = total[half:].astype(BF16)
 
 
-def grad_call(lefts, right, right_other, width, halo, name):
+def grad_call(lefts, right, right_other, first, width, halo, name):
     own, other, edge = lefts
     _, rows, length = own.shape
     lead = lambda g: (g, 0, 0)
-    column = lambda g: (0, g)
-    below = lambda g: (length // HALO, g)
+    column = lambda g: (0, first + g)
+    below = lambda g: (length // HALO, first + g)
     specs = [pl.BlockSpec((1, rows, length), lead)] * 2
     args = [own, other]
     if halo:
@@ -853,37 +906,51 @@
     )(tie(places, after), *([x] * len(pieces)), *pieces, tokens)
 
 
-def columns_kernel(count, place_ref, g_ref, *refs):
-    w_refs, (out_ref, w) = refs[:count], refs[-2:]
+def columns_kernel(count, split, place_ref, g_ref, *refs):
+    out_ref, w = refs[-2:]
     height = D // count
-    for at in range(count):
-        w[:, pl.ds(pl.multiple_of(place_ref[at] * height, 128), height)] = w_refs[at][...]
+    step = pl.program_id(0)
+
+    def put(at, ref):
+        w[:, pl.ds(pl.multiple_of(place_ref[at] * height, 128), height)] = ref[...]
+
+    for at in range(2 if split else count):
+        put(at, refs[at])
+    for at in range(2, count if split else 2):
+        for index in range(2):
+            side = place_ref[count]
+
+            @pl.when(step == (side if index == 0 else 1 - side))
+            def _():
+                put(at, refs[2 + 2 * (at - 2) + index])
+
     product = mm(g_ref[...], w[...])
 
-    @pl.when(pl.program_id(0) == 0)
+    @pl.when(step == 0)
     def _():
         out_ref[...] = product
 
-    @pl.when(pl.program_id(0) > 0)
+    @pl.when(step > 0)
     def _():
         out_ref[...] += product
 
 
-def columns_call(g, pieces, places):
+def columns_call(g, pieces, places, count, split):
     length, depth = g.shape
     height = pieces[0].shape[1]
-    count = len(pieces)
     block = depth // 2
     down = lambda k, place: (k, 0)
+    whole = lambda k, place: (0, 0)
     grid_spec = pltpu.PrefetchScalarGridSpec(
         num_scalar_prefetch=1,
-        grid=(depth // block,),
-        in_specs=[pl.BlockSpec((length, block), lambda k, place: (0, k))] + [pl.BlockSpec((block, height), down)] * count,
-        out_specs=pl.BlockSpec((length, D), lambda k, place: (0, 0)),
+        grid=(2,),
+        in_specs=[pl.BlockSpec((length, block), lambda k, place: (0, k))]
+        + [pl.BlockSpec((block, height), whole if split and at >= 2 else down) for at in range(len(pieces))],
+        out_specs=pl.BlockSpec((length, D), whole),
         scratch_shapes=[pltpu.VMEM((block, D), BF16)],
     )
     return pl.pallas_call(
-        functools.partial(columns_kernel, count),
+        functools.partial(columns_kernel, count, split),
         grid_spec=grid_spec,
         out_shape=jax.ShapeDtypeStruct((length, D), F32),
         compiler_params=pltpu.CompilerParams(vmem_limit_bytes=VMEM_LIMIT),
@@ -1016,15 +1083,10 @@
     def across(value):
         return move(value, lambda s, f: (s, f ^ 1))
 
-    def gather(value, crossed, middle, near):
-        pieces = [(value, 0), (crossed, 1)] + near
-        pieces += [(across(tie(piece, middle)), step ^ 1) for piece, step in near]
-        return [piece for piece, _ in pieces], jnp.stack([shard ^ step for _, step in pieces]).astype(jnp.int32)
-
     def send_near(value):
         return [(move(value, lambda s, f: (s, f ^ step)), step) for step in range(2, shards, 2)]
 
-    def gather_quarters(value, crossed, middle):
+    def gather_quarters(value, crossed):
         quarter = value.shape[0] // 4
         side = rank & 1
         remote = []
@@ -1034,20 +1096,28 @@
                 sent = lax.dynamic_slice_in_dim(value, (2 * side + part) * quarter, quarter, 0)
                 near.append(move(tie(sent, *near), lambda s, f: (s, f ^ step)))
                 far.append(move(near[part], lambda s, f: (s ^ 1, f)))
-            remote.append((near + far, step))
-        remote += [([across(piece) for piece in pieces[:-1]] + [across(tie(pieces[-1], *middle))], step ^ 1) for pieces, step in remote]
-        places = [shard, shard ^ 1] + [shard ^ step for _, step in remote] + [side]
-        return [value, crossed] + sum([pieces for pieces, _ in remote], []), jnp.stack(places).astype(jnp.int32)
-
-    def in_order(pieces, places, quarters):
+            remote.append((near, far))
+        crossed_near = [[across(piece) for piece in near] for near, _ in remote]
+        places = [shard, shard ^ 1] + [shard ^ step for step in range(2, shards, 2)]
+        places += [shard ^ step ^ 1 for step in range(2, shards, 2)] + [side]
+
+        def pieces(ready):
+            made = [value, crossed] + [piece for near, far in remote for piece in near + far]
+            for near, (_, far) in zip(crossed_near, remote):
+                made += near + [None] * 2 if ready is None else near + [across(far[0]), across(tie(far[1], ready))]
+            return made
+
+        return pieces, jnp.stack(places).astype(jnp.int32)
+
+    def in_order(pieces, places, cuts):
         height = pieces[0].shape[1]
         whole = jnp.zeros((pieces[0].shape[0], height * shards), pieces[0].dtype)
         for at, piece in enumerate(pieces):
             first, place = 0, at
-            if quarters and at >= 2:
-                place, index = 2 + (at - 2) // 4, (at - 2) % 4
-                side = places[shards] if index < 2 else 1 - places[shards]
-                first = (2 * side + index % 2) * piece.shape[0]
+            if at >= 2:
+                place, index = 2 + (at - 2) // (2 * cuts), (at - 2) % (2 * cuts)
+                side = places[shards] if index < cuts else 1 - places[shards]
+                first = (cuts * side + index % cuts) * piece.shape[0]
             whole = lax.dynamic_update_slice(whole, piece, (first, places[place] * height))
         return [whole], jnp.zeros((1,), jnp.int32)
 
@@ -1089,12 +1159,10 @@
         core = shard & 1
         return lax.dynamic_index_in_dim(blocks, core, 1, False), lax.dynamic_index_in_dim(blocks, 1 - core, 1, False)
 
-    own, other = halves(normed.T)
-    own_halo, other_halo = halves(normed_long[:HALO].T)
-    lefts = pick_call(table, own, across(other), own_halo, across(other_halo))
     own_g = turned[:INNER]
     crossed_v, crossed_g, crossed_o = across(own_v), across(own_g), across(w_out)
-    pieces_v, places_v = gather_quarters(own_v, crossed_v, (lefts[0], crossed_v, crossed_g, crossed_o))
+    pieces_of, places_v = gather_quarters(tie(own_v, halo), crossed_v)
+    pieces_v = pieces_of(None)
 
     def flip(axis, bit):
         return lambda s, f: (s ^ bit, f) if axis == "seq" else (s, f ^ bit)
@@ -1103,16 +1171,22 @@
         return [(kept, move(tie(sent, *ahead), flip(*orders[part][0]))) for part, (kept, sent) in enumerate(terms)]
 
     lanes_whole = w_in.shape[0] % 128 == 0
-    last_near, first_far, count = pieces_v[3], pieces_v[4], shards
-    if not lanes_whole:
-        pieces_v, places_v = in_order(pieces_v, places_v, True)
-        count = 1
-    projected = weight_call(normed_long, pieces_v, places_v, count, width_v, width_v // 4, lanes_whole, "project_v")
-    near_g = send_near(tie(own_g, last_near, first_far))
-    pieces_g, places = gather(own_g, crossed_g, projected, near_g)
-    near_o = send_near(tie(w_out, near_g[0][0], projected))
+    last_near, first_far, places = pieces_v[3], pieces_v[4], places_v
+    side = rank & 1
+    half_g = lax.dynamic_slice_in_dim(own_g, side * (INNER // 2), INNER // 2, 0)
+    near_g = [piece for piece, _ in send_near(tie(half_g, last_near, first_far))]
+    if lanes_whole:
+        pick_v = lambda first: pieces_v[:2] + sum([pieces_v[at + first : at + first + 2] for at in range(2, len(pieces_v), 4)], [])
+        projected = weight_call(normed_long, pick_v(0), places_v, shards, width_v, width_v // 4, "project_near", "near")
+        pieces_v = pieces_of(projected)
+        projected = weight_call(normed_long, pick_v(2), places_v, shards, width_v, width_v // 4, "project_far", "far", projected)
+    else:
+        pieces_v, places_v = in_order(pieces_of(last_near), places_v, 2)
+        projected = weight_call(normed_long, pieces_v, places_v, 1, width_v, width_v // 4, "project_v")
+    far_g = [move(tie(piece, projected), lambda s, f: (s ^ 1, f)) for piece in near_g]
+    near_o = send_near(tie(w_out, near_g[0], projected))
     lanes = lambda vec: jnp.pad(vec, (0, 128 - HEADS)).reshape(1, 128)
-    rows, ecd, decay_all = step_call(projected, lanes(dt_bias), lanes(a_log))
+    rows, step_table, ecd, decay_all = step_call(projected, lanes(dt_bias), lanes(a_log))
     v = projected
     made = conv_call(ranks, v, conv_weight, conv_bias.reshape(1, CONV), rows, decay_all, ())
     x_act, slope, b_act, c_act, b_turned, c_turned, states = made
@@ -1120,29 +1194,43 @@
     y_inside = inside_call(x_act, b_act, c_act, b_turned, rows, skip_wide)
     carried, totals = carry_call(ranks, exchange(states), None, [y_inside])
     s_in = exchange(carried)
-    pieces_o, _ = gather(w_out, crossed_o, carried, near_o)
-    places_o = places
-    if not lanes_whole:
-        pieces_g, places = in_order(pieces_g, places, False)
-    gate_in = weight_call(normed, pieces_g, places, count, INNER, INNER // 3, False, "project_gate")
-    d_normed_out = weight_back_call(cotan, pieces_o, places_o)
+    pieces_g = [own_g, crossed_g] + sum([[near, far] for near, far in zip(near_g, far_g)], [])
+    for near, far in zip(near_g, far_g):
+        pieces_g += [across(tie(near, projected)), across(tie(far, carried))]
+    if lanes_whole:
+        places_g, count_g = places, shards
+        gate_in = weight_call(tie(normed, carried), pieces_g, places_g, count_g, INNER, INNER // 2, "project_gate", "halves")
+    else:
+        (pieces_g, places_g), count_g = in_order(pieces_g, places, 1), 1
+        gate_in = weight_call(normed, pieces_g, places_g, count_g, INNER, INNER // 2, "project_gate")
+    places_o = places[:shards]
+    pieces_o = [w_out, crossed_o] + [piece for piece, _ in near_o]
+    pieces_o += [across(tie(piece, carried)) for piece, _ in near_o]
+    height_o = w_out.shape[0] * shards
+    d_normed_out = weight_back_call(tie(cotan, gate_in, s_in), pieces_o[:2], places_o[:2], height_o)
+    d_normed_out = weight_back_call(tie(cotan, s_in), pieces_o[2:], places_o[2:], height_o, d_normed_out)
     made = gate_call(y_inside, gate_in, d_normed_out, c_act, c_turned, ecd, out_gain.reshape(1, INNER), s_in)
     normed_out, d_gate, d_mixed, d_gain_out, states = made
     d_w_out = lax.dot_general(normed_out, cotan, TN, preferred_element_type=F32).astype(BF16)
     d_w_out_sum = lax.psum_scatter(d_w_out, both, scatter_dimension=0, tiled=True).astype(F32)
-    gate_terms = grad_call(lefts, d_gate, across(d_gate), INNER // 3, False, "d_w_gate")
-    (carried,) = carry_call(ranks, exchange(states), totals, [d_w_out] + [kept for kept, _ in gate_terms])
-    block_out = residual_call(normed_out, pieces_o, places_o, tokens, carried)
+    d_gate_other = across(d_gate)
+    block_out = residual_call(normed_out, pieces_o, places_o, tokens, states)
+    own, other = halves(tie(normed, states).T)
+    own_halo, other_halo = halves(tie(normed_long[:HALO], states).T)
+    other, other_halo = across(other), across(other_halo)
+    (carried,) = carry_call(ranks, exchange(states), totals, [d_w_out, block_out])
+    lefts = pick_call(tie(table, carried), own, other, own_halo, other_halo)
+    gate_terms = grad_call(lefts, d_gate, d_gate_other, 0, INNER // 3, False, "d_w_gate")
     r_in = exchange(carried)
     gate_parts = first_step(gate_terms, r_in)
     d_v_long, sums, heads = back_call(
-        x_act, d_mixed, slope, v, conv_weight, b_act, c_act, b_turned, c_turned, rows, skip_wide, s_in, r_in, [block_out]
+        x_act, d_mixed, slope, v, conv_weight, b_act, c_act, b_turned, c_turned, rows, step_table, skip_wide, s_in, r_in, [kept for kept, _ in gate_terms]
     )
     d_v_long = tie(d_v_long, *[got for _, got in gate_parts])
     spill = move(d_v_long[tokens.shape[1] :], lambda s, f: (s - 1, f) if s > 0 else None)
-    part = columns_call(tie(d_gate, d_v_long), pieces_g, places)
+    part = columns_call(tie(d_gate, d_v_long), pieces_g, places_g, count_g, lanes_whole)
     d_v_other = tie(across(d_v_long), spill, part)
-    rest_terms = grad_call(lefts, d_v_long, d_v_other, (CONV + 128) // 3, True, "d_w_rest")
+    rest_terms = grad_call(lefts, d_v_long, d_v_other, 0, (CONV + 128) // 3, True, "d_w_rest")
     rest_parts = first_step(rest_terms)
     d_tokens, d_norm_gain = tokens_call(
         part, tie(d_v_long, rest_terms[0][0]), spill, pieces_v, places_v, lanes_whole,
@@ -1150,12 +1238,13 @@
     )
     rest_parts = [(kept, tie(got, d_tokens)) for kept, got in rest_parts]
 
+    heads = heads[:, :, 0].reshape(2, QUADS, 8)[:, :, :4].reshape(2, HEADS)
     d_skip = sums[KW + 1, :INNER].reshape(HEADS, HEAD_DIM).sum(axis=1)
     pieces = [
         sums[:KW].reshape(-1),
         sums[KW],
-        heads[:, 0:4, 0].reshape(-1),
-        heads[:, 8:12, 0].reshape(-1) * -jnp.exp(a_log),
+        heads[0],
+        heads[1] * -jnp.exp(a_log),
         d_skip,
         d_gain_out.reshape(-1),
     ]

time: 490 us -> 478 us (0.976)
  waiting for transfers between devices: 95.3 us -> 85 us
  starting transfers between devices: 68.1 us -> 74.9 us
  local copies, waits for them, and re-layouts: 43.2 us -> 37.9 us
    pallas_call x1, Pallas kernels: 52.4 us -> 41.7 us  [back_call(): pl.pallas_call(back_kernel, grid=(QUADS + 2,), in_specs=[pl.BlockSpec((le...]
    all_to_all x4, waiting for transfers between devices: 13.4 us -> 3.56 us  [exchange(): lax.all_to_all(states, 'seq', split_axis=0, concat_axis=0, tiled=True)]
    ppermute x48 -> x50, starting transfers between devices: 46.2 us -> 52.6 us  [move(): return lax.ppermute(value, both, pairs)]
    pallas_call x3 -> x4, Pallas kernels: 36.3 us -> 41.5 us  [the longest x3 28.7 us: weight_call(): pl.pallas_call(functools.partial(weight_kernel, height, split, count), gr...]
    unnamed x74 -> x96, local copies, waits for them, and re-layouts: 11.7 us -> 15.4 us
    pallas_call x1 -> x2, Pallas kernels: 11.9 us -> 15.2 us  [weight_back_call(): pl.pallas_call(weight_back_kernel, grid_spec=grid_spec, out_shape=jax.Sha...]
    ppermute x48 -> x50, waiting for transfers between devices: 81.9 us -> 81.4 us  [move(): return lax.ppermute(value, both, pairs)]
  transfers between devices with their start and end apart: 53 -> 55, of which waited for: 23 -> 22; matrix products, arithmetic and copies ran while one was open for 10% -> 8% of each run, Pallas kernels for 47% -> 46%
where the time goes in v4:
time: 478 us; the launch traced here: 469 us
  Pallas kernels  240 us (50%)
  waiting for transfers between devices  85 us (18%)
  starting transfers between devices  74.9 us (16%)
  local copies, waits for them, and re-layouts  37.9 us (8%)
  between operations  15 us (3%)
  matrix products  9.52 us (2%)
  other arithmetic  7.04 us (1%)
    ppermute x50, waiting for transfers between devices, move(): return lax.ppermute(value, both, pairs)  81.4 us
    ppermute x50, starting transfers between devices, move(): return lax.ppermute(value, both, pairs)  52.6 us
    pallas_call x1, Pallas kernels, back_call(): pl.pallas_call(back_kernel, grid=(QUADS + 2,), in_specs=[pl.BlockSpec((le...  41.7 us
    pallas_call x3, Pallas kernels, weight_call(): pl.pallas_call(functools.partial(weight_kernel, height, split, count), gr...  28.7 us
    pallas_call x7, Pallas kernels, fold_call(): pl.pallas_call(functools.partial(fold_kernel, parts, groups, which), in_s...  25.7 us
    pallas_call x2, Pallas kernels, grad_call(): pl.pallas_call(functools.partial(grad_kernel, halo), grid=(3,), in_specs=...  24.4 us
    all_to_all x4, starting transfers between devices, exchange(): lax.all_to_all(states, 'seq', split_axis=0, concat_axis=0, tiled=True)  22.3 us
    pallas_call x1, Pallas kernels, tokens_call(): pl.pallas_call(functools.partial(tokens_kernel, count, quarters), grid_sp...  19.5 us
  transfers between devices with their start and end apart: 55, of which 22 were waited for; matrix products, arithmetic and copies ran while one was open for 8% of the time, Pallas kernels for 46%

profile of v4, /device:TPU:0, one launch (start us, length us, event | category | flops | bytes accessed | tf_op | source)
XLA Modules:
  0.0 469.1 jit_solution(15198930198151909389)
XLA Ops:
  10.8 4.4 collective-permute-start
  19.5 15.6 %collective-permute-done.2.rest_2_.refs_8_ = bf16[896,384]{1,0:T(8,128)(2,1)} collective-permute-done((bf16[896,384]{1,0:T(8,128)(2,1)S(1)}, bf16[896,384]{1,0:T(8,128)(2,1)}, u32[]{:S(2)}, u32[]{:S(2)}) %collective-permute-start.2) | collective-permute-done | bytes 688160 | tf_op jit(solution)/shard_map/ppermute | solution.py:1081
  36.6 2.4 collective-permute-start.3
  39.0 3.3 slice.90.rest_0_.refs_0_
  43.0 2.5 constant_dynamic-slice_fusion.2
  46.0 5.4 %collective-permute-done.4.rest_3_.refs_9_ = bf16[896,384]{1,0:T(8,128)(2,1)} collective-permute-done((bf16[896,384]{1,0:T(8,128)(2,1)}, bf16[896,384]{1,0:T(8,128)(2,1)}, u32[]{:S(2)}, u32[]{:S(2)}) %collective-permute-start.4) | collective-permute-done | bytes 688160 | tf_op jit(solution)/shard_map/ppermute | solution.py:1081
  51.4 2.5 collective-permute-start.5
  58.3 8.6 %project_near.1.rest_6_ = bf16[528,3584]{1,0:T(8,128)(2,1)} custom-call(s32[5]{0:T(128)} %stack.139.place_ref, bf16[528,1536]{1,0:T(8,128)(2,1)} %fusion.2.x_ref, bf16[3584,384]{1,0:T(8,128)(2,1)} %copy-done, bf16[3584,384]{1,0:T(8,128)(2,1)} %collective-permute-done.1.rest_1_.refs_7_, bf16[896,384]{1,0:T(8,128)(2,1)} %collective-permute-done.2.rest_2_.refs_8_, ...), custom_call_target="tpu_custom_call" | custom-call | flops 1000000 | bytes 1000000 | tf_op jit(solution)/shard_map/project_near/pallas_call | solution.py:713
  66.9 3.3 collective-permute-done.5.rest_3_.refs_11_
  73.3 8.6 %project_far.1.dt_ref.v_ref = bf16[528,3584]{1,0:T(8,128)(2,1)} custom-call(s32[5]{0:T(128)} %stack.139.place_ref, bf16[528,1536]{1,0:T(8,128)(2,1)} %fusion.2.x_ref, bf16[3584,384]{1,0:T(8,128)(2,1)} %copy-done, bf16[3584,384]{1,0:T(8,128)(2,1)} %collective-permute-done.1.rest_1_.refs_7_, ...), custom_call_target="tpu_custom_call", output_to_operand_aliasing={{}: (8, {})} | custom-call | flops 1000000 | bytes 1000000 | tf_op jit(solution)/shard_map/project_far/pallas_call | solution.py:713
  85.0 2.7 steps.1
  87.7 14.1 %conv_states.1 = (bf16[512,3072]{1,0:T(8,128)(2,1)}, bf16[512,3328]{1,0:T(8,128)(2,1)}, bf16[512,128]{1,0:T(8,128)(2,1)}, bf16[512,128]{1,0:T(8,128)(2,1)}, bf16...) custom-call(bf16[528,3584]{1,0:T(8,128)(2,1)} %project_far.1.dt_ref.v_ref, ...), custom_call_target="tpu_custom_call" | custom-call | flops 1000000 | bytes 1000000 | tf_op jit(solution)/shard_map/conv_states/pallas_call | solution.py:199
  101.8 5.8 %all-to-all-start = ((bf16[8,16,3328]{2,1,0:T(8,128)(2,1)}), bf16[8,16,3328]{2,1,0:T(8,128)(2,1)S(1)}, u32[]{:S(2)}, u32[]{:S(2)}) async-start(bf16[8,16,3328]{2,1,0:T(8,128)(2,1)} %bitcast.89), calls=%async_computation | async-start | bytes 1703936 | tf_op jit(solution)/shard_map/all_to_all | solution.py:1125
  110.9 15.4 %ssd_inside.1.rest_0_.y_ref = f32[512,3072]{1,0:T(8,128)} custom-call(bf16[512,3072]{1,0:T(8,128)(2,1)} %get-tuple-element.103.x_ref, bf16[512,128]{1,0:T(8,128)(2,1)} %get-tuple-element.104.b_ref, bf16[512,128]{1,0:T(8,128)(2,1)} %get-tuple-element.105.c_ref, bf16[128,512]{1,0:T(8,128)(2,1)} %get-tuple-element.106.bt_ref, ...), custom_call_target="tpu_custom_call" | custom-call | flops 1000000 | bytes 1000000 | tf_op jit(solution)/shard_map/ssd_inside/pallas_call | solution.py:315
  126.2 3.0 all-to-all-done
  130.1 2.8 carry.1
  132.9 2.7 collective-permute-done.15.rest_0_.refs_6_
  135.6 6.6 %all-to-all-start.1 = ((bf16[8,16,3072]{2,1,0:T(8,128)(2,1)}), bf16[8,16,3072]{2,1,0:T(8,128)(2,1)}, u32[]{:S(2)}, u32[]{:S(2)}) async-start(bf16[8,16,3072]{2,1,0:T(8,128)(2,1)} %bitcast.91), calls=%async_computation.1 | async-start | bytes 1572864 | tf_op jit(solution)/shard_map/all_to_all | solution.py:1125
  146.2 2.6 slice.89.x_ref
  151.0 11.5 %project_gate.1.gate_ref = bf16[512,3072]{1,0:T(8,128)(2,1)} custom-call(s32[5]{0:T(128)} %stack.139.place_ref, bf16[512,1536]{1,0:T(8,128)(2,1)} %slice.89.x_ref, bf16[3072,384]{1,0:T(8,128)(2,1)} %slice.90.rest_0_.refs_0_, bf16[3072,384]{1,0:T(8,128)(2,1)} %collective-permute-done.10.rest_1_.refs_1_, bf16[1536,384]{1,0:T(8,128)(2,1)} %copy-done.6, ...), custom_call_target="tpu_custom_call" | custom-call | flops 1000000 | bytes 1000000 | tf_op jit(solution)/shard_map/project_gate/pallas_call | solution.py:713
  163.0 7.6 %d_normed_out.2.rest_2_ = f32[512,3072]{1,0:T(8,128)} custom-call(s32[2]{0:T(128)} %pad_add_fusion.3.place_ref, bf16[512,1536]{1,0:T(8,128)(2,1)} %bitcast.77, bf16[768,1536]{1,0:T(8,128)(2,1)} %refs_4_.2, bf16[768,1536]{1,0:T(8,128)(2,1)} %collective-permute-done.17.rest_1_.refs_5_), custom_call_target="tpu_custom_call" | custom-call | flops 1000000 | bytes 1000000 | tf_op jit(solution)/shard_map/d_normed_out/pallas_call | solution.py:745
  170.6 7.6 %d_normed_out.3.dn_ref = f32[512,3072]{1,0:T(8,128)} custom-call(s32[2]{0:T(128)} %pad_add_fusion.2.place_ref, bf16[512,1536]{1,0:T(8,128)(2,1)} %bitcast.78, bf16[768,1536]{1,0:T(8,128)(2,1)} %collective-permute-done.15.rest_0_.refs_6_, bf16[768,1536]{1,0:T(8,128)(2,1)} %collective-permute-done.16.rest_1_.refs_7_, ...), custom_call_target="tpu_custom_call", output_to_operand_aliasing={{}: (4, {})} | custom-call | flops 1000000 | bytes 1000000 | tf_op jit(solution)/shard_map/d_normed_out/pallas_call | solution.py:745
  178.2 15.3 %gated_norm.1 = (bf16[512,3072]{1,0:T(8,128)(2,1)}, bf16[512,3072]{1,0:T(8,128)(2,1)}, bf16[512,3072]{1,0:T(8,128)(2,1)}, f32[1,3072]{1,0:T(1,128)}, bf16[128,3072]{1,0:T(8,128)(2,1)}) custom-call(f32[512,3072]{1,0:T(8,128)} %ssd_inside.1.rest_0_.y_ref, bf16[512,3072]{1,0:T(8,128)(2,1)} %project_gate.1.gate_ref, f32[512,3072]{1,0:T(8,128)} %d_normed_out.3.dn_ref, ...), custom_call_target="tpu_custom_call" | custom-call | flops 1000000 | bytes 1000000 | tf_op jit(solution)/shard_map/gated_norm/pallas_call | solution.py:396
  193.6 4.0 all-to-all-start.2
  197.9 9.5 %convolution_convert_fusion.rest_1_ = bf16[3072,1536]{1,0:T(8,128)(2,1)} fusion(bf16[512,3072]{1,0:T(8,128)(2,1)} %get-tuple-element.121.refs_0_.refs_1_.refs_2_.refs_3_, bf16[1,512,1536]{2,1,0:T(8,128)(2,1)S(1)} %copy-done.5), kind=kOutput, calls=%fused_computation | convolution fusion | flops 4836556800 | bytes 14155776 | tf_op jit(solution)/shard_map/dot_general | solution.py:1214
  207.4 11.3 %block_out.1.rest_2_ = f32[1,512,1536]{2,1,0:T(8,128)} custom-call(s32[4]{0:T(128)} %pad_add_fusion.1.place_ref, bf16[512,3072]{1,0:T(8,128)(2,1)} %get-tuple-element.121.refs_0_.refs_1_.refs_2_.refs_3_, bf16[512,3072]{1,0:T(8,128)(2,1)} %get-tuple-element.121.refs_0_.refs_1_.refs_2_.refs_3_, ...), custom_call_target="tpu_custom_call" | custom-call | flops 40000000000 | bytes 1000000 | tf_op jit(solution)/shard_map/block_out/pallas_call | solution.py:899
  219.6 2.7 carry_back.1
  222.4 5.9 %all-to-all-start.3 = ((bf16[8,16,3072]{2,1,0:T(8,128)(2,1)}), bf16[8,16,3072]{2,1,0:T(8,128)(2,1)}, u32[]{:S(2)}, u32[]{:S(2)}) async-start(bf16[8,16,3072]{2,1,0:T(8,128)(2,1)} %bitcast.87), calls=%async_computation.3 | async-start | bytes 1572864 | tf_op jit(solution)/shard_map/all_to_all | solution.py:1125
  234.2 7.6 %pick_rows.1 = (bf16[3,16,48,512]{3,2,1,0:T(8,128)(2,1)}, bf16[3,16,48,512]{3,2,1,0:T(8,128)(2,1)}, bf16[3,16,48,32]{3,2,1,0:T(8,128)(2,1)}) custom-call(s32[3,16]{1,0:T(4,128)} %pad_add_fusion.table_ref, bf16[16,48,512]{2,1,0:T(8,128)(2,1)} %get-tuple-element.188.own, bf16[16,48,512]{2,1,0:T(8,128)(2,1)} %copy-done.30, bf16[16,48,16]{2,1,0:T(8,128)(2,1)} %bitcast.90, ...), custom_call_target="tpu_custom_call" | custom-call | flops 1000000 | bytes 1000000 | tf_op jit(solution)/shard_map/pick_rows/pallas_call | solution.py:773
  241.8 10.5 %d_w_gate.1 = (bf16[384,1024]{1,0:T(8,128)(2,1)}, bf16[384,1024]{1,0:T(8,128)(2,1)}, bf16[384,1024]{1,0:T(8,128)(2,1)}, bf16[384,1024]{1,0:T(8,128)(2,1)}, bf16[...) custom-call(bf16[3,768,512]{2,1,0:T(8,128)(2,1)} %bitcast.79, bf16[3,768,512]{2,1,0:T(8,128)(2,1)} %bitcast.81, ...), custom_call_target="tpu_custom_call" | custom-call | flops 1000000 | bytes 1000000 | tf_op jit(solution)/shard_map/d_w_gate/pallas_call | solution.py:821
  257.2 41.7 %ssd_back.1 = (bf16[528,3584]{1,0:T(8,128)(2,1)}, f32[8,3328]{1,0:T(8,128)}, f32[2,96,128]{2,1,0:T(8,128)}) custom-call(bf16[512,3072]{1,0:T(8,128)(2,1)} %get-tuple-element.103.x_ref, bf16[512,3072]{1,0:T(8,128)(2,1)} %get-tuple-element.123.dm_ref, bf16[512,3328]{1,0:T(8,128)(2,1)} %get-tuple-element.124.slope_ref, ...), custom_call_target="tpu_custom_call" | custom-call | flops 40000000000 | bytes 1000000 | tf_op jit(solution)/shard_map/ssd_back/pallas_call | solution.py:597
  303.1 12.7 %d_normed_gate.1.refs_0_ = f32[512,1536]{1,0:T(8,128)} custom-call(s32[5]{0:T(128)} %stack.139.place_ref, bf16[512,3072]{1,0:T(8,128)(2,1)} %get-tuple-element.143.refs_2_.g_ref, bf16[3072,384]{1,0:T(8,128)(2,1)} %slice.90.rest_0_.refs_0_, bf16[3072,384]{1,0:T(8,128)(2,1)} %collective-permute-done.10.rest_1_.refs_1_, bf16[1536,384]{1,0:T(8,128)(2,1)} %copy-done.6, ...), custom_call_target="tpu_custom_call" | custom-call | flops 1000000 | bytes 1000000 | tf_op jit(solution)/shard_map/d_normed_gate/pallas_call | solution.py:952
  317.8 13.9 %d_w_rest.1 = (bf16[384,1152]{1,0:T(8,128)(2,1)}, bf16[384,1152]{1,0:T(8,128)(2,1)}, bf16[384,1152]{1,0:T(8,128)(2,1)}, bf16[384,1152]{1,0:T(8,128)(2,1)}, bf16[...) custom-call(bf16[3,768,512]{2,1,0:T(8,128)(2,1)} %bitcast.80, bf16[3,768,512]{2,1,0:T(8,128)(2,1)} %bitcast.82, ...), custom_call_target="tpu_custom_call" | custom-call | flops 1000000 | bytes 1000000 | tf_op jit(solution)/shard_map/d_w_rest/pallas_call | solution.py:821
  331.7 2.4 collective-permute-start.26
  337.4 19.5 %d_tokens.1 = (f32[1,512,1536]{2,1,0:T(8,128)}, f32[1,1536]{1,0:T(1,128)}) custom-call(s32[5]{0:T(128)} %stack.139.place_ref, f32[512,1536]{1,0:T(8,128)} %d_normed_gate.1.refs_0_, bf16[528,3584]{1,0:T(8,128)(2,1)} %get-tuple-element.147.refs_3_.refs_5_.refs_1_, bf16[16,3584]{1,0:T(8,128)(2,1)} %copy-done.35, bf16[1,512,1536]{2,1,0:T(8,128)(2,1)} %refs_3_.1, ...), custom_call_target="tpu_custom_call" | custom-call | flops 1000000 | bytes 1000000 | tf_op jit(solution)/shard_map/d_tokens/pallas_call | solution.py:1045
  357.9 5.6 %collective-permute-done.28.refs_11_ = bf16[384,1152]{1,0:T(8,128)(2,1)S(1)} collective-permute-done((bf16[384,1152]{1,0:T(8,128)(2,1)}, bf16[384,1152]{1,0:T(8,128)(2,1)S(1)}, u32[]{:S(2)}, u32[]{:S(2)}) %collective-permute-start.28) | collective-permute-done | bytes 884768 | tf_op jit(solution)/shard_map/ppermute | solution.py:1081
  364.5 5.5 %fold_sent.3 = (bf16[192,2176]{1,0:T(8,128)(2,1)}, bf16[192,2176]{1,0:T(8,128)(2,1)}, bf16[192,2176]{1,0:T(8,128)(2,1)}) custom-call(bf16[384,1024]{1,0:T(8,128)(2,1)} %get-tuple-element.132.rest_0_.refs_0_, bf16[384,1024]{1,0:T(8,128)(2,1)} %copy-done.19, bf16[384,1152]{1,0:T(8,128)(2,1)} %get-tuple-element.146.refs_2_, bf16[384,1152]{1,0:T(8,128)(2,1)} %copy-done.10, ...), custom_call_target="tpu_custom_call" | custom-call | flops 1000000 | bytes 1000000 | tf_op jit(solution)/shard_map/fold_sent/pallas_call | solution.py:866
  373.6 5.5 %fold_kept.3 = (bf16[192,2176]{1,0:T(8,128)(2,1)}, bf16[192,2176]{1,0:T(8,128)(2,1)}, bf16[192,2176]{1,0:T(8,128)(2,1)}) custom-call(bf16[384,1024]{1,0:T(8,128)(2,1)} %get-tuple-element.132.rest_0_.refs_0_, bf16[384,1024]{1,0:T(8,128)(2,1)} %copy-done.19, bf16[384,1152]{1,0:T(8,128)(2,1)} %get-tuple-element.146.refs_2_, bf16[384,1152]{1,0:T(8,128)(2,1)} %copy-done.10, ...), custom_call_target="tpu_custom_call" | custom-call | flops 1000000 | bytes 1000000 | tf_op jit(solution)/shard_map/fold_kept/pallas_call | solution.py:866
  379.1 13.1 %collective-permute-done.46 = f32[160,128]{1,0:T(8,128)S(1)} collective-permute-done((f32[160,128]{1,0:T(8,128)S(1)}, f32[160,128]{1,0:T(8,128)S(1)}, u32[]{:S(2)}, u32[]{:S(2)}) %collective-permute-start.46) | collective-permute-done | bytes 81952 | tf_op jit(solution)/shard_map/ppermute | solution.py:1081
  399.1 3.6 fold_kept.4
  407.5 3.6 fold_sent.4
  413.7 6.1 %collective-permute-done.38.refs_1_ = bf16[96,2176]{1,0:T(8,128)(2,1)S(1)} collective-permute-done((bf16[96,2176]{1,0:T(8,128)(2,1)}, bf16[96,2176]{1,0:T(8,128)(2,1)S(1)}, u32[]{:S(2)}, u32[]{:S(2)}) %collective-permute-start.38) | collective-permute-done | bytes 417824 | tf_op jit(solution)/shard_map/ppermute | solution.py:1081
  422.2 2.5 fold_kept.5
  427.8 2.5 fold_sent.5
  435.1 8.6 %collective-permute-done.41 = f32[1,1536]{1,0:T(1,128)S(1)} collective-permute-done((f32[1,1536]{1,0:T(1,128)S(1)}, f32[1,1536]{1,0:T(1,128)S(1)}, u32[]{:S(2)}, u32[]{:S(2)}) %collective-permute-start.41) | collective-permute-done | bytes 6176 | tf_op jit(solution)/shard_map/ppermute | solution.py:1081
  449.9 4.5 collective-permute-done.43.refs_3_
  454.4 2.6 collective-permute-done.44.refs_5_
  457.6 2.5 fold_last.1
  (243 shorter events, 91.9 us)
Async XLA Ops:
  9.5 47.7 %collective-permute-start.1 = (bf16[3584,384]{1,0:T(8,128)(2,1)S(1)}, bf16[3584,384]{1,0:T(8,128)(2,1)}, u32[]{:S(2)}, u32[]{:S(2)}) collective-permute-start(bf16[3584,384]{1,0:T(8,128)(2,1)S(1)} %pad.15.rest_0_.refs_6_), channel_id=1, source_target_pairs={{0,1},{1,0},{2,3},{3,2},{4,5},{5,4},{6,7},{7,6},{8,9},{9,8},{10,11... | collective-permute-start | bytes 8257544 | tf_op jit(solution)/shard_map/ppermute | solution.py:1081
  10.8 6.1 %collective-permute-start = (bf16[16,1536]{1,0:T(8,128)(2,1)S(1)}, bf16[16,1536]{1,0:T(8,128)(2,1)S(1)}, u32[]{:S(2)}, u32[]{:S(2)}) collective-permute-start(bf16[16,1536]{1,0:T(8,128)(2,1)S(1)} %slice_bitcast_fusion), channel_id=1, source_target_pairs={{0,4},{1,5},{2,6},{3,7},{4,8},{5,9},{6,10},{7,11},{8,12},{9,13},{1... | collective-permute-start | bytes 147464 | tf_op jit(solution)/shard_map/ppermute | solution.py:1081
  18.0 17.1 %collective-permute-start.2 = (bf16[896,384]{1,0:T(8,128)(2,1)S(1)}, bf16[896,384]{1,0:T(8,128)(2,1)}, u32[]{:S(2)}, u32[]{:S(2)}) collective-permute-start(bf16[896,384]{1,0:T(8,128)(2,1)S(1)} %get-tuple-element.186), channel_id=1, source_target_pairs={{0,2},{1,3},{2,0},{3,1},{4,6},{5,7},{6,4},{7,5},{8,10},{9,11},{10,... | collective-permute-start | bytes 2064392 | tf_op jit(solution)/shard_map/ppermute | solution.py:1081
  35.0 16.4 %collective-permute-start.4 = (bf16[896,384]{1,0:T(8,128)(2,1)}, bf16[896,384]{1,0:T(8,128)(2,1)}, u32[]{:S(2)}, u32[]{:S(2)}) collective-permute-start(bf16[896,384]{1,0:T(8,128)(2,1)} %get-tuple-element.99), channel_id=1, source_target_pairs={{0,2},{1,3},{2,0},{3,1},{4,6},{5,7},{6,4},{7,5},{8,10},{9,11},{10,... | collective-permute-start | bytes 2064392 | tf_op jit(solution)/shard_map/ppermute | solution.py:1081
  36.6 17.4 %collective-permute-start.3 = (bf16[896,384]{1,0:T(8,128)(2,1)}, bf16[896,384]{1,0:T(8,128)(2,1)S(1)}, u32[]{:S(2)}, u32[]{:S(2)}) collective-permute-start(bf16[896,384]{1,0:T(8,128)(2,1)} %collective-permute-done.2.rest_2_.refs_8_), channel_id=1, source_target_pairs={{0,4},{1,5},{2,6},{3,7},{4,0},{5,1},{6,2},{7,3},{8,12},{9,13},{10,... | collective-permute-start | bytes 2064392 | tf_op jit(solution)/shard_map/ppermute | solution.py:1081
  45.9 11.3 %collective-permute-start.7 = (bf16[896,384]{1,0:T(8,128)(2,1)}, bf16[896,384]{1,0:T(8,128)(2,1)S(1)}, u32[]{:S(2)}, u32[]{:S(2)}) collective-permute-start(bf16[896,384]{1,0:T(8,128)(2,1)} %collective-permute-done.2.rest_2_.refs_8_), channel_id=1, source_target_pairs={{0,1},{1,0},{2,3},{3,2},{4,5},{5,4},{6,7},{7,6},{8,9},{9,8},{10,11... | collective-permute-start | bytes 2064392 | tf_op jit(solution)/shard_map/ppermute | solution.py:1081
  51.4 18.8 %collective-permute-start.5 = (bf16[896,384]{1,0:T(8,128)(2,1)}, bf16[896,384]{1,0:T(8,128)(2,1)S(1)}, u32[]{:S(2)}, u32[]{:S(2)}) collective-permute-start(bf16[896,384]{1,0:T(8,128)(2,1)} %collective-permute-done.4.rest_3_.refs_9_), channel_id=1, source_target_pairs={{0,4},{1,5},{2,6},{3,7},{4,0},{5,1},{6,2},{7,3},{8,12},{9,13},{10,... | collective-permute-start | bytes 2064392 | tf_op jit(solution)/shard_map/ppermute | solution.py:1081
  54.0 28.4 %collective-permute-start.11 = (bf16[1536,384]{1,0:T(8,128)(2,1)}, bf16[1536,384]{1,0:T(8,128)(2,1)S(1)}, u32[]{:S(2)}, u32[]{:S(2)}) collective-permute-start(bf16[1536,384]{1,0:T(8,128)(2,1)} %constant_dynamic-slice_fusion.2), channel_id=1, source_target_pairs={{0,2},{1,3},{2,0},{3,1},{4,6},{5,7},{6,4},{7,5},{8,10},{9,11},{10,... | collective-permute-start | bytes 3538952 | tf_op jit(solution)/shard_map/ppermute | solution.py:1081
  57.2 13.1 %collective-permute-start.6 = (bf16[896,384]{1,0:T(8,128)(2,1)S(1)}, bf16[896,384]{1,0:T(8,128)(2,1)S(1)}, u32[]{:S(2)}, u32[]{:S(2)}) collective-permute-start(bf16[896,384]{1,0:T(8,128)(2,1)S(1)} %collective-permute-done.3.rest_2_.refs_10_), channel_id=1, source_target_pairs={{0,1},{1,0},{2,3},{3,2},{4,5},{5,4},{6,7},{7,6},{8,9},{9,8},{10,11... | collective-permute-start | bytes 2064392 | tf_op jit(solution)/shard_map/ppermute | solution.py:1081
  82.3 53.2 %collective-permute-start.15 = (bf16[768,1536]{1,0:T(8,128)(2,1)}, bf16[768,1536]{1,0:T(8,128)(2,1)}, u32[]{:S(2)}, u32[]{:S(2)}) collective-permute-start(bf16[768,1536]{1,0:T(8,128)(2,1)} %refs_4_.2), channel_id=1, source_target_pairs={{0,2},{1,3},{2,0},{3,1},{4,6},{5,7},{6,4},{7,5},{8,10},{9,11},{10,... | collective-permute-start | bytes 7077896 | tf_op jit(solution)/shard_map/ppermute | solution.py:1081
  101.8 27.4 %all-to-all-start = ((bf16[8,16,3328]{2,1,0:T(8,128)(2,1)}), bf16[8,16,3328]{2,1,0:T(8,128)(2,1)S(1)}, u32[]{:S(2)}, u32[]{:S(2)}) async-start(bf16[8,16,3328]{2,1,0:T(8,128)(2,1)} %bitcast.89), calls=%async_computation | async-start | bytes 1703936 | tf_op jit(solution)/shard_map/all_to_all | solution.py:1125
  107.6 36.8 %collective-permute-start.12 = (bf16[1536,384]{1,0:T(8,128)(2,1)}, bf16[1536,384]{1,0:T(8,128)(2,1)}, u32[]{:S(2)}, u32[]{:S(2)}) collective-permute-start(bf16[1536,384]{1,0:T(8,128)(2,1)} %copy-done.6), channel_id=1, source_target_pairs={{0,4},{1,5},{2,6},{3,7},{4,0},{5,1},{6,2},{7,3},{8,12},{9,13},{10,... | collective-permute-start | bytes 3538952 | tf_op jit(solution)/shard_map/ppermute | solution.py:1081
  109.6 39.3 %collective-permute-start.10 = (bf16[3072,384]{1,0:T(8,128)(2,1)S(1)}, bf16[3072,384]{1,0:T(8,128)(2,1)}, u32[]{:S(2)}, u32[]{:S(2)}) collective-permute-start(bf16[3072,384]{1,0:T(8,128)(2,1)S(1)} %copy-done.1), channel_id=1, source_target_pairs={{0,1},{1,0},{2,3},{3,2},{4,5},{5,4},{6,7},{7,6},{8,9},{9,8},{10,11... | collective-permute-start | bytes 7077896 | tf_op jit(solution)/shard_map/ppermute | solution.py:1081
  109.6 53.4 %collective-permute-start.17 = (bf16[768,1536]{1,0:T(8,128)(2,1)}, bf16[768,1536]{1,0:T(8,128)(2,1)}, u32[]{:S(2)}, u32[]{:S(2)}) collective-permute-start(bf16[768,1536]{1,0:T(8,128)(2,1)} %refs_4_.2), channel_id=1, source_target_pairs={{0,1},{1,0},{2,3},{3,2},{4,5},{5,4},{6,7},{7,6},{8,9},{9,8},{10,11... | collective-permute-start | bytes 7077896 | tf_op jit(solution)/shard_map/ppermute | solution.py:1081
  135.6 35.1 %collective-permute-start.16 = (bf16[768,1536]{1,0:T(8,128)(2,1)}, bf16[768,1536]{1,0:T(8,128)(2,1)}, u32[]{:S(2)}, u32[]{:S(2)}) collective-permute-start(bf16[768,1536]{1,0:T(8,128)(2,1)} %collective-permute-done.15.rest_0_.refs_6_), channel_id=1, source_target_pairs={{0,1},{1,0},{2,3},{3,2},{4,5},{5,4},{6,7},{7,6},{8,9},{9,8},{10,11... | collective-permute-start | bytes 7077896 | tf_op jit(solution)/shard_map/ppermute | solution.py:1081
  135.6 27.4 %all-to-all-start.1 = ((bf16[8,16,3072]{2,1,0:T(8,128)(2,1)}), bf16[8,16,3072]{2,1,0:T(8,128)(2,1)}, u32[]{:S(2)}, u32[]{:S(2)}) async-start(bf16[8,16,3072]{2,1,0:T(8,128)(2,1)} %bitcast.91), calls=%async_computation.1 | async-start | bytes 1572864 | tf_op jit(solution)/shard_map/all_to_all | solution.py:1125
  142.2 6.7 %collective-permute-start.13 = (bf16[1536,384]{1,0:T(8,128)(2,1)S(1)}, bf16[1536,384]{1,0:T(8,128)(2,1)S(1)}, u32[]{:S(2)}, u32[]{:S(2)}) collective-permute-start(bf16[1536,384]{1,0:T(8,128)(2,1)S(1)} %copy-done.7), channel_id=1, source_target_pairs={{0,1},{1,0},{2,3},{3,2},{4,5},{5,4},{6,7},{7,6},{8,9},{9,8},{10,11... | collective-permute-start | bytes 3538952 | tf_op jit(solution)/shard_map/ppermute | solution.py:1081
  193.6 25.1 %all-to-all-start.2 = ((bf16[8,16,3072]{2,1,0:T(8,128)(2,1)}), bf16[8,16,3072]{2,1,0:T(8,128)(2,1)S(1)}, u32[]{:S(2)}, u32[]{:S(2)}) async-start(bf16[8,16,3072]{2,1,0:T(8,128)(2,1)} %bitcast.92), calls=%async_computation.2 | async-start | bytes 1572864 | tf_op jit(solution)/shard_map/all_to_all | solution.py:1125
  197.6 262.6 %reduce-scatter.2.cloned.1.call-start = ((), (), s32[]{:S(2)}) async-start(), calls=%async_computation.5 | async-start | bytes 9732096 | tf_op jit(solution)/shard_map/reduce_scatter | solution.py:1215
  197.6 44.2 %collective-permute-start.20 = (bf16[512,3072]{1,0:T(8,128)(2,1)}, bf16[512,3072]{1,0:T(8,128)(2,1)}, u32[]{:S(2)}, u32[]{:S(2)}) collective-permute-start(bf16[512,3072]{1,0:T(8,128)(2,1)} %get-tuple-element.143.refs_2_.g_ref), channel_id=1, source_target_pairs={{0,1},{1,0},{2,3},{3,2},{4,5},{5,4},{6,7},{7,6},{8,9},{9,8},{10,11... | collective-permute-start | bytes 9437192 | tf_op jit(solution)/shard_map/ppermute | solution.py:1081
  222.4 30.0 %all-to-all-start.3 = ((bf16[8,16,3072]{2,1,0:T(8,128)(2,1)}), bf16[8,16,3072]{2,1,0:T(8,128)(2,1)}, u32[]{:S(2)}, u32[]{:S(2)}) async-start(bf16[8,16,3072]{2,1,0:T(8,128)(2,1)} %bitcast.87), calls=%async_computation.3 | async-start | bytes 1572864 | tf_op jit(solution)/shard_map/all_to_all | solution.py:1125
  252.3 46.5 %collective-permute-start.23 = (bf16[384,1024]{1,0:T(8,128)(2,1)}, bf16[384,1024]{1,0:T(8,128)(2,1)S(1)}, u32[]{:S(2)}, u32[]{:S(2)}) collective-permute-start(bf16[384,1024]{1,0:T(8,128)(2,1)} %get-tuple-element.141), channel_id=1, source_target_pairs={{0,8},{1,9},{2,10},{3,11},{4,12},{5,13},{6,14},{7,15},{8,0},{9,1},... | collective-permute-start | bytes 2359304 | tf_op jit(solution)/shard_map/ppermute | solution.py:1081
  254.4 44.5 %collective-permute-start.22 = (bf16[384,1024]{1,0:T(8,128)(2,1)}, bf16[384,1024]{1,0:T(8,128)(2,1)S(1)}, u32[]{:S(2)}, u32[]{:S(2)}) collective-permute-start(bf16[384,1024]{1,0:T(8,128)(2,1)} %get-tuple-element.139), channel_id=1, source_target_pairs={{0,2},{1,3},{2,0},{3,1},{4,6},{5,7},{6,4},{7,5},{8,10},{9,11},{10,... | collective-permute-start | bytes 2359304 | tf_op jit(solution)/shard_map/ppermute | solution.py:1081
  255.7 43.2 %collective-permute-start.21 = (bf16[384,1024]{1,0:T(8,128)(2,1)}, bf16[384,1024]{1,0:T(8,128)(2,1)S(1)}, u32[]{:S(2)}, u32[]{:S(2)}) collective-permute-start(bf16[384,1024]{1,0:T(8,128)(2,1)} %get-tuple-element.137), channel_id=1, source_target_pairs={{0,4},{1,5},{2,6},{3,7},{4,0},{5,1},{6,2},{7,3},{8,12},{9,13},{10,... | collective-permute-start | bytes 2359304 | tf_op jit(solution)/shard_map/ppermute | solution.py:1081
  300.7 15.2 %collective-permute-start.24 = (bf16[528,3584]{1,0:T(8,128)(2,1)}, bf16[528,3584]{1,0:T(8,128)(2,1)S(1)}, u32[]{:S(2)}, u32[]{:S(2)}) collective-permute-start(bf16[528,3584]{1,0:T(8,128)(2,1)} %get-tuple-element.147.refs_3_.refs_5_.refs_1_), channel_id=1, source_target_pairs={{0,1},{1,0},{2,3},{3,2},{4,5},{5,4},{6,7},{7,6},{8,9},{9,8},{10,11... | collective-permute-start | bytes 11354120 | tf_op jit(solution)/shard_map/ppermute | solution.py:1081
  301.6 14.3 %collective-permute-start.25 = (bf16[16,3584]{1,0:T(8,128)(2,1)S(1)}, bf16[16,3584]{1,0:T(8,128)(2,1)S(1)}, u32[]{:S(2)}, u32[]{:S(2)}) collective-permute-start(bf16[16,3584]{1,0:T(8,128)(2,1)S(1)} %slice.74), channel_id=1, source_target_pairs={{4,0},{5,1},{6,2},{7,3},{8,4},{9,5},{10,6},{11,7},{12,8},{13,9},{1... | collective-permute-start | bytes 344072 | tf_op jit(solution)/shard_map/ppermute | solution.py:1081
  331.7 25.3 %collective-permute-start.26 = (bf16[384,1152]{1,0:T(8,128)(2,1)}, bf16[384,1152]{1,0:T(8,128)(2,1)S(1)}, u32[]{:S(2)}, u32[]{:S(2)}) collective-permute-start(bf16[384,1152]{1,0:T(8,128)(2,1)} %get-tuple-element.150), channel_id=1, source_target_pairs={{0,4},{1,5},{2,6},{3,7},{4,0},{5,1},{6,2},{7,3},{8,12},{9,13},{10,... | collective-permute-start | bytes 2654216 | tf_op jit(solution)/shard_map/ppermute | solution.py:1081
  334.1 23.8 %collective-permute-start.27 = (bf16[384,1152]{1,0:T(8,128)(2,1)}, bf16[384,1152]{1,0:T(8,128)(2,1)S(1)}, u32[]{:S(2)}, u32[]{:S(2)}) collective-permute-start(bf16[384,1152]{1,0:T(8,128)(2,1)} %get-tuple-element.153), channel_id=1, source_target_pairs={{0,2},{1,3},{2,0},{3,1},{4,6},{5,7},{6,4},{7,5},{8,10},{9,11},{10,... | collective-permute-start | bytes 2654216 | tf_op jit(solution)/shard_map/ppermute | solution.py:1081
  335.2 28.3 %collective-permute-start.28 = (bf16[384,1152]{1,0:T(8,128)(2,1)}, bf16[384,1152]{1,0:T(8,128)(2,1)S(1)}, u32[]{:S(2)}, u32[]{:S(2)}) collective-permute-start(bf16[384,1152]{1,0:T(8,128)(2,1)} %get-tuple-element.156), channel_id=1, source_target_pairs={{0,8},{1,9},{2,10},{3,11},{4,12},{5,13},{6,14},{7,15},{8,0},{9,1},... | collective-permute-start | bytes 2654216 | tf_op jit(solution)/shard_map/ppermute | solution.py:1081
  336.7 36.0 %collective-permute-start.45 = (f32[160,128]{1,0:T(8,128)S(1)}, f32[160,128]{1,0:T(8,128)S(1)}, u32[]{:S(2)}, u32[]{:S(2)}) collective-permute-start(f32[160,128]{1,0:T(8,128)S(1)} %pad_bitcast_fusion), channel_id=1, source_target_pairs={{0,1},{1,0},{2,3},{3,2},{4,5},{5,4},{6,7},{7,6},{8,9},{9,8},{10,11... | collective-permute-start | bytes 245768 | tf_op jit(solution)/shard_map/ppermute | solution.py:1081
  370.0 27.6 %collective-permute-start.32 = (bf16[192,2176]{1,0:T(8,128)(2,1)}, bf16[192,2176]{1,0:T(8,128)(2,1)S(1)}, u32[]{:S(2)}, u32[]{:S(2)}) collective-permute-start(bf16[192,2176]{1,0:T(8,128)(2,1)} %get-tuple-element.160), channel_id=1, source_target_pairs={{0,2},{1,3},{2,0},{3,1},{4,6},{5,7},{6,4},{7,5},{8,10},{9,11},{10,... | collective-permute-start | bytes 2506760 | tf_op jit(solution)/shard_map/ppermute | solution.py:1081
  370.6 27.0 %collective-permute-start.33 = (bf16[192,2176]{1,0:T(8,128)(2,1)}, bf16[192,2176]{1,0:T(8,128)(2,1)S(1)}, u32[]{:S(2)}, u32[]{:S(2)}) collective-permute-start(bf16[192,2176]{1,0:T(8,128)(2,1)} %get-tuple-element.162), channel_id=1, source_target_pairs={{0,8},{1,9},{2,10},{3,11},{4,12},{5,13},{6,14},{7,15},{8,0},{9,1},... | collective-permute-start | bytes 2506760 | tf_op jit(solution)/shard_map/ppermute | solution.py:1081
  371.5 26.2 %collective-permute-start.34 = (bf16[192,2176]{1,0:T(8,128)(2,1)}, bf16[192,2176]{1,0:T(8,128)(2,1)S(1)}, u32[]{:S(2)}, u32[]{:S(2)}) collective-permute-start(bf16[192,2176]{1,0:T(8,128)(2,1)} %get-tuple-element.164), channel_id=1, source_target_pairs={{0,4},{1,5},{2,6},{3,7},{4,0},{5,1},{6,2},{7,3},{8,12},{9,13},{10,... | collective-permute-start | bytes 2506760 | tf_op jit(solution)/shard_map/ppermute | solution.py:1081
  372.8 19.4 %collective-permute-start.46 = (f32[160,128]{1,0:T(8,128)S(1)}, f32[160,128]{1,0:T(8,128)S(1)}, u32[]{:S(2)}, u32[]{:S(2)}) collective-permute-start(f32[160,128]{1,0:T(8,128)S(1)} %fusion.4), channel_id=1, source_target_pairs={{0,4},{1,5},{2,6},{3,7},{4,0},{5,1},{6,2},{7,3},{8,12},{9,13},{10,... | collective-permute-start | bytes 245768 | tf_op jit(solution)/shard_map/ppermute | solution.py:1081
  379.1 14.8 %collective-permute-start.31 = (f32[1,1536]{1,0:T(1,128)S(1)}, f32[1,1536]{1,0:T(1,128)S(1)}, u32[]{:S(2)}, u32[]{:S(2)}) collective-permute-start(f32[1,1536]{1,0:T(1,128)S(1)} %copy-done.42), channel_id=1, source_target_pairs={{0,5},{1,4},{2,7},{3,6},{4,1},{5,0},{6,3},{7,2},{8,13},{9,12},{10,... | collective-permute-start | bytes 18440 | tf_op jit(solution)/shard_map/ppermute | solution.py:1081
  395.8 10.3 %collective-permute-start.47 = (f32[160,128]{1,0:T(8,128)S(1)}, f32[160,128]{1,0:T(8,128)S(1)}, u32[]{:S(2)}, u32[]{:S(2)}) collective-permute-start(f32[160,128]{1,0:T(8,128)S(1)} %fusion.8), channel_id=1, source_target_pairs={{0,2},{1,3},{2,0},{3,1},{4,6},{5,7},{6,4},{7,5},{8,10},{9,11},{10,... | collective-permute-start | bytes 245768 | tf_op jit(solution)/shard_map/ppermute | solution.py:1081
  402.6 9.2 %collective-permute-start.37 = (f32[1,1536]{1,0:T(1,128)S(1)}, f32[1,1536]{1,0:T(1,128)S(1)}, u32[]{:S(2)}, u32[]{:S(2)}) collective-permute-start(f32[1,1536]{1,0:T(1,128)S(1)} %add_add_fusion.1), channel_id=1, source_target_pairs={{0,10},{1,11},{2,8},{3,9},{4,14},{5,15},{6,12},{7,13},{8,2},{9,3},... | collective-permute-start | bytes 18440 | tf_op jit(solution)/shard_map/ppermute | solution.py:1081
  403.8 9.4 %collective-permute-start.36 = (f32[1,1536]{1,0:T(1,128)S(1)}, f32[1,1536]{1,0:T(1,128)S(1)}, u32[]{:S(2)}, u32[]{:S(2)}) collective-permute-start(f32[1,1536]{1,0:T(1,128)S(1)} %add_add_fusion.1), channel_id=1, source_target_pairs={{0,8},{1,9},{2,10},{3,11},{4,12},{5,13},{6,14},{7,15},{8,0},{9,1},... | collective-permute-start | bytes 18440 | tf_op jit(solution)/shard_map/ppermute | solution.py:1081
  404.4 9.3 %collective-permute-start.35 = (f32[1,1536]{1,0:T(1,128)S(1)}, f32[1,1536]{1,0:T(1,128)S(1)}, u32[]{:S(2)}, u32[]{:S(2)}) collective-permute-start(f32[1,1536]{1,0:T(1,128)S(1)} %add_add_fusion.1), channel_id=1, source_target_pairs={{0,2},{1,3},{2,0},{3,1},{4,6},{5,7},{6,4},{7,5},{8,10},{9,11},{10,... | collective-permute-start | bytes 18440 | tf_op jit(solution)/shard_map/ppermute | solution.py:1081
  406.1 20.5 %collective-permute-start.48 = (f32[160,128]{1,0:T(8,128)S(1)}, f32[160,128]{1,0:T(8,128)S(1)}, u32[]{:S(2)}, u32[]{:S(2)}) collective-permute-start(f32[160,128]{1,0:T(8,128)S(1)} %add.205), channel_id=1, source_target_pairs={{0,8},{1,9},{2,10},{3,11},{4,12},{5,13},{6,14},{7,15},{8,0},{9,1},... | collective-permute-start | bytes 245768 | tf_op jit(solution)/shard_map/ppermute | solution.py:1081
  411.1 8.7 %collective-permute-start.38 = (bf16[96,2176]{1,0:T(8,128)(2,1)}, bf16[96,2176]{1,0:T(8,128)(2,1)S(1)}, u32[]{:S(2)}, u32[]{:S(2)}) collective-permute-start(bf16[96,2176]{1,0:T(8,128)(2,1)} %get-tuple-element.167), channel_id=1, source_target_pairs={{0,8},{1,9},{2,10},{3,11},{4,12},{5,13},{6,14},{7,15},{8,0},{9,1},... | collective-permute-start | bytes 1253384 | tf_op jit(solution)/shard_map/ppermute | solution.py:1081
  411.8 8.5 %collective-permute-start.39 = (bf16[96,2176]{1,0:T(8,128)(2,1)}, bf16[96,2176]{1,0:T(8,128)(2,1)S(1)}, u32[]{:S(2)}, u32[]{:S(2)}) collective-permute-start(bf16[96,2176]{1,0:T(8,128)(2,1)} %get-tuple-element.169), channel_id=1, source_target_pairs={{0,4},{1,5},{2,6},{3,7},{4,0},{5,1},{6,2},{7,3},{8,12},{9,13},{10,... | collective-permute-start | bytes 1253384 | tf_op jit(solution)/shard_map/ppermute | solution.py:1081
  413.2 8.3 %collective-permute-start.40 = (bf16[96,2176]{1,0:T(8,128)(2,1)}, bf16[96,2176]{1,0:T(8,128)(2,1)S(1)}, u32[]{:S(2)}, u32[]{:S(2)}) collective-permute-start(bf16[96,2176]{1,0:T(8,128)(2,1)} %get-tuple-element.171), channel_id=1, source_target_pairs={{0,2},{1,3},{2,0},{3,1},{4,6},{5,7},{6,4},{7,5},{8,10},{9,11},{10,... | collective-permute-start | bytes 1253384 | tf_op jit(solution)/shard_map/ppermute | solution.py:1081
  424.8 18.9 %collective-permute-start.41 = (f32[1,1536]{1,0:T(1,128)S(1)}, f32[1,1536]{1,0:T(1,128)S(1)}, u32[]{:S(2)}, u32[]{:S(2)}) collective-permute-start(f32[1,1536]{1,0:T(1,128)S(1)} %add_add_fusion), channel_id=1, source_target_pairs={{0,16},{1,17},{2,18},{3,19},{4,20},{5,21},{6,22},{7,23},{8,24},{9,... | collective-permute-start | bytes 18440 | tf_op jit(solution)/shard_map/ppermute | solution.py:1081
  426.6 18.8 %collective-permute-start.49 = (f32[160,128]{1,0:T(8,128)S(1)}, f32[160,128]{1,0:T(8,128)S(1)}, u32[]{:S(2)}, u32[]{:S(2)}) collective-permute-start(f32[160,128]{1,0:T(8,128)S(1)} %add.206), channel_id=1, source_target_pairs={{0,16},{1,17},{2,18},{3,19},{4,20},{5,21},{6,22},{7,23},{8,24},{9,... | collective-permute-start | bytes 245768 | tf_op jit(solution)/shard_map/ppermute | solution.py:1081
  430.3 19.6 %collective-permute-start.42 = (bf16[48,2176]{1,0:T(8,128)(2,1)}, bf16[48,2176]{1,0:T(8,128)(2,1)S(1)}, u32[]{:S(2)}, u32[]{:S(2)}) collective-permute-start(bf16[48,2176]{1,0:T(8,128)(2,1)} %get-tuple-element.174), channel_id=1, source_target_pairs={{0,16},{1,17},{2,18},{3,19},{4,20},{5,21},{6,22},{7,23},{8,24},{9,... | collective-permute-start | bytes 626696 | tf_op jit(solution)/shard_map/ppermute | solution.py:1081
  432.1 22.3 %collective-permute-start.43 = (bf16[48,2176]{1,0:T(8,128)(2,1)}, bf16[48,2176]{1,0:T(8,128)(2,1)S(1)}, u32[]{:S(2)}, u32[]{:S(2)}) collective-permute-start(bf16[48,2176]{1,0:T(8,128)(2,1)} %get-tuple-element.176), channel_id=1, source_target_pairs={{0,16},{1,17},{2,18},{3,19},{4,20},{5,21},{6,22},{7,23},{8,24},{9,... | collective-permute-start | bytes 626696 | tf_op jit(solution)/shard_map/ppermute | solution.py:1081
  433.2 23.7 %collective-permute-start.44 = (bf16[48,2176]{1,0:T(8,128)(2,1)}, bf16[48,2176]{1,0:T(8,128)(2,1)S(1)}, u32[]{:S(2)}, u32[]{:S(2)}) collective-permute-start(bf16[48,2176]{1,0:T(8,128)(2,1)} %get-tuple-element.178), channel_id=1, source_target_pairs={{0,16},{1,17},{2,18},{3,19},{4,20},{5,21},{6,22},{7,23},{8,24},{9,... | collective-permute-start | bytes 626696 | tf_op jit(solution)/shard_map/ppermute | solution.py:1081
  (55 other events, 423.9 us)
Sparse Core Ops, SparseCore 0:
  207.5 153.0 reduce-scatter.1

commit v5 on v4

--- a/solution.py
+++ b/solution.py
@@ -831,46 +831,57 @@
     return [(made[2 * part], made[2 * part + 1]) for part in range(3)]
 
 
-def fold_kernel(parts, groups, which, *refs):
-    ins, outs = refs[: 2 * parts * groups], refs[2 * parts * groups :]
-    for part in range(parts):
-        at = 0
-        for group in range(groups):
-            kept, got = ins[2 * (part * groups + group)], ins[2 * (part * groups + group) + 1]
-            rows, width = kept.shape
-            half = rows // 2
-            lines = slice(0, rows) if which == "last" else slice(0, half) if which == "kept" else slice(half, rows)
-            total = kept[lines, :].astype(F32) + got[lines, :].astype(F32)
-            if which == "last":
-                gate = INNER // parts
-                other = width - gate
-                outs[0][:, part * gate : (part + 1) * gate] = total[:, :gate]
-                begin = INNER + part * other
-                end = min(begin + other, outs[0].shape[1])
-                outs[0][:, begin:end] = total[:, gate : gate + end - begin]
-            else:
-                outs[part][:, at : at + width] = total.astype(BF16)
-            at += width
-
-
-def fold_call(pairs, which, width=0):
-    parts, groups = len(pairs), len(pairs[0])
-    arrays = [array for part in pairs for pair in part for array in pair]
-    rows = arrays[0].shape[0]
-    half = rows // 2
-    if which == "last":
+def fold_kernel(counts, rows, first, last, *refs):
+    at = 0
+
+    def added(count):
+        nonlocal at
+        total = refs[at][first : first + rows, :].astype(F32)
+        for ref in refs[at + 1 : at + count]:
+            total = total + ref[first : first + rows, :].astype(F32)
+        at += count
+        return total
+
+    parts = len(counts)
+    for part, (gate_count, rest_count, both_count) in enumerate(counts):
+        gate, rest = added(gate_count), added(rest_count)
+        wide = gate.shape[1]
+        if both_count:
+            both = added(both_count)
+            gate, rest = gate + both[:, :wide], rest + both[:, wide:]
+        if last:
+            out_ref = refs[-1]
+            out_ref[:, part * wide : (part + 1) * wide] = gate
+            begin = parts * wide + part * rest.shape[1]
+            end = min(begin + rest.shape[1], out_ref.shape[1])
+            out_ref[:, begin:end] = rest[:, : end - begin]
+        else:
+            refs[part - parts][:, :wide] = gate.astype(BF16)
+            refs[part - parts][:, wide:] = rest.astype(BF16)
+
+
+def fold_call(parts, first, rows, width=0):
+    arrays = [array for terms in parts for group in terms for array in group]
+    counts = [tuple(len(group) for group in terms) for terms in parts]
+    if rows % 16 == 0 and first % rows == 0:
+        specs = [pl.BlockSpec((rows, array.shape[1]), lambda g: (first // rows, 0)) for array in arrays]
+        begin = 0
+    else:
+        specs = [pl.BlockSpec(array.shape, lambda g: (0, 0)) for array in arrays]
+        begin = first
+    if width:
         shapes = [jax.ShapeDtypeStruct((rows, width), F32)]
     else:
-        shapes = [jax.ShapeDtypeStruct((half, sum(kept.shape[1] for kept, _ in part)), BF16) for part in pairs]
-    vmem = pl.BlockSpec(memory_space=pltpu.VMEM)
+        shapes = [jax.ShapeDtypeStruct((rows, gate[0].shape[1] + rest[0].shape[1]), BF16) for gate, rest, _ in parts]
     return pl.pallas_call(
-        functools.partial(fold_kernel, parts, groups, which),
-        in_specs=[vmem] * len(arrays),
-        out_specs=[vmem] * len(shapes),
+        functools.partial(fold_kernel, counts, rows, begin, bool(width)),
+        grid=(1,),
+        in_specs=specs,
+        out_specs=[pl.BlockSpec(shape.shape, lambda g: (0, 0)) for shape in shapes],
         out_shape=shapes,
         compiler_params=pltpu.CompilerParams(vmem_limit_bytes=VMEM_LIMIT),
         cost_estimate=COST,
-        name="fold_" + which,
+        name="fold",
     )(*arrays)
 
 
@@ -1228,15 +1239,10 @@
     )
     d_v_long = tie(d_v_long, *[got for _, got in gate_parts])
     spill = move(d_v_long[tokens.shape[1] :], lambda s, f: (s - 1, f) if s > 0 else None)
-    part = columns_call(tie(d_gate, d_v_long), pieces_g, places_g, count_g, lanes_whole)
-    d_v_other = tie(across(d_v_long), spill, part)
+    d_v_other = tie(across(d_v_long), spill)
     rest_terms = grad_call(lefts, d_v_long, d_v_other, 0, (CONV + 128) // 3, True, "d_w_rest")
     rest_parts = first_step(rest_terms)
-    d_tokens, d_norm_gain = tokens_call(
-        part, tie(d_v_long, rest_terms[0][0]), spill, pieces_v, places_v, lanes_whole,
-        tokens, cotangent, norm_gain.reshape(1, D),
-    )
-    rest_parts = [(kept, tie(got, d_tokens)) for kept, got in rest_parts]
+    part_gate = columns_call(tie(d_gate, rest_terms[0][0]), pieces_g, places_g, count_g, lanes_whole)
 
     heads = heads[:, :, 0].reshape(2, QUADS, 8)[:, :, :4].reshape(2, HEADS)
     d_skip = sums[KW + 1, :INNER].reshape(HEADS, HEAD_DIM).sum(axis=1)
@@ -1253,26 +1259,34 @@
     flat = jnp.pad(flat, (0, -width % 1024)).reshape(-1, 128)
     flat = flat + across(flat)
     small_bits = seq_bits[:1] + chip_bits + seq_bits[1:]
-    flat = flat + move(flat, flip(*small_bits[0]))
-
-    def four(value, first, second):
-        parts = [move(value, flip(*first)), move(value, flip(*second))]
-        corner = lambda s, f: flip(*first)(*flip(*second)(s, f))
-        return (value + parts[0]) + (parts[1] + move(value, corner))
-
-    all_bits = [("fsdp", 1)] + small_bits
-    pairs = [[gate_parts[part], rest_parts[part]] for part in range(3)]
-    for at in range(1, len(orders[0])):
-        sent = fold_call(pairs, "sent")
-        kept = fold_call(pairs, "kept")
-        pairs = [[(kept[part], move(sent[part], flip(*orders[part][at])))] for part in range(3)]
-        flat = flat + move(tie(flat, kept[0]), flip(*small_bits[at]))
-        use = all_bits[2 * at - 2 : 2 * at]
-        if len(use) == 2:
-            d_norm_gain = four(tie(d_norm_gain, kept[0]), *use)
-        elif use:
-            d_norm_gain = d_norm_gain + move(tie(d_norm_gain, kept[0]), flip(*use[0]))
-    (d_w_in,) = fold_call(pairs, "last", w_in.shape[1])
+    flat = flat + move(tie(flat, part_gate), flip(*small_bits[0]))
+
+    def summed(value, bits, taken=()):
+        if not bits:
+            return move(value, functools.reduce(lambda goal, bit: lambda s, f: flip(*bit)(*goal(s, f)), taken, lambda s, f: (s, f))) if taken else value
+        return summed(value, bits[:-1], taken) + summed(value, bits[:-1], taken + (bits[-1],))
+
+    all_bits = (("fsdp", 1),) + tuple(small_bits)
+    rounds = len(orders[0])
+    rest_parts = [(kept, tie(got, part_gate, flat)) for kept, got in rest_parts]
+    parts = [(list(gate_parts[part]), list(rest_parts[part]), []) for part in range(3)]
+    rows_left = rest_parts[0][0].shape[0]
+    for at in range(1, rounds):
+        rows_left //= 2
+        sent = fold_call(parts, rows_left, rows_left)
+        got = [move(sent[part], flip(*orders[part][at])) for part in range(3)]
+        if at == 1:
+            d_tokens, d_norm_gain = tokens_call(
+                tie(part_gate, sent[0]), d_v_long, spill, pieces_v, places_v, lanes_whole, tokens, cotangent, norm_gain.reshape(1, D)
+            )
+            got = [tie(array, d_tokens) for array in got]
+            flat = flat + move(tie(flat, d_tokens), flip(*small_bits[at]))
+        else:
+            d_norm_gain = tie(d_norm_gain, sent[0])
+            flat = flat + move(tie(flat, sent[0]), flip(*small_bits[at]))
+        d_norm_gain = summed(d_norm_gain, all_bits[2 * at - 2 :] if at + 1 == rounds else all_bits[2 * at - 2 : 2 * at])
+        parts = [(gate, rest, wide + [array]) for (gate, rest, wide), array in zip(parts, got)]
+    (d_w_in,) = fold_call(parts, 0, rows_left, w_in.shape[1])
     flat = flat.reshape(-1)
     small, at = [], 0
     for piece in pieces:

time: 478 us -> 470 us (0.983)
  Pallas kernels: 240 us -> 227 us
    pallas_call x7 -> x4, Pallas kernels: 25.7 us -> 13.5 us  [fold_call(): pl.pallas_call(functools.partial(fold_kernel, counts, rows, begin, bool(w...]
    unnamed x96 -> x84, local copies, waits for them, and re-layouts: 15.4 us -> 13.8 us
  transfers between devices with their start and end apart: 55 -> 55, of which waited for: 22 -> 22; matrix products, arithmetic and copies ran while one was open for 8% -> 9% of each run, Pallas kernels for 46% -> 44%
where the time goes in v5:
time: 470 us; the launch traced here: 461 us
  Pallas kernels  227 us (48%)
  waiting for transfers between devices  88.2 us (19%)
  starting transfers between devices  72.3 us (15%)
  local copies, waits for them, and re-layouts  40.2 us (9%)
  between operations  14.8 us (3%)
  matrix products  9.54 us (2%)
  other arithmetic  8.28 us (2%)
    ppermute x50, waiting for transfers between devices, move(): return lax.ppermute(value, both, pairs)  84.8 us
    ppermute x50, starting transfers between devices, move(): return lax.ppermute(value, both, pairs)  49.7 us
    pallas_call x1, Pallas kernels, back_call(): pl.pallas_call(back_kernel, grid=(QUADS + 2,), in_specs=[pl.BlockSpec((le...  41.7 us
    pallas_call x3, Pallas kernels, weight_call(): pl.pallas_call(functools.partial(weight_kernel, height, split, count), gr...  28.8 us
    pallas_call x2, Pallas kernels, grad_call(): pl.pallas_call(functools.partial(grad_kernel, halo), grid=(3,), in_specs=...  23.8 us
    all_to_all x4, starting transfers between devices, exchange(): lax.all_to_all(states, 'seq', split_axis=0, concat_axis=0, tiled=True)  22.5 us
    pallas_call x1, Pallas kernels, tokens_call(): pl.pallas_call(functools.partial(tokens_kernel, count, quarters), grid_sp...  19.5 us
    pallas_call x1, Pallas kernels, inside_call(): pl.pallas_call(inside_kernel, grid=(QUADS,), in_specs=[pl.BlockSpec((leng...  15.4 us
  transfers between devices with their start and end apart: 55, of which 22 were waited for; matrix products, arithmetic and copies ran while one was open for 9% of the time, Pallas kernels for 44%

profile of v5, /device:TPU:0, one launch (start us, length us, event | category | flops | bytes accessed | tf_op | source)
XLA Modules:
  0.0 460.7 jit_solution(8724628434715940325)
XLA Ops:
  10.8 4.4 collective-permute-start
  19.5 15.6 %collective-permute-done.2.rest_2_.refs_8_ = bf16[896,384]{1,0:T(8,128)(2,1)} collective-permute-done((bf16[896,384]{1,0:T(8,128)(2,1)S(1)}, bf16[896,384]{1,0:T(8,128)(2,1)}, u32[]{:S(2)}, u32[]{:S(2)}) %collective-permute-start.2) | collective-permute-done | bytes 688160 | tf_op jit(solution)/shard_map/ppermute | solution.py:1092
  36.6 2.4 collective-permute-start.3
  39.0 3.3 slice.90.rest_0_.refs_0_
  42.9 2.5 constant_dynamic-slice_fusion.2
  45.9 5.5 %collective-permute-done.4.rest_3_.refs_9_ = bf16[896,384]{1,0:T(8,128)(2,1)} collective-permute-done((bf16[896,384]{1,0:T(8,128)(2,1)}, bf16[896,384]{1,0:T(8,128)(2,1)}, u32[]{:S(2)}, u32[]{:S(2)}) %collective-permute-start.4) | collective-permute-done | bytes 688160 | tf_op jit(solution)/shard_map/ppermute | solution.py:1092
  51.4 2.5 collective-permute-start.5
  58.3 8.7 %project_near.1.rest_6_ = bf16[528,3584]{1,0:T(8,128)(2,1)} custom-call(s32[5]{0:T(128)} %stack.139.place_ref, bf16[528,1536]{1,0:T(8,128)(2,1)} %fusion.2.x_ref, bf16[3584,384]{1,0:T(8,128)(2,1)} %copy-done, bf16[3584,384]{1,0:T(8,128)(2,1)} %collective-permute-done.1.rest_1_.refs_7_, bf16[896,384]{1,0:T(8,128)(2,1)} %collective-permute-done.2.rest_2_.refs_8_, ...), custom_call_target="tpu_custom_call" | custom-call | flops 1000000 | bytes 1000000 | tf_op jit(solution)/shard_map/project_near/pallas_call | solution.py:713
  67.0 3.3 collective-permute-done.5.rest_3_.refs_11_
  70.3 2.1 collective-permute-done.9.rest_5_.refs_15_
  73.3 8.6 %project_far.1.dt_ref.v_ref = bf16[528,3584]{1,0:T(8,128)(2,1)} custom-call(s32[5]{0:T(128)} %stack.139.place_ref, bf16[528,1536]{1,0:T(8,128)(2,1)} %fusion.2.x_ref, bf16[3584,384]{1,0:T(8,128)(2,1)} %copy-done, bf16[3584,384]{1,0:T(8,128)(2,1)} %collective-permute-done.1.rest_1_.refs_7_, ...), custom_call_target="tpu_custom_call", output_to_operand_aliasing={{}: (8, {})} | custom-call | flops 1000000 | bytes 1000000 | tf_op jit(solution)/shard_map/project_far/pallas_call | solution.py:713
  85.0 2.7 steps.1
  87.7 14.1 %conv_states.1 = (bf16[512,3072]{1,0:T(8,128)(2,1)}, bf16[512,3328]{1,0:T(8,128)(2,1)}, bf16[512,128]{1,0:T(8,128)(2,1)}, bf16[512,128]{1,0:T(8,128)(2,1)}, bf16...) custom-call(bf16[528,3584]{1,0:T(8,128)(2,1)} %project_far.1.dt_ref.v_ref, ...), custom_call_target="tpu_custom_call" | custom-call | flops 1000000 | bytes 1000000 | tf_op jit(solution)/shard_map/conv_states/pallas_call | solution.py:199
  101.8 5.8 %all-to-all-start = ((bf16[8,16,3328]{2,1,0:T(8,128)(2,1)}), bf16[8,16,3328]{2,1,0:T(8,128)(2,1)S(1)}, u32[]{:S(2)}, u32[]{:S(2)}) async-start(bf16[8,16,3328]{2,1,0:T(8,128)(2,1)} %bitcast.89), calls=%async_computation | async-start | bytes 1703936 | tf_op jit(solution)/shard_map/all_to_all | solution.py:1136
  110.9 15.4 %ssd_inside.1.rest_0_.y_ref = f32[512,3072]{1,0:T(8,128)} custom-call(bf16[512,3072]{1,0:T(8,128)(2,1)} %get-tuple-element.97.x_ref, bf16[512,128]{1,0:T(8,128)(2,1)} %get-tuple-element.98.b_ref, bf16[512,128]{1,0:T(8,128)(2,1)} %get-tuple-element.99.c_ref, bf16[128,512]{1,0:T(8,128)(2,1)} %get-tuple-element.100.bt_ref, ...), custom_call_target="tpu_custom_call" | custom-call | flops 1000000 | bytes 1000000 | tf_op jit(solution)/shard_map/ssd_inside/pallas_call | solution.py:315
  126.2 3.0 all-to-all-done
  130.1 2.8 carry.1
  132.9 2.7 collective-permute-done.15.rest_0_.refs_6_
  135.6 6.4 %all-to-all-start.1 = ((bf16[8,16,3072]{2,1,0:T(8,128)(2,1)}), bf16[8,16,3072]{2,1,0:T(8,128)(2,1)}, u32[]{:S(2)}, u32[]{:S(2)}) async-start(bf16[8,16,3072]{2,1,0:T(8,128)(2,1)} %bitcast.91), calls=%async_computation.1 | async-start | bytes 1572864 | tf_op jit(solution)/shard_map/all_to_all | solution.py:1136
  142.3 2.2 collective-permute-done.12.rest_3_.refs_3_
  146.3 2.6 slice.89.x_ref
  151.0 11.5 %project_gate.1.gate_ref = bf16[512,3072]{1,0:T(8,128)(2,1)} custom-call(s32[5]{0:T(128)} %stack.139.place_ref, bf16[512,1536]{1,0:T(8,128)(2,1)} %slice.89.x_ref, bf16[3072,384]{1,0:T(8,128)(2,1)} %slice.90.rest_0_.refs_0_, bf16[3072,384]{1,0:T(8,128)(2,1)} %collective-permute-done.10.rest_1_.refs_1_, bf16[1536,384]{1,0:T(8,128)(2,1)} %copy-done.12, ...), custom_call_target="tpu_custom_call" | custom-call | flops 1000000 | bytes 1000000 | tf_op jit(solution)/shard_map/project_gate/pallas_call | solution.py:713
  162.8 7.6 %d_normed_out.2.rest_2_ = f32[512,3072]{1,0:T(8,128)} custom-call(s32[2]{0:T(128)} %pad_add_fusion.3.place_ref, bf16[512,1536]{1,0:T(8,128)(2,1)} %bitcast.77, bf16[768,1536]{1,0:T(8,128)(2,1)} %refs_4_.2, bf16[768,1536]{1,0:T(8,128)(2,1)} %collective-permute-done.17.rest_1_.refs_5_), custom_call_target="tpu_custom_call" | custom-call | flops 1000000 | bytes 1000000 | tf_op jit(solution)/shard_map/d_normed_out/pallas_call | solution.py:745
  170.5 7.6 %d_normed_out.3.dn_ref = f32[512,3072]{1,0:T(8,128)} custom-call(s32[2]{0:T(128)} %pad_add_fusion.2.place_ref, bf16[512,1536]{1,0:T(8,128)(2,1)} %bitcast.78, bf16[768,1536]{1,0:T(8,128)(2,1)} %collective-permute-done.15.rest_0_.refs_6_, bf16[768,1536]{1,0:T(8,128)(2,1)} %collective-permute-done.16.rest_1_.refs_7_, ...), custom_call_target="tpu_custom_call", output_to_operand_aliasing={{}: (4, {})} | custom-call | flops 1000000 | bytes 1000000 | tf_op jit(solution)/shard_map/d_normed_out/pallas_call | solution.py:745
  178.0 15.3 %gated_norm.1 = (bf16[512,3072]{1,0:T(8,128)(2,1)}, bf16[512,3072]{1,0:T(8,128)(2,1)}, bf16[512,3072]{1,0:T(8,128)(2,1)}, f32[1,3072]{1,0:T(1,128)}, bf16[128,3072]{1,0:T(8,128)(2,1)}) custom-call(f32[512,3072]{1,0:T(8,128)} %ssd_inside.1.rest_0_.y_ref, bf16[512,3072]{1,0:T(8,128)(2,1)} %project_gate.1.gate_ref, f32[512,3072]{1,0:T(8,128)} %d_normed_out.3.dn_ref, ...), custom_call_target="tpu_custom_call" | custom-call | flops 1000000 | bytes 1000000 | tf_op jit(solution)/shard_map/gated_norm/pallas_call | solution.py:396
  193.4 4.2 all-to-all-start.2
  197.9 9.5 %convolution_convert_fusion.rest_1_ = bf16[3072,1536]{1,0:T(8,128)(2,1)} fusion(bf16[512,3072]{1,0:T(8,128)(2,1)} %get-tuple-element.115.refs_0_.refs_1_.refs_2_.refs_3_, bf16[1,512,1536]{2,1,0:T(8,128)(2,1)S(1)} %copy-done.7), kind=kOutput, calls=%fused_computation | convolution fusion | flops 4836556800 | bytes 14155776 | tf_op jit(solution)/shard_map/dot_general | solution.py:1225
  207.5 11.3 %block_out.1.rest_2_ = f32[1,512,1536]{2,1,0:T(8,128)} custom-call(s32[4]{0:T(128)} %pad_add_fusion.1.place_ref, bf16[512,3072]{1,0:T(8,128)(2,1)} %get-tuple-element.115.refs_0_.refs_1_.refs_2_.refs_3_, bf16[512,3072]{1,0:T(8,128)(2,1)} %get-tuple-element.115.refs_0_.refs_1_.refs_2_.refs_3_, ...), custom_call_target="tpu_custom_call" | custom-call | flops 40000000000 | bytes 1000000 | tf_op jit(solution)/shard_map/block_out/pallas_call | solution.py:910
  219.7 2.8 carry_back.1
  222.4 6.2 %all-to-all-start.3 = ((bf16[8,16,3072]{2,1,0:T(8,128)(2,1)}), bf16[8,16,3072]{2,1,0:T(8,128)(2,1)}, u32[]{:S(2)}, u32[]{:S(2)}) async-start(bf16[8,16,3072]{2,1,0:T(8,128)(2,1)} %bitcast.87), calls=%async_computation.3 | async-start | bytes 1572864 | tf_op jit(solution)/shard_map/all_to_all | solution.py:1136
  234.5 7.6 %pick_rows.1 = (bf16[3,16,48,512]{3,2,1,0:T(8,128)(2,1)}, bf16[3,16,48,512]{3,2,1,0:T(8,128)(2,1)}, bf16[3,16,48,32]{3,2,1,0:T(8,128)(2,1)}) custom-call(s32[3,16]{1,0:T(4,128)} %pad_add_fusion.table_ref, bf16[16,48,512]{2,1,0:T(8,128)(2,1)} %get-tuple-element.176.own, bf16[16,48,512]{2,1,0:T(8,128)(2,1)} %copy-done.27, bf16[16,48,16]{2,1,0:T(8,128)(2,1)} %bitcast.90, ...), custom_call_target="tpu_custom_call" | custom-call | flops 1000000 | bytes 1000000 | tf_op jit(solution)/shard_map/pick_rows/pallas_call | solution.py:773
  242.2 10.5 %d_w_gate.1 = (bf16[384,1024]{1,0:T(8,128)(2,1)}, bf16[384,1024]{1,0:T(8,128)(2,1)}, bf16[384,1024]{1,0:T(8,128)(2,1)}, bf16[384,1024]{1,0:T(8,128)(2,1)}, bf16[...) custom-call(bf16[3,768,512]{2,1,0:T(8,128)(2,1)} %bitcast.79, bf16[3,768,512]{2,1,0:T(8,128)(2,1)} %bitcast.81, ...), custom_call_target="tpu_custom_call" | custom-call | flops 1000000 | bytes 1000000 | tf_op jit(solution)/shard_map/d_w_gate/pallas_call | solution.py:821
  257.3 41.7 %ssd_back.1 = (bf16[528,3584]{1,0:T(8,128)(2,1)}, f32[8,3328]{1,0:T(8,128)}, f32[2,96,128]{2,1,0:T(8,128)}) custom-call(bf16[512,3072]{1,0:T(8,128)(2,1)} %get-tuple-element.97.x_ref, bf16[512,3072]{1,0:T(8,128)(2,1)} %get-tuple-element.124.dm_ref, bf16[512,3328]{1,0:T(8,128)(2,1)} %get-tuple-element.125.slope_ref, ...), custom_call_target="tpu_custom_call" | custom-call | flops 40000000000 | bytes 1000000 | tf_op jit(solution)/shard_map/ssd_back/pallas_call | solution.py:597
  303.9 5.3 %collective-permute-done.25.refs_2_ = bf16[16,3584]{1,0:T(8,128)(2,1)S(1)} collective-permute-done((bf16[16,3584]{1,0:T(8,128)(2,1)S(1)}, bf16[16,3584]{1,0:T(8,128)(2,1)S(1)}, u32[]{:S(2)}, u32[]{:S(2)}) %collective-permute-start.25) | collective-permute-done | bytes 114720 | tf_op jit(solution)/shard_map/ppermute | solution.py:1092
  309.2 13.4 %d_w_rest.1 = (bf16[384,1152]{1,0:T(8,128)(2,1)}, bf16[384,1152]{1,0:T(8,128)(2,1)}, bf16[384,1152]{1,0:T(8,128)(2,1)}, bf16[384,1152]{1,0:T(8,128)(2,1)}, bf16[...) custom-call(bf16[3,768,512]{2,1,0:T(8,128)(2,1)} %bitcast.80, bf16[3,768,512]{2,1,0:T(8,128)(2,1)} %bitcast.82, ...), custom_call_target="tpu_custom_call" | custom-call | flops 1000000 | bytes 1000000 | tf_op jit(solution)/shard_map/d_w_rest/pallas_call | solution.py:821
  330.4 12.9 %d_normed_gate.1.refs_0_ = f32[512,1536]{1,0:T(8,128)} custom-call(s32[5]{0:T(128)} %stack.139.place_ref, bf16[512,3072]{1,0:T(8,128)(2,1)} %get-tuple-element.140.refs_2_.g_ref, bf16[3072,384]{1,0:T(8,128)(2,1)} %slice.90.rest_0_.refs_0_, bf16[3072,384]{1,0:T(8,128)(2,1)} %collective-permute-done.10.rest_1_.refs_1_, bf16[1536,384]{1,0:T(8,128)(2,1)} %copy-done.12, ...), custom_call_target="tpu_custom_call" | custom-call | flops 1000000 | bytes 1000000 | tf_op jit(solution)/shard_map/d_normed_gate/pallas_call | solution.py:963
  343.3 4.5 collective-permute-done.28
  347.9 5.5 %collective-permute-done.30.refs_11_.refs_13_.refs_15_.refs_17_ = bf16[384,1152]{1,0:T(8,128)(2,1)S(1)} collective-permute-done((bf16[384,1152]{1,0:T(8,128)(2,1)}, bf16[384,1152]{1,0:T(8,128)(2,1)S(1)}, u32[]{:S(2)}, u32[]{:S(2)}) %collective-permute-start.30) | collective-permute-done | bytes 884768 | tf_op jit(solution)/shard_map/ppermute | solution.py:1092
  354.4 4.0 fold.4
  361.8 19.5 %d_tokens.1 = (f32[1,512,1536]{2,1,0:T(8,128)}, f32[1,1536]{1,0:T(1,128)}) custom-call(s32[5]{0:T(128)} %stack.139.place_ref, f32[512,1536]{1,0:T(8,128)} %d_normed_gate.1.refs_0_, bf16[528,3584]{1,0:T(8,128)(2,1)} %get-tuple-element.137.refs_3_.refs_5_.refs_1_, bf16[16,3584]{1,0:T(8,128)(2,1)} %copy-done.32, bf16[1,512,1536]{2,1,0:T(8,128)(2,1)} %refs_3_.1, ...), custom_call_target="tpu_custom_call" | custom-call | flops 1000000 | bytes 1000000 | tf_op jit(solution)/shard_map/d_tokens/pallas_call | solution.py:1056
  382.3 2.4 collective-permute-done.33
  389.2 3.4 fold.5
  400.0 8.3 %collective-permute-done.41.refs_11_.refs_12_ = bf16[96,2176]{1,0:T(8,128)(2,1)S(1)} collective-permute-done((bf16[96,2176]{1,0:T(8,128)(2,1)}, bf16[96,2176]{1,0:T(8,128)(2,1)S(1)}, u32[]{:S(2)}, u32[]{:S(2)}) %collective-permute-start.41) | collective-permute-done | bytes 417824 | tf_op jit(solution)/shard_map/ppermute | solution.py:1092
  410.7 2.8 fold.6
  421.5 11.1 %collective-permute-done.43 = f32[1,1536]{1,0:T(1,128)S(1)} collective-permute-done((f32[1,1536]{1,0:T(1,128)S(1)}, f32[1,1536]{1,0:T(1,128)S(1)}, u32[]{:S(2)}, u32[]{:S(2)}) %collective-permute-start.43) | collective-permute-done | bytes 6176 | tf_op jit(solution)/shard_map/ppermute | solution.py:1092
  433.3 5.6 %collective-permute-done.49 = f32[160,128]{1,0:T(8,128)S(1)} collective-permute-done((f32[160,128]{1,0:T(8,128)S(1)}, f32[160,128]{1,0:T(8,128)S(1)}, u32[]{:S(2)}, u32[]{:S(2)}) %collective-permute-start.49) | collective-permute-done | bytes 81952 | tf_op jit(solution)/shard_map/ppermute | solution.py:1092
  443.3 3.7 collective-permute-done.46.refs_20_
  448.4 3.3 fold.7
  (228 shorter events, 87.7 us)
Async XLA Ops:
  9.5 47.7 %collective-permute-start.1 = (bf16[3584,384]{1,0:T(8,128)(2,1)S(1)}, bf16[3584,384]{1,0:T(8,128)(2,1)}, u32[]{:S(2)}, u32[]{:S(2)}) collective-permute-start(bf16[3584,384]{1,0:T(8,128)(2,1)S(1)} %pad.15.rest_0_.refs_6_), channel_id=1, source_target_pairs={{0,1},{1,0},{2,3},{3,2},{4,5},{5,4},{6,7},{7,6},{8,9},{9,8},{10,11... | collective-permute-start | bytes 8257544 | tf_op jit(solution)/shard_map/ppermute | solution.py:1092
  10.8 6.1 %collective-permute-start = (bf16[16,1536]{1,0:T(8,128)(2,1)S(1)}, bf16[16,1536]{1,0:T(8,128)(2,1)S(1)}, u32[]{:S(2)}, u32[]{:S(2)}) collective-permute-start(bf16[16,1536]{1,0:T(8,128)(2,1)S(1)} %slice_bitcast_fusion), channel_id=1, source_target_pairs={{0,4},{1,5},{2,6},{3,7},{4,8},{5,9},{6,10},{7,11},{8,12},{9,13},{1... | collective-permute-start | bytes 147464 | tf_op jit(solution)/shard_map/ppermute | solution.py:1092
  18.0 17.1 %collective-permute-start.2 = (bf16[896,384]{1,0:T(8,128)(2,1)S(1)}, bf16[896,384]{1,0:T(8,128)(2,1)}, u32[]{:S(2)}, u32[]{:S(2)}) collective-permute-start(bf16[896,384]{1,0:T(8,128)(2,1)S(1)} %get-tuple-element.174), channel_id=1, source_target_pairs={{0,2},{1,3},{2,0},{3,1},{4,6},{5,7},{6,4},{7,5},{8,10},{9,11},{10,... | collective-permute-start | bytes 2064392 | tf_op jit(solution)/shard_map/ppermute | solution.py:1092
  35.0 16.4 %collective-permute-start.4 = (bf16[896,384]{1,0:T(8,128)(2,1)}, bf16[896,384]{1,0:T(8,128)(2,1)}, u32[]{:S(2)}, u32[]{:S(2)}) collective-permute-start(bf16[896,384]{1,0:T(8,128)(2,1)} %get-tuple-element.93), channel_id=1, source_target_pairs={{0,2},{1,3},{2,0},{3,1},{4,6},{5,7},{6,4},{7,5},{8,10},{9,11},{10,... | collective-permute-start | bytes 2064392 | tf_op jit(solution)/shard_map/ppermute | solution.py:1092
  36.6 17.4 %collective-permute-start.3 = (bf16[896,384]{1,0:T(8,128)(2,1)}, bf16[896,384]{1,0:T(8,128)(2,1)S(1)}, u32[]{:S(2)}, u32[]{:S(2)}) collective-permute-start(bf16[896,384]{1,0:T(8,128)(2,1)} %collective-permute-done.2.rest_2_.refs_8_), channel_id=1, source_target_pairs={{0,4},{1,5},{2,6},{3,7},{4,0},{5,1},{6,2},{7,3},{8,12},{9,13},{10,... | collective-permute-start | bytes 2064392 | tf_op jit(solution)/shard_map/ppermute | solution.py:1092
  45.8 11.3 %collective-permute-start.7 = (bf16[896,384]{1,0:T(8,128)(2,1)}, bf16[896,384]{1,0:T(8,128)(2,1)S(1)}, u32[]{:S(2)}, u32[]{:S(2)}) collective-permute-start(bf16[896,384]{1,0:T(8,128)(2,1)} %collective-permute-done.2.rest_2_.refs_8_), channel_id=1, source_target_pairs={{0,1},{1,0},{2,3},{3,2},{4,5},{5,4},{6,7},{7,6},{8,9},{9,8},{10,11... | collective-permute-start | bytes 2064392 | tf_op jit(solution)/shard_map/ppermute | solution.py:1092
  51.4 5.7 %collective-permute-start.8 = (bf16[896,384]{1,0:T(8,128)(2,1)}, bf16[896,384]{1,0:T(8,128)(2,1)S(1)}, u32[]{:S(2)}, u32[]{:S(2)}) collective-permute-start(bf16[896,384]{1,0:T(8,128)(2,1)} %collective-permute-done.4.rest_3_.refs_9_), channel_id=1, source_target_pairs={{0,1},{1,0},{2,3},{3,2},{4,5},{5,4},{6,7},{7,6},{8,9},{9,8},{10,11... | collective-permute-start | bytes 2064392 | tf_op jit(solution)/shard_map/ppermute | solution.py:1092
  51.4 18.8 %collective-permute-start.5 = (bf16[896,384]{1,0:T(8,128)(2,1)}, bf16[896,384]{1,0:T(8,128)(2,1)S(1)}, u32[]{:S(2)}, u32[]{:S(2)}) collective-permute-start(bf16[896,384]{1,0:T(8,128)(2,1)} %collective-permute-done.4.rest_3_.refs_9_), channel_id=1, source_target_pairs={{0,4},{1,5},{2,6},{3,7},{4,0},{5,1},{6,2},{7,3},{8,12},{9,13},{10,... | collective-permute-start | bytes 2064392 | tf_op jit(solution)/shard_map/ppermute | solution.py:1092
  54.0 28.4 %collective-permute-start.11 = (bf16[1536,384]{1,0:T(8,128)(2,1)}, bf16[1536,384]{1,0:T(8,128)(2,1)S(1)}, u32[]{:S(2)}, u32[]{:S(2)}) collective-permute-start(bf16[1536,384]{1,0:T(8,128)(2,1)} %constant_dynamic-slice_fusion.2), channel_id=1, source_target_pairs={{0,2},{1,3},{2,0},{3,1},{4,6},{5,7},{6,4},{7,5},{8,10},{9,11},{10,... | collective-permute-start | bytes 3538952 | tf_op jit(solution)/shard_map/ppermute | solution.py:1092
  57.2 13.1 %collective-permute-start.6 = (bf16[896,384]{1,0:T(8,128)(2,1)S(1)}, bf16[896,384]{1,0:T(8,128)(2,1)S(1)}, u32[]{:S(2)}, u32[]{:S(2)}) collective-permute-start(bf16[896,384]{1,0:T(8,128)(2,1)S(1)} %collective-permute-done.3.rest_2_.refs_10_), channel_id=1, source_target_pairs={{0,1},{1,0},{2,3},{3,2},{4,5},{5,4},{6,7},{7,6},{8,9},{9,8},{10,11... | collective-permute-start | bytes 2064392 | tf_op jit(solution)/shard_map/ppermute | solution.py:1092
  82.3 53.3 %collective-permute-start.15 = (bf16[768,1536]{1,0:T(8,128)(2,1)}, bf16[768,1536]{1,0:T(8,128)(2,1)}, u32[]{:S(2)}, u32[]{:S(2)}) collective-permute-start(bf16[768,1536]{1,0:T(8,128)(2,1)} %refs_4_.2), channel_id=1, source_target_pairs={{0,2},{1,3},{2,0},{3,1},{4,6},{5,7},{6,4},{7,5},{8,10},{9,11},{10,... | collective-permute-start | bytes 7077896 | tf_op jit(solution)/shard_map/ppermute | solution.py:1092
  101.8 27.4 %all-to-all-start = ((bf16[8,16,3328]{2,1,0:T(8,128)(2,1)}), bf16[8,16,3328]{2,1,0:T(8,128)(2,1)S(1)}, u32[]{:S(2)}, u32[]{:S(2)}) async-start(bf16[8,16,3328]{2,1,0:T(8,128)(2,1)} %bitcast.89), calls=%async_computation | async-start | bytes 1703936 | tf_op jit(solution)/shard_map/all_to_all | solution.py:1136
  107.6 36.9 %collective-permute-start.12 = (bf16[1536,384]{1,0:T(8,128)(2,1)}, bf16[1536,384]{1,0:T(8,128)(2,1)}, u32[]{:S(2)}, u32[]{:S(2)}) collective-permute-start(bf16[1536,384]{1,0:T(8,128)(2,1)} %copy-done.12), channel_id=1, source_target_pairs={{0,4},{1,5},{2,6},{3,7},{4,0},{5,1},{6,2},{7,3},{8,12},{9,13},{10,... | collective-permute-start | bytes 3538952 | tf_op jit(solution)/shard_map/ppermute | solution.py:1092
  109.6 39.4 %collective-permute-start.10 = (bf16[3072,384]{1,0:T(8,128)(2,1)S(1)}, bf16[3072,384]{1,0:T(8,128)(2,1)}, u32[]{:S(2)}, u32[]{:S(2)}) collective-permute-start(bf16[3072,384]{1,0:T(8,128)(2,1)S(1)} %copy-done.1), channel_id=1, source_target_pairs={{0,1},{1,0},{2,3},{3,2},{4,5},{5,4},{6,7},{7,6},{8,9},{9,8},{10,11... | collective-permute-start | bytes 7077896 | tf_op jit(solution)/shard_map/ppermute | solution.py:1092
  109.6 53.2 %collective-permute-start.17 = (bf16[768,1536]{1,0:T(8,128)(2,1)}, bf16[768,1536]{1,0:T(8,128)(2,1)}, u32[]{:S(2)}, u32[]{:S(2)}) collective-permute-start(bf16[768,1536]{1,0:T(8,128)(2,1)} %refs_4_.2), channel_id=1, source_target_pairs={{0,1},{1,0},{2,3},{3,2},{4,5},{5,4},{6,7},{7,6},{8,9},{9,8},{10,11... | collective-permute-start | bytes 7077896 | tf_op jit(solution)/shard_map/ppermute | solution.py:1092
  135.6 34.8 %collective-permute-start.16 = (bf16[768,1536]{1,0:T(8,128)(2,1)}, bf16[768,1536]{1,0:T(8,128)(2,1)}, u32[]{:S(2)}, u32[]{:S(2)}) collective-permute-start(bf16[768,1536]{1,0:T(8,128)(2,1)} %collective-permute-done.15.rest_0_.refs_6_), channel_id=1, source_target_pairs={{0,1},{1,0},{2,3},{3,2},{4,5},{5,4},{6,7},{7,6},{8,9},{9,8},{10,11... | collective-permute-start | bytes 7077896 | tf_op jit(solution)/shard_map/ppermute | solution.py:1092
  135.6 27.2 %all-to-all-start.1 = ((bf16[8,16,3072]{2,1,0:T(8,128)(2,1)}), bf16[8,16,3072]{2,1,0:T(8,128)(2,1)}, u32[]{:S(2)}, u32[]{:S(2)}) async-start(bf16[8,16,3072]{2,1,0:T(8,128)(2,1)} %bitcast.91), calls=%async_computation.1 | async-start | bytes 1572864 | tf_op jit(solution)/shard_map/all_to_all | solution.py:1136
  142.0 7.0 %collective-permute-start.13 = (bf16[1536,384]{1,0:T(8,128)(2,1)S(1)}, bf16[1536,384]{1,0:T(8,128)(2,1)S(1)}, u32[]{:S(2)}, u32[]{:S(2)}) collective-permute-start(bf16[1536,384]{1,0:T(8,128)(2,1)S(1)} %copy-done.13), channel_id=1, source_target_pairs={{0,1},{1,0},{2,3},{3,2},{4,5},{5,4},{6,7},{7,6},{8,9},{9,8},{10,11... | collective-permute-start | bytes 3538952 | tf_op jit(solution)/shard_map/ppermute | solution.py:1092
  144.4 4.5 collective-permute-start.14
  193.4 25.4 %all-to-all-start.2 = ((bf16[8,16,3072]{2,1,0:T(8,128)(2,1)}), bf16[8,16,3072]{2,1,0:T(8,128)(2,1)S(1)}, u32[]{:S(2)}, u32[]{:S(2)}) async-start(bf16[8,16,3072]{2,1,0:T(8,128)(2,1)} %bitcast.92), calls=%async_computation.2 | async-start | bytes 1572864 | tf_op jit(solution)/shard_map/all_to_all | solution.py:1136
  197.6 254.2 %reduce-scatter.2.cloned.1.call-start = ((), (), s32[]{:S(2)}) async-start(), calls=%async_computation.5 | async-start | bytes 9732096 | tf_op jit(solution)/shard_map/reduce_scatter | solution.py:1226
  197.6 44.6 %collective-permute-start.20 = (bf16[512,3072]{1,0:T(8,128)(2,1)}, bf16[512,3072]{1,0:T(8,128)(2,1)}, u32[]{:S(2)}, u32[]{:S(2)}) collective-permute-start(bf16[512,3072]{1,0:T(8,128)(2,1)} %get-tuple-element.140.refs_2_.g_ref), channel_id=1, source_target_pairs={{0,1},{1,0},{2,3},{3,2},{4,5},{5,4},{6,7},{7,6},{8,9},{9,8},{10,11... | collective-permute-start | bytes 9437192 | tf_op jit(solution)/shard_map/ppermute | solution.py:1092
  222.4 30.3 %all-to-all-start.3 = ((bf16[8,16,3072]{2,1,0:T(8,128)(2,1)}), bf16[8,16,3072]{2,1,0:T(8,128)(2,1)}, u32[]{:S(2)}, u32[]{:S(2)}) async-start(bf16[8,16,3072]{2,1,0:T(8,128)(2,1)} %bitcast.87), calls=%async_computation.3 | async-start | bytes 1572864 | tf_op jit(solution)/shard_map/all_to_all | solution.py:1136
  252.7 46.3 %collective-permute-start.23 = (bf16[384,1024]{1,0:T(8,128)(2,1)}, bf16[384,1024]{1,0:T(8,128)(2,1)S(1)}, u32[]{:S(2)}, u32[]{:S(2)}) collective-permute-start(bf16[384,1024]{1,0:T(8,128)(2,1)} %get-tuple-element.136), channel_id=1, source_target_pairs={{0,8},{1,9},{2,10},{3,11},{4,12},{5,13},{6,14},{7,15},{8,0},{9,1},... | collective-permute-start | bytes 2359304 | tf_op jit(solution)/shard_map/ppermute | solution.py:1092
  254.7 44.3 %collective-permute-start.22 = (bf16[384,1024]{1,0:T(8,128)(2,1)}, bf16[384,1024]{1,0:T(8,128)(2,1)}, u32[]{:S(2)}, u32[]{:S(2)}) collective-permute-start(bf16[384,1024]{1,0:T(8,128)(2,1)} %get-tuple-element.134), channel_id=1, source_target_pairs={{0,2},{1,3},{2,0},{3,1},{4,6},{5,7},{6,4},{7,5},{8,10},{9,11},{10,... | collective-permute-start | bytes 2359304 | tf_op jit(solution)/shard_map/ppermute | solution.py:1092
  255.8 43.2 %collective-permute-start.21 = (bf16[384,1024]{1,0:T(8,128)(2,1)}, bf16[384,1024]{1,0:T(8,128)(2,1)}, u32[]{:S(2)}, u32[]{:S(2)}) collective-permute-start(bf16[384,1024]{1,0:T(8,128)(2,1)} %get-tuple-element.132), channel_id=1, source_target_pairs={{0,4},{1,5},{2,6},{3,7},{4,0},{5,1},{6,2},{7,3},{8,12},{9,13},{10,... | collective-permute-start | bytes 2359304 | tf_op jit(solution)/shard_map/ppermute | solution.py:1092
  299.0 10.2 %collective-permute-start.24 = (bf16[528,3584]{1,0:T(8,128)(2,1)}, bf16[528,3584]{1,0:T(8,128)(2,1)}, u32[]{:S(2)}, u32[]{:S(2)}) collective-permute-start(bf16[528,3584]{1,0:T(8,128)(2,1)} %get-tuple-element.137.refs_3_.refs_5_.refs_1_), channel_id=1, source_target_pairs={{0,1},{1,0},{2,3},{3,2},{4,5},{5,4},{6,7},{7,6},{8,9},{9,8},{10,11... | collective-permute-start | bytes 11354120 | tf_op jit(solution)/shard_map/ppermute | solution.py:1092
  301.9 7.3 %collective-permute-start.25 = (bf16[16,3584]{1,0:T(8,128)(2,1)S(1)}, bf16[16,3584]{1,0:T(8,128)(2,1)S(1)}, u32[]{:S(2)}, u32[]{:S(2)}) collective-permute-start(bf16[16,3584]{1,0:T(8,128)(2,1)S(1)} %slice.74), channel_id=1, source_target_pairs={{4,0},{5,1},{6,2},{7,3},{8,4},{9,5},{10,6},{11,7},{12,8},{13,9},{1... | collective-permute-start | bytes 344072 | tf_op jit(solution)/shard_map/ppermute | solution.py:1092
  322.6 25.3 %collective-permute-start.26 = (bf16[384,1152]{1,0:T(8,128)(2,1)}, bf16[384,1152]{1,0:T(8,128)(2,1)S(1)}, u32[]{:S(2)}, u32[]{:S(2)}) collective-permute-start(bf16[384,1152]{1,0:T(8,128)(2,1)} %get-tuple-element.141), channel_id=1, source_target_pairs={{0,4},{1,5},{2,6},{3,7},{4,0},{5,1},{6,2},{7,3},{8,12},{9,13},{10,... | collective-permute-start | bytes 2654216 | tf_op jit(solution)/shard_map/ppermute | solution.py:1092
  324.1 23.8 %collective-permute-start.29 = (bf16[384,1152]{1,0:T(8,128)(2,1)}, bf16[384,1152]{1,0:T(8,128)(2,1)S(1)}, u32[]{:S(2)}, u32[]{:S(2)}) collective-permute-start(bf16[384,1152]{1,0:T(8,128)(2,1)} %get-tuple-element.148), channel_id=1, source_target_pairs={{0,2},{1,3},{2,0},{3,1},{4,6},{5,7},{6,4},{7,5},{8,10},{9,11},{10,... | collective-permute-start | bytes 2654216 | tf_op jit(solution)/shard_map/ppermute | solution.py:1092
  325.0 28.4 %collective-permute-start.30 = (bf16[384,1152]{1,0:T(8,128)(2,1)}, bf16[384,1152]{1,0:T(8,128)(2,1)S(1)}, u32[]{:S(2)}, u32[]{:S(2)}) collective-permute-start(bf16[384,1152]{1,0:T(8,128)(2,1)} %get-tuple-element.151), channel_id=1, source_target_pairs={{0,8},{1,9},{2,10},{3,11},{4,12},{5,13},{6,14},{7,15},{8,0},{9,1},... | collective-permute-start | bytes 2654216 | tf_op jit(solution)/shard_map/ppermute | solution.py:1092
  343.3 4.5 collective-permute-start.28
  358.5 28.6 %collective-permute-start.35 = (bf16[192,2176]{1,0:T(8,128)(2,1)}, bf16[192,2176]{1,0:T(8,128)(2,1)S(1)}, u32[]{:S(2)}, u32[]{:S(2)}) collective-permute-start(bf16[192,2176]{1,0:T(8,128)(2,1)} %get-tuple-element.158), channel_id=1, source_target_pairs={{0,8},{1,9},{2,10},{3,11},{4,12},{5,13},{6,14},{7,15},{8,0},{9,1},... | collective-permute-start | bytes 2506760 | tf_op jit(solution)/shard_map/ppermute | solution.py:1092
  359.3 27.8 %collective-permute-start.36 = (bf16[192,2176]{1,0:T(8,128)(2,1)}, bf16[192,2176]{1,0:T(8,128)(2,1)S(1)}, u32[]{:S(2)}, u32[]{:S(2)}) collective-permute-start(bf16[192,2176]{1,0:T(8,128)(2,1)} %get-tuple-element.160), channel_id=1, source_target_pairs={{0,4},{1,5},{2,6},{3,7},{4,0},{5,1},{6,2},{7,3},{8,12},{9,13},{10,... | collective-permute-start | bytes 2506760 | tf_op jit(solution)/shard_map/ppermute | solution.py:1092
  360.2 26.9 %collective-permute-start.34 = (bf16[192,2176]{1,0:T(8,128)(2,1)}, bf16[192,2176]{1,0:T(8,128)(2,1)S(1)}, u32[]{:S(2)}, u32[]{:S(2)}) collective-permute-start(bf16[192,2176]{1,0:T(8,128)(2,1)} %get-tuple-element.153), channel_id=1, source_target_pairs={{0,2},{1,3},{2,0},{3,1},{4,6},{5,7},{6,4},{7,5},{8,10},{9,11},{10,... | collective-permute-start | bytes 2506760 | tf_op jit(solution)/shard_map/ppermute | solution.py:1092
  385.3 10.8 %collective-permute-start.47 = (f32[160,128]{1,0:T(8,128)S(1)}, f32[160,128]{1,0:T(8,128)S(1)}, u32[]{:S(2)}, u32[]{:S(2)}) collective-permute-start(f32[160,128]{1,0:T(8,128)S(1)} %fusion.8), channel_id=1, source_target_pairs={{0,2},{1,3},{2,0},{3,1},{4,6},{5,7},{6,4},{7,5},{8,10},{9,11},{10,... | collective-permute-start | bytes 245768 | tf_op jit(solution)/shard_map/ppermute | solution.py:1092
  392.5 5.6 %collective-permute-start.39 = (f32[1,1536]{1,0:T(1,128)S(1)}, f32[1,1536]{1,0:T(1,128)S(1)}, u32[]{:S(2)}, u32[]{:S(2)}) collective-permute-start(f32[1,1536]{1,0:T(1,128)S(1)} %add_add_fusion.1), channel_id=1, source_target_pairs={{0,10},{1,11},{2,8},{3,9},{4,14},{5,15},{6,12},{7,13},{8,2},{9,3},... | collective-permute-start | bytes 18440 | tf_op jit(solution)/shard_map/ppermute | solution.py:1092
  394.3 5.0 %collective-permute-start.38 = (f32[1,1536]{1,0:T(1,128)S(1)}, f32[1,1536]{1,0:T(1,128)S(1)}, u32[]{:S(2)}, u32[]{:S(2)}) collective-permute-start(f32[1,1536]{1,0:T(1,128)S(1)} %add_add_fusion.1), channel_id=1, source_target_pairs={{0,8},{1,9},{2,10},{3,11},{4,12},{5,13},{6,14},{7,15},{8,0},{9,1},... | collective-permute-start | bytes 18440 | tf_op jit(solution)/shard_map/ppermute | solution.py:1092
  395.0 5.0 %collective-permute-start.37 = (f32[1,1536]{1,0:T(1,128)S(1)}, f32[1,1536]{1,0:T(1,128)S(1)}, u32[]{:S(2)}, u32[]{:S(2)}) collective-permute-start(f32[1,1536]{1,0:T(1,128)S(1)} %add_add_fusion.1), channel_id=1, source_target_pairs={{0,2},{1,3},{2,0},{3,1},{4,6},{5,7},{6,4},{7,5},{8,10},{9,11},{10,... | collective-permute-start | bytes 18440 | tf_op jit(solution)/shard_map/ppermute | solution.py:1092
  396.0 13.1 %collective-permute-start.40 = (bf16[96,2176]{1,0:T(8,128)(2,1)}, bf16[96,2176]{1,0:T(8,128)(2,1)S(1)}, u32[]{:S(2)}, u32[]{:S(2)}) collective-permute-start(bf16[96,2176]{1,0:T(8,128)(2,1)} %get-tuple-element.162), channel_id=1, source_target_pairs={{0,8},{1,9},{2,10},{3,11},{4,12},{5,13},{6,14},{7,15},{8,0},{9,1},... | collective-permute-start | bytes 1253384 | tf_op jit(solution)/shard_map/ppermute | solution.py:1092
  397.6 18.0 %collective-permute-start.48 = (f32[160,128]{1,0:T(8,128)S(1)}, f32[160,128]{1,0:T(8,128)S(1)}, u32[]{:S(2)}, u32[]{:S(2)}) collective-permute-start(f32[160,128]{1,0:T(8,128)S(1)} %add.205), channel_id=1, source_target_pairs={{0,8},{1,9},{2,10},{3,11},{4,12},{5,13},{6,14},{7,15},{8,0},{9,1},... | collective-permute-start | bytes 245768 | tf_op jit(solution)/shard_map/ppermute | solution.py:1092
  398.1 10.2 %collective-permute-start.41 = (bf16[96,2176]{1,0:T(8,128)(2,1)}, bf16[96,2176]{1,0:T(8,128)(2,1)S(1)}, u32[]{:S(2)}, u32[]{:S(2)}) collective-permute-start(bf16[96,2176]{1,0:T(8,128)(2,1)} %get-tuple-element.164), channel_id=1, source_target_pairs={{0,4},{1,5},{2,6},{3,7},{4,0},{5,1},{6,2},{7,3},{8,12},{9,13},{10,... | collective-permute-start | bytes 1253384 | tf_op jit(solution)/shard_map/ppermute | solution.py:1092
  399.3 9.9 %collective-permute-start.42 = (bf16[96,2176]{1,0:T(8,128)(2,1)}, bf16[96,2176]{1,0:T(8,128)(2,1)S(1)}, u32[]{:S(2)}, u32[]{:S(2)}) collective-permute-start(bf16[96,2176]{1,0:T(8,128)(2,1)} %get-tuple-element.165), channel_id=1, source_target_pairs={{0,2},{1,3},{2,0},{3,1},{4,6},{5,7},{6,4},{7,5},{8,10},{9,11},{10,... | collective-permute-start | bytes 1253384 | tf_op jit(solution)/shard_map/ppermute | solution.py:1092
  413.5 19.1 %collective-permute-start.43 = (f32[1,1536]{1,0:T(1,128)S(1)}, f32[1,1536]{1,0:T(1,128)S(1)}, u32[]{:S(2)}, u32[]{:S(2)}) collective-permute-start(f32[1,1536]{1,0:T(1,128)S(1)} %add_add_fusion), channel_id=1, source_target_pairs={{0,16},{1,17},{2,18},{3,19},{4,20},{5,21},{6,22},{7,23},{8,24},{9,... | collective-permute-start | bytes 18440 | tf_op jit(solution)/shard_map/ppermute | solution.py:1092
  415.6 31.5 %collective-permute-start.44 = (bf16[48,2176]{1,0:T(8,128)(2,1)}, bf16[48,2176]{1,0:T(8,128)(2,1)S(1)}, u32[]{:S(2)}, u32[]{:S(2)}) collective-permute-start(bf16[48,2176]{1,0:T(8,128)(2,1)} %get-tuple-element.166), channel_id=1, source_target_pairs={{0,16},{1,17},{2,18},{3,19},{4,20},{5,21},{6,22},{7,23},{8,24},{9,... | collective-permute-start | bytes 626696 | tf_op jit(solution)/shard_map/ppermute | solution.py:1092
  416.5 22.4 %collective-permute-start.49 = (f32[160,128]{1,0:T(8,128)S(1)}, f32[160,128]{1,0:T(8,128)S(1)}, u32[]{:S(2)}, u32[]{:S(2)}) collective-permute-start(f32[160,128]{1,0:T(8,128)S(1)} %add.206), channel_id=1, source_target_pairs={{0,16},{1,17},{2,18},{3,19},{4,20},{5,21},{6,22},{7,23},{8,24},{9,... | collective-permute-start | bytes 245768 | tf_op jit(solution)/shard_map/ppermute | solution.py:1092
  418.6 24.8 %collective-permute-start.45 = (bf16[48,2176]{1,0:T(8,128)(2,1)}, bf16[48,2176]{1,0:T(8,128)(2,1)S(1)}, u32[]{:S(2)}, u32[]{:S(2)}) collective-permute-start(bf16[48,2176]{1,0:T(8,128)(2,1)} %get-tuple-element.168), channel_id=1, source_target_pairs={{0,16},{1,17},{2,18},{3,19},{4,20},{5,21},{6,22},{7,23},{8,24},{9,... | collective-permute-start | bytes 626696 | tf_op jit(solution)/shard_map/ppermute | solution.py:1092
  419.4 27.6 %collective-permute-start.46 = (bf16[48,2176]{1,0:T(8,128)(2,1)}, bf16[48,2176]{1,0:T(8,128)(2,1)S(1)}, u32[]{:S(2)}, u32[]{:S(2)}) collective-permute-start(bf16[48,2176]{1,0:T(8,128)(2,1)} %get-tuple-element.169), channel_id=1, source_target_pairs={{0,16},{1,17},{2,18},{3,19},{4,20},{5,21},{6,22},{7,23},{8,24},{9,... | collective-permute-start | bytes 626696 | tf_op jit(solution)/shard_map/ppermute | solution.py:1092
  (49 other events, 379.8 us)
Sparse Core Ops, SparseCore 0:
  207.6 159.2 reduce-scatter.1
